TPU v7x, 128 devices: a whole 4x4x4 slice. The times are simulated.
128 devices in a mesh: curve: 8 (over x, core), seg: 16 (over y, z).
Axes of the slice: x: 4, y: 4, z: 4, core: 2. Of those that a mesh axis runs over, the one named last changes fastest.
Arguments:
- adjoint: float32 [9, 8192, 512], P(None, ('curve', 'seg')), may hold values from -6 to 6
- material: float32 [3, 8192], P(None, ('curve', 'seg')), may hold values from 0.5 to 2
- face_partner: int32 [8192, 6], P(('curve', 'seg')), may hold values from 0 to 447, as said below
- send_faces: int32 [128, 4, 16], P(('curve', 'seg')), may hold values from 0 to 383, as said below
- migration: int32 [3, 8192], P(None, ('curve', 'seg')), may hold values from 0 to 15, as said below
- children: int32 [2, 1024], P(None, ('curve', 'seg')), may hold values from -1 to 15, as said below
Outputs:
- adjoint_next: float32 [9, 8192, 512], P(None, ('curve', 'seg'))
- parent_adjoint: float32 [9, 1024, 512], P(None, ('curve', 'seg'))
Inputs may be any that keep to these rules, and one draw needn't show every extreme that they name: `face_partner`: Each face is the partner of exactly one face. `send_faces`: slot t of side -x or +x is the face at position (t // 4, t % 4) in (y, z), of side -y or +y at (x, z); entries are 6 l + f of this partition's elements. `migration`: the eight children of each parent lie on one partition of the owner's segment group, one per octant. Each partition keeps all children of 4 of its own parents (row 1 is then the parent) and holds the children of 4 foreign parents (row 1 is then the slot, below 2, unique per owner). At most 2 foreign parents of one owner lie on one partition, and some partition holds exactly 2 for some owner. Row 0 is the owner itself with row 1 equal to -1 for the 4 parents whose children stayed; otherwise the holder and the slot of the matching migration entry.
All inputs are finite; a program needn't handle non-finite values.
Results may differ from a plain program's by a relative error of at most 0.000052.
Values sent between devices are 32-bit elements; how exact they have to be, the bound alone decides.
No kernel may reach another device: no remote copies, remote signals or barrier semaphores. Data moves between devices by JAX's collectives and lax.ppermute only.
A program may use at most 128 MiB of HBM per device.

v0:
```python
import functools

import jax
import jax.numpy as jnp
import numpy as np
from jax import lax
from jax.experimental import pallas as pl
from jax.experimental.pallas import tpu as pltpu
from jax.sharding import PartitionSpec as P

NP = 8
NODES = 512
E_DEV = 64
CAP = 16
P_DEV = 8
N_CURVE = 8
N_SEG = 16
LOCAL = 6 * E_DEV

voigt_index = ((3, 8, 7), (8, 4, 6), (7, 6, 5))
time_step = 0.8 / (NP * NP)
lift_half = 0.25 * NP * (NP - 1)
BF = jnp.bfloat16
F32 = jnp.float32


def lobatto_nodes(edge_nodes):
    return -np.cos(np.pi * np.arange(edge_nodes) / (edge_nodes - 1))


def derivative_line(edge_nodes):
    points = lobatto_nodes(edge_nodes)
    node_ids = np.arange(edge_nodes)
    weight = np.where((node_ids == 0) | (node_ids == edge_nodes - 1), 2.0, 1.0)
    row_ids = node_ids[:, None]
    column_ids = node_ids[None, :]
    differ = points[:, None] - points[None, :]
    safe_gap = np.where(row_ids == column_ids, 1.0, differ)
    matrix = weight[:, None] / weight[None, :] * (-1.0) ** (row_ids + column_ids) / safe_gap
    matrix = np.where(row_ids == column_ids, 0.0, matrix)
    return matrix - np.eye(edge_nodes) * matrix.sum(axis=1)[:, None]


def refine_line(edge_nodes, upper):
    points = lobatto_nodes(edge_nodes)
    targets = (points + (2.0 * upper - 1.0)) / 2.0
    columns = []
    for column in range(edge_nodes):
        factor = np.ones(edge_nodes)
        for other_node in range(edge_nodes):
            if other_node != column:
                factor = (
                    factor * (targets - points[other_node]) / (points[column] - points[other_node])
                )
        columns.append(factor)
    return np.stack(columns, axis=1)


def refine_parts():
    blocks = []
    for octant in range(8):
        lines = [refine_line(NP, octant // 4 % 2), refine_line(NP, octant // 2 % 2), refine_line(NP, octant % 2)]
        blocks.append(np.kron(np.kron(lines[0], lines[1]), lines[2]))
    whole = np.stack(blocks).astype(np.float32)
    high = whole.astype(BF)
    low = (whole - high.astype(np.float32)).astype(BF)
    return high, low


_line = derivative_line(NP)
_line[0, 0] += lift_half
_line[7, 7] -= lift_half
ODD = 0.5 * (_line[:4, :4] - _line[:3:-1, :4])
EVEN = 0.5 * (_line[:4, :4] + _line[:3:-1, :4])


def line_product(x):
    odd = [x[a] - x[7 - a] for a in range(4)]
    even = [x[a] + x[7 - a] for a in range(4)]
    out = [None] * 8
    for m in range(4):
        p = sum(odd[a] * float(ODD[a, m]) for a in range(4))
        q = sum(even[a] * float(EVEN[a, m]) for a in range(4))
        out[m] = p + q
        out[7 - m] = p - q
    return out


def low_half():
    return lax.broadcasted_iota(jnp.int32, (8, 128), 1) < 64


def swap_halves(x):
    return pltpu.roll(x, 64, 1)


def lane_patterns():
    low = low_half()
    out = []
    for matrix in (ODD, EVEN):
        straight = [[None] * 2 for _ in range(2)]
        crossed = [[None] * 2 for _ in range(2)]
        for j in range(2):
            for m in range(2):
                straight[j][m] = jnp.where(low, float(matrix[2 * j, 2 * m]), float(matrix[2 * j + 1, 2 * m + 1]))
                crossed[j][m] = jnp.where(low, float(matrix[2 * j + 1, 2 * m]), float(matrix[2 * j, 2 * m + 1]))
        out.append((straight, crossed))
    return out


def lane_product(x, patterns):
    back = [swap_halves(x[3]), swap_halves(x[2])]
    sums = []
    for parts, (straight, crossed) in zip(
        ([x[0] - back[0], x[1] - back[1]], [x[0] + back[0], x[1] + back[1]]), patterns
    ):
        turned = [swap_halves(part) for part in parts]
        sums.append(
            [
                parts[0] * straight[0][m] + turned[0] * crossed[0][m] + parts[1] * straight[1][m] + turned[1] * crossed[1][m]
                for m in range(2)
            ]
        )
    p, q = sums
    return [p[0] + q[0], p[1] + q[1], swap_halves(p[1] - q[1]), swap_halves(p[0] - q[0])]


def split(x):
    high = x.astype(BF)
    return high, (x - high.astype(F32)).astype(BF)


def along(k, start=None):
    return pl.ds(k, 8, stride=8)


def image_rows(get, mat, direction):
    inv_density, lame, shear = mat
    trace = get(3) + get(4) + get(5)
    out = []
    for k in range(3):
        term = shear * get(voigt_index[direction][k])
        if k == direction:
            term = 2.0 * term + lame * trace
        out.append(term)
    return out + [inv_density * get(i) for i in range(3)]


def target_row(value, direction):
    return value if value < 3 else voigt_index[value - 3][direction]


def build_table(v_ref, mat, t_ref):
    low = low_half()

    def put(value, block, direction, x0, x1):
        pair = jnp.concatenate([x0, x1], axis=0)
        high, rest = split(pair)
        rows = pl.ds(value * 64 + block * 16, 16)
        t_ref[rows, pl.ds(direction * 128, 128)] = high
        t_ref[rows, pl.ds(LOCAL + direction * 128, 128)] = rest

    for direction in range(2):
        for j in range(4):
            if direction == 0:
                ends = [image_rows(lambda i, r=r: v_ref[i, j, pl.ds(r, 8), :], mat, 0) for r in (0, 56)]
            else:
                ends = [image_rows(lambda i, r=r: v_ref[i, j, along(r), :], mat, 1) for r in (0, 7)]
            for value in range(6):
                a0, a1 = ends[0][value], ends[1][value]
                put(
                    value,
                    j,
                    direction,
                    jnp.where(low, a0, swap_halves(a1)),
                    jnp.where(low, swap_halves(a0), a1),
                )
    for pair in range(4):
        blocks = []
        for b in (2 * pair, 2 * pair + 1):
            blocks.append(
                image_rows(
                    lambda i, b=b: jnp.where(
                        low, v_ref[i, 0, along(b), :], v_ref[i, 3, along(b), :]
                    ),
                    mat,
                    2,
                )
            )
        for value in range(6):
            put(value, pair, 2, blocks[0][value], blocks[1][value])


def materials(mat_ref):
    return mat_ref[0], mat_ref[1], mat_ref[2]


def send_values(send_ref, t_ref, out_refs):
    rows = lax.dot_general(
        send_ref[...], t_ref[...], (((1,), (1,)), ((), ())), preferred_element_type=F32
    )
    for k in range(4):
        out_refs[k][...] = rows[16 * k : 16 * k + 16]


def begin_kernel(
    adjoint_ref, mat_ref, partner_ref, sent_ref,
    v_ref, t_ref, local_ref, remote_ref, send_ref, p0, p1, p2, p3, turn_ref,
):
    low = lax.broadcasted_iota(jnp.int32, (64, 128), 1) < 64

    def body(i, carry):
        x = adjoint_ref[i]
        turn_ref[...] = jnp.concatenate([x, x], axis=0).T
        for j in range(4):
            v_ref[i, j] = jnp.where(
                low, turn_ref[pl.ds(2 * j, 64, stride=8), :], turn_ref[pl.ds(2 * j + 1, 64, stride=8), :]
            )
        return carry

    lax.fori_loop(0, 9, body, 0)
    partner = partner_ref[...]
    face = lax.broadcasted_iota(jnp.int32, (1, LOCAL), 1) // 64
    weight = jnp.where(face % 2 == 0, lift_half, -lift_half)
    for start in range(0, LOCAL, 64):
        source = lax.broadcasted_iota(jnp.int32, (64, LOCAL), 0) + start
        block = jnp.where(source == partner, weight, 0.0).astype(BF)
        local_ref[pl.ds(start, 64), :] = block
        local_ref[pl.ds(LOCAL + start, 64), :] = block
    source = lax.broadcasted_iota(jnp.int32, (64, LOCAL), 0) + LOCAL
    block = jnp.where(source == partner, weight, 0.0).astype(BF)
    remote_ref[pl.ds(0, 64), :] = block
    remote_ref[pl.ds(64, 64), :] = block
    chosen = jnp.where(
        lax.broadcasted_iota(jnp.int32, (64, LOCAL), 1) == sent_ref[...], 1.0, 0.0
    ).astype(BF)
    send_ref[:, pl.ds(0, LOCAL)] = chosen
    send_ref[:, pl.ds(LOCAL, LOCAL)] = chosen
    build_table(v_ref, materials(mat_ref), t_ref)
    send_values(send_ref, t_ref, (p0, p1, p2, p3))


def first_volume_kernel(v_ref, t_ref, local_ref, mat_ref, vol_ref, part_ref):
    volume_kernel(v_ref, t_ref, local_ref, mat_ref, None, vol_ref, part_ref, None)


def volume_kernel(v_ref, t_ref, local_ref, mat_ref, acc_ref, vol_ref, part_ref, sum_ref):
    mat = materials(mat_ref)
    inv_density, lame, shear = mat

    def scaled(get, direction):
        out = []
        for k in range(3):
            if k == direction:
                out.append(
                    (k, [2.0 * shear * d + lame * (s0 + s1 + s2) for d, s0, s1, s2 in zip(get(3 + k), get(3), get(4), get(5))])
                )
            else:
                out.append((k, [shear * x for x in get(voigt_index[direction][k])]))
        for i in range(3):
            out.append((voigt_index[i][direction], [inv_density * x for x in get(i)]))
        return out

    def tiles(j, carry):
        for row, x in scaled(lambda i: [v_ref[i, j, along(b), :] for b in range(8)], 1):
            for b, y in enumerate(line_product(x)):
                vol_ref[row, j, along(b), :] = y
        for row, x in scaled(lambda i: [v_ref[i, j, pl.ds(8 * a, 8), :] for a in range(8)], 0):
            for a, y in enumerate(line_product(x)):
                if row not in (3, 7):
                    y = y + vol_ref[row, j, pl.ds(8 * a, 8), :]
                vol_ref[row, j, pl.ds(8 * a, 8), :] = y
        return carry

    lax.fori_loop(0, 4, tiles, 0)
    patterns = lane_patterns()

    def groups(a, carry):
        rows = pl.ds(pl.multiple_of(a * 8, 8), 8)
        for row, x in scaled(lambda i: [v_ref[i, j, rows, :] for j in range(4)], 2):
            for j, y in enumerate(lane_product(x, patterns)):
                if row != 5:
                    y = y + vol_ref[row, j, rows, :]
                vol_ref[row, j, rows, :] = y
        if sum_ref is not None:
            for i in range(9):
                for j in range(4):
                    sum_ref[i, j, rows, :] = acc_ref[i, j, rows, :] + v_ref[i, j, rows, :]
        return carry

    lax.fori_loop(0, 8, groups, 0)
    for k in range(6):
        part_ref[pl.ds(64 * k, 64), :] = jnp.dot(
            t_ref[pl.ds(64 * k, 64), :], local_ref[...], preferred_element_type=F32
        )


def add_faces(vol_ref, part_ref, r_refs, remote_ref, factor, out_ref, face_ref):
    for i in range(9):
        out_ref[i] = vol_ref[i] * factor
    arrived = jnp.concatenate([r[...] for r in r_refs], axis=0).T
    both = jnp.concatenate(split(arrived), axis=1)
    face_ref[...] = (part_ref[...] + jnp.dot(both, remote_ref[...], preferred_element_type=F32)) * factor
    low = low_half()
    for direction in range(3):
        for value in range(6):
            row = target_row(value, direction)
            for j in range(4):
                x0 = face_ref[pl.ds(value * 64 + 16 * j, 8), pl.ds(direction * 128, 128)]
                x1 = face_ref[pl.ds(value * 64 + 16 * j + 8, 8), pl.ds(direction * 128, 128)]
                if direction < 2:
                    y0 = jnp.where(low, x0, swap_halves(x1))
                    y1 = jnp.where(low, swap_halves(x0), x1)
                    rows = (pl.ds(0, 8), pl.ds(56, 8)) if direction == 0 else (along(0), along(7))
                    out_ref[row, j, rows[0], :] += y0
                    out_ref[row, j, rows[1], :] += y1
                else:
                    for b, x in ((2 * j, x0), (2 * j + 1, x1)):
                        out_ref[row, 0, along(b), :] += jnp.where(low, x, 0.0)
                        out_ref[row, 3, along(b), :] += jnp.where(low, 0.0, x)


def finish_kernel(
    factor, vol_ref, part_ref, r0, r1, r2, r3, remote_ref, mat_ref, send_ref,
    v_ref, t_ref, p0, p1, p2, p3, face_ref,
):
    add_faces(vol_ref, part_ref, (r0, r1, r2, r3), remote_ref, factor, v_ref, face_ref)
    build_table(v_ref, materials(mat_ref), t_ref)
    send_values(send_ref, t_ref, (p0, p1, p2, p3))


def end_kernel(
    factor, keys_ref, vol_ref, part_ref, r0, r1, r2, r3, remote_ref, acc_ref, place_ref, high_ref, low_ref,
    next_ref, home_ref, away_ref, v_ref, face_ref, turn_ref, sorted_ref, parent_ref,
):
    add_faces(vol_ref, part_ref, (r0, r1, r2, r3), remote_ref, factor, v_ref, face_ref)
    place = jnp.where(
        lax.broadcasted_iota(jnp.int32, (64, 64), 0) == place_ref[...], 1.0, 0.0
    ).astype(BF)

    def body(i, carry):
        for j in range(4):
            tile = acc_ref[i, j] + v_ref[i, j]
            turn_ref[pl.ds(2 * j, 64, stride=8), :] = tile
            turn_ref[pl.ds(2 * j + 1, 64, stride=8), :] = pltpu.roll(tile, 64, 1)
        x = turn_ref[...].T[:64]
        next_ref[i] = x
        high, rest = split(x)
        sorted_ref[i] = (
            jnp.dot(place, high, preferred_element_type=F32)
            + jnp.dot(place, rest, preferred_element_type=F32)
        )
        return carry

    lax.fori_loop(0, 9, body, 0)
    parent_ref[...] = jnp.zeros_like(parent_ref)

    def octants(c, carry):
        x = jnp.concatenate(
            [sorted_ref[i, pl.ds(pl.multiple_of(c * 8, 8), 8), :] for i in range(9)]
            + [jnp.zeros((8, NODES), F32)],
            axis=0,
        )
        high, rest = split(x)
        parent_ref[...] += (
            jnp.dot(high, high_ref[c], preferred_element_type=F32)
            + jnp.dot(rest, high_ref[c], preferred_element_type=F32)
            + jnp.dot(high, low_ref[c], preferred_element_type=F32)
        )
        return carry

    lax.fori_loop(0, 8, octants, 0)
    away_ref[...] = jnp.zeros_like(away_ref)
    home_ref[...] = jnp.zeros_like(home_ref)
    for g in range(P_DEV):
        key = keys_ref[g]

        @pl.when(key < P_DEV)
        def _():
            for i in range(9):
                home_ref[i, pl.ds(key, 1), :] = parent_ref[pl.ds(8 * i + g, 1), :]

        @pl.when(key >= P_DEV)
        def _():
            owner = (key - P_DEV) // 2
            slot = (key - P_DEV) % 2
            for i in range(9):
                for j in range(4):
                    away_ref[owner, i, pl.ds(slot * 4 + j, 1), :] = parent_ref[
                        pl.ds(8 * i + g, 1), pl.ds(128 * j, 128)
                    ]


def parent_kernel(table_ref, home_ref, arrived_ref, out_ref):
    out_ref[...] = home_ref[...]
    for p in range(P_DEV):
        holder = table_ref[0, p]
        slot = table_ref[1, p]

        @pl.when(slot >= 0)
        def _():
            for i in range(9):
                for j in range(4):
                    out_ref[i, pl.ds(p, 1), pl.ds(128 * j, 128)] = arrived_ref[
                        holder, i, pl.ds(slot * 4 + j, 1), :
                    ]


def shape(*dims, dtype=F32):
    return jax.ShapeDtypeStruct(dims, dtype)


VMEM = pl.BlockSpec(memory_space=pltpu.VMEM)
SMEM = pl.BlockSpec(memory_space=pltpu.SMEM)


def call(kernel, outs, scratch=(), smem=(), count=0, flops=10**8, traffic=6 * 10**6):
    return pl.pallas_call(
        kernel,
        out_shape=outs,
        in_specs=[SMEM if k in smem else VMEM for k in range(count)],
        out_specs=jax.tree.map(lambda _: VMEM, outs),
        scratch_shapes=list(scratch),
        compiler_params=pltpu.CompilerParams(vmem_limit_bytes=32 * 2**20),
        cost_estimate=pl.CostEstimate(flops=flops, bytes_accessed=traffic, transcendentals=0),
    )


def exchange_pairs():
    along_x = [[(k, (k + 1) % N_CURVE) for k in range(start, N_CURVE, 2)] for start in (0, 1)]
    along_y = [[(k, (k + 1) % N_SEG) for k in range(start, N_SEG, 2)] for start in (0, 1)]
    both = lambda pairs: pairs + [(b, a) for a, b in pairs]
    return [("curve", both(p)) for p in along_x] + [("seg", both(p)) for p in along_y]


def shards(adjoint, material, face_partner, send_faces, migration, children):
    own_curve = lax.axis_index("curve")
    own_seg = lax.axis_index("seg")
    double = lambda x: jnp.broadcast_to(jnp.concatenate([x, x])[None, :], (8, 128))
    mat = jnp.stack([double(1.0 / material[0]), double(material[1]), double(material[2])])
    even_x = (own_curve % 2 == 0).astype(jnp.int32)
    even_y = (own_seg % 2 == 0).astype(jnp.int32)
    remote = face_partner - LOCAL
    side = remote // CAP
    block = side ^ jnp.where(side < 2, even_x, even_y)
    lane = lambda q: (q % 6) * E_DEV + q // 6
    partner = jnp.where(remote < 0, lane(face_partner), LOCAL + block * CAP + remote % CAP)
    partner = partner.T.reshape(1, LOCAL)
    sides = lane(send_faces[0])
    flipped = sides.reshape(2, 2, CAP)[:, ::-1]
    even = jnp.stack([even_x, even_y])[:, None, None]
    sent = jnp.where(even == 1, flipped, sides.reshape(2, 2, CAP)).reshape(4 * CAP, 1)

    owner, slot, octant = migration[0], migration[1], migration[2]
    key = jnp.where(owner == own_seg, slot, P_DEV + 2 * owner + slot)
    first = octant == 0
    rank = jnp.sum((first[:, None] & (key[:, None] < key[None, :])).astype(jnp.int32), axis=0)
    place = (octant * P_DEV + rank).reshape(1, E_DEV)
    keys = jnp.sum(
        jnp.where(first[:, None] & (rank[:, None] == jnp.arange(P_DEV)[None, :]), key[:, None], 0), axis=0
    )
    source = jnp.stack([children[0], jnp.where(children[0] == own_seg, -1, children[1])])

    state = shape(9, 4, 64, 128)
    table = shape(LOCAL, 2 * LOCAL, dtype=BF)
    face_part = shape(LOCAL, LOCAL)
    payload = [shape(CAP, LOCAL)] * 4
    face_scratch = pltpu.VMEM((LOCAL, LOCAL), F32)
    turn = pltpu.VMEM((NODES, 128), F32)

    outs = call(
        begin_kernel,
        [state, table, shape(2 * LOCAL, LOCAL, dtype=BF), shape(128, LOCAL, dtype=BF), shape(64, 2 * LOCAL, dtype=BF)]
        + payload,
        [turn],
        count=4,
    )(adjoint, mat, partner, sent)
    v, t, local_hot, remote_hot, send_hot = outs[:5]
    out_going = outs[5:]
    pairs = exchange_pairs()
    for step in range(1, 5):
        arrived = [lax.ppermute(x, axis, p) for x, (axis, p) in zip(out_going, pairs)]
        if step == 1:
            vol, part = call(first_volume_kernel, [state, face_part], count=4)(v, t, local_hot, mat)
            acc = v
        else:
            vol, part, acc = call(volume_kernel, [state, face_part, state], count=5)(v, t, local_hot, mat, acc)
        factor = time_step / step
        if step < 4:
            outs = call(
                functools.partial(finish_kernel, factor), [state, table] + payload, [face_scratch], count=9
            )(vol, part, *arrived, remote_hot, mat, send_hot)
            v, t, out_going = outs[0], outs[1], outs[2:]
    high, low = refine_parts()
    updated, home, away = call(
        functools.partial(end_kernel, factor),
        [shape(9, E_DEV, NODES), shape(9, P_DEV, NODES), shape(N_SEG, 9, 8, 128)],
        [
            pltpu.VMEM((9, 4, 64, 128), F32),
            face_scratch,
            turn,
            pltpu.VMEM((9, E_DEV, NODES), F32),
            pltpu.VMEM((80, NODES), F32),
        ],
        smem=(0,),
        count=12,
    )(keys, vol, part, *arrived, remote_hot, acc, place, jnp.asarray(high), jnp.asarray(low))
    fetched = lax.all_to_all(away, "seg", split_axis=0, concat_axis=0, tiled=True)
    parents = call(parent_kernel, [shape(9, P_DEV, NODES)], smem=(0,), count=3)(source, home, fetched)[0]
    return (updated, parents)


def solution(mesh):
    in_specs = (
        P(None, ("curve", "seg"), None),
        P(None, ("curve", "seg")),
        P(("curve", "seg"), None),
        P(("curve", "seg"), None, None),
        P(None, ("curve", "seg")),
        P(None, ("curve", "seg")),
    )
    out_specs = (P(None, ("curve", "seg"), None), P(None, ("curve", "seg"), None))
    return jax.shard_map(shards, mesh=mesh, in_specs=in_specs, out_specs=out_specs, check_vma=False)
```

profile of v0, /device:TPU:0, one launch (start us, length us, event | category | flops | bytes accessed | tf_op | source)
XLA Modules:
  0.0 75.5 jit_solution(12745121871792317747)
XLA Ops:
  0.7 0.7 broadcast_divide_fusion
  1.3 0.7 sign_compare_fusion.2
  2.1 0.1 add_compare_fusion
  2.2 0.1 broadcast_select_fusion
  2.2 0.1 reshape.77.sent_ref
  2.3 0.7 fusion.3
  3.1 0.1 reshape.75.partner_ref
  3.1 0.8 %divide_bitcast_fusion = (f32[64]{0:T(128)S(1)}, f32[64]{0:T(128)S(1)}, f32[64]{0:T(128)S(1)}) fusion(f32[3,64]{1,0:T(4,128)} %param.9), kind=kLoop, calls=%fused_computation.42 | loop fusion | flops 64 | bytes 1536 | tf_op jit(solution)/shard_map/div | solution.py:440
  3.9 0.1 pad_maximum_fusion.3
  4.0 0.1 pad_maximum_fusion.1
  4.1 0.0 copy-start.2
  4.1 1.3 %copy-done.2 = f32[9,64,512]{2,1,0:T(8,128)S(1)} copy-done((f32[9,64,512]{2,1,0:T(8,128)S(1)}, f32[9,64,512]{2,1,0:T(8,128)}, u32[]{:S(2)}) %copy-start.2) | copy-done | bytes 1179672
  5.4 2.0 %shard_map.95 = (f32[9,4,64,128]{3,2,1,0:T(8,128)S(1)}, bf16[384,768]{1,0:T(8,128)(2,1)S(1)}, bf16[768,384]{1,0:T(8,128)(2,1)S(1)}, bf16[128,384]{1,0:T(8,128)(2...) custom-call(f32[9,64,512]{2,1,0:T(8,128)S(1)} %copy-done.2, ...), custom_call_target="tpu_custom_call" | custom-call | flops 100000000 | bytes 6000000 | tf_op jit(solution)/shard_map/pallas_call | solution.py:471
  7.3 0.1 collective-permute-start
  7.4 2.9 %collective-permute-start.1 = (f32[16,384]{1,0:T(8,128)S(1)}, f32[16,384]{1,0:T(8,128)S(1)}, u32[]{:S(2)}, u32[]{:S(2)}) collective-permute-start(f32[16,384]{1,0:T(8,128)S(1)} %get-tuple-element.49), channel_id=1, source_target_pairs={{16,32},{48,64},{80,96},{112,0},{32,16},{64,48},{96,80},{0,112},{1... | collective-permute-start | bytes 73736 | tf_op jit(solution)/shard_map/ppermute | solution.py:482
  10.4 1.9 %collective-permute-start.2 = (f32[16,384]{1,0:T(8,128)S(1)}, f32[16,384]{1,0:T(8,128)S(1)}, u32[]{:S(2)}, u32[]{:S(2)}) collective-permute-start(f32[16,384]{1,0:T(8,128)S(1)} %get-tuple-element.50), channel_id=1, source_target_pairs={{0,1},{2,3},{4,5},{6,7},{8,9},{10,11},{12,13},{14,15},{1,0},{3,2},... | collective-permute-start | bytes 73736 | tf_op jit(solution)/shard_map/ppermute | solution.py:482
  12.3 5.0 %collective-permute-start.3 = (f32[16,384]{1,0:T(8,128)S(1)}, f32[16,384]{1,0:T(8,128)S(1)}, u32[]{:S(2)}, u32[]{:S(2)}) collective-permute-start(f32[16,384]{1,0:T(8,128)S(1)} %get-tuple-element.51), channel_id=1, source_target_pairs={{1,2},{3,4},{5,6},{7,8},{9,10},{11,12},{13,14},{15,0},{2,1},{4,3},... | collective-permute-start | bytes 73736 | tf_op jit(solution)/shard_map/ppermute | solution.py:482
  17.3 3.2 %shard_map.96 = (f32[9,4,64,128]{3,2,1,0:T(8,128)S(1)}, f32[384,384]{1,0:T(8,128)S(1)}) custom-call(f32[9,4,64,128]{3,2,1,0:T(8,128)S(1)} %get-tuple-element.43.v_ref.acc_ref, bf16[384,768]{1,0:T(8,128)(2,1)S(1)} %get-tuple-element.44.t_ref, bf16[768,384]{1,0:T(8,128)(2,1)S(1)} %get-tuple-element.45.local_ref, f32[3,8,128]{2,1,0:T(8,128)S(1)} %pad_maximum_fusion.mat_ref), custom_call_target="tpu_custom_call" | custom-call | flops 100000000 | bytes 6000000 | tf_op jit(solution)/shard_map/pallas_call | solution.py:484
  20.5 0.0 collective-permute-done.r0
  20.5 0.0 collective-permute-done.1.r1
  20.5 0.0 collective-permute-done.3.r3
  20.5 1.3 %shard_map.97 = (f32[9,4,64,128]{3,2,1,0:T(8,128)S(1)}, bf16[384,768]{1,0:T(8,128)(2,1)S(1)}, f32[16,384]{1,0:T(8,128)S(1)}, f32[16,384]{1,0:T(8,128)S(1)}, f32[...) custom-call(f32[9,4,64,128]{3,2,1,0:T(8,128)S(1)} %get-tuple-element.46.vol_ref, f32[384,384]{1,0:T(8,128)S(1)} %get-tuple-element.47.part_ref, ...), custom_call_target="tpu_custom_call" | custom-call | flops 100000000 | bytes 6000000 | tf_op jit(solution)/shard_map/pallas_call | solution.py:490
  21.8 0.1 collective-permute-start.4
  21.9 0.9 %collective-permute-start.5 = (f32[16,384]{1,0:T(8,128)S(1)}, f32[16,384]{1,0:T(8,128)S(1)}, u32[]{:S(2)}, u32[]{:S(2)}) collective-permute-start(f32[16,384]{1,0:T(8,128)S(1)} %get-tuple-element.59), channel_id=1, source_target_pairs={{16,32},{48,64},{80,96},{112,0},{32,16},{64,48},{96,80},{0,112},{1... | collective-permute-start | bytes 73736 | tf_op jit(solution)/shard_map/ppermute | solution.py:482
  22.8 3.9 %collective-permute-start.7 = (f32[16,384]{1,0:T(8,128)S(1)}, f32[16,384]{1,0:T(8,128)S(1)}, u32[]{:S(2)}, u32[]{:S(2)}) collective-permute-start(f32[16,384]{1,0:T(8,128)S(1)} %get-tuple-element.61), channel_id=1, source_target_pairs={{1,2},{3,4},{5,6},{7,8},{9,10},{11,12},{13,14},{15,0},{2,1},{4,3},... | collective-permute-start | bytes 73736 | tf_op jit(solution)/shard_map/ppermute | solution.py:482
  26.7 0.1 convert_reduce_fusion
  26.8 3.5 %shard_map.98 = (f32[9,4,64,128]{3,2,1,0:T(8,128)S(1)}, f32[384,384]{1,0:T(8,128)S(1)}, f32[9,4,64,128]{3,2,1,0:T(8,128)S(1)}) custom-call(f32[9,4,64,128]{3,2,1,0:T(8,128)S(1)} %get-tuple-element.54.v_ref, bf16[384,768]{1,0:T(8,128)(2,1)S(1)} %get-tuple-element.55.t_ref, bf16[768,384]{1,0:T(8,128)(2,1)S(1)} %get-tuple-element.45.local_ref, ...), custom_call_target="tpu_custom_call" | custom-call | flops 100000000 | bytes 6000000 | tf_op jit(solution)/shard_map/pallas_call | solution.py:487
  30.3 0.0 collective-permute-done.5.r1
  30.3 0.0 collective-permute-done.6.r2
  30.4 1.3 %shard_map.99 = (f32[9,4,64,128]{3,2,1,0:T(8,128)S(1)}, bf16[384,768]{1,0:T(8,128)(2,1)S(1)}, f32[16,384]{1,0:T(8,128)S(1)}, f32[16,384]{1,0:T(8,128)S(1)}, f32[...) custom-call(f32[9,4,64,128]{3,2,1,0:T(8,128)S(1)} %get-tuple-element.56.vol_ref, f32[384,384]{1,0:T(8,128)S(1)} %get-tuple-element.57.part_ref, ...), custom_call_target="tpu_custom_call" | custom-call | flops 100000000 | bytes 6000000 | tf_op jit(solution)/shard_map/pallas_call | solution.py:490
  31.6 0.1 collective-permute-start.10
  31.7 3.6 %collective-permute-start.11 = (f32[16,384]{1,0:T(8,128)S(1)}, f32[16,384]{1,0:T(8,128)S(1)}, u32[]{:S(2)}, u32[]{:S(2)}) collective-permute-start(f32[16,384]{1,0:T(8,128)S(1)} %get-tuple-element.70), channel_id=1, source_target_pairs={{1,2},{3,4},{5,6},{7,8},{9,10},{11,12},{13,14},{15,0},{2,1},{4,3},... | collective-permute-start | bytes 73736 | tf_op jit(solution)/shard_map/ppermute | solution.py:482
  35.3 0.7 collective-permute-start.9
  36.0 3.4 %shard_map.100 = (f32[9,4,64,128]{3,2,1,0:T(8,128)S(1)}, f32[384,384]{1,0:T(8,128)S(1)}, f32[9,4,64,128]{3,2,1,0:T(8,128)S(1)}) custom-call(f32[9,4,64,128]{3,2,1,0:T(8,128)S(1)} %get-tuple-element.62.v_ref, bf16[384,768]{1,0:T(8,128)(2,1)S(1)} %get-tuple-element.63.t_ref, bf16[768,384]{1,0:T(8,128)(2,1)S(1)} %get-tuple-element.45.local_ref, ...), custom_call_target="tpu_custom_call" | custom-call | flops 100000000 | bytes 6000000 | tf_op jit(solution)/shard_map/pallas_call | solution.py:487
  39.4 0.0 collective-permute-done.10.r2
  39.4 0.0 collective-permute-done.8.r0
  39.4 0.4 collective-permute-done.9.r1
  39.7 1.3 %shard_map.101 = (f32[9,4,64,128]{3,2,1,0:T(8,128)S(1)}, bf16[384,768]{1,0:T(8,128)(2,1)S(1)}, f32[16,384]{1,0:T(8,128)S(1)}, f32[16,384]{1,0:T(8,128)S(1)}, f32...) custom-call(f32[9,4,64,128]{3,2,1,0:T(8,128)S(1)} %get-tuple-element.65.vol_ref, f32[384,384]{1,0:T(8,128)S(1)} %get-tuple-element.66.part_ref, ...), custom_call_target="tpu_custom_call" | custom-call | flops 100000000 | bytes 6000000 | tf_op jit(solution)/shard_map/pallas_call | solution.py:490
  41.0 0.4 collective-permute-start.12
  41.4 1.7 %collective-permute-start.13 = (f32[16,384]{1,0:T(8,128)S(1)}, f32[16,384]{1,0:T(8,128)S(1)}, u32[]{:S(2)}, u32[]{:S(2)}) collective-permute-start(f32[16,384]{1,0:T(8,128)S(1)} %get-tuple-element.77), channel_id=1, source_target_pairs={{16,32},{48,64},{80,96},{112,0},{32,16},{64,48},{96,80},{0,112},{1... | collective-permute-start | bytes 73736 | tf_op jit(solution)/shard_map/ppermute | solution.py:482
  43.1 1.9 %collective-permute-start.15 = (f32[16,384]{1,0:T(8,128)S(1)}, f32[16,384]{1,0:T(8,128)S(1)}, u32[]{:S(2)}, u32[]{:S(2)}) collective-permute-start(f32[16,384]{1,0:T(8,128)S(1)} %get-tuple-element.79), channel_id=1, source_target_pairs={{1,2},{3,4},{5,6},{7,8},{9,10},{11,12},{13,14},{15,0},{2,1},{4,3},... | collective-permute-start | bytes 73736 | tf_op jit(solution)/shard_map/ppermute | solution.py:482
  45.1 0.1 select_reduce_fusion.keys_ref
  45.2 3.4 %shard_map.102 = (f32[9,4,64,128]{3,2,1,0:T(8,128)S(1)}, f32[384,384]{1,0:T(8,128)S(1)}, f32[9,4,64,128]{3,2,1,0:T(8,128)S(1)}) custom-call(f32[9,4,64,128]{3,2,1,0:T(8,128)S(1)} %get-tuple-element.71.v_ref, bf16[384,768]{1,0:T(8,128)(2,1)S(1)} %get-tuple-element.72.t_ref, bf16[768,384]{1,0:T(8,128)(2,1)S(1)} %get-tuple-element.45.local_ref, ...), custom_call_target="tpu_custom_call" | custom-call | flops 100000000 | bytes 6000000 | tf_op jit(solution)/shard_map/pallas_call | solution.py:487
  48.6 1.7 %collective-permute-done.15.r3 = f32[16,384]{1,0:T(8,128)S(1)} collective-permute-done((f32[16,384]{1,0:T(8,128)S(1)}, f32[16,384]{1,0:T(8,128)S(1)}, u32[]{:S(2)}, u32[]{:S(2)}) %collective-permute-start.15) | collective-permute-done | bytes 24608 | tf_op jit(solution)/shard_map/ppermute | solution.py:482
  50.3 9.1 %shard_map.103 = (f32[9,64,512]{2,1,0:T(8,128)}, f32[9,8,512]{2,1,0:T(8,128)S(1)}, f32[16,9,8,128]{3,2,1,0:T(8,128)}) custom-call(s32[8]{0:T(128)S(1)} %select_reduce_fusion.keys_ref, f32[9,4,64,128]{3,2,1,0:T(8,128)S(1)} %get-tuple-element.74.vol_ref, f32[384,384]{1,0:T(8,128)S(1)} %get-tuple-element.75.part_ref, f32[16,384]{1,0:T(8,128)S(1)} %collective-permute-done.12.r0, ...), custom_call_target="tpu_custom_call" | custom-call | flops 100000000 | bytes 6000000 | tf_op jit(solution)/shard_map/pallas_call | solution.py:495
  59.4 3.7 %all-to-all-start = ((f32[16,9,8,128]{3,2,1,0:T(8,128)}), f32[16,9,8,128]{3,2,1,0:T(8,128)S(1)}, u32[]{:S(2)}, u32[]{:S(2)}) async-start(f32[16,9,8,128]{3,2,1,0:T(8,128)} %get-tuple-element.83), calls=%async_computation | async-start | bytes 1179648 | tf_op jit(solution)/shard_map/all_to_all | solution.py:508
  63.2 11.0 %all-to-all-done.arrived_ref = f32[16,9,8,128]{3,2,1,0:T(8,128)S(1)} async-done(((f32[16,9,8,128]{3,2,1,0:T(8,128)}), f32[16,9,8,128]{3,2,1,0:T(8,128)S(1)}, u32[]{:S(2)}, u32[]{:S(2)}) %all-to-all-start) | async-done | bytes 589856 | tf_op jit(solution)/shard_map/all_to_all | solution.py:508
  74.2 1.3 %shard_map.104 = f32[9,8,512]{2,1,0:T(8,128)} custom-call(s32[2,8]{1,0:T(2,128)S(1)} %pad_add_fusion.table_ref, f32[9,8,512]{2,1,0:T(8,128)S(1)} %get-tuple-element.82.home_ref, f32[16,9,8,128]{3,2,1,0:T(8,128)S(1)} %all-to-all-done.arrived_ref), custom_call_target="tpu_custom_call" | custom-call | flops 100000000 | bytes 6000000 | tf_op jit(solution)/shard_map/pallas_call | solution.py:509
  (31 shorter events, 0.2 us)
Async XLA Ops:
  0.6 16.6 %copy-start.3 = (s32[3,64]{1,0:T(4,128)S(1)}, s32[3,64]{1,0:T(4,128)}, u32[]{:S(2)}) copy-start(s32[3,64]{1,0:T(4,128)} %param.12) | copy-start | bytes 2308
  4.1 1.3 %copy-start.2 = (f32[9,64,512]{2,1,0:T(8,128)S(1)}, f32[9,64,512]{2,1,0:T(8,128)}, u32[]{:S(2)}) copy-start(f32[9,64,512]{2,1,0:T(8,128)} %adjoint_ref.1) | copy-start | bytes 3538948
  7.3 13.2 %collective-permute-start = (f32[16,384]{1,0:T(8,128)S(1)}, f32[16,384]{1,0:T(8,128)S(1)}, u32[]{:S(2)}, u32[]{:S(2)}) collective-permute-start(f32[16,384]{1,0:T(8,128)S(1)} %get-tuple-element.48), channel_id=1, source_target_pairs={{0,16},{32,48},{64,80},{96,112},{16,0},{48,32},{80,64},{112,96},{1... | collective-permute-start | bytes 73736 | tf_op jit(solution)/shard_map/ppermute | solution.py:482
  7.4 13.1 %collective-permute-start.1 = (f32[16,384]{1,0:T(8,128)S(1)}, f32[16,384]{1,0:T(8,128)S(1)}, u32[]{:S(2)}, u32[]{:S(2)}) collective-permute-start(f32[16,384]{1,0:T(8,128)S(1)} %get-tuple-element.49), channel_id=1, source_target_pairs={{16,32},{48,64},{80,96},{112,0},{32,16},{64,48},{96,80},{0,112},{1... | collective-permute-start | bytes 73736 | tf_op jit(solution)/shard_map/ppermute | solution.py:482
  10.4 10.1 %collective-permute-start.2 = (f32[16,384]{1,0:T(8,128)S(1)}, f32[16,384]{1,0:T(8,128)S(1)}, u32[]{:S(2)}, u32[]{:S(2)}) collective-permute-start(f32[16,384]{1,0:T(8,128)S(1)} %get-tuple-element.50), channel_id=1, source_target_pairs={{0,1},{2,3},{4,5},{6,7},{8,9},{10,11},{12,13},{14,15},{1,0},{3,2},... | collective-permute-start | bytes 73736 | tf_op jit(solution)/shard_map/ppermute | solution.py:482
  12.3 8.2 %collective-permute-start.3 = (f32[16,384]{1,0:T(8,128)S(1)}, f32[16,384]{1,0:T(8,128)S(1)}, u32[]{:S(2)}, u32[]{:S(2)}) collective-permute-start(f32[16,384]{1,0:T(8,128)S(1)} %get-tuple-element.51), channel_id=1, source_target_pairs={{1,2},{3,4},{5,6},{7,8},{9,10},{11,12},{13,14},{15,0},{2,1},{4,3},... | collective-permute-start | bytes 73736 | tf_op jit(solution)/shard_map/ppermute | solution.py:482
  21.8 8.5 %collective-permute-start.4 = (f32[16,384]{1,0:T(8,128)S(1)}, f32[16,384]{1,0:T(8,128)S(1)}, u32[]{:S(2)}, u32[]{:S(2)}) collective-permute-start(f32[16,384]{1,0:T(8,128)S(1)} %get-tuple-element.58), channel_id=1, source_target_pairs={{0,16},{32,48},{64,80},{96,112},{16,0},{48,32},{80,64},{112,96},{1... | collective-permute-start | bytes 73736 | tf_op jit(solution)/shard_map/ppermute | solution.py:482
  21.9 8.4 %collective-permute-start.5 = (f32[16,384]{1,0:T(8,128)S(1)}, f32[16,384]{1,0:T(8,128)S(1)}, u32[]{:S(2)}, u32[]{:S(2)}) collective-permute-start(f32[16,384]{1,0:T(8,128)S(1)} %get-tuple-element.59), channel_id=1, source_target_pairs={{16,32},{48,64},{80,96},{112,0},{32,16},{64,48},{96,80},{0,112},{1... | collective-permute-start | bytes 73736 | tf_op jit(solution)/shard_map/ppermute | solution.py:482
  22.8 7.5 %collective-permute-start.6 = (f32[16,384]{1,0:T(8,128)S(1)}, f32[16,384]{1,0:T(8,128)S(1)}, u32[]{:S(2)}, u32[]{:S(2)}) collective-permute-start(f32[16,384]{1,0:T(8,128)S(1)} %get-tuple-element.60), channel_id=1, source_target_pairs={{0,1},{2,3},{4,5},{6,7},{8,9},{10,11},{12,13},{14,15},{1,0},{3,2},... | collective-permute-start | bytes 73736 | tf_op jit(solution)/shard_map/ppermute | solution.py:482
  22.8 7.5 %collective-permute-start.7 = (f32[16,384]{1,0:T(8,128)S(1)}, f32[16,384]{1,0:T(8,128)S(1)}, u32[]{:S(2)}, u32[]{:S(2)}) collective-permute-start(f32[16,384]{1,0:T(8,128)S(1)} %get-tuple-element.61), channel_id=1, source_target_pairs={{1,2},{3,4},{5,6},{7,8},{9,10},{11,12},{13,14},{15,0},{2,1},{4,3},... | collective-permute-start | bytes 73736 | tf_op jit(solution)/shard_map/ppermute | solution.py:482
  31.6 7.7 %collective-permute-start.10 = (f32[16,384]{1,0:T(8,128)S(1)}, f32[16,384]{1,0:T(8,128)S(1)}, u32[]{:S(2)}, u32[]{:S(2)}) collective-permute-start(f32[16,384]{1,0:T(8,128)S(1)} %get-tuple-element.69), channel_id=1, source_target_pairs={{0,1},{2,3},{4,5},{6,7},{8,9},{10,11},{12,13},{14,15},{1,0},{3,2},... | collective-permute-start | bytes 73736 | tf_op jit(solution)/shard_map/ppermute | solution.py:482
  31.7 7.7 %collective-permute-start.11 = (f32[16,384]{1,0:T(8,128)S(1)}, f32[16,384]{1,0:T(8,128)S(1)}, u32[]{:S(2)}, u32[]{:S(2)}) collective-permute-start(f32[16,384]{1,0:T(8,128)S(1)} %get-tuple-element.70), channel_id=1, source_target_pairs={{1,2},{3,4},{5,6},{7,8},{9,10},{11,12},{13,14},{15,0},{2,1},{4,3},... | collective-permute-start | bytes 73736 | tf_op jit(solution)/shard_map/ppermute | solution.py:482
  35.3 4.1 %collective-permute-start.8 = (f32[16,384]{1,0:T(8,128)S(1)}, f32[16,384]{1,0:T(8,128)S(1)}, u32[]{:S(2)}, u32[]{:S(2)}) collective-permute-start(f32[16,384]{1,0:T(8,128)S(1)} %get-tuple-element.67), channel_id=1, source_target_pairs={{0,16},{32,48},{64,80},{96,112},{16,0},{48,32},{80,64},{112,96},{1... | collective-permute-start | bytes 73736 | tf_op jit(solution)/shard_map/ppermute | solution.py:482
  35.3 4.5 %collective-permute-start.9 = (f32[16,384]{1,0:T(8,128)S(1)}, f32[16,384]{1,0:T(8,128)S(1)}, u32[]{:S(2)}, u32[]{:S(2)}) collective-permute-start(f32[16,384]{1,0:T(8,128)S(1)} %get-tuple-element.68), channel_id=1, source_target_pairs={{16,32},{48,64},{80,96},{112,0},{32,16},{64,48},{96,80},{0,112},{1... | collective-permute-start | bytes 73736 | tf_op jit(solution)/shard_map/ppermute | solution.py:482
  36.0 14.3 %copy-start.1 = (bf16[8,512,512]{2,1,0:T(8,128)(2,1)S(1)}, bf16[8,512,512]{2,1,0:T(8,128)(2,1)}, u32[]{:S(2)}) copy-start(bf16[8,512,512]{2,1,0:T(8,128)(2,1)} %constant.99.clone.low_ref) | copy-start | bytes 12582916
  39.7 10.5 %copy-start = (bf16[8,512,512]{2,1,0:T(8,128)(2,1)S(1)}, bf16[8,512,512]{2,1,0:T(8,128)(2,1)}, u32[]{:S(2)}) copy-start(bf16[8,512,512]{2,1,0:T(8,128)(2,1)} %constant.98.clone.high_ref) | copy-start | bytes 12582916
  41.0 7.6 %collective-permute-start.12 = (f32[16,384]{1,0:T(8,128)S(1)}, f32[16,384]{1,0:T(8,128)S(1)}, u32[]{:S(2)}, u32[]{:S(2)}) collective-permute-start(f32[16,384]{1,0:T(8,128)S(1)} %get-tuple-element.76), channel_id=1, source_target_pairs={{0,16},{32,48},{64,80},{96,112},{16,0},{48,32},{80,64},{112,96},{1... | collective-permute-start | bytes 73736 | tf_op jit(solution)/shard_map/ppermute | solution.py:482
  41.4 7.2 %collective-permute-start.13 = (f32[16,384]{1,0:T(8,128)S(1)}, f32[16,384]{1,0:T(8,128)S(1)}, u32[]{:S(2)}, u32[]{:S(2)}) collective-permute-start(f32[16,384]{1,0:T(8,128)S(1)} %get-tuple-element.77), channel_id=1, source_target_pairs={{16,32},{48,64},{80,96},{112,0},{32,16},{64,48},{96,80},{0,112},{1... | collective-permute-start | bytes 73736 | tf_op jit(solution)/shard_map/ppermute | solution.py:482
  43.1 5.5 %collective-permute-start.14 = (f32[16,384]{1,0:T(8,128)S(1)}, f32[16,384]{1,0:T(8,128)S(1)}, u32[]{:S(2)}, u32[]{:S(2)}) collective-permute-start(f32[16,384]{1,0:T(8,128)S(1)} %get-tuple-element.78), channel_id=1, source_target_pairs={{0,1},{2,3},{4,5},{6,7},{8,9},{10,11},{12,13},{14,15},{1,0},{3,2},... | collective-permute-start | bytes 73736 | tf_op jit(solution)/shard_map/ppermute | solution.py:482
  43.1 7.1 %collective-permute-start.15 = (f32[16,384]{1,0:T(8,128)S(1)}, f32[16,384]{1,0:T(8,128)S(1)}, u32[]{:S(2)}, u32[]{:S(2)}) collective-permute-start(f32[16,384]{1,0:T(8,128)S(1)} %get-tuple-element.79), channel_id=1, source_target_pairs={{1,2},{3,4},{5,6},{7,8},{9,10},{11,12},{13,14},{15,0},{2,1},{4,3},... | collective-permute-start | bytes 73736 | tf_op jit(solution)/shard_map/ppermute | solution.py:482
  59.4 3.7 %copy-start.4 = (s32[2,8]{1,0:T(2,128)S(1)}, s32[2,8]{1,0:T(2,128)}, u32[]{:S(2)}) copy-start(s32[2,8]{1,0:T(2,128)} %param.13) | copy-start | bytes 196
  59.4 14.8 %all-to-all-start = ((f32[16,9,8,128]{3,2,1,0:T(8,128)}), f32[16,9,8,128]{3,2,1,0:T(8,128)S(1)}, u32[]{:S(2)}, u32[]{:S(2)}) async-start(f32[16,9,8,128]{3,2,1,0:T(8,128)} %get-tuple-element.83), calls=%async_computation | async-start | bytes 1179648 | tf_op jit(solution)/shard_map/all_to_all | solution.py:508
where the time goes:
time: 75.9 us; the launch traced here: 75.5 us
  Pallas kernels  29.7 us (39%)
  starting transfers between devices  26.9 us (35%)
  waiting for transfers between devices  13.1 us (17%)
  other arithmetic  3.46 us (5%)
  local copies, waits for them, and re-layouts  1.5 us (2%)
  between operations  0.9 us (1%)
    ppermute x16, starting transfers between devices, shards(): lax.ppermute(x, axis, p)  23.2 us
    all_to_all x1, waiting for transfers between devices, shards(): lax.all_to_all(away, 'seg', split_axis=0, concat_axis=0, tiled=True)  11 us
    pallas_call x3, Pallas kernels, shards(): call(volume_kernel, [state, face_part, state], count=5)  10.3 us
    pallas_call x1, Pallas kernels, shards(): call(functools.partial(end_kernel, factor), [shape(9, E_DEV, NODES), shap...  9.15 us
    pallas_call x3, Pallas kernels, shards(): call(functools.partial(finish_kernel, factor), [state, table] + payload,...  3.8 us
    all_to_all x1, starting transfers between devices, shards(): lax.all_to_all(away, 'seg', split_axis=0, concat_axis=0, tiled=True)  3.71 us
    pallas_call x1, Pallas kernels, shards(): call(first_volume_kernel, [state, face_part], count=4)(v, t, local_hot, mat)  3.19 us
    ppermute x16, waiting for transfers between devices, shards(): lax.ppermute(x, axis, p)  2.05 us
  transfers between devices with their start and end apart: 17, of which 3 were waited for; matrix products, arithmetic and copies ran while one was open for 0% of the time, Pallas kernels for 18%

commit v1 on v0

--- a/solution.py
+++ b/solution.py
@@ -57,14 +57,15 @@
 
 
 def refine_parts():
-    blocks = []
-    for octant in range(8):
-        lines = [refine_line(NP, octant // 4 % 2), refine_line(NP, octant // 2 % 2), refine_line(NP, octant % 2)]
-        blocks.append(np.kron(np.kron(lines[0], lines[1]), lines[2]))
-    whole = np.stack(blocks).astype(np.float32)
-    high = whole.astype(BF)
-    low = (whole - high.astype(np.float32)).astype(BF)
-    return high, low
+    lines = [refine_line(NP, upper) for upper in range(2)]
+    plane = np.concatenate([np.kron(lines[k // 2], lines[k % 2]) for k in range(4)], axis=0).astype(np.float32)
+    high = plane.astype(BF)
+    low = (plane - high.astype(np.float32)).astype(BF)
+    columns = [
+        np.repeat(lines[upper][a, 2 * t : 2 * t + 2], 64) for upper in range(2) for a in range(8) for t in range(4)
+    ]
+    patterns = np.broadcast_to(np.stack(columns)[:, None, :], (64, 8, 128)).astype(np.float32)
+    return np.concatenate([high, low], axis=1), np.concatenate([high, high], axis=1), patterns
 
 
 _line = derivative_line(NP)
@@ -204,13 +205,68 @@
 
 
 def begin_kernel(
-    adjoint_ref, mat_ref, partner_ref, sent_ref,
-    v_ref, t_ref, local_ref, remote_ref, send_ref, p0, p1, p2, p3, turn_ref,
+    adjoint_ref, material_ref, faces_ref, sides_ref,
+    v_ref, mat_ref, t_ref, local_ref, remote_ref, send_ref, p0, p1, p2, p3,
+    staged_ref, sem, turn_ref, small_ref,
 ):
+    def fetch(i):
+        return pltpu.make_async_copy(adjoint_ref.at[i], staged_ref.at[i], sem.at[i])
+
+    for i in range(9):
+        fetch(i).start()
+    even_x = 1 - lax.axis_index("curve") % 2
+    even_y = 1 - lax.axis_index("seg") % 2
+
+    def lane(q):
+        element = (q * 10923) >> 16
+        return (q - 6 * element) * E_DEV + element
+
+    for i in range(3):
+        row = material_ref[pl.ds(i, 1), :]
+        if i == 0:
+            row = 1.0 / row
+        mat_ref[i] = jnp.broadcast_to(jnp.concatenate([row, row], axis=1), (8, 128))
+    small_ref[...] = jnp.zeros_like(small_ref)
+    faces = faces_ref[...].astype(F32)
+    small_ref[pl.ds(0, 64), pl.ds(0, 6)] = faces
+    small_ref[pl.ds(64, 64), pl.ds(0, 6)] = faces
+    turned = small_ref[...].T
+    low_row = lax.broadcasted_iota(jnp.int32, (1, 128), 1) < 64
+    weight = jnp.where(low_row, lift_half, -lift_half)
+    for direction in range(3):
+        q = jnp.where(
+            low_row, turned[2 * direction : 2 * direction + 1], turned[2 * direction + 1 : 2 * direction + 2]
+        ).astype(jnp.int32)
+        remote = q - LOCAL
+        side = remote >> 4
+        block = side ^ jnp.where(side < 2, even_x, even_y)
+        partner = jnp.where(remote < 0, lane(q), LOCAL + block * CAP + (remote & 15))
+        lanes = pl.ds(direction * 128, 128)
+        for start in range(0, LOCAL + 64, 64):
+            source = lax.broadcasted_iota(jnp.int32, (64, 128), 0) + start
+            hot = jnp.where(source == partner, weight, 0.0).astype(BF)
+            for part in range(2):
+                if start < LOCAL:
+                    local_ref[pl.ds(part * LOCAL + start, 64), lanes] = hot
+                else:
+                    remote_ref[pl.ds(part * 64, 64), lanes] = hot
+    small_ref[pl.ds(0, 4), pl.ds(0, CAP)] = sides_ref[0].astype(F32)
+    turned = small_ref[...].T
+    columns = [lane(turned[0:CAP, r : r + 1].astype(jnp.int32)) for r in range(4)]
+    for axis, even in ((0, even_x), (1, even_y)):
+        first, second = columns[2 * axis], columns[2 * axis + 1]
+        for k, column in enumerate((first + even * (second - first), second + even * (first - second))):
+            hot = jnp.where(
+                lax.broadcasted_iota(jnp.int32, (CAP, LOCAL), 1) == column, 1.0, 0.0
+            ).astype(BF)
+            rows = pl.ds((2 * axis + k) * CAP, CAP)
+            send_ref[rows, pl.ds(0, LOCAL)] = hot
+            send_ref[rows, pl.ds(LOCAL, LOCAL)] = hot
     low = lax.broadcasted_iota(jnp.int32, (64, 128), 1) < 64
 
     def body(i, carry):
-        x = adjoint_ref[i]
+        fetch(i).wait()
+        x = staged_ref[i]
         turn_ref[...] = jnp.concatenate([x, x], axis=0).T
         for j in range(4):
             v_ref[i, j] = jnp.where(
@@ -219,23 +275,6 @@
         return carry
 
     lax.fori_loop(0, 9, body, 0)
-    partner = partner_ref[...]
-    face = lax.broadcasted_iota(jnp.int32, (1, LOCAL), 1) // 64
-    weight = jnp.where(face % 2 == 0, lift_half, -lift_half)
-    for start in range(0, LOCAL, 64):
-        source = lax.broadcasted_iota(jnp.int32, (64, LOCAL), 0) + start
-        block = jnp.where(source == partner, weight, 0.0).astype(BF)
-        local_ref[pl.ds(start, 64), :] = block
-        local_ref[pl.ds(LOCAL + start, 64), :] = block
-    source = lax.broadcasted_iota(jnp.int32, (64, LOCAL), 0) + LOCAL
-    block = jnp.where(source == partner, weight, 0.0).astype(BF)
-    remote_ref[pl.ds(0, 64), :] = block
-    remote_ref[pl.ds(64, 64), :] = block
-    chosen = jnp.where(
-        lax.broadcasted_iota(jnp.int32, (64, LOCAL), 1) == sent_ref[...], 1.0, 0.0
-    ).astype(BF)
-    send_ref[:, pl.ds(0, LOCAL)] = chosen
-    send_ref[:, pl.ds(LOCAL, LOCAL)] = chosen
     build_table(v_ref, materials(mat_ref), t_ref)
     send_values(send_ref, t_ref, (p0, p1, p2, p3))
 
@@ -282,17 +321,15 @@
                 if row != 5:
                     y = y + vol_ref[row, j, rows, :]
                 vol_ref[row, j, rows, :] = y
+        chunk = pl.ds(pl.multiple_of(a * 48, 16), 48)
+        part_ref[chunk, :] = jnp.dot(t_ref[chunk, :], local_ref[...], preferred_element_type=F32)
         if sum_ref is not None:
             for i in range(9):
                 for j in range(4):
                     sum_ref[i, j, rows, :] = acc_ref[i, j, rows, :] + v_ref[i, j, rows, :]
         return carry
 
-    lax.fori_loop(0, 8, groups, 0)
-    for k in range(6):
-        part_ref[pl.ds(64 * k, 64), :] = jnp.dot(
-            t_ref[pl.ds(64 * k, 64), :], local_ref[...], preferred_element_type=F32
-        )
+    lax.fori_loop(0, 8, groups, 0, unroll=4)
 
 
 def add_faces(vol_ref, part_ref, r_refs, remote_ref, factor, out_ref, face_ref):
@@ -330,47 +367,45 @@
 
 
 def end_kernel(
-    factor, keys_ref, vol_ref, part_ref, r0, r1, r2, r3, remote_ref, acc_ref, place_ref, high_ref, low_ref,
-    next_ref, home_ref, away_ref, v_ref, face_ref, turn_ref, sorted_ref, parent_ref,
+    factor, keys_ref, vol_ref, part_ref, r0, r1, r2, r3, remote_ref, acc_ref, place_ref, wa_ref, wb_ref, lines_ref,
+    total_ref, home_ref, away_ref, v_ref, face_ref, turn_ref, rows_ref, parent_ref,
 ):
     add_faces(vol_ref, part_ref, (r0, r1, r2, r3), remote_ref, factor, v_ref, face_ref)
     place = jnp.where(
-        lax.broadcasted_iota(jnp.int32, (64, 64), 0) == place_ref[...], 1.0, 0.0
+        lax.broadcasted_iota(jnp.int32, (64, 128), 0) == place_ref[...], 1.0, 0.0
     ).astype(BF)
+    wide = lax.broadcasted_iota(jnp.int32, (64, 128), 1) < 64
+    low = low_half()
 
     def body(i, carry):
         for j in range(4):
             tile = acc_ref[i, j] + v_ref[i, j]
-            turn_ref[pl.ds(2 * j, 64, stride=8), :] = tile
-            turn_ref[pl.ds(2 * j + 1, 64, stride=8), :] = pltpu.roll(tile, 64, 1)
-        x = turn_ref[...].T[:64]
-        next_ref[i] = x
-        high, rest = split(x)
-        sorted_ref[i] = (
-            jnp.dot(place, high, preferred_element_type=F32)
-            + jnp.dot(place, rest, preferred_element_type=F32)
+            total_ref[i, j] = tile
+            high = tile.astype(BF).astype(F32)
+            rest = tile - high
+            turn_ref[pl.ds(2 * j, 64, stride=8), :] = jnp.where(wide, high, pltpu.roll(rest, 64, 1))
+            turn_ref[pl.ds(2 * j + 1, 64, stride=8), :] = jnp.where(wide, pltpu.roll(high, 64, 1), rest)
+        ranked = lax.dot_general(
+            place, turn_ref[...].astype(BF), (((1,), (1,)), ((), ())), preferred_element_type=F32
         )
+        for upper in range(2):
+            for t in range(4):
+                x = [ranked[8 * (4 * upper + k) : 8 * (4 * upper + k) + 8, 128 * t : 128 * t + 128] for k in range(4)]
+                for pair in range(2):
+                    x0, x1 = x[2 * pair], x[2 * pair + 1]
+                    lanes = pl.ds(128 * pair, 128)
+                    rows_ref[pl.ds(64 * upper + 16 * t, 8), lanes] = jnp.where(low, x0, swap_halves(x1))
+                    rows_ref[pl.ds(64 * upper + 16 * t + 8, 8), lanes] = jnp.where(low, swap_halves(x0), x1)
+        high, rest = split(rows_ref[...])
+        plane = jnp.dot(high, wa_ref[...], preferred_element_type=F32)
+        plane = plane + pltpu.roll(plane, 64, 1) + jnp.dot(rest, wb_ref[...], preferred_element_type=F32)
+        for t in range(4):
+            parent_ref[i, t] = sum(
+                plane[8 * k : 8 * k + 8] * lines_ref[4 * k + t] for k in range(16)
+            )
         return carry
 
     lax.fori_loop(0, 9, body, 0)
-    parent_ref[...] = jnp.zeros_like(parent_ref)
-
-    def octants(c, carry):
-        x = jnp.concatenate(
-            [sorted_ref[i, pl.ds(pl.multiple_of(c * 8, 8), 8), :] for i in range(9)]
-            + [jnp.zeros((8, NODES), F32)],
-            axis=0,
-        )
-        high, rest = split(x)
-        parent_ref[...] += (
-            jnp.dot(high, high_ref[c], preferred_element_type=F32)
-            + jnp.dot(rest, high_ref[c], preferred_element_type=F32)
-            + jnp.dot(high, low_ref[c], preferred_element_type=F32)
-        )
-        return carry
-
-    lax.fori_loop(0, 8, octants, 0)
-    away_ref[...] = jnp.zeros_like(away_ref)
     home_ref[...] = jnp.zeros_like(home_ref)
     for g in range(P_DEV):
         key = keys_ref[g]
@@ -378,32 +413,52 @@
         @pl.when(key < P_DEV)
         def _():
             for i in range(9):
-                home_ref[i, pl.ds(key, 1), :] = parent_ref[pl.ds(8 * i + g, 1), :]
+                for t in range(4):
+                    home_ref[i, t, pl.ds(key, 1), :] = parent_ref[i, t, pl.ds(g, 1), :]
 
         @pl.when(key >= P_DEV)
         def _():
             owner = (key - P_DEV) // 2
             slot = (key - P_DEV) % 2
             for i in range(9):
-                for j in range(4):
-                    away_ref[owner, i, pl.ds(slot * 4 + j, 1), :] = parent_ref[
-                        pl.ds(8 * i + g, 1), pl.ds(128 * j, 128)
-                    ]
-
-
-def parent_kernel(table_ref, home_ref, arrived_ref, out_ref):
-    out_ref[...] = home_ref[...]
+                for t in range(4):
+                    away_ref[owner, i, pl.ds(slot * 4 + t, 1), :] = parent_ref[i, t, pl.ds(g, 1), :]
+
+
+def next_kernel(total_ref, next_ref, turn_ref):
+    def body(i, carry):
+        for j in range(4):
+            tile = total_ref[i, j]
+            turn_ref[pl.ds(2 * j, 64, stride=8), :] = tile
+            turn_ref[pl.ds(2 * j + 1, 64, stride=8), :] = pltpu.roll(tile, 64, 1)
+        next_ref[i] = turn_ref[...].T[:64]
+        return carry
+
+    lax.fori_loop(0, 9, body, 0)
+
+
+def parent_kernel(table_ref, home_ref, arrived_ref, out_ref, block_ref, sem):
+    def fetch(p):
+        return pltpu.make_async_copy(arrived_ref.at[table_ref[0, p]], block_ref.at[p], sem.at[p])
+
     for p in range(P_DEV):
-        holder = table_ref[0, p]
+
+        @pl.when(table_ref[1, p] >= 0)
+        def _():
+            fetch(p).start()
+
+    for i in range(9):
+        for t in range(4):
+            out_ref[i, :, pl.ds(128 * t, 128)] = home_ref[i, t]
+    for p in range(P_DEV):
         slot = table_ref[1, p]
 
         @pl.when(slot >= 0)
         def _():
+            fetch(p).wait()
             for i in range(9):
-                for j in range(4):
-                    out_ref[i, pl.ds(p, 1), pl.ds(128 * j, 128)] = arrived_ref[
-                        holder, i, pl.ds(slot * 4 + j, 1), :
-                    ]
+                for t in range(4):
+                    out_ref[i, pl.ds(p, 1), pl.ds(128 * t, 128)] = block_ref[p, i, pl.ds(slot * 4 + t, 1), :]
 
 
 def shape(*dims, dtype=F32):
@@ -412,13 +467,17 @@
 
 VMEM = pl.BlockSpec(memory_space=pltpu.VMEM)
 SMEM = pl.BlockSpec(memory_space=pltpu.SMEM)
-
-
-def call(kernel, outs, scratch=(), smem=(), count=0, flops=10**8, traffic=6 * 10**6):
+ANYWHERE = pl.BlockSpec(memory_space=pl.ANY)
+HBM = pl.BlockSpec(memory_space=pltpu.HBM)
+
+
+def call(kernel, outs, scratch=(), smem=(), hbm=(), anywhere=(), count=0, flops=10**8, traffic=6 * 10**6):
     return pl.pallas_call(
         kernel,
         out_shape=outs,
-        in_specs=[SMEM if k in smem else VMEM for k in range(count)],
+        in_specs=[
+            SMEM if k in smem else HBM if k in hbm else ANYWHERE if k in anywhere else VMEM for k in range(count)
+        ],
         out_specs=jax.tree.map(lambda _: VMEM, outs),
         scratch_shapes=list(scratch),
         compiler_params=pltpu.CompilerParams(vmem_limit_bytes=32 * 2**20),
@@ -434,28 +493,13 @@
 
 
 def shards(adjoint, material, face_partner, send_faces, migration, children):
-    own_curve = lax.axis_index("curve")
     own_seg = lax.axis_index("seg")
-    double = lambda x: jnp.broadcast_to(jnp.concatenate([x, x])[None, :], (8, 128))
-    mat = jnp.stack([double(1.0 / material[0]), double(material[1]), double(material[2])])
-    even_x = (own_curve % 2 == 0).astype(jnp.int32)
-    even_y = (own_seg % 2 == 0).astype(jnp.int32)
-    remote = face_partner - LOCAL
-    side = remote // CAP
-    block = side ^ jnp.where(side < 2, even_x, even_y)
-    lane = lambda q: (q % 6) * E_DEV + q // 6
-    partner = jnp.where(remote < 0, lane(face_partner), LOCAL + block * CAP + remote % CAP)
-    partner = partner.T.reshape(1, LOCAL)
-    sides = lane(send_faces[0])
-    flipped = sides.reshape(2, 2, CAP)[:, ::-1]
-    even = jnp.stack([even_x, even_y])[:, None, None]
-    sent = jnp.where(even == 1, flipped, sides.reshape(2, 2, CAP)).reshape(4 * CAP, 1)
-
     owner, slot, octant = migration[0], migration[1], migration[2]
     key = jnp.where(owner == own_seg, slot, P_DEV + 2 * owner + slot)
     first = octant == 0
     rank = jnp.sum((first[:, None] & (key[:, None] < key[None, :])).astype(jnp.int32), axis=0)
-    place = (octant * P_DEV + rank).reshape(1, E_DEV)
+    place = octant * P_DEV + rank
+    place = jnp.concatenate([place, place]).reshape(1, 128)
     keys = jnp.sum(
         jnp.where(first[:, None] & (rank[:, None] == jnp.arange(P_DEV)[None, :]), key[:, None], 0), axis=0
     )
@@ -470,13 +514,15 @@
 
     outs = call(
         begin_kernel,
-        [state, table, shape(2 * LOCAL, LOCAL, dtype=BF), shape(128, LOCAL, dtype=BF), shape(64, 2 * LOCAL, dtype=BF)]
+        [state, shape(3, 8, 128), table]
+        + [shape(2 * LOCAL, LOCAL, dtype=BF), shape(128, LOCAL, dtype=BF), shape(64, 2 * LOCAL, dtype=BF)]
         + payload,
-        [turn],
+        [pltpu.VMEM((9, E_DEV, NODES), F32), pltpu.SemaphoreType.DMA((9,)), turn, pltpu.VMEM((128, 128), F32)],
+        hbm=(0,),
         count=4,
-    )(adjoint, mat, partner, sent)
-    v, t, local_hot, remote_hot, send_hot = outs[:5]
-    out_going = outs[5:]
+    )(adjoint, material, face_partner, send_faces)
+    v, mat, t, local_hot, remote_hot, send_hot = outs[:6]
+    out_going = outs[6:]
     pairs = exchange_pairs()
     for step in range(1, 5):
         arrived = [lax.ppermute(x, axis, p) for x, (axis, p) in zip(out_going, pairs)]
@@ -491,22 +537,30 @@
                 functools.partial(finish_kernel, factor), [state, table] + payload, [face_scratch], count=9
             )(vol, part, *arrived, remote_hot, mat, send_hot)
             v, t, out_going = outs[0], outs[1], outs[2:]
-    high, low = refine_parts()
-    updated, home, away = call(
+    wa, wb, lines = (jnp.asarray(x) for x in refine_parts())
+    total, home, away = call(
         functools.partial(end_kernel, factor),
-        [shape(9, E_DEV, NODES), shape(9, P_DEV, NODES), shape(N_SEG, 9, 8, 128)],
+        [state, shape(9, 4, P_DEV, 128), shape(N_SEG, 9, 8, 128)],
         [
             pltpu.VMEM((9, 4, 64, 128), F32),
             face_scratch,
             turn,
-            pltpu.VMEM((9, E_DEV, NODES), F32),
-            pltpu.VMEM((80, NODES), F32),
+            pltpu.VMEM((128, 256), F32),
+            pltpu.VMEM((9, 4, 8, 128), F32),
         ],
         smem=(0,),
-        count=12,
-    )(keys, vol, part, *arrived, remote_hot, acc, place, jnp.asarray(high), jnp.asarray(low))
+        count=13,
+    )(keys, vol, part, *arrived, remote_hot, acc, place, wa, wb, lines)
     fetched = lax.all_to_all(away, "seg", split_axis=0, concat_axis=0, tiled=True)
-    parents = call(parent_kernel, [shape(9, P_DEV, NODES)], smem=(0,), count=3)(source, home, fetched)[0]
+    updated = call(next_kernel, [shape(9, E_DEV, NODES)], [turn], count=1)(total)[0]
+    parents = call(
+        parent_kernel,
+        [shape(9, P_DEV, NODES)],
+        [pltpu.VMEM((P_DEV, 9, 8, 128), F32), pltpu.SemaphoreType.DMA((P_DEV,))],
+        smem=(0,),
+        anywhere=(2,),
+        count=3,
+    )(source, home, fetched)[0]
     return (updated, parents)
 
 

time: 75.9 us -> 75.2 us (level)
  other arithmetic: 3.46 us -> 0.33 us
  starting transfers between devices: 26.9 us -> 29.4 us
  Pallas kernels: 29.7 us -> 27.6 us
  local copies, waits for them, and re-layouts: 1.5 us -> 3.43 us
    pallas_call x3, Pallas kernels: 10.3 us -> 5.97 us  [shards(): call(volume_kernel, [state, face_part, state], count=5)]
    pallas_call x3 -> x4, Pallas kernels: 12.4 us -> 16.2 us  [the longest x1 7.58 us: shards(): call(functools.partial(end_kernel, factor), [state, shape(9, 4, P_DEV, 12...]
    ppermute x16, waiting for transfers between devices: 2.05 us -> 4.49 us  [shards(): lax.ppermute(x, axis, p)]
    all_to_all x1, waiting for transfers between devices: 11 us -> 8.71 us  [shards(): lax.all_to_all(away, 'seg', split_axis=0, concat_axis=0, tiled=True)]
    unnamed x10 -> x17, local copies, waits for them, and re-layouts: 1.28 us -> 3.43 us
    ppermute x16, starting transfers between devices: 23.2 us -> 25.2 us  [shards(): lax.ppermute(x, axis, p)]
    pallas_call x1, Pallas kernels: 3.19 us -> 1.69 us  [shards(): call(first_volume_kernel, [state, face_part], count=4)(v, t, local_hot, mat)]
    div x2 -> x0, other arithmetic: 1.49 us -> none  [the longest x1 0.8 us: shards(): 1.0 / material[0]]
  transfers between devices with their start and end apart: 17 -> 17, of which waited for: 3 -> 5; matrix products, arithmetic and copies ran while one was open for 0% -> 0% of each run, Pallas kernels for 18% -> 14%
where the time goes in v1:
time: 75.2 us; the launch traced here: 74.8 us
  starting transfers between devices  29.4 us (39%)
  Pallas kernels  27.6 us (37%)
  waiting for transfers between devices  13.2 us (18%)
  local copies, waits for them, and re-layouts  3.43 us (5%)
  between operations  0.86 us (1%)
    ppermute x16, starting transfers between devices, shards(): lax.ppermute(x, axis, p)  25.2 us
    all_to_all x1, waiting for transfers between devices, shards(): lax.all_to_all(away, 'seg', split_axis=0, concat_axis=0, tiled=True)  8.71 us
    pallas_call x1, Pallas kernels, shards(): call(functools.partial(end_kernel, factor), [state, shape(9, 4, P_DEV, 12...  7.58 us
    pallas_call x3, Pallas kernels, shards(): call(volume_kernel, [state, face_part, state], count=5)  5.97 us
    ppermute x16, waiting for transfers between devices, shards(): lax.ppermute(x, axis, p)  4.49 us
    all_to_all x1, starting transfers between devices, shards(): lax.all_to_all(away, 'seg', split_axis=0, concat_axis=0, tiled=True)  4.19 us
    pallas_call x1, Pallas kernels, shards(): call(begin_kernel, [state, shape(3, 8, 128), table] + [shape(2 * LOCAL, L...  3.82 us
    pallas_call x3, Pallas kernels, shards(): call(functools.partial(finish_kernel, factor), [state, table] + payload,...  3.77 us
  transfers between devices with their start and end apart: 17, of which 5 were waited for; matrix products, arithmetic and copies ran while one was open for 0% of the time, Pallas kernels for 14%

profile of v1, /device:TPU:0, one launch (start us, length us, event | category | flops | bytes accessed | tf_op | source)
XLA Modules:
  0.0 74.8 jit_solution(8475751050478335812)
XLA Ops:
  0.6 0.8 %copy.12.faces_ref = s32[64,6]{1,0:T(8,128)S(1)} copy(s32[64,6]{0,1:T(8,128)} %param.11) | data formatting | bytes 3072 | tf_op args[2]
  1.4 1.3 %copy-done = f32[9,64,512]{2,1,0:T(8,128)S(1)} copy-done((f32[9,64,512]{2,1,0:T(8,128)S(1)}, f32[9,64,512]{2,1,0:T(8,128)}, u32[]{:S(2)}) %copy-start) | copy-done | bytes 1179672
  2.7 0.7 copy-done.4
  3.4 0.7 copy-done.5
  4.1 3.8 %shard_map.104 = (f32[9,4,64,128]{3,2,1,0:T(8,128)S(1)}, f32[3,8,128]{2,1,0:T(8,128)S(1)}, bf16[384,768]{1,0:T(8,128)(2,1)S(1)}, bf16[768,384]{1,0:T(8,128)(2,1)...) custom-call(f32[9,64,512]{2,1,0:T(8,128)S(1)} %copy-done, ...), custom_call_target="tpu_custom_call" | custom-call | flops 100000000 | bytes 6000000 | tf_op jit(solution)/shard_map/pallas_call | solution.py:515
  7.9 0.1 collective-permute-start
  8.0 2.9 %collective-permute-start.1 = (f32[16,384]{1,0:T(8,128)S(1)}, f32[16,384]{1,0:T(8,128)S(1)}, u32[]{:S(2)}, u32[]{:S(2)}) collective-permute-start(f32[16,384]{1,0:T(8,128)S(1)} %get-tuple-element.51), channel_id=1, source_target_pairs={{16,32},{48,64},{80,96},{112,0},{32,16},{64,48},{96,80},{0,112},{1... | collective-permute-start | bytes 73736 | tf_op jit(solution)/shard_map/ppermute | solution.py:528
  10.9 1.9 %collective-permute-start.2 = (f32[16,384]{1,0:T(8,128)S(1)}, f32[16,384]{1,0:T(8,128)S(1)}, u32[]{:S(2)}, u32[]{:S(2)}) collective-permute-start(f32[16,384]{1,0:T(8,128)S(1)} %get-tuple-element.52), channel_id=1, source_target_pairs={{0,1},{2,3},{4,5},{6,7},{8,9},{10,11},{12,13},{14,15},{1,0},{3,2},... | collective-permute-start | bytes 73736 | tf_op jit(solution)/shard_map/ppermute | solution.py:528
  12.8 5.0 %collective-permute-start.3 = (f32[16,384]{1,0:T(8,128)S(1)}, f32[16,384]{1,0:T(8,128)S(1)}, u32[]{:S(2)}, u32[]{:S(2)}) collective-permute-start(f32[16,384]{1,0:T(8,128)S(1)} %get-tuple-element.53), channel_id=1, source_target_pairs={{1,2},{3,4},{5,6},{7,8},{9,10},{11,12},{13,14},{15,0},{2,1},{4,3},... | collective-permute-start | bytes 73736 | tf_op jit(solution)/shard_map/ppermute | solution.py:528
  17.8 0.1 convert_reduce_fusion
  17.9 1.7 %shard_map.105 = (f32[9,4,64,128]{3,2,1,0:T(8,128)S(1)}, f32[384,384]{1,0:T(8,128)S(1)}) custom-call(f32[9,4,64,128]{3,2,1,0:T(8,128)S(1)} %get-tuple-element.44.v_ref.acc_ref, bf16[384,768]{1,0:T(8,128)(2,1)S(1)} %get-tuple-element.45.t_ref, bf16[768,384]{1,0:T(8,128)(2,1)S(1)} %get-tuple-element.46.local_ref, f32[3,8,128]{2,1,0:T(8,128)S(1)} %get-tuple-element.47.mat_ref), custom_call_target="tpu_custom_call" | custom-call | flops 100000000 | bytes 6000000 | tf_op jit(solution)/shard_map/pallas_call | solution.py:530
  19.6 0.0 collective-permute-done.r0
  19.7 0.0 collective-permute-done.1.r1
  19.7 0.0 collective-permute-done.2.r2
  19.7 0.3 collective-permute-done.3.r3
  20.0 1.3 %shard_map.106 = (f32[9,4,64,128]{3,2,1,0:T(8,128)S(1)}, bf16[384,768]{1,0:T(8,128)(2,1)S(1)}, f32[16,384]{1,0:T(8,128)S(1)}, f32[16,384]{1,0:T(8,128)S(1)}, f32...) custom-call(f32[9,4,64,128]{3,2,1,0:T(8,128)S(1)} %get-tuple-element.48.vol_ref, f32[384,384]{1,0:T(8,128)S(1)} %get-tuple-element.49.part_ref, ...), custom_call_target="tpu_custom_call" | custom-call | flops 100000000 | bytes 6000000 | tf_op jit(solution)/shard_map/pallas_call | solution.py:536
  21.3 0.1 collective-permute-start.4
  21.3 0.9 %collective-permute-start.5 = (f32[16,384]{1,0:T(8,128)S(1)}, f32[16,384]{1,0:T(8,128)S(1)}, u32[]{:S(2)}, u32[]{:S(2)}) collective-permute-start(f32[16,384]{1,0:T(8,128)S(1)} %get-tuple-element.61), channel_id=1, source_target_pairs={{16,32},{48,64},{80,96},{112,0},{32,16},{64,48},{96,80},{0,112},{1... | collective-permute-start | bytes 73736 | tf_op jit(solution)/shard_map/ppermute | solution.py:528
  22.3 0.0 collective-permute-start.6
  22.3 5.0 %collective-permute-start.7 = (f32[16,384]{1,0:T(8,128)S(1)}, f32[16,384]{1,0:T(8,128)S(1)}, u32[]{:S(2)}, u32[]{:S(2)}) collective-permute-start(f32[16,384]{1,0:T(8,128)S(1)} %get-tuple-element.63), channel_id=1, source_target_pairs={{1,2},{3,4},{5,6},{7,8},{9,10},{11,12},{13,14},{15,0},{2,1},{4,3},... | collective-permute-start | bytes 73736 | tf_op jit(solution)/shard_map/ppermute | solution.py:528
  27.2 2.0 %shard_map.107 = (f32[9,4,64,128]{3,2,1,0:T(8,128)S(1)}, f32[384,384]{1,0:T(8,128)S(1)}, f32[9,4,64,128]{3,2,1,0:T(8,128)S(1)}) custom-call(f32[9,4,64,128]{3,2,1,0:T(8,128)S(1)} %get-tuple-element.56.v_ref, bf16[384,768]{1,0:T(8,128)(2,1)S(1)} %get-tuple-element.57.t_ref, bf16[768,384]{1,0:T(8,128)(2,1)S(1)} %get-tuple-element.46.local_ref, ...), custom_call_target="tpu_custom_call" | custom-call | flops 100000000 | bytes 6000000 | tf_op jit(solution)/shard_map/pallas_call | solution.py:533
  29.2 0.0 collective-permute-done.4.r0
  29.2 0.0 collective-permute-done.6.r2
  29.2 0.2 collective-permute-done.7.r3
  29.4 1.3 %shard_map.108 = (f32[9,4,64,128]{3,2,1,0:T(8,128)S(1)}, bf16[384,768]{1,0:T(8,128)(2,1)S(1)}, f32[16,384]{1,0:T(8,128)S(1)}, f32[16,384]{1,0:T(8,128)S(1)}, f32...) custom-call(f32[9,4,64,128]{3,2,1,0:T(8,128)S(1)} %get-tuple-element.58.vol_ref, f32[384,384]{1,0:T(8,128)S(1)} %get-tuple-element.59.part_ref, ...), custom_call_target="tpu_custom_call" | custom-call | flops 100000000 | bytes 6000000 | tf_op jit(solution)/shard_map/pallas_call | solution.py:536
  30.7 0.1 collective-permute-start.10
  30.8 5.1 %collective-permute-start.11 = (f32[16,384]{1,0:T(8,128)S(1)}, f32[16,384]{1,0:T(8,128)S(1)}, u32[]{:S(2)}, u32[]{:S(2)}) collective-permute-start(f32[16,384]{1,0:T(8,128)S(1)} %get-tuple-element.72), channel_id=1, source_target_pairs={{1,2},{3,4},{5,6},{7,8},{9,10},{11,12},{13,14},{15,0},{2,1},{4,3},... | collective-permute-start | bytes 73736 | tf_op jit(solution)/shard_map/ppermute | solution.py:528
  35.8 0.0 collective-permute-start.8
  35.8 0.7 collective-permute-start.9
  36.5 0.1 select_reduce_fusion.keys_ref
  36.6 2.0 %shard_map.109 = (f32[9,4,64,128]{3,2,1,0:T(8,128)S(1)}, f32[384,384]{1,0:T(8,128)S(1)}, f32[9,4,64,128]{3,2,1,0:T(8,128)S(1)}) custom-call(f32[9,4,64,128]{3,2,1,0:T(8,128)S(1)} %get-tuple-element.64.v_ref, bf16[384,768]{1,0:T(8,128)(2,1)S(1)} %get-tuple-element.65.t_ref, bf16[768,384]{1,0:T(8,128)(2,1)S(1)} %get-tuple-element.46.local_ref, ...), custom_call_target="tpu_custom_call" | custom-call | flops 100000000 | bytes 6000000 | tf_op jit(solution)/shard_map/pallas_call | solution.py:533
  38.6 0.0 collective-permute-done.10.r2
  38.6 0.0 collective-permute-done.8.r0
  38.6 1.6 %collective-permute-done.9.r1 = f32[16,384]{1,0:T(8,128)S(1)} collective-permute-done((f32[16,384]{1,0:T(8,128)S(1)}, f32[16,384]{1,0:T(8,128)S(1)}, u32[]{:S(2)}, u32[]{:S(2)}) %collective-permute-start.9) | collective-permute-done | bytes 24608 | tf_op jit(solution)/shard_map/ppermute | solution.py:528
  40.3 1.3 %shard_map.110 = (f32[9,4,64,128]{3,2,1,0:T(8,128)S(1)}, bf16[384,768]{1,0:T(8,128)(2,1)S(1)}, f32[16,384]{1,0:T(8,128)S(1)}, f32[16,384]{1,0:T(8,128)S(1)}, f32...) custom-call(f32[9,4,64,128]{3,2,1,0:T(8,128)S(1)} %get-tuple-element.67.vol_ref, f32[384,384]{1,0:T(8,128)S(1)} %get-tuple-element.68.part_ref, ...), custom_call_target="tpu_custom_call" | custom-call | flops 100000000 | bytes 6000000 | tf_op jit(solution)/shard_map/pallas_call | solution.py:536
  41.5 0.1 collective-permute-start.12
  41.6 0.8 %collective-permute-start.13 = (f32[16,384]{1,0:T(8,128)S(1)}, f32[16,384]{1,0:T(8,128)S(1)}, u32[]{:S(2)}, u32[]{:S(2)}) collective-permute-start(f32[16,384]{1,0:T(8,128)S(1)} %get-tuple-element.79), channel_id=1, source_target_pairs={{16,32},{48,64},{80,96},{112,0},{32,16},{64,48},{96,80},{0,112},{1... | collective-permute-start | bytes 73736 | tf_op jit(solution)/shard_map/ppermute | solution.py:528
  42.4 0.0 collective-permute-start.14
  42.4 2.7 %collective-permute-start.15 = (f32[16,384]{1,0:T(8,128)S(1)}, f32[16,384]{1,0:T(8,128)S(1)}, u32[]{:S(2)}, u32[]{:S(2)}) collective-permute-start(f32[16,384]{1,0:T(8,128)S(1)} %get-tuple-element.81), channel_id=1, source_target_pairs={{1,2},{3,4},{5,6},{7,8},{9,10},{11,12},{13,14},{15,0},{2,1},{4,3},... | collective-permute-start | bytes 73736 | tf_op jit(solution)/shard_map/ppermute | solution.py:528
  45.1 0.1 add_bitcast_fusion.place_ref
  45.1 2.0 %shard_map.111 = (f32[9,4,64,128]{3,2,1,0:T(8,128)S(1)}, f32[384,384]{1,0:T(8,128)S(1)}, f32[9,4,64,128]{3,2,1,0:T(8,128)S(1)}) custom-call(f32[9,4,64,128]{3,2,1,0:T(8,128)S(1)} %get-tuple-element.73.v_ref, bf16[384,768]{1,0:T(8,128)(2,1)S(1)} %get-tuple-element.74.t_ref, bf16[768,384]{1,0:T(8,128)(2,1)S(1)} %get-tuple-element.46.local_ref, ...), custom_call_target="tpu_custom_call" | custom-call | flops 100000000 | bytes 6000000 | tf_op jit(solution)/shard_map/pallas_call | solution.py:533
  47.2 0.0 collective-permute-done.12.r0
  47.2 2.3 %collective-permute-done.15.r3 = f32[16,384]{1,0:T(8,128)S(1)} collective-permute-done((f32[16,384]{1,0:T(8,128)S(1)}, f32[16,384]{1,0:T(8,128)S(1)}, u32[]{:S(2)}, u32[]{:S(2)}) %collective-permute-start.15) | collective-permute-done | bytes 24608 | tf_op jit(solution)/shard_map/ppermute | solution.py:528
  49.5 7.6 %shard_map.112 = (f32[9,4,64,128]{3,2,1,0:T(8,128)S(1)}, f32[9,4,8,128]{3,2,1,0:T(8,128)S(1)}, f32[16,9,8,128]{3,2,1,0:T(8,128)}) custom-call(s32[8]{0:T(128)S(1)} %select_reduce_fusion.keys_ref, f32[9,4,64,128]{3,2,1,0:T(8,128)S(1)} %get-tuple-element.76.vol_ref, f32[384,384]{1,0:T(8,128)S(1)} %get-tuple-element.77.part_ref, ...), custom_call_target="tpu_custom_call" | custom-call | flops 100000000 | bytes 6000000 | tf_op jit(solution)/shard_map/pallas_call | solution.py:541
  57.1 4.2 %all-to-all-start = ((f32[16,9,8,128]{3,2,1,0:T(8,128)}), f32[16,9,8,128]{3,2,1,0:T(8,128)S(1)}, u32[]{:S(2)}, u32[]{:S(2)}) async-start(f32[16,9,8,128]{3,2,1,0:T(8,128)} %get-tuple-element.85), calls=%async_computation | async-start | bytes 1179648 | tf_op jit(solution)/shard_map/all_to_all | solution.py:554
  61.4 3.1 %shard_map.113 = f32[9,64,512]{2,1,0:T(8,128)} custom-call(f32[9,4,64,128]{3,2,1,0:T(8,128)S(1)} %get-tuple-element.83.total_ref), custom_call_target="tpu_custom_call" | custom-call | flops 100000000 | bytes 6000000 | tf_op jit(solution)/shard_map/pallas_call | solution.py:555
  64.5 8.7 %all-to-all-done.arrived_ref = f32[16,9,8,128]{3,2,1,0:T(8,128)S(1)} async-done(((f32[16,9,8,128]{3,2,1,0:T(8,128)}), f32[16,9,8,128]{3,2,1,0:T(8,128)S(1)}, u32[]{:S(2)}, u32[]{:S(2)}) %all-to-all-start) | async-done | bytes 589856 | tf_op jit(solution)/shard_map/all_to_all | solution.py:554
  73.2 1.7 %shard_map.114 = f32[9,8,512]{2,1,0:T(8,128)} custom-call(s32[2,8]{1,0:T(2,128)S(1)} %pad_add_fusion.table_ref, f32[9,4,8,128]{3,2,1,0:T(8,128)S(1)} %get-tuple-element.84.home_ref, f32[16,9,8,128]{3,2,1,0:T(8,128)S(1)} %all-to-all-done.arrived_ref), custom_call_target="tpu_custom_call" | custom-call | flops 100000000 | bytes 6000000 | tf_op jit(solution)/shard_map/pallas_call | solution.py:556
  (23 shorter events, 0.1 us)
Async XLA Ops:
  0.6 17.2 %copy-start.6 = (s32[3,64]{1,0:T(4,128)S(1)}, s32[3,64]{1,0:T(4,128)}, u32[]{:S(2)}) copy-start(s32[3,64]{1,0:T(4,128)} %param.13) | copy-start | bytes 2308
  1.4 1.3 %copy-start = (f32[9,64,512]{2,1,0:T(8,128)S(1)}, f32[9,64,512]{2,1,0:T(8,128)}, u32[]{:S(2)}) copy-start(f32[9,64,512]{2,1,0:T(8,128)} %adjoint_ref.1) | copy-start | bytes 3538948
  2.7 0.7 copy-start.4
  3.4 0.7 copy-start.5
  7.9 11.8 %collective-permute-start = (f32[16,384]{1,0:T(8,128)S(1)}, f32[16,384]{1,0:T(8,128)S(1)}, u32[]{:S(2)}, u32[]{:S(2)}) collective-permute-start(f32[16,384]{1,0:T(8,128)S(1)} %get-tuple-element.50), channel_id=1, source_target_pairs={{0,16},{32,48},{64,80},{96,112},{16,0},{48,32},{80,64},{112,96},{1... | collective-permute-start | bytes 73736 | tf_op jit(solution)/shard_map/ppermute | solution.py:528
  8.0 11.7 %collective-permute-start.1 = (f32[16,384]{1,0:T(8,128)S(1)}, f32[16,384]{1,0:T(8,128)S(1)}, u32[]{:S(2)}, u32[]{:S(2)}) collective-permute-start(f32[16,384]{1,0:T(8,128)S(1)} %get-tuple-element.51), channel_id=1, source_target_pairs={{16,32},{48,64},{80,96},{112,0},{32,16},{64,48},{96,80},{0,112},{1... | collective-permute-start | bytes 73736 | tf_op jit(solution)/shard_map/ppermute | solution.py:528
  10.9 8.7 %collective-permute-start.2 = (f32[16,384]{1,0:T(8,128)S(1)}, f32[16,384]{1,0:T(8,128)S(1)}, u32[]{:S(2)}, u32[]{:S(2)}) collective-permute-start(f32[16,384]{1,0:T(8,128)S(1)} %get-tuple-element.52), channel_id=1, source_target_pairs={{0,1},{2,3},{4,5},{6,7},{8,9},{10,11},{12,13},{14,15},{1,0},{3,2},... | collective-permute-start | bytes 73736 | tf_op jit(solution)/shard_map/ppermute | solution.py:528
  12.8 7.1 %collective-permute-start.3 = (f32[16,384]{1,0:T(8,128)S(1)}, f32[16,384]{1,0:T(8,128)S(1)}, u32[]{:S(2)}, u32[]{:S(2)}) collective-permute-start(f32[16,384]{1,0:T(8,128)S(1)} %get-tuple-element.53), channel_id=1, source_target_pairs={{1,2},{3,4},{5,6},{7,8},{9,10},{11,12},{13,14},{15,0},{2,1},{4,3},... | collective-permute-start | bytes 73736 | tf_op jit(solution)/shard_map/ppermute | solution.py:528
  21.3 8.0 %collective-permute-start.4 = (f32[16,384]{1,0:T(8,128)S(1)}, f32[16,384]{1,0:T(8,128)S(1)}, u32[]{:S(2)}, u32[]{:S(2)}) collective-permute-start(f32[16,384]{1,0:T(8,128)S(1)} %get-tuple-element.60), channel_id=1, source_target_pairs={{0,16},{32,48},{64,80},{96,112},{16,0},{48,32},{80,64},{112,96},{1... | collective-permute-start | bytes 73736 | tf_op jit(solution)/shard_map/ppermute | solution.py:528
  21.3 7.9 %collective-permute-start.5 = (f32[16,384]{1,0:T(8,128)S(1)}, f32[16,384]{1,0:T(8,128)S(1)}, u32[]{:S(2)}, u32[]{:S(2)}) collective-permute-start(f32[16,384]{1,0:T(8,128)S(1)} %get-tuple-element.61), channel_id=1, source_target_pairs={{16,32},{48,64},{80,96},{112,0},{32,16},{64,48},{96,80},{0,112},{1... | collective-permute-start | bytes 73736 | tf_op jit(solution)/shard_map/ppermute | solution.py:528
  22.3 7.0 %collective-permute-start.6 = (f32[16,384]{1,0:T(8,128)S(1)}, f32[16,384]{1,0:T(8,128)S(1)}, u32[]{:S(2)}, u32[]{:S(2)}) collective-permute-start(f32[16,384]{1,0:T(8,128)S(1)} %get-tuple-element.62), channel_id=1, source_target_pairs={{0,1},{2,3},{4,5},{6,7},{8,9},{10,11},{12,13},{14,15},{1,0},{3,2},... | collective-permute-start | bytes 73736 | tf_op jit(solution)/shard_map/ppermute | solution.py:528
  22.3 7.1 %collective-permute-start.7 = (f32[16,384]{1,0:T(8,128)S(1)}, f32[16,384]{1,0:T(8,128)S(1)}, u32[]{:S(2)}, u32[]{:S(2)}) collective-permute-start(f32[16,384]{1,0:T(8,128)S(1)} %get-tuple-element.63), channel_id=1, source_target_pairs={{1,2},{3,4},{5,6},{7,8},{9,10},{11,12},{13,14},{15,0},{2,1},{4,3},... | collective-permute-start | bytes 73736 | tf_op jit(solution)/shard_map/ppermute | solution.py:528
  30.7 7.9 %collective-permute-start.10 = (f32[16,384]{1,0:T(8,128)S(1)}, f32[16,384]{1,0:T(8,128)S(1)}, u32[]{:S(2)}, u32[]{:S(2)}) collective-permute-start(f32[16,384]{1,0:T(8,128)S(1)} %get-tuple-element.71), channel_id=1, source_target_pairs={{0,1},{2,3},{4,5},{6,7},{8,9},{10,11},{12,13},{14,15},{1,0},{3,2},... | collective-permute-start | bytes 73736 | tf_op jit(solution)/shard_map/ppermute | solution.py:528
  30.8 7.9 %collective-permute-start.11 = (f32[16,384]{1,0:T(8,128)S(1)}, f32[16,384]{1,0:T(8,128)S(1)}, u32[]{:S(2)}, u32[]{:S(2)}) collective-permute-start(f32[16,384]{1,0:T(8,128)S(1)} %get-tuple-element.72), channel_id=1, source_target_pairs={{1,2},{3,4},{5,6},{7,8},{9,10},{11,12},{13,14},{15,0},{2,1},{4,3},... | collective-permute-start | bytes 73736 | tf_op jit(solution)/shard_map/ppermute | solution.py:528
  35.8 2.8 %collective-permute-start.8 = (f32[16,384]{1,0:T(8,128)S(1)}, f32[16,384]{1,0:T(8,128)S(1)}, u32[]{:S(2)}, u32[]{:S(2)}) collective-permute-start(f32[16,384]{1,0:T(8,128)S(1)} %get-tuple-element.69), channel_id=1, source_target_pairs={{0,16},{32,48},{64,80},{96,112},{16,0},{48,32},{80,64},{112,96},{1... | collective-permute-start | bytes 73736 | tf_op jit(solution)/shard_map/ppermute | solution.py:528
  35.8 4.5 %collective-permute-start.9 = (f32[16,384]{1,0:T(8,128)S(1)}, f32[16,384]{1,0:T(8,128)S(1)}, u32[]{:S(2)}, u32[]{:S(2)}) collective-permute-start(f32[16,384]{1,0:T(8,128)S(1)} %get-tuple-element.70), channel_id=1, source_target_pairs={{16,32},{48,64},{80,96},{112,0},{32,16},{64,48},{96,80},{0,112},{1... | collective-permute-start | bytes 73736 | tf_op jit(solution)/shard_map/ppermute | solution.py:528
  41.5 5.6 %collective-permute-start.12 = (f32[16,384]{1,0:T(8,128)S(1)}, f32[16,384]{1,0:T(8,128)S(1)}, u32[]{:S(2)}, u32[]{:S(2)}) collective-permute-start(f32[16,384]{1,0:T(8,128)S(1)} %get-tuple-element.78), channel_id=1, source_target_pairs={{0,16},{32,48},{64,80},{96,112},{16,0},{48,32},{80,64},{112,96},{1... | collective-permute-start | bytes 73736 | tf_op jit(solution)/shard_map/ppermute | solution.py:528
  41.6 5.6 %collective-permute-start.13 = (f32[16,384]{1,0:T(8,128)S(1)}, f32[16,384]{1,0:T(8,128)S(1)}, u32[]{:S(2)}, u32[]{:S(2)}) collective-permute-start(f32[16,384]{1,0:T(8,128)S(1)} %get-tuple-element.79), channel_id=1, source_target_pairs={{16,32},{48,64},{80,96},{112,0},{32,16},{64,48},{96,80},{0,112},{1... | collective-permute-start | bytes 73736 | tf_op jit(solution)/shard_map/ppermute | solution.py:528
  42.4 4.8 %collective-permute-start.14 = (f32[16,384]{1,0:T(8,128)S(1)}, f32[16,384]{1,0:T(8,128)S(1)}, u32[]{:S(2)}, u32[]{:S(2)}) collective-permute-start(f32[16,384]{1,0:T(8,128)S(1)} %get-tuple-element.80), channel_id=1, source_target_pairs={{0,1},{2,3},{4,5},{6,7},{8,9},{10,11},{12,13},{14,15},{1,0},{3,2},... | collective-permute-start | bytes 73736 | tf_op jit(solution)/shard_map/ppermute | solution.py:528
  42.4 7.1 %collective-permute-start.15 = (f32[16,384]{1,0:T(8,128)S(1)}, f32[16,384]{1,0:T(8,128)S(1)}, u32[]{:S(2)}, u32[]{:S(2)}) collective-permute-start(f32[16,384]{1,0:T(8,128)S(1)} %get-tuple-element.81), channel_id=1, source_target_pairs={{1,2},{3,4},{5,6},{7,8},{9,10},{11,12},{13,14},{15,0},{2,1},{4,3},... | collective-permute-start | bytes 73736 | tf_op jit(solution)/shard_map/ppermute | solution.py:528
  45.1 4.4 %copy-start.1 = (f32[64,8,128]{2,1,0:T(8,128)S(1)}, f32[64,8,128]{2,1,0:T(8,128)}, u32[]{:S(2)}) copy-start(f32[64,8,128]{2,1,0:T(8,128)} %constant.21.clone.lines_ref) | copy-start | bytes 786436
  45.1 4.4 %copy-start.2 = (bf16[256,128]{1,0:T(8,128)(2,1)S(1)}, bf16[256,128]{1,0:T(8,128)(2,1)}, u32[]{:S(2)}) copy-start(bf16[256,128]{1,0:T(8,128)(2,1)} %constant.20.clone.wb_ref) | copy-start | bytes 196612
  45.1 4.4 %copy-start.3 = (bf16[256,128]{1,0:T(8,128)(2,1)S(1)}, bf16[256,128]{1,0:T(8,128)(2,1)}, u32[]{:S(2)}) copy-start(bf16[256,128]{1,0:T(8,128)(2,1)} %constant.7.clone.wa_ref) | copy-start | bytes 196612
  57.1 4.2 %copy-start.7 = (s32[2,8]{1,0:T(2,128)S(1)}, s32[2,8]{1,0:T(2,128)}, u32[]{:S(2)}) copy-start(s32[2,8]{1,0:T(2,128)} %param.14) | copy-start | bytes 196
  57.1 16.0 %all-to-all-start = ((f32[16,9,8,128]{3,2,1,0:T(8,128)}), f32[16,9,8,128]{3,2,1,0:T(8,128)S(1)}, u32[]{:S(2)}, u32[]{:S(2)}) async-start(f32[16,9,8,128]{3,2,1,0:T(8,128)} %get-tuple-element.85), calls=%async_computation | async-start | bytes 1179648 | tf_op jit(solution)/shard_map/all_to_all | solution.py:554

commit v2 on v1

--- a/solution.py
+++ b/solution.py
@@ -204,16 +204,7 @@
         out_refs[k][...] = rows[16 * k : 16 * k + 16]
 
 
-def begin_kernel(
-    adjoint_ref, material_ref, faces_ref, sides_ref,
-    v_ref, mat_ref, t_ref, local_ref, remote_ref, send_ref, p0, p1, p2, p3,
-    staged_ref, sem, turn_ref, small_ref,
-):
-    def fetch(i):
-        return pltpu.make_async_copy(adjoint_ref.at[i], staged_ref.at[i], sem.at[i])
-
-    for i in range(9):
-        fetch(i).start()
+def index_kernel(pack_ref, mat_ref, local_ref, remote_ref, send_ref, small_ref):
     even_x = 1 - lax.axis_index("curve") % 2
     even_y = 1 - lax.axis_index("seg") % 2
 
@@ -222,20 +213,15 @@
         return (q - 6 * element) * E_DEV + element
 
     for i in range(3):
-        row = material_ref[pl.ds(i, 1), :]
+        row = pack_ref[pl.ds(i, 1), :]
         if i == 0:
             row = 1.0 / row
-        mat_ref[i] = jnp.broadcast_to(jnp.concatenate([row, row], axis=1), (8, 128))
-    small_ref[...] = jnp.zeros_like(small_ref)
-    faces = faces_ref[...].astype(F32)
-    small_ref[pl.ds(0, 64), pl.ds(0, 6)] = faces
-    small_ref[pl.ds(64, 64), pl.ds(0, 6)] = faces
-    turned = small_ref[...].T
+        mat_ref[i] = jnp.broadcast_to(row, (8, 128))
     low_row = lax.broadcasted_iota(jnp.int32, (1, 128), 1) < 64
     weight = jnp.where(low_row, lift_half, -lift_half)
     for direction in range(3):
         q = jnp.where(
-            low_row, turned[2 * direction : 2 * direction + 1], turned[2 * direction + 1 : 2 * direction + 2]
+            low_row, pack_ref[pl.ds(3 + 2 * direction, 1), :], pack_ref[pl.ds(4 + 2 * direction, 1), :]
         ).astype(jnp.int32)
         remote = q - LOCAL
         side = remote >> 4
@@ -250,9 +236,10 @@
                     local_ref[pl.ds(part * LOCAL + start, 64), lanes] = hot
                 else:
                     remote_ref[pl.ds(part * 64, 64), lanes] = hot
-    small_ref[pl.ds(0, 4), pl.ds(0, CAP)] = sides_ref[0].astype(F32)
+    small_ref[pl.ds(0, 16), :] = pack_ref[...]
+    small_ref[pl.ds(16, 112), :] = jnp.zeros((112, 128), F32)
     turned = small_ref[...].T
-    columns = [lane(turned[0:CAP, r : r + 1].astype(jnp.int32)) for r in range(4)]
+    columns = [lane(turned[0:CAP, 9 + r : 10 + r].astype(jnp.int32)) for r in range(4)]
     for axis, even in ((0, even_x), (1, even_y)):
         first, second = columns[2 * axis], columns[2 * axis + 1]
         for k, column in enumerate((first + even * (second - first), second + even * (first - second))):
@@ -262,19 +249,18 @@
             rows = pl.ds((2 * axis + k) * CAP, CAP)
             send_ref[rows, pl.ds(0, LOCAL)] = hot
             send_ref[rows, pl.ds(LOCAL, LOCAL)] = hot
+
+
+def begin_kernel(adjoint_ref, mat_ref, send_ref, v_ref, t_ref, p0, p1, p2, p3, turn_ref):
     low = lax.broadcasted_iota(jnp.int32, (64, 128), 1) < 64
-
-    def body(i, carry):
-        fetch(i).wait()
-        x = staged_ref[i]
-        turn_ref[...] = jnp.concatenate([x, x], axis=0).T
+    for i in range(9):
+        x = adjoint_ref[i]
+        turn = turn_ref.at[i % 3]
+        turn[...] = jnp.concatenate([x, x], axis=0).T
         for j in range(4):
             v_ref[i, j] = jnp.where(
-                low, turn_ref[pl.ds(2 * j, 64, stride=8), :], turn_ref[pl.ds(2 * j + 1, 64, stride=8), :]
+                low, turn[pl.ds(2 * j, 64, stride=8), :], turn[pl.ds(2 * j + 1, 64, stride=8), :]
             )
-        return carry
-
-    lax.fori_loop(0, 9, body, 0)
     build_table(v_ref, materials(mat_ref), t_ref)
     send_values(send_ref, t_ref, (p0, p1, p2, p3))
 
@@ -358,7 +344,7 @@
 
 
 def finish_kernel(
-    factor, vol_ref, part_ref, r0, r1, r2, r3, remote_ref, mat_ref, send_ref,
+    factor, vol_ref, part_ref, r3, r2, r1, r0, remote_ref, mat_ref, send_ref,
     v_ref, t_ref, p0, p1, p2, p3, face_ref,
 ):
     add_faces(vol_ref, part_ref, (r0, r1, r2, r3), remote_ref, factor, v_ref, face_ref)
@@ -367,8 +353,8 @@
 
 
 def end_kernel(
-    factor, keys_ref, vol_ref, part_ref, r0, r1, r2, r3, remote_ref, acc_ref, place_ref, wa_ref, wb_ref, lines_ref,
-    total_ref, home_ref, away_ref, v_ref, face_ref, turn_ref, rows_ref, parent_ref,
+    factor, keys_ref, vol_ref, part_ref, r3, r2, r1, r0, remote_ref, acc_ref, place_ref, wa_ref, wb_ref, lines_ref,
+    total_ref, home_ref, away_ref, v_ref, face_ref, turn_ref, ranked_ref, rows_ref, plane_ref, parent_ref,
 ):
     add_faces(vol_ref, part_ref, (r0, r1, r2, r3), remote_ref, factor, v_ref, face_ref)
     place = jnp.where(
@@ -376,36 +362,38 @@
     ).astype(BF)
     wide = lax.broadcasted_iota(jnp.int32, (64, 128), 1) < 64
     low = low_half()
-
-    def body(i, carry):
+    for i in range(9):
         for j in range(4):
             tile = acc_ref[i, j] + v_ref[i, j]
             total_ref[i, j] = tile
             high = tile.astype(BF).astype(F32)
             rest = tile - high
-            turn_ref[pl.ds(2 * j, 64, stride=8), :] = jnp.where(wide, high, pltpu.roll(rest, 64, 1))
-            turn_ref[pl.ds(2 * j + 1, 64, stride=8), :] = jnp.where(wide, pltpu.roll(high, 64, 1), rest)
-        ranked = lax.dot_general(
-            place, turn_ref[...].astype(BF), (((1,), (1,)), ((), ())), preferred_element_type=F32
+            turn_ref[i, pl.ds(2 * j, 64, stride=8), :] = jnp.where(wide, high, pltpu.roll(rest, 64, 1))
+            turn_ref[i, pl.ds(2 * j + 1, 64, stride=8), :] = jnp.where(wide, pltpu.roll(high, 64, 1), rest)
+        ranked_ref[i] = lax.dot_general(
+            place, turn_ref[i].astype(BF), (((1,), (1,)), ((), ())), preferred_element_type=F32
         )
+    for i in range(9):
         for upper in range(2):
             for t in range(4):
-                x = [ranked[8 * (4 * upper + k) : 8 * (4 * upper + k) + 8, 128 * t : 128 * t + 128] for k in range(4)]
+                x = [ranked_ref[i, pl.ds(8 * (4 * upper + k), 8), pl.ds(128 * t, 128)] for k in range(4)]
                 for pair in range(2):
                     x0, x1 = x[2 * pair], x[2 * pair + 1]
                     lanes = pl.ds(128 * pair, 128)
-                    rows_ref[pl.ds(64 * upper + 16 * t, 8), lanes] = jnp.where(low, x0, swap_halves(x1))
-                    rows_ref[pl.ds(64 * upper + 16 * t + 8, 8), lanes] = jnp.where(low, swap_halves(x0), x1)
-        high, rest = split(rows_ref[...])
+                    rows_ref[i, pl.ds(64 * upper + 16 * t, 8), lanes] = jnp.where(low, x0, swap_halves(x1))
+                    rows_ref[i, pl.ds(64 * upper + 16 * t + 8, 8), lanes] = jnp.where(low, swap_halves(x0), x1)
+        high, rest = split(rows_ref[i])
         plane = jnp.dot(high, wa_ref[...], preferred_element_type=F32)
-        plane = plane + pltpu.roll(plane, 64, 1) + jnp.dot(rest, wb_ref[...], preferred_element_type=F32)
-        for t in range(4):
-            parent_ref[i, t] = sum(
-                plane[8 * k : 8 * k + 8] * lines_ref[4 * k + t] for k in range(16)
-            )
-        return carry
-
-    lax.fori_loop(0, 9, body, 0)
+        plane_ref[i] = plane + pltpu.roll(plane, 64, 1) + jnp.dot(rest, wb_ref[...], preferred_element_type=F32)
+    for t in range(4):
+        sums = [None] * 9
+        for k in range(16):
+            line = lines_ref[4 * k + t]
+            for i in range(9):
+                term = plane_ref[i, pl.ds(8 * k, 8), :] * line
+                sums[i] = term if k == 0 else sums[i] + term
+        for i in range(9):
+            parent_ref[i, t] = sums[i]
     home_ref[...] = jnp.zeros_like(home_ref)
     for g in range(P_DEV):
         key = keys_ref[g]
@@ -437,28 +425,21 @@
     lax.fori_loop(0, 9, body, 0)
 
 
-def parent_kernel(table_ref, home_ref, arrived_ref, out_ref, block_ref, sem):
-    def fetch(p):
-        return pltpu.make_async_copy(arrived_ref.at[table_ref[0, p]], block_ref.at[p], sem.at[p])
-
-    for p in range(P_DEV):
-
-        @pl.when(table_ref[1, p] >= 0)
-        def _():
-            fetch(p).start()
-
+def parent_kernel(table_ref, home_ref, arrived_ref, out_ref):
     for i in range(9):
         for t in range(4):
             out_ref[i, :, pl.ds(128 * t, 128)] = home_ref[i, t]
     for p in range(P_DEV):
+        holder = table_ref[0, p]
         slot = table_ref[1, p]
 
         @pl.when(slot >= 0)
         def _():
-            fetch(p).wait()
             for i in range(9):
                 for t in range(4):
-                    out_ref[i, pl.ds(p, 1), pl.ds(128 * t, 128)] = block_ref[p, i, pl.ds(slot * 4 + t, 1), :]
+                    out_ref[i, pl.ds(p, 1), pl.ds(128 * t, 128)] = arrived_ref[
+                        holder, i, pl.ds(slot * 4 + t, 1), :
+                    ]
 
 
 def shape(*dims, dtype=F32):
@@ -467,17 +448,13 @@
 
 VMEM = pl.BlockSpec(memory_space=pltpu.VMEM)
 SMEM = pl.BlockSpec(memory_space=pltpu.SMEM)
-ANYWHERE = pl.BlockSpec(memory_space=pl.ANY)
-HBM = pl.BlockSpec(memory_space=pltpu.HBM)
-
-
-def call(kernel, outs, scratch=(), smem=(), hbm=(), anywhere=(), count=0, flops=10**8, traffic=6 * 10**6):
+
+
+def call(kernel, outs, scratch=(), smem=(), count=0, flops=10**8, traffic=6 * 10**6):
     return pl.pallas_call(
         kernel,
         out_shape=outs,
-        in_specs=[
-            SMEM if k in smem else HBM if k in hbm else ANYWHERE if k in anywhere else VMEM for k in range(count)
-        ],
+        in_specs=[SMEM if k in smem else VMEM for k in range(count)],
         out_specs=jax.tree.map(lambda _: VMEM, outs),
         scratch_shapes=list(scratch),
         compiler_params=pltpu.CompilerParams(vmem_limit_bytes=32 * 2**20),
@@ -512,20 +489,30 @@
     face_scratch = pltpu.VMEM((LOCAL, LOCAL), F32)
     turn = pltpu.VMEM((NODES, 128), F32)
 
-    outs = call(
-        begin_kernel,
-        [state, shape(3, 8, 128), table]
-        + [shape(2 * LOCAL, LOCAL, dtype=BF), shape(128, LOCAL, dtype=BF), shape(64, 2 * LOCAL, dtype=BF)]
-        + payload,
-        [pltpu.VMEM((9, E_DEV, NODES), F32), pltpu.SemaphoreType.DMA((9,)), turn, pltpu.VMEM((128, 128), F32)],
-        hbm=(0,),
-        count=4,
-    )(adjoint, material, face_partner, send_faces)
-    v, mat, t, local_hot, remote_hot, send_hot = outs[:6]
-    out_going = outs[6:]
+    twice = lambda x: jnp.concatenate([x, x], axis=1)
+    pack = jnp.concatenate(
+        [
+            twice(material),
+            twice(face_partner.T.astype(F32)),
+            jnp.pad(send_faces[0].astype(F32), ((0, 3), (0, 128 - CAP))),
+        ],
+        axis=0,
+    )
+    mat, local_hot, remote_hot, send_hot = call(
+        index_kernel,
+        [shape(3, 8, 128)]
+        + [shape(2 * LOCAL, LOCAL, dtype=BF), shape(128, LOCAL, dtype=BF), shape(64, 2 * LOCAL, dtype=BF)],
+        [pltpu.VMEM((128, 128), F32)],
+        count=1,
+        traffic=4 * 10**7,
+    )(pack)
+    outs = call(begin_kernel, [state, table] + payload, [pltpu.VMEM((3, NODES, 128), F32)], count=3)(
+        adjoint, mat, send_hot
+    )
+    v, t, out_going = outs[0], outs[1], outs[2:]
     pairs = exchange_pairs()
     for step in range(1, 5):
-        arrived = [lax.ppermute(x, axis, p) for x, (axis, p) in zip(out_going, pairs)]
+        arrived = [lax.ppermute(out_going[k], *pairs[k]) for k in (3, 2, 1, 0)]
         if step == 1:
             vol, part = call(first_volume_kernel, [state, face_part], count=4)(v, t, local_hot, mat)
             acc = v
@@ -544,8 +531,10 @@
         [
             pltpu.VMEM((9, 4, 64, 128), F32),
             face_scratch,
-            turn,
-            pltpu.VMEM((128, 256), F32),
+            pltpu.VMEM((9, NODES, 128), F32),
+            pltpu.VMEM((9, 64, NODES), F32),
+            pltpu.VMEM((9, 128, 256), F32),
+            pltpu.VMEM((9, 128, 128), F32),
             pltpu.VMEM((9, 4, 8, 128), F32),
         ],
         smem=(0,),
@@ -553,14 +542,7 @@
     )(keys, vol, part, *arrived, remote_hot, acc, place, wa, wb, lines)
     fetched = lax.all_to_all(away, "seg", split_axis=0, concat_axis=0, tiled=True)
     updated = call(next_kernel, [shape(9, E_DEV, NODES)], [turn], count=1)(total)[0]
-    parents = call(
-        parent_kernel,
-        [shape(9, P_DEV, NODES)],
-        [pltpu.VMEM((P_DEV, 9, 8, 128), F32), pltpu.SemaphoreType.DMA((P_DEV,))],
-        smem=(0,),
-        anywhere=(2,),
-        count=3,
-    )(source, home, fetched)[0]
+    parents = call(parent_kernel, [shape(9, P_DEV, NODES)], smem=(0,), count=3)(source, home, fetched)[0]
     return (updated, parents)
 
 

time: 75.2 us -> 65.9 us (0.88)
  Pallas kernels: 27.6 us -> 21.1 us
  other arithmetic: 0.33 us -> 2.54 us
  local copies, waits for them, and re-layouts: 3.43 us -> 1.28 us
  starting transfers between devices: 29.4 us -> 27.3 us
    pallas_call x1, Pallas kernels: 7.58 us -> 3.72 us  [shards(): call(functools.partial(end_kernel, factor), [state, shape(9, 4, P_DEV, 12...]
    ppermute x16, starting transfers between devices: 25.2 us -> 22.3 us  [shards(): arrived = [lax.ppermute(out_going[k], *pairs[k]) for k in (3, 2, 1, 0)]]
    pallas_call x2 -> x3, Pallas kernels: 5.48 us -> 2.88 us  [the longest x1 1.33 us: shards(): call(parent_kernel, [shape(9, P_DEV, NODES)], smem=(0,), count=3)]
    unnamed x17 -> x12, local copies, waits for them, and re-layouts: 3.43 us -> 1.28 us
    convert_element_type x0 -> x2, other arithmetic: none -> 1.38 us  [the longest x1 0.7 us: shards(): face_partner.T.astype(F32)]
    concatenate x0 -> x1, other arithmetic: none -> 0.83 us  [shards(): jnp.concatenate([twice(material), twice(face_partner.T.astype(F32)), jnp....]
    all_to_all x1, starting transfers between devices: 4.19 us -> 4.99 us  [shards(): lax.all_to_all(away, 'seg', split_axis=0, concat_axis=0, tiled=True)]
  transfers between devices with their start and end apart: 17 -> 17, of which waited for: 5 -> 8; matrix products, arithmetic and copies ran while one was open for 0% -> 1% of each run, Pallas kernels for 14% -> 16%
where the time goes in v2:
time: 65.9 us; the launch traced here: 65.6 us
  starting transfers between devices  27.3 us (41%)
  Pallas kernels  21.1 us (32%)
  waiting for transfers between devices  12.5 us (19%)
  other arithmetic  2.54 us (4%)
  local copies, waits for them, and re-layouts  1.28 us (2%)
  between operations  0.79 us (1%)
    ppermute x16, starting transfers between devices, shards(): arrived = [lax.ppermute(out_going[k], *pairs[k]) for k in (3, 2, 1, 0)]  22.3 us
    all_to_all x1, waiting for transfers between devices, shards(): lax.all_to_all(away, 'seg', split_axis=0, concat_axis=0, tiled=True)  8.23 us
    pallas_call x3, Pallas kernels, shards(): call(volume_kernel, [state, face_part, state], count=5)  5.97 us
    all_to_all x1, starting transfers between devices, shards(): lax.all_to_all(away, 'seg', split_axis=0, concat_axis=0, tiled=True)  4.99 us
    ppermute x16, waiting for transfers between devices, shards(): arrived = [lax.ppermute(out_going[k], *pairs[k]) for k in (3, 2, 1, 0)]  4.31 us
    pallas_call x3, Pallas kernels, shards(): call(functools.partial(finish_kernel, factor), [state, table] + payload,...  3.78 us
    pallas_call x1, Pallas kernels, shards(): call(functools.partial(end_kernel, factor), [state, shape(9, 4, P_DEV, 12...  3.72 us
    pallas_call x1, Pallas kernels, shards(): call(next_kernel, [shape(9, E_DEV, NODES)], [turn], count=1)(total)[0]  3.1 us
  transfers between devices with their start and end apart: 17, of which 8 were waited for; matrix products, arithmetic and copies ran while one was open for 1% of the time, Pallas kernels for 16%

profile of v2, /device:TPU:0, one launch (start us, length us, event | category | flops | bytes accessed | tf_op | source)
XLA Modules:
  0.0 65.6 jit_solution(8965865543795674512)
XLA Ops:
  0.6 0.7 %convert_bitcast_fusion = f32[6,64]{1,0:T(8,128)S(1)} fusion(s32[64,6]{0,1:T(8,128)} %param.11), kind=kLoop, calls=%fused_computation.3 | loop fusion | flops 384 | bytes 3072 | tf_op jit(solution)/shard_map/convert_element_type | solution.py:496
  1.3 0.7 %convert_bitcast_fusion.1 = f32[4,16]{1,0:T(4,128)S(1)} fusion(s32[1,4,16]{2,1,0:T(4,128)} %param.12), kind=kLoop, calls=%fused_computation.7 | loop fusion | flops 64 | bytes 512 | tf_op jit(solution)/shard_map/convert_element_type | solution.py:497
  2.0 0.8 %select_maximum_fusion.pack_ref = f32[16,128]{1,0:T(8,128)S(1)} fusion(f32[4,16]{1,0:T(4,128)S(1)} %convert_bitcast_fusion.1, f32[6,64]{1,0:T(8,128)S(1)} %convert_bitcast_fusion, f32[3,64]{1,0:T(4,128)} %param.10), kind=kLoop, calls=%fused_computation.1 | loop fusion | flops 12288 | bytes 10752 | tf_op jit(solution)/shard_map/concatenate | solution.py:493
  2.9 0.3 shard_map.104
  3.2 0.0 copy-start
  3.2 1.3 %copy-done = f32[9,64,512]{2,1,0:T(8,128)S(1)} copy-done((f32[9,64,512]{2,1,0:T(8,128)S(1)}, f32[9,64,512]{2,1,0:T(8,128)}, u32[]{:S(2)}) %copy-start) | copy-done | bytes 1179672
  4.5 1.2 %shard_map.105 = (f32[9,4,64,128]{3,2,1,0:T(8,128)S(1)}, bf16[384,768]{1,0:T(8,128)(2,1)S(1)}, f32[16,384]{1,0:T(8,128)S(1)}, f32[16,384]{1,0:T(8,128)S(1)}, f32...) custom-call(f32[9,64,512]{2,1,0:T(8,128)S(1)} %copy-done, f32[3,8,128]{2,1,0:T(8,128)S(1)} %get-tuple-element.44.mat_ref, ...), custom_call_target="tpu_custom_call" | custom-call | flops 100000000 | bytes 6000000 | tf_op jit(solution)/shard_map/pallas_call | solution.py:509
  5.7 6.6 %collective-permute-start = (f32[16,384]{1,0:T(8,128)S(1)}, f32[16,384]{1,0:T(8,128)S(1)}, u32[]{:S(2)}, u32[]{:S(2)}) collective-permute-start(f32[16,384]{1,0:T(8,128)S(1)} %get-tuple-element.51), channel_id=1, source_target_pairs={{1,2},{3,4},{5,6},{7,8},{9,10},{11,12},{13,14},{15,0},{2,1},{4,3},... | collective-permute-start | bytes 73736 | tf_op jit(solution)/shard_map/ppermute | solution.py:515
  12.3 0.0 collective-permute-start.1
  12.3 1.9 %collective-permute-start.2 = (f32[16,384]{1,0:T(8,128)S(1)}, f32[16,384]{1,0:T(8,128)S(1)}, u32[]{:S(2)}, u32[]{:S(2)}) collective-permute-start(f32[16,384]{1,0:T(8,128)S(1)} %get-tuple-element.53), channel_id=1, source_target_pairs={{16,32},{48,64},{80,96},{112,0},{32,16},{64,48},{96,80},{0,112},{1... | collective-permute-start | bytes 73736 | tf_op jit(solution)/shard_map/ppermute | solution.py:515
  14.3 0.1 convert_reduce_fusion
  14.4 1.7 %shard_map.106 = (f32[9,4,64,128]{3,2,1,0:T(8,128)S(1)}, f32[384,384]{1,0:T(8,128)S(1)}) custom-call(f32[9,4,64,128]{3,2,1,0:T(8,128)S(1)} %get-tuple-element.46.v_ref.acc_ref, bf16[384,768]{1,0:T(8,128)(2,1)S(1)} %get-tuple-element.47.t_ref, bf16[768,384]{1,0:T(8,128)(2,1)S(1)} %get-tuple-element.48.local_ref, f32[3,8,128]{2,1,0:T(8,128)S(1)} %get-tuple-element.44.mat_ref), custom_call_target="tpu_custom_call" | custom-call | flops 100000000 | bytes 6000000 | tf_op jit(solution)/shard_map/pallas_call | solution.py:517
  16.1 0.0 collective-permute-done.r3
  16.1 0.1 collective-permute-done.1.r2
  16.1 0.6 collective-permute-done.2.r1
  16.8 0.0 collective-permute-done.3.r0
  16.8 1.3 %shard_map.107 = (f32[9,4,64,128]{3,2,1,0:T(8,128)S(1)}, bf16[384,768]{1,0:T(8,128)(2,1)S(1)}, f32[16,384]{1,0:T(8,128)S(1)}, f32[16,384]{1,0:T(8,128)S(1)}, f32...) custom-call(f32[9,4,64,128]{3,2,1,0:T(8,128)S(1)} %get-tuple-element.49.vol_ref, f32[384,384]{1,0:T(8,128)S(1)} %get-tuple-element.50.part_ref, ...), custom_call_target="tpu_custom_call" | custom-call | flops 100000000 | bytes 6000000 | tf_op jit(solution)/shard_map/pallas_call | solution.py:523
  18.0 2.8 %collective-permute-start.4 = (f32[16,384]{1,0:T(8,128)S(1)}, f32[16,384]{1,0:T(8,128)S(1)}, u32[]{:S(2)}, u32[]{:S(2)}) collective-permute-start(f32[16,384]{1,0:T(8,128)S(1)} %get-tuple-element.60), channel_id=1, source_target_pairs={{1,2},{3,4},{5,6},{7,8},{9,10},{11,12},{13,14},{15,0},{2,1},{4,3},... | collective-permute-start | bytes 73736 | tf_op jit(solution)/shard_map/ppermute | solution.py:515
  20.8 0.8 %collective-permute-start.6 = (f32[16,384]{1,0:T(8,128)S(1)}, f32[16,384]{1,0:T(8,128)S(1)}, u32[]{:S(2)}, u32[]{:S(2)}) collective-permute-start(f32[16,384]{1,0:T(8,128)S(1)} %get-tuple-element.62), channel_id=1, source_target_pairs={{16,32},{48,64},{80,96},{112,0},{32,16},{64,48},{96,80},{0,112},{1... | collective-permute-start | bytes 73736 | tf_op jit(solution)/shard_map/ppermute | solution.py:515
  21.6 0.8 %collective-permute-start.7 = (f32[16,384]{1,0:T(8,128)S(1)}, f32[16,384]{1,0:T(8,128)S(1)}, u32[]{:S(2)}, u32[]{:S(2)}) collective-permute-start(f32[16,384]{1,0:T(8,128)S(1)} %get-tuple-element.63), channel_id=1, source_target_pairs={{0,16},{32,48},{64,80},{96,112},{16,0},{48,32},{80,64},{112,96},{1... | collective-permute-start | bytes 73736 | tf_op jit(solution)/shard_map/ppermute | solution.py:515
  22.4 2.0 %shard_map.108 = (f32[9,4,64,128]{3,2,1,0:T(8,128)S(1)}, f32[384,384]{1,0:T(8,128)S(1)}, f32[9,4,64,128]{3,2,1,0:T(8,128)S(1)}) custom-call(f32[9,4,64,128]{3,2,1,0:T(8,128)S(1)} %get-tuple-element.56.v_ref, bf16[384,768]{1,0:T(8,128)(2,1)S(1)} %get-tuple-element.57.t_ref, bf16[768,384]{1,0:T(8,128)(2,1)S(1)} %get-tuple-element.48.local_ref, ...), custom_call_target="tpu_custom_call" | custom-call | flops 100000000 | bytes 6000000 | tf_op jit(solution)/shard_map/pallas_call | solution.py:520
  24.4 0.9 %collective-permute-done.4.r3 = f32[16,384]{1,0:T(8,128)S(1)} collective-permute-done((f32[16,384]{1,0:T(8,128)S(1)}, f32[16,384]{1,0:T(8,128)S(1)}, u32[]{:S(2)}, u32[]{:S(2)}) %collective-permute-start.4) | collective-permute-done | bytes 24608 | tf_op jit(solution)/shard_map/ppermute | solution.py:515
  25.3 0.0 collective-permute-done.5.r2
  25.3 0.0 collective-permute-done.6.r1
  25.3 1.3 %shard_map.109 = (f32[9,4,64,128]{3,2,1,0:T(8,128)S(1)}, bf16[384,768]{1,0:T(8,128)(2,1)S(1)}, f32[16,384]{1,0:T(8,128)S(1)}, f32[16,384]{1,0:T(8,128)S(1)}, f32...) custom-call(f32[9,4,64,128]{3,2,1,0:T(8,128)S(1)} %get-tuple-element.58.vol_ref, f32[384,384]{1,0:T(8,128)S(1)} %get-tuple-element.59.part_ref, ...), custom_call_target="tpu_custom_call" | custom-call | flops 100000000 | bytes 6000000 | tf_op jit(solution)/shard_map/pallas_call | solution.py:523
  26.5 1.1 %collective-permute-start.10 = (f32[16,384]{1,0:T(8,128)S(1)}, f32[16,384]{1,0:T(8,128)S(1)}, u32[]{:S(2)}, u32[]{:S(2)}) collective-permute-start(f32[16,384]{1,0:T(8,128)S(1)} %get-tuple-element.71), channel_id=1, source_target_pairs={{16,32},{48,64},{80,96},{112,0},{32,16},{64,48},{96,80},{0,112},{1... | collective-permute-start | bytes 73736 | tf_op jit(solution)/shard_map/ppermute | solution.py:515
  27.7 0.0 collective-permute-start.11
  27.7 3.5 %collective-permute-start.8 = (f32[16,384]{1,0:T(8,128)S(1)}, f32[16,384]{1,0:T(8,128)S(1)}, u32[]{:S(2)}, u32[]{:S(2)}) collective-permute-start(f32[16,384]{1,0:T(8,128)S(1)} %get-tuple-element.69), channel_id=1, source_target_pairs={{1,2},{3,4},{5,6},{7,8},{9,10},{11,12},{13,14},{15,0},{2,1},{4,3},... | collective-permute-start | bytes 73736 | tf_op jit(solution)/shard_map/ppermute | solution.py:515
  31.2 0.0 collective-permute-start.9
  31.2 0.1 select_reduce_fusion.keys_ref
  31.3 2.0 %shard_map.110 = (f32[9,4,64,128]{3,2,1,0:T(8,128)S(1)}, f32[384,384]{1,0:T(8,128)S(1)}, f32[9,4,64,128]{3,2,1,0:T(8,128)S(1)}) custom-call(f32[9,4,64,128]{3,2,1,0:T(8,128)S(1)} %get-tuple-element.64.v_ref, bf16[384,768]{1,0:T(8,128)(2,1)S(1)} %get-tuple-element.65.t_ref, bf16[768,384]{1,0:T(8,128)(2,1)S(1)} %get-tuple-element.48.local_ref, ...), custom_call_target="tpu_custom_call" | custom-call | flops 100000000 | bytes 6000000 | tf_op jit(solution)/shard_map/pallas_call | solution.py:520
  33.3 0.0 collective-permute-done.10.r1
  33.3 0.0 collective-permute-done.11.r0
  33.3 1.5 %collective-permute-done.8.r3 = f32[16,384]{1,0:T(8,128)S(1)} collective-permute-done((f32[16,384]{1,0:T(8,128)S(1)}, f32[16,384]{1,0:T(8,128)S(1)}, u32[]{:S(2)}, u32[]{:S(2)}) %collective-permute-start.8) | collective-permute-done | bytes 24608 | tf_op jit(solution)/shard_map/ppermute | solution.py:515
  34.8 0.2 collective-permute-done.9.r2
  35.0 1.3 %shard_map.111 = (f32[9,4,64,128]{3,2,1,0:T(8,128)S(1)}, bf16[384,768]{1,0:T(8,128)(2,1)S(1)}, f32[16,384]{1,0:T(8,128)S(1)}, f32[16,384]{1,0:T(8,128)S(1)}, f32...) custom-call(f32[9,4,64,128]{3,2,1,0:T(8,128)S(1)} %get-tuple-element.67.vol_ref, f32[384,384]{1,0:T(8,128)S(1)} %get-tuple-element.68.part_ref, ...), custom_call_target="tpu_custom_call" | custom-call | flops 100000000 | bytes 6000000 | tf_op jit(solution)/shard_map/pallas_call | solution.py:523
  36.3 3.4 %collective-permute-start.12 = (f32[16,384]{1,0:T(8,128)S(1)}, f32[16,384]{1,0:T(8,128)S(1)}, u32[]{:S(2)}, u32[]{:S(2)}) collective-permute-start(f32[16,384]{1,0:T(8,128)S(1)} %get-tuple-element.78), channel_id=1, source_target_pairs={{1,2},{3,4},{5,6},{7,8},{9,10},{11,12},{13,14},{15,0},{2,1},{4,3},... | collective-permute-start | bytes 73736 | tf_op jit(solution)/shard_map/ppermute | solution.py:515
  39.7 1.3 %collective-permute-start.15 = (f32[16,384]{1,0:T(8,128)S(1)}, f32[16,384]{1,0:T(8,128)S(1)}, u32[]{:S(2)}, u32[]{:S(2)}) collective-permute-start(f32[16,384]{1,0:T(8,128)S(1)} %get-tuple-element.81), channel_id=1, source_target_pairs={{0,16},{32,48},{64,80},{96,112},{16,0},{48,32},{80,64},{112,96},{1... | collective-permute-start | bytes 73736 | tf_op jit(solution)/shard_map/ppermute | solution.py:515
  41.0 0.1 add_bitcast_fusion.place_ref
  41.1 2.0 %shard_map.112 = (f32[9,4,64,128]{3,2,1,0:T(8,128)S(1)}, f32[384,384]{1,0:T(8,128)S(1)}, f32[9,4,64,128]{3,2,1,0:T(8,128)S(1)}) custom-call(f32[9,4,64,128]{3,2,1,0:T(8,128)S(1)} %get-tuple-element.73.v_ref, bf16[384,768]{1,0:T(8,128)(2,1)S(1)} %get-tuple-element.74.t_ref, bf16[768,384]{1,0:T(8,128)(2,1)S(1)} %get-tuple-element.48.local_ref, ...), custom_call_target="tpu_custom_call" | custom-call | flops 100000000 | bytes 6000000 | tf_op jit(solution)/shard_map/pallas_call | solution.py:520
  43.1 0.4 collective-permute-done.12.r3
  43.5 0.0 collective-permute-done.13.r2
  43.5 0.6 collective-permute-done.14.r1
  44.2 3.7 %shard_map.113 = (f32[9,4,64,128]{3,2,1,0:T(8,128)S(1)}, f32[9,4,8,128]{3,2,1,0:T(8,128)S(1)}, f32[16,9,8,128]{3,2,1,0:T(8,128)}) custom-call(s32[8]{0:T(128)S(1)} %select_reduce_fusion.keys_ref, f32[9,4,64,128]{3,2,1,0:T(8,128)S(1)} %get-tuple-element.76.vol_ref, f32[384,384]{1,0:T(8,128)S(1)} %get-tuple-element.77.part_ref, ...), custom_call_target="tpu_custom_call" | custom-call | flops 100000000 | bytes 6000000 | tf_op jit(solution)/shard_map/pallas_call | solution.py:528
  47.9 5.0 %all-to-all-start = ((f32[16,9,8,128]{3,2,1,0:T(8,128)}), f32[16,9,8,128]{3,2,1,0:T(8,128)S(1)}, u32[]{:S(2)}, u32[]{:S(2)}) async-start(f32[16,9,8,128]{3,2,1,0:T(8,128)} %get-tuple-element.85), calls=%async_computation | async-start | bytes 1179648 | tf_op jit(solution)/shard_map/all_to_all | solution.py:543
  52.9 3.1 %shard_map.114 = f32[9,64,512]{2,1,0:T(8,128)} custom-call(f32[9,4,64,128]{3,2,1,0:T(8,128)S(1)} %get-tuple-element.83.total_ref), custom_call_target="tpu_custom_call" | custom-call | flops 100000000 | bytes 6000000 | tf_op jit(solution)/shard_map/pallas_call | solution.py:544
  56.0 8.2 %all-to-all-done.arrived_ref = f32[16,9,8,128]{3,2,1,0:T(8,128)S(1)} async-done(((f32[16,9,8,128]{3,2,1,0:T(8,128)}), f32[16,9,8,128]{3,2,1,0:T(8,128)S(1)}, u32[]{:S(2)}, u32[]{:S(2)}) %all-to-all-start) | async-done | bytes 589856 | tf_op jit(solution)/shard_map/all_to_all | solution.py:543
  64.3 1.3 %shard_map.115 = f32[9,8,512]{2,1,0:T(8,128)} custom-call(s32[2,8]{1,0:T(2,128)S(1)} %pad_add_fusion.table_ref, f32[9,4,8,128]{3,2,1,0:T(8,128)S(1)} %get-tuple-element.84.home_ref, f32[16,9,8,128]{3,2,1,0:T(8,128)S(1)} %all-to-all-done.arrived_ref), custom_call_target="tpu_custom_call" | custom-call | flops 100000000 | bytes 6000000 | tf_op jit(solution)/shard_map/pallas_call | solution.py:545
  (22 shorter events, 0.1 us)
Async XLA Ops:
  0.6 13.6 %copy-start.4 = (s32[3,64]{1,0:T(4,128)S(1)}, s32[3,64]{1,0:T(4,128)}, u32[]{:S(2)}) copy-start(s32[3,64]{1,0:T(4,128)} %param.13) | copy-start | bytes 2308
  3.2 1.3 %copy-start = (f32[9,64,512]{2,1,0:T(8,128)S(1)}, f32[9,64,512]{2,1,0:T(8,128)}, u32[]{:S(2)}) copy-start(f32[9,64,512]{2,1,0:T(8,128)} %adjoint_ref.1) | copy-start | bytes 3538948
  5.7 10.4 %collective-permute-start = (f32[16,384]{1,0:T(8,128)S(1)}, f32[16,384]{1,0:T(8,128)S(1)}, u32[]{:S(2)}, u32[]{:S(2)}) collective-permute-start(f32[16,384]{1,0:T(8,128)S(1)} %get-tuple-element.51), channel_id=1, source_target_pairs={{1,2},{3,4},{5,6},{7,8},{9,10},{11,12},{13,14},{15,0},{2,1},{4,3},... | collective-permute-start | bytes 73736 | tf_op jit(solution)/shard_map/ppermute | solution.py:515
  12.3 3.8 %collective-permute-start.1 = (f32[16,384]{1,0:T(8,128)S(1)}, f32[16,384]{1,0:T(8,128)S(1)}, u32[]{:S(2)}, u32[]{:S(2)}) collective-permute-start(f32[16,384]{1,0:T(8,128)S(1)} %get-tuple-element.52), channel_id=1, source_target_pairs={{0,1},{2,3},{4,5},{6,7},{8,9},{10,11},{12,13},{14,15},{1,0},{3,2},... | collective-permute-start | bytes 73736 | tf_op jit(solution)/shard_map/ppermute | solution.py:515
  12.3 4.5 %collective-permute-start.2 = (f32[16,384]{1,0:T(8,128)S(1)}, f32[16,384]{1,0:T(8,128)S(1)}, u32[]{:S(2)}, u32[]{:S(2)}) collective-permute-start(f32[16,384]{1,0:T(8,128)S(1)} %get-tuple-element.53), channel_id=1, source_target_pairs={{16,32},{48,64},{80,96},{112,0},{32,16},{64,48},{96,80},{0,112},{1... | collective-permute-start | bytes 73736 | tf_op jit(solution)/shard_map/ppermute | solution.py:515
  14.2 2.5 %collective-permute-start.3 = (f32[16,384]{1,0:T(8,128)S(1)}, f32[16,384]{1,0:T(8,128)S(1)}, u32[]{:S(2)}, u32[]{:S(2)}) collective-permute-start(f32[16,384]{1,0:T(8,128)S(1)} %get-tuple-element.54), channel_id=1, source_target_pairs={{0,16},{32,48},{64,80},{96,112},{16,0},{48,32},{80,64},{112,96},{1... | collective-permute-start | bytes 73736 | tf_op jit(solution)/shard_map/ppermute | solution.py:515
  18.0 7.2 %collective-permute-start.4 = (f32[16,384]{1,0:T(8,128)S(1)}, f32[16,384]{1,0:T(8,128)S(1)}, u32[]{:S(2)}, u32[]{:S(2)}) collective-permute-start(f32[16,384]{1,0:T(8,128)S(1)} %get-tuple-element.60), channel_id=1, source_target_pairs={{1,2},{3,4},{5,6},{7,8},{9,10},{11,12},{13,14},{15,0},{2,1},{4,3},... | collective-permute-start | bytes 73736 | tf_op jit(solution)/shard_map/ppermute | solution.py:515
  20.8 4.5 %collective-permute-start.5 = (f32[16,384]{1,0:T(8,128)S(1)}, f32[16,384]{1,0:T(8,128)S(1)}, u32[]{:S(2)}, u32[]{:S(2)}) collective-permute-start(f32[16,384]{1,0:T(8,128)S(1)} %get-tuple-element.61), channel_id=1, source_target_pairs={{0,1},{2,3},{4,5},{6,7},{8,9},{10,11},{12,13},{14,15},{1,0},{3,2},... | collective-permute-start | bytes 73736 | tf_op jit(solution)/shard_map/ppermute | solution.py:515
  20.8 4.5 %collective-permute-start.6 = (f32[16,384]{1,0:T(8,128)S(1)}, f32[16,384]{1,0:T(8,128)S(1)}, u32[]{:S(2)}, u32[]{:S(2)}) collective-permute-start(f32[16,384]{1,0:T(8,128)S(1)} %get-tuple-element.62), channel_id=1, source_target_pairs={{16,32},{48,64},{80,96},{112,0},{32,16},{64,48},{96,80},{0,112},{1... | collective-permute-start | bytes 73736 | tf_op jit(solution)/shard_map/ppermute | solution.py:515
  21.6 3.7 %collective-permute-start.7 = (f32[16,384]{1,0:T(8,128)S(1)}, f32[16,384]{1,0:T(8,128)S(1)}, u32[]{:S(2)}, u32[]{:S(2)}) collective-permute-start(f32[16,384]{1,0:T(8,128)S(1)} %get-tuple-element.63), channel_id=1, source_target_pairs={{0,16},{32,48},{64,80},{96,112},{16,0},{48,32},{80,64},{112,96},{1... | collective-permute-start | bytes 73736 | tf_op jit(solution)/shard_map/ppermute | solution.py:515
  26.5 6.8 %collective-permute-start.10 = (f32[16,384]{1,0:T(8,128)S(1)}, f32[16,384]{1,0:T(8,128)S(1)}, u32[]{:S(2)}, u32[]{:S(2)}) collective-permute-start(f32[16,384]{1,0:T(8,128)S(1)} %get-tuple-element.71), channel_id=1, source_target_pairs={{16,32},{48,64},{80,96},{112,0},{32,16},{64,48},{96,80},{0,112},{1... | collective-permute-start | bytes 73736 | tf_op jit(solution)/shard_map/ppermute | solution.py:515
  27.7 5.7 %collective-permute-start.11 = (f32[16,384]{1,0:T(8,128)S(1)}, f32[16,384]{1,0:T(8,128)S(1)}, u32[]{:S(2)}, u32[]{:S(2)}) collective-permute-start(f32[16,384]{1,0:T(8,128)S(1)} %get-tuple-element.72), channel_id=1, source_target_pairs={{0,16},{32,48},{64,80},{96,112},{16,0},{48,32},{80,64},{112,96},{1... | collective-permute-start | bytes 73736 | tf_op jit(solution)/shard_map/ppermute | solution.py:515
  27.7 7.1 %collective-permute-start.8 = (f32[16,384]{1,0:T(8,128)S(1)}, f32[16,384]{1,0:T(8,128)S(1)}, u32[]{:S(2)}, u32[]{:S(2)}) collective-permute-start(f32[16,384]{1,0:T(8,128)S(1)} %get-tuple-element.69), channel_id=1, source_target_pairs={{1,2},{3,4},{5,6},{7,8},{9,10},{11,12},{13,14},{15,0},{2,1},{4,3},... | collective-permute-start | bytes 73736 | tf_op jit(solution)/shard_map/ppermute | solution.py:515
  31.2 3.8 %collective-permute-start.9 = (f32[16,384]{1,0:T(8,128)S(1)}, f32[16,384]{1,0:T(8,128)S(1)}, u32[]{:S(2)}, u32[]{:S(2)}) collective-permute-start(f32[16,384]{1,0:T(8,128)S(1)} %get-tuple-element.70), channel_id=1, source_target_pairs={{0,1},{2,3},{4,5},{6,7},{8,9},{10,11},{12,13},{14,15},{1,0},{3,2},... | collective-permute-start | bytes 73736 | tf_op jit(solution)/shard_map/ppermute | solution.py:515
  36.3 7.2 %collective-permute-start.12 = (f32[16,384]{1,0:T(8,128)S(1)}, f32[16,384]{1,0:T(8,128)S(1)}, u32[]{:S(2)}, u32[]{:S(2)}) collective-permute-start(f32[16,384]{1,0:T(8,128)S(1)} %get-tuple-element.78), channel_id=1, source_target_pairs={{1,2},{3,4},{5,6},{7,8},{9,10},{11,12},{13,14},{15,0},{2,1},{4,3},... | collective-permute-start | bytes 73736 | tf_op jit(solution)/shard_map/ppermute | solution.py:515
  39.7 3.8 %collective-permute-start.13 = (f32[16,384]{1,0:T(8,128)S(1)}, f32[16,384]{1,0:T(8,128)S(1)}, u32[]{:S(2)}, u32[]{:S(2)}) collective-permute-start(f32[16,384]{1,0:T(8,128)S(1)} %get-tuple-element.79), channel_id=1, source_target_pairs={{0,1},{2,3},{4,5},{6,7},{8,9},{10,11},{12,13},{14,15},{1,0},{3,2},... | collective-permute-start | bytes 73736 | tf_op jit(solution)/shard_map/ppermute | solution.py:515
  39.7 4.5 %collective-permute-start.14 = (f32[16,384]{1,0:T(8,128)S(1)}, f32[16,384]{1,0:T(8,128)S(1)}, u32[]{:S(2)}, u32[]{:S(2)}) collective-permute-start(f32[16,384]{1,0:T(8,128)S(1)} %get-tuple-element.80), channel_id=1, source_target_pairs={{16,32},{48,64},{80,96},{112,0},{32,16},{64,48},{96,80},{0,112},{1... | collective-permute-start | bytes 73736 | tf_op jit(solution)/shard_map/ppermute | solution.py:515
  39.7 4.5 %collective-permute-start.15 = (f32[16,384]{1,0:T(8,128)S(1)}, f32[16,384]{1,0:T(8,128)S(1)}, u32[]{:S(2)}, u32[]{:S(2)}) collective-permute-start(f32[16,384]{1,0:T(8,128)S(1)} %get-tuple-element.81), channel_id=1, source_target_pairs={{0,16},{32,48},{64,80},{96,112},{16,0},{48,32},{80,64},{112,96},{1... | collective-permute-start | bytes 73736 | tf_op jit(solution)/shard_map/ppermute | solution.py:515
  41.1 3.1 %copy-start.1 = (f32[64,8,128]{2,1,0:T(8,128)S(1)}, f32[64,8,128]{2,1,0:T(8,128)}, u32[]{:S(2)}) copy-start(f32[64,8,128]{2,1,0:T(8,128)} %constant.23.clone.lines_ref) | copy-start | bytes 786436
  41.1 3.1 %copy-start.2 = (bf16[256,128]{1,0:T(8,128)(2,1)S(1)}, bf16[256,128]{1,0:T(8,128)(2,1)}, u32[]{:S(2)}) copy-start(bf16[256,128]{1,0:T(8,128)(2,1)} %constant.21.clone.wa_ref) | copy-start | bytes 196612
  41.1 3.1 %copy-start.3 = (bf16[256,128]{1,0:T(8,128)(2,1)S(1)}, bf16[256,128]{1,0:T(8,128)(2,1)}, u32[]{:S(2)}) copy-start(bf16[256,128]{1,0:T(8,128)(2,1)} %constant.22.clone.wb_ref) | copy-start | bytes 196612
  47.9 5.0 %copy-start.5 = (s32[2,8]{1,0:T(2,128)S(1)}, s32[2,8]{1,0:T(2,128)}, u32[]{:S(2)}) copy-start(s32[2,8]{1,0:T(2,128)} %param.14) | copy-start | bytes 196
  47.9 16.4 %all-to-all-start = ((f32[16,9,8,128]{3,2,1,0:T(8,128)}), f32[16,9,8,128]{3,2,1,0:T(8,128)S(1)}, u32[]{:S(2)}, u32[]{:S(2)}) async-start(f32[16,9,8,128]{3,2,1,0:T(8,128)} %get-tuple-element.85), calls=%async_computation | async-start | bytes 1179648 | tf_op jit(solution)/shard_map/all_to_all | solution.py:543

commit v3 on v2

--- a/solution.py
+++ b/solution.py
@@ -204,29 +204,29 @@
         out_refs[k][...] = rows[16 * k : 16 * k + 16]
 
 
-def index_kernel(pack_ref, mat_ref, local_ref, remote_ref, send_ref, small_ref):
-    even_x = 1 - lax.axis_index("curve") % 2
-    even_y = 1 - lax.axis_index("seg") % 2
-
-    def lane(q):
-        element = (q * 10923) >> 16
-        return (q - 6 * element) * E_DEV + element
-
-    for i in range(3):
-        row = pack_ref[pl.ds(i, 1), :]
-        if i == 0:
-            row = 1.0 / row
-        mat_ref[i] = jnp.broadcast_to(row, (8, 128))
+def parities():
+    return 1 - lax.axis_index("curve") % 2, 1 - lax.axis_index("seg") % 2
+
+
+def table_lane(q):
+    element = (q * 10923) >> 16
+    return (q - 6 * element) * E_DEV + element
+
+
+def partner_tables(faces_ref, local_ref, remote_ref):
+    even_x, even_y = parities()
     low_row = lax.broadcasted_iota(jnp.int32, (1, 128), 1) < 64
     weight = jnp.where(low_row, lift_half, -lift_half)
     for direction in range(3):
         q = jnp.where(
-            low_row, pack_ref[pl.ds(3 + 2 * direction, 1), :], pack_ref[pl.ds(4 + 2 * direction, 1), :]
+            low_row,
+            faces_ref[pl.ds(2 * direction, 1), :],
+            pltpu.roll(faces_ref[pl.ds(2 * direction + 1, 1), :], 64, 1),
         ).astype(jnp.int32)
         remote = q - LOCAL
         side = remote >> 4
         block = side ^ jnp.where(side < 2, even_x, even_y)
-        partner = jnp.where(remote < 0, lane(q), LOCAL + block * CAP + (remote & 15))
+        partner = jnp.where(remote < 0, table_lane(q), LOCAL + block * CAP + (remote & 15))
         lanes = pl.ds(direction * 128, 128)
         for start in range(0, LOCAL + 64, 64):
             source = lax.broadcasted_iota(jnp.int32, (64, 128), 0) + start
@@ -236,10 +236,14 @@
                     local_ref[pl.ds(part * LOCAL + start, 64), lanes] = hot
                 else:
                     remote_ref[pl.ds(part * 64, 64), lanes] = hot
-    small_ref[pl.ds(0, 16), :] = pack_ref[...]
-    small_ref[pl.ds(16, 112), :] = jnp.zeros((112, 128), F32)
+
+
+def send_table(pack_ref, send_ref, small_ref):
+    even_x, even_y = parities()
+    small_ref[pl.ds(0, 8), :] = pack_ref[0]
+    small_ref[pl.ds(8, 120), :] = jnp.zeros((120, 128), F32)
     turned = small_ref[...].T
-    columns = [lane(turned[0:CAP, 9 + r : 10 + r].astype(jnp.int32)) for r in range(4)]
+    columns = [table_lane(turned[0:CAP, 3 + r : 4 + r].astype(jnp.int32)) for r in range(4)]
     for axis, even in ((0, even_x), (1, even_y)):
         first, second = columns[2 * axis], columns[2 * axis + 1]
         for k, column in enumerate((first + even * (second - first), second + even * (first - second))):
@@ -251,7 +255,17 @@
             send_ref[rows, pl.ds(LOCAL, LOCAL)] = hot
 
 
-def begin_kernel(adjoint_ref, mat_ref, send_ref, v_ref, t_ref, p0, p1, p2, p3, turn_ref):
+def begin_kernel(
+    pack_ref, adjoint_ref, v_ref, t_ref, mat_ref, send_ref, p0, p1, p2, p3, turn_ref, small_ref
+):
+    low_row = lax.broadcasted_iota(jnp.int32, (1, 128), 1) < 64
+    for i in range(3):
+        row = pack_ref[0, pl.ds(i, 1), :]
+        row = jnp.where(low_row, row, pltpu.roll(row, 64, 1))
+        if i == 0:
+            row = 1.0 / row
+        mat_ref[i] = jnp.broadcast_to(row, (8, 128))
+    send_table(pack_ref, send_ref, small_ref)
     low = lax.broadcasted_iota(jnp.int32, (64, 128), 1) < 64
     for i in range(9):
         x = adjoint_ref[i]
@@ -265,13 +279,13 @@
     send_values(send_ref, t_ref, (p0, p1, p2, p3))
 
 
-def first_volume_kernel(v_ref, t_ref, local_ref, mat_ref, vol_ref, part_ref):
-    volume_kernel(v_ref, t_ref, local_ref, mat_ref, None, vol_ref, part_ref, None)
-
-
-def volume_kernel(v_ref, t_ref, local_ref, mat_ref, acc_ref, vol_ref, part_ref, sum_ref):
-    mat = materials(mat_ref)
-    inv_density, lame, shear = mat
+def first_volume_kernel(factor, faces_ref, v_ref, t_ref, mat_ref, vol_ref, part_ref, local_ref, remote_ref):
+    partner_tables(faces_ref, local_ref, remote_ref)
+    volume_kernel(factor, v_ref, t_ref, local_ref, mat_ref, None, vol_ref, part_ref, None)
+
+
+def volume_kernel(factor, v_ref, t_ref, local_ref, mat_ref, acc_ref, vol_ref, part_ref, sum_ref):
+    inv_density, lame, shear = [m * factor for m in materials(mat_ref)]
 
     def scaled(get, direction):
         out = []
@@ -286,18 +300,20 @@
             out.append((voigt_index[i][direction], [inv_density * x for x in get(i)]))
         return out
 
-    def tiles(j, carry):
+    def tiles(j):
         for row, x in scaled(lambda i: [v_ref[i, j, along(b), :] for b in range(8)], 1):
             for b, y in enumerate(line_product(x)):
                 vol_ref[row, j, along(b), :] = y
+        chunk = pl.ds(j * 96, 96)
+        part_ref[chunk, :] = jnp.dot(t_ref[chunk, :], local_ref[...], preferred_element_type=F32) * factor
         for row, x in scaled(lambda i: [v_ref[i, j, pl.ds(8 * a, 8), :] for a in range(8)], 0):
             for a, y in enumerate(line_product(x)):
                 if row not in (3, 7):
                     y = y + vol_ref[row, j, pl.ds(8 * a, 8), :]
                 vol_ref[row, j, pl.ds(8 * a, 8), :] = y
-        return carry
-
-    lax.fori_loop(0, 4, tiles, 0)
+
+    for j in range(4):
+        tiles(j)
     patterns = lane_patterns()
 
     def groups(a, carry):
@@ -307,8 +323,6 @@
                 if row != 5:
                     y = y + vol_ref[row, j, rows, :]
                 vol_ref[row, j, rows, :] = y
-        chunk = pl.ds(pl.multiple_of(a * 48, 16), 48)
-        part_ref[chunk, :] = jnp.dot(t_ref[chunk, :], local_ref[...], preferred_element_type=F32)
         if sum_ref is not None:
             for i in range(9):
                 for j in range(4):
@@ -318,12 +332,10 @@
     lax.fori_loop(0, 8, groups, 0, unroll=4)
 
 
-def add_faces(vol_ref, part_ref, r_refs, remote_ref, factor, out_ref, face_ref):
-    for i in range(9):
-        out_ref[i] = vol_ref[i] * factor
-    arrived = jnp.concatenate([r[...] for r in r_refs], axis=0).T
+def add_faces(part_ref, r_refs, remote_ref, factor, out_ref, face_ref):
+    arrived = jnp.concatenate([r[...] for r in r_refs], axis=0).T * factor
     both = jnp.concatenate(split(arrived), axis=1)
-    face_ref[...] = (part_ref[...] + jnp.dot(both, remote_ref[...], preferred_element_type=F32)) * factor
+    face_ref[...] = part_ref[...] + jnp.dot(both, remote_ref[...], preferred_element_type=F32)
     low = low_half()
     for direction in range(3):
         for value in range(6):
@@ -344,19 +356,23 @@
 
 
 def finish_kernel(
-    factor, vol_ref, part_ref, r3, r2, r1, r0, remote_ref, mat_ref, send_ref,
+    factor, order, vol_ref, part_ref, ra, rb, rc, rd, remote_ref, mat_ref, send_ref,
     v_ref, t_ref, p0, p1, p2, p3, face_ref,
 ):
-    add_faces(vol_ref, part_ref, (r0, r1, r2, r3), remote_ref, factor, v_ref, face_ref)
+    add_faces(part_ref, in_order(order, (ra, rb, rc, rd)), remote_ref, factor, v_ref, face_ref)
     build_table(v_ref, materials(mat_ref), t_ref)
     send_values(send_ref, t_ref, (p0, p1, p2, p3))
 
 
+def in_order(order, refs):
+    return [refs[order.index(k)] for k in range(4)]
+
+
 def end_kernel(
-    factor, keys_ref, vol_ref, part_ref, r3, r2, r1, r0, remote_ref, acc_ref, place_ref, wa_ref, wb_ref, lines_ref,
-    total_ref, home_ref, away_ref, v_ref, face_ref, turn_ref, ranked_ref, rows_ref, plane_ref, parent_ref,
+    factor, order, keys_ref, vol_ref, part_ref, ra, rb, rc, rd, remote_ref, acc_ref, place_ref, wa_ref, wb_ref, lines_ref,
+    total_ref, home_ref, away_ref, face_ref, turn_ref, ranked_ref, rows_ref, plane_ref, parent_ref,
 ):
-    add_faces(vol_ref, part_ref, (r0, r1, r2, r3), remote_ref, factor, v_ref, face_ref)
+    add_faces(part_ref, in_order(order, (ra, rb, rc, rd)), remote_ref, factor, total_ref, face_ref)
     place = jnp.where(
         lax.broadcasted_iota(jnp.int32, (64, 128), 0) == place_ref[...], 1.0, 0.0
     ).astype(BF)
@@ -364,7 +380,7 @@
     low = low_half()
     for i in range(9):
         for j in range(4):
-            tile = acc_ref[i, j] + v_ref[i, j]
+            tile = acc_ref[i, j] + total_ref[i, j]
             total_ref[i, j] = tile
             high = tile.astype(BF).astype(F32)
             rest = tile - high
@@ -450,13 +466,14 @@
 SMEM = pl.BlockSpec(memory_space=pltpu.SMEM)
 
 
-def call(kernel, outs, scratch=(), smem=(), count=0, flops=10**8, traffic=6 * 10**6):
+def call(kernel, outs, scratch=(), smem=(), aliases={}, count=0, flops=10**8, traffic=6 * 10**6):
     return pl.pallas_call(
         kernel,
         out_shape=outs,
         in_specs=[SMEM if k in smem else VMEM for k in range(count)],
         out_specs=jax.tree.map(lambda _: VMEM, outs),
         scratch_shapes=list(scratch),
+        input_output_aliases=aliases,
         compiler_params=pltpu.CompilerParams(vmem_limit_bytes=32 * 2**20),
         cost_estimate=pl.CostEstimate(flops=flops, bytes_accessed=traffic, transcendentals=0),
     )
@@ -489,47 +506,52 @@
     face_scratch = pltpu.VMEM((LOCAL, LOCAL), F32)
     turn = pltpu.VMEM((NODES, 128), F32)
 
-    twice = lambda x: jnp.concatenate([x, x], axis=1)
     pack = jnp.concatenate(
         [
-            twice(material),
-            twice(face_partner.T.astype(F32)),
-            jnp.pad(send_faces[0].astype(F32), ((0, 3), (0, 128 - CAP))),
+            jnp.pad(material[None], ((0, 0), (0, 0), (0, 64))),
+            jnp.pad(send_faces, ((0, 0), (0, 1), (0, 128 - CAP))).astype(F32),
         ],
-        axis=0,
+        axis=1,
     )
-    mat, local_hot, remote_hot, send_hot = call(
-        index_kernel,
-        [shape(3, 8, 128)]
-        + [shape(2 * LOCAL, LOCAL, dtype=BF), shape(128, LOCAL, dtype=BF), shape(64, 2 * LOCAL, dtype=BF)],
-        [pltpu.VMEM((128, 128), F32)],
-        count=1,
-        traffic=4 * 10**7,
-    )(pack)
-    outs = call(begin_kernel, [state, table] + payload, [pltpu.VMEM((3, NODES, 128), F32)], count=3)(
-        adjoint, mat, send_hot
-    )
-    v, t, out_going = outs[0], outs[1], outs[2:]
+    faces = jnp.pad(face_partner.T.astype(F32), ((0, 2), (0, 64)))
+    outs = call(
+        begin_kernel,
+        [state, table, shape(3, 8, 128), shape(64, 2 * LOCAL, dtype=BF)] + payload,
+        [pltpu.VMEM((3, NODES, 128), F32), pltpu.VMEM((128, 128), F32)],
+        count=2,
+    )(pack, adjoint)
+    v, t, mat, send_hot = outs[:4]
+    out_going = outs[4:]
     pairs = exchange_pairs()
     for step in range(1, 5):
-        arrived = [lax.ppermute(out_going[k], *pairs[k]) for k in (3, 2, 1, 0)]
+        factor = time_step / step
+        order = (1, 0, 3, 2) if step == 3 else (3, 2, 1, 0)
+        arrived = [lax.ppermute(out_going[k], *pairs[k]) for k in order]
         if step == 1:
-            vol, part = call(first_volume_kernel, [state, face_part], count=4)(v, t, local_hot, mat)
+            vol, part, local_hot, remote_hot = call(
+                functools.partial(first_volume_kernel, factor),
+                [state, face_part, shape(2 * LOCAL, LOCAL, dtype=BF), shape(128, LOCAL, dtype=BF)],
+                count=4,
+            )(faces, v, t, mat)
             acc = v
         else:
-            vol, part, acc = call(volume_kernel, [state, face_part, state], count=5)(v, t, local_hot, mat, acc)
-        factor = time_step / step
+            vol, part, acc = call(
+                functools.partial(volume_kernel, factor), [state, face_part, state], count=5
+            )(v, t, local_hot, mat, acc)
         if step < 4:
             outs = call(
-                functools.partial(finish_kernel, factor), [state, table] + payload, [face_scratch], count=9
+                functools.partial(finish_kernel, factor, order),
+                [state, table] + payload,
+                [face_scratch],
+                aliases={0: 0},
+                count=9,
             )(vol, part, *arrived, remote_hot, mat, send_hot)
             v, t, out_going = outs[0], outs[1], outs[2:]
     wa, wb, lines = (jnp.asarray(x) for x in refine_parts())
     total, home, away = call(
-        functools.partial(end_kernel, factor),
+        functools.partial(end_kernel, factor, order),
         [state, shape(9, 4, P_DEV, 128), shape(N_SEG, 9, 8, 128)],
         [
-            pltpu.VMEM((9, 4, 64, 128), F32),
             face_scratch,
             pltpu.VMEM((9, NODES, 128), F32),
             pltpu.VMEM((9, 64, NODES), F32),
@@ -538,6 +560,7 @@
             pltpu.VMEM((9, 4, 8, 128), F32),
         ],
         smem=(0,),
+        aliases={1: 0},
         count=13,
     )(keys, vol, part, *arrived, remote_hot, acc, place, wa, wb, lines)
     fetched = lax.all_to_all(away, "seg", split_axis=0, concat_axis=0, tiled=True)

time: 65.9 us -> 64.2 us (0.974)
  waiting for transfers between devices: 12.5 us -> 10.6 us
  Pallas kernels: 21.1 us -> 22 us
  other arithmetic: 2.54 us -> 1.72 us
    ppermute x16, waiting for transfers between devices: 4.31 us -> 1.81 us  [shards(): arrived = [lax.ppermute(out_going[k], *pairs[k]) for k in order]]
    pallas_call x10 -> x9, Pallas kernels: 16.7 us -> 17.6 us  [the longest x3 6.78 us: shards(): call(functools.partial(volume_kernel, factor), [state, face_part, state],...]
    all_to_all x1, starting transfers between devices: 4.99 us -> 5.78 us  [shards(): lax.all_to_all(away, 'seg', split_axis=0, concat_axis=0, tiled=True)]
    convert_element_type x2, other arithmetic: 1.38 us -> 0.7 us  [the longest x1 0.7 us: shards(): jnp.pad(send_faces, ((0, 0), (0, 1), (0, 128 - CAP))).astype(F32)]
  transfers between devices with their start and end apart: 17 -> 17, of which waited for: 8 -> 5; matrix products, arithmetic and copies ran while one was open for 1% -> 1% of each run, Pallas kernels for 16% -> 19%
where the time goes in v3:
time: 64.2 us; the launch traced here: 63.9 us
  starting transfers between devices  27.4 us (43%)
  Pallas kernels  22 us (34%)
  waiting for transfers between devices  10.6 us (17%)
  other arithmetic  1.72 us (3%)
  local copies, waits for them, and re-layouts  1.3 us (2%)
  between operations  0.81 us (1%)
    ppermute x16, starting transfers between devices, shards(): arrived = [lax.ppermute(out_going[k], *pairs[k]) for k in order]  21.7 us
    all_to_all x1, waiting for transfers between devices, shards(): lax.all_to_all(away, 'seg', split_axis=0, concat_axis=0, tiled=True)  8.81 us
    pallas_call x3, Pallas kernels, shards(): call(functools.partial(volume_kernel, factor), [state, face_part, state],...  6.78 us
    all_to_all x1, starting transfers between devices, shards(): lax.all_to_all(away, 'seg', split_axis=0, concat_axis=0, tiled=True)  5.78 us
    pallas_call x1, Pallas kernels, shards(): call(functools.partial(end_kernel, factor, order), [state, shape(9, 4, P_...  3.65 us
    pallas_call x3, Pallas kernels, shards(): call(functools.partial(finish_kernel, factor, order), [state, table] + pa...  3.58 us
    pallas_call x1, Pallas kernels, shards(): call(next_kernel, [shape(9, E_DEV, NODES)], [turn], count=1)(total)[0]  3.1 us
    pallas_call x1, Pallas kernels, shards(): call(functools.partial(first_volume_kernel, factor), [state, face_part, s...  2.1 us
  transfers between devices with their start and end apart: 17, of which 5 were waited for; matrix products, arithmetic and copies ran while one was open for 1% of the time, Pallas kernels for 19%

profile of v3, /device:TPU:0, one launch (start us, length us, event | category | flops | bytes accessed | tf_op | source)
XLA Modules:
  0.0 63.9 jit_solution(12613602729715409774)
XLA Ops:
  0.7 0.7 %pad_convert_fusion = f32[1,5,128]{2,1,0:T(8,128)S(1)} fusion(s32[1,4,16]{2,1,0:T(4,128)} %param.12), kind=kLoop, calls=%fused_computation.3 | loop fusion | flops 640 | bytes 2816 | tf_op jit(solution)/shard_map/convert_element_type | solution.py:512
  1.3 0.7 %select_maximum_fusion.pack_ref = f32[1,8,128]{2,1,0:T(8,128)S(1)} fusion(f32[1,3,64]{2,1,0:T(4,128)} %bitcast.17, f32[1,5,128]{2,1,0:T(8,128)S(1)} %pad_convert_fusion), kind=kLoop, calls=%fused_computation.1 | loop fusion | flops 3072 | bytes 7424 | tf_op jit(solution)/shard_map/concatenate | solution.py:509
  2.0 1.3 %copy-done = f32[9,64,512]{2,1,0:T(8,128)S(1)} copy-done((f32[9,64,512]{2,1,0:T(8,128)S(1)}, f32[9,64,512]{2,1,0:T(8,128)}, u32[]{:S(2)}) %copy-start) | copy-done | bytes 1179672
  3.3 1.5 %shard_map.104 = (f32[9,4,64,128]{3,2,1,0:T(8,128)S(1)}, bf16[384,768]{1,0:T(8,128)(2,1)S(1)}, f32[3,8,128]{2,1,0:T(8,128)S(1)}, bf16[64,768]{1,0:T(8,128)(2,1)S...) custom-call(f32[1,8,128]{2,1,0:T(8,128)S(1)} %select_maximum_fusion.pack_ref, ...), custom_call_target="tpu_custom_call" | custom-call | flops 100000000 | bytes 6000000 | tf_op jit(solution)/shard_map/pallas_call | solution.py:517
  4.8 6.6 %collective-permute-start = (f32[16,384]{1,0:T(8,128)S(1)}, f32[16,384]{1,0:T(8,128)S(1)}, u32[]{:S(2)}, u32[]{:S(2)}) collective-permute-start(f32[16,384]{1,0:T(8,128)S(1)} %get-tuple-element.49), channel_id=1, source_target_pairs={{1,2},{3,4},{5,6},{7,8},{9,10},{11,12},{13,14},{15,0},{2,1},{4,3},... | collective-permute-start | bytes 73736 | tf_op jit(solution)/shard_map/ppermute | solution.py:529
  11.4 0.0 collective-permute-start.1
  11.4 1.9 %collective-permute-start.2 = (f32[16,384]{1,0:T(8,128)S(1)}, f32[16,384]{1,0:T(8,128)S(1)}, u32[]{:S(2)}, u32[]{:S(2)}) collective-permute-start(f32[16,384]{1,0:T(8,128)S(1)} %get-tuple-element.51), channel_id=1, source_target_pairs={{16,32},{48,64},{80,96},{112,0},{32,16},{64,48},{96,80},{0,112},{1... | collective-permute-start | bytes 73736 | tf_op jit(solution)/shard_map/ppermute | solution.py:529
  13.4 0.0 collective-permute-start.3
  13.4 0.1 convert_reduce_fusion
  13.5 2.1 %shard_map.105 = (f32[9,4,64,128]{3,2,1,0:T(8,128)S(1)}, f32[384,384]{1,0:T(8,128)S(1)}, bf16[768,384]{1,0:T(8,128)(2,1)S(1)}, bf16[128,384]{1,0:T(8,128)(2,1)S(1)}) custom-call(f32[8,128]{1,0:T(8,128)S(1)} %pad.12.faces_ref, f32[9,4,64,128]{3,2,1,0:T(8,128)S(1)} %get-tuple-element.44.v_ref.acc_ref, bf16[384,768]{1,0:T(8,128)(2,1)S(1)} %get-tuple-element.45.t_ref, ...), custom_call_target="tpu_custom_call" | custom-call | flops 100000000 | bytes 6000000 | tf_op jit(solution)/shard_map/pallas_call | solution.py:531
  15.6 0.0 collective-permute-done.ra
  15.6 0.0 collective-permute-done.1.rb
  15.7 0.2 collective-permute-done.2.rc
  15.9 0.0 collective-permute-done.3.rd
  15.9 1.2 %shard_map.106 = (f32[9,4,64,128]{3,2,1,0:T(8,128)S(1)}, bf16[384,768]{1,0:T(8,128)(2,1)S(1)}, f32[16,384]{1,0:T(8,128)S(1)}, f32[16,384]{1,0:T(8,128)S(1)}, f32...) custom-call(f32[9,4,64,128]{3,2,1,0:T(8,128)S(1)} %get-tuple-element.47.vol_ref, ...), custom_call_target="tpu_custom_call", output_to_operand_aliasing={{0}: (0, {})} | custom-call | flops 100000000 | bytes 6000000 | tf_op jit(solution)/shard_map/pallas_call | solution.py:542
  17.1 2.8 %collective-permute-start.4 = (f32[16,384]{1,0:T(8,128)S(1)}, f32[16,384]{1,0:T(8,128)S(1)}, u32[]{:S(2)}, u32[]{:S(2)}) collective-permute-start(f32[16,384]{1,0:T(8,128)S(1)} %get-tuple-element.60), channel_id=1, source_target_pairs={{1,2},{3,4},{5,6},{7,8},{9,10},{11,12},{13,14},{15,0},{2,1},{4,3},... | collective-permute-start | bytes 73736 | tf_op jit(solution)/shard_map/ppermute | solution.py:529
  19.9 0.0 collective-permute-start.5
  19.9 0.8 %collective-permute-start.6 = (f32[16,384]{1,0:T(8,128)S(1)}, f32[16,384]{1,0:T(8,128)S(1)}, u32[]{:S(2)}, u32[]{:S(2)}) collective-permute-start(f32[16,384]{1,0:T(8,128)S(1)} %get-tuple-element.62), channel_id=1, source_target_pairs={{16,32},{48,64},{80,96},{112,0},{32,16},{64,48},{96,80},{0,112},{1... | collective-permute-start | bytes 73736 | tf_op jit(solution)/shard_map/ppermute | solution.py:529
  20.6 0.8 %collective-permute-start.7 = (f32[16,384]{1,0:T(8,128)S(1)}, f32[16,384]{1,0:T(8,128)S(1)}, u32[]{:S(2)}, u32[]{:S(2)}) collective-permute-start(f32[16,384]{1,0:T(8,128)S(1)} %get-tuple-element.63), channel_id=1, source_target_pairs={{0,16},{32,48},{64,80},{96,112},{16,0},{48,32},{80,64},{112,96},{1... | collective-permute-start | bytes 73736 | tf_op jit(solution)/shard_map/ppermute | solution.py:529
  21.5 2.2 %shard_map.107 = (f32[9,4,64,128]{3,2,1,0:T(8,128)S(1)}, f32[384,384]{1,0:T(8,128)S(1)}, f32[9,4,64,128]{3,2,1,0:T(8,128)S(1)}) custom-call(f32[9,4,64,128]{3,2,1,0:T(8,128)S(1)} %get-tuple-element.55.v_ref, bf16[384,768]{1,0:T(8,128)(2,1)S(1)} %get-tuple-element.56.t_ref, bf16[768,384]{1,0:T(8,128)(2,1)S(1)} %get-tuple-element.57.local_ref, ...), custom_call_target="tpu_custom_call" | custom-call | flops 100000000 | bytes 6000000 | tf_op jit(solution)/shard_map/pallas_call | solution.py:538
  23.7 0.6 collective-permute-done.4.ra
  24.3 0.0 collective-permute-done.5.rb
  24.3 0.0 collective-permute-done.6.rc
  24.3 0.0 collective-permute-done.7.rd
  24.3 1.2 %shard_map.108 = (f32[9,4,64,128]{3,2,1,0:T(8,128)S(1)}, bf16[384,768]{1,0:T(8,128)(2,1)S(1)}, f32[16,384]{1,0:T(8,128)S(1)}, f32[16,384]{1,0:T(8,128)S(1)}, f32...) custom-call(f32[9,4,64,128]{3,2,1,0:T(8,128)S(1)} %get-tuple-element.58.vol_ref, ...), custom_call_target="tpu_custom_call", output_to_operand_aliasing={{0}: (0, {})} | custom-call | flops 100000000 | bytes 6000000 | tf_op jit(solution)/shard_map/pallas_call | solution.py:542
  25.5 2.8 %collective-permute-start.10 = (f32[16,384]{1,0:T(8,128)S(1)}, f32[16,384]{1,0:T(8,128)S(1)}, u32[]{:S(2)}, u32[]{:S(2)}) collective-permute-start(f32[16,384]{1,0:T(8,128)S(1)} %get-tuple-element.71), channel_id=1, source_target_pairs={{1,2},{3,4},{5,6},{7,8},{9,10},{11,12},{13,14},{15,0},{2,1},{4,3},... | collective-permute-start | bytes 73736 | tf_op jit(solution)/shard_map/ppermute | solution.py:529
  28.3 0.0 collective-permute-start.11
  28.3 1.6 %collective-permute-start.8 = (f32[16,384]{1,0:T(8,128)S(1)}, f32[16,384]{1,0:T(8,128)S(1)}, u32[]{:S(2)}, u32[]{:S(2)}) collective-permute-start(f32[16,384]{1,0:T(8,128)S(1)} %get-tuple-element.69), channel_id=1, source_target_pairs={{16,32},{48,64},{80,96},{112,0},{32,16},{64,48},{96,80},{0,112},{1... | collective-permute-start | bytes 73736 | tf_op jit(solution)/shard_map/ppermute | solution.py:529
  29.9 0.0 collective-permute-start.9
  29.9 0.1 select_reduce_fusion.keys_ref
  30.0 2.3 %shard_map.109 = (f32[9,4,64,128]{3,2,1,0:T(8,128)S(1)}, f32[384,384]{1,0:T(8,128)S(1)}, f32[9,4,64,128]{3,2,1,0:T(8,128)S(1)}) custom-call(f32[9,4,64,128]{3,2,1,0:T(8,128)S(1)} %get-tuple-element.64.v_ref, bf16[384,768]{1,0:T(8,128)(2,1)S(1)} %get-tuple-element.65.t_ref, bf16[768,384]{1,0:T(8,128)(2,1)S(1)} %get-tuple-element.57.local_ref, ...), custom_call_target="tpu_custom_call" | custom-call | flops 100000000 | bytes 6000000 | tf_op jit(solution)/shard_map/pallas_call | solution.py:538
  32.3 0.4 collective-permute-done.10.rc
  32.7 0.0 collective-permute-done.11.rd
  32.7 0.0 collective-permute-done.8.ra
  32.8 1.2 %shard_map.110 = (f32[9,4,64,128]{3,2,1,0:T(8,128)S(1)}, bf16[384,768]{1,0:T(8,128)(2,1)S(1)}, f32[16,384]{1,0:T(8,128)S(1)}, f32[16,384]{1,0:T(8,128)S(1)}, f32...) custom-call(f32[9,4,64,128]{3,2,1,0:T(8,128)S(1)} %get-tuple-element.67.vol_ref, ...), custom_call_target="tpu_custom_call", output_to_operand_aliasing={{0}: (0, {})} | custom-call | flops 100000000 | bytes 6000000 | tf_op jit(solution)/shard_map/pallas_call | solution.py:542
  34.0 2.8 %collective-permute-start.12 = (f32[16,384]{1,0:T(8,128)S(1)}, f32[16,384]{1,0:T(8,128)S(1)}, u32[]{:S(2)}, u32[]{:S(2)}) collective-permute-start(f32[16,384]{1,0:T(8,128)S(1)} %get-tuple-element.78), channel_id=1, source_target_pairs={{1,2},{3,4},{5,6},{7,8},{9,10},{11,12},{13,14},{15,0},{2,1},{4,3},... | collective-permute-start | bytes 73736 | tf_op jit(solution)/shard_map/ppermute | solution.py:529
  36.7 0.0 collective-permute-start.13
  36.7 0.6 collective-permute-start.14
  37.3 1.0 %collective-permute-start.15 = (f32[16,384]{1,0:T(8,128)S(1)}, f32[16,384]{1,0:T(8,128)S(1)}, u32[]{:S(2)}, u32[]{:S(2)}) collective-permute-start(f32[16,384]{1,0:T(8,128)S(1)} %get-tuple-element.81), channel_id=1, source_target_pairs={{0,16},{32,48},{64,80},{96,112},{16,0},{48,32},{80,64},{112,96},{1... | collective-permute-start | bytes 73736 | tf_op jit(solution)/shard_map/ppermute | solution.py:529
  38.3 0.1 add_bitcast_fusion.place_ref
  38.4 2.3 %shard_map.111 = (f32[9,4,64,128]{3,2,1,0:T(8,128)S(1)}, f32[384,384]{1,0:T(8,128)S(1)}, f32[9,4,64,128]{3,2,1,0:T(8,128)S(1)}) custom-call(f32[9,4,64,128]{3,2,1,0:T(8,128)S(1)} %get-tuple-element.73.v_ref, bf16[384,768]{1,0:T(8,128)(2,1)S(1)} %get-tuple-element.74.t_ref, bf16[768,384]{1,0:T(8,128)(2,1)S(1)} %get-tuple-element.57.local_ref, ...), custom_call_target="tpu_custom_call" | custom-call | flops 100000000 | bytes 6000000 | tf_op jit(solution)/shard_map/pallas_call | solution.py:538
  40.7 0.5 collective-permute-done.12.ra
  41.2 0.0 collective-permute-done.14.rc
  41.2 3.7 %shard_map.112 = (f32[9,4,64,128]{3,2,1,0:T(8,128)S(1)}, f32[9,4,8,128]{3,2,1,0:T(8,128)S(1)}, f32[16,9,8,128]{3,2,1,0:T(8,128)}) custom-call(s32[8]{0:T(128)S(1)} %select_reduce_fusion.keys_ref, f32[9,4,64,128]{3,2,1,0:T(8,128)S(1)} %get-tuple-element.76.vol_ref, f32[384,384]{1,0:T(8,128)S(1)} %get-tuple-element.77.part_ref, ...), custom_call_target="tpu_custom_call", output_to_operand_aliasing={{0}: (1, {})} | custom-call | flops 100000000 | bytes 6000000 | tf_op jit(solution)/shard_map/pallas_call | solution.py:551
  44.9 5.8 %all-to-all-start = ((f32[16,9,8,128]{3,2,1,0:T(8,128)}), f32[16,9,8,128]{3,2,1,0:T(8,128)S(1)}, u32[]{:S(2)}, u32[]{:S(2)}) async-start(f32[16,9,8,128]{3,2,1,0:T(8,128)} %get-tuple-element.85), calls=%async_computation | async-start | bytes 1179648 | tf_op jit(solution)/shard_map/all_to_all | solution.py:566
  50.7 3.1 %shard_map.113 = f32[9,64,512]{2,1,0:T(8,128)} custom-call(f32[9,4,64,128]{3,2,1,0:T(8,128)S(1)} %get-tuple-element.83.total_ref), custom_call_target="tpu_custom_call" | custom-call | flops 100000000 | bytes 6000000 | tf_op jit(solution)/shard_map/pallas_call | solution.py:567
  53.8 8.8 %all-to-all-done.arrived_ref = f32[16,9,8,128]{3,2,1,0:T(8,128)S(1)} async-done(((f32[16,9,8,128]{3,2,1,0:T(8,128)}), f32[16,9,8,128]{3,2,1,0:T(8,128)S(1)}, u32[]{:S(2)}, u32[]{:S(2)}) %all-to-all-start) | async-done | bytes 589856 | tf_op jit(solution)/shard_map/all_to_all | solution.py:566
  62.6 1.3 %shard_map.114 = f32[9,8,512]{2,1,0:T(8,128)} custom-call(s32[2,8]{1,0:T(2,128)S(1)} %pad_add_fusion.table_ref, f32[9,4,8,128]{3,2,1,0:T(8,128)S(1)} %get-tuple-element.84.home_ref, f32[16,9,8,128]{3,2,1,0:T(8,128)S(1)} %all-to-all-done.arrived_ref), custom_call_target="tpu_custom_call" | custom-call | flops 100000000 | bytes 6000000 | tf_op jit(solution)/shard_map/pallas_call | solution.py:568
  (24 shorter events, 0.1 us)
Async XLA Ops:
  0.6 12.7 %copy-start.5 = (s32[3,64]{1,0:T(4,128)S(1)}, s32[3,64]{1,0:T(4,128)}, u32[]{:S(2)}) copy-start(s32[3,64]{1,0:T(4,128)} %param.13) | copy-start | bytes 2308
  0.6 12.8 %copy-start.4 = (s32[64,6]{0,1:T(8,128)S(1)}, s32[64,6]{0,1:T(8,128)}, u32[]{:S(2)}) copy-start(s32[64,6]{0,1:T(8,128)} %param.11) | copy-start | bytes 4612
  2.0 1.3 %copy-start = (f32[9,64,512]{2,1,0:T(8,128)S(1)}, f32[9,64,512]{2,1,0:T(8,128)}, u32[]{:S(2)}) copy-start(f32[9,64,512]{2,1,0:T(8,128)} %adjoint_ref.1) | copy-start | bytes 3538948
  4.8 10.8 %collective-permute-start = (f32[16,384]{1,0:T(8,128)S(1)}, f32[16,384]{1,0:T(8,128)S(1)}, u32[]{:S(2)}, u32[]{:S(2)}) collective-permute-start(f32[16,384]{1,0:T(8,128)S(1)} %get-tuple-element.49), channel_id=1, source_target_pairs={{1,2},{3,4},{5,6},{7,8},{9,10},{11,12},{13,14},{15,0},{2,1},{4,3},... | collective-permute-start | bytes 73736 | tf_op jit(solution)/shard_map/ppermute | solution.py:529
  11.4 4.2 %collective-permute-start.1 = (f32[16,384]{1,0:T(8,128)S(1)}, f32[16,384]{1,0:T(8,128)S(1)}, u32[]{:S(2)}, u32[]{:S(2)}) collective-permute-start(f32[16,384]{1,0:T(8,128)S(1)} %get-tuple-element.50), channel_id=1, source_target_pairs={{0,1},{2,3},{4,5},{6,7},{8,9},{10,11},{12,13},{14,15},{1,0},{3,2},... | collective-permute-start | bytes 73736 | tf_op jit(solution)/shard_map/ppermute | solution.py:529
  11.4 4.5 %collective-permute-start.2 = (f32[16,384]{1,0:T(8,128)S(1)}, f32[16,384]{1,0:T(8,128)S(1)}, u32[]{:S(2)}, u32[]{:S(2)}) collective-permute-start(f32[16,384]{1,0:T(8,128)S(1)} %get-tuple-element.51), channel_id=1, source_target_pairs={{16,32},{48,64},{80,96},{112,0},{32,16},{64,48},{96,80},{0,112},{1... | collective-permute-start | bytes 73736 | tf_op jit(solution)/shard_map/ppermute | solution.py:529
  13.4 2.5 %collective-permute-start.3 = (f32[16,384]{1,0:T(8,128)S(1)}, f32[16,384]{1,0:T(8,128)S(1)}, u32[]{:S(2)}, u32[]{:S(2)}) collective-permute-start(f32[16,384]{1,0:T(8,128)S(1)} %get-tuple-element.52), channel_id=1, source_target_pairs={{0,16},{32,48},{64,80},{96,112},{16,0},{48,32},{80,64},{112,96},{1... | collective-permute-start | bytes 73736 | tf_op jit(solution)/shard_map/ppermute | solution.py:529
  17.1 7.2 %collective-permute-start.4 = (f32[16,384]{1,0:T(8,128)S(1)}, f32[16,384]{1,0:T(8,128)S(1)}, u32[]{:S(2)}, u32[]{:S(2)}) collective-permute-start(f32[16,384]{1,0:T(8,128)S(1)} %get-tuple-element.60), channel_id=1, source_target_pairs={{1,2},{3,4},{5,6},{7,8},{9,10},{11,12},{13,14},{15,0},{2,1},{4,3},... | collective-permute-start | bytes 73736 | tf_op jit(solution)/shard_map/ppermute | solution.py:529
  19.9 4.5 %collective-permute-start.5 = (f32[16,384]{1,0:T(8,128)S(1)}, f32[16,384]{1,0:T(8,128)S(1)}, u32[]{:S(2)}, u32[]{:S(2)}) collective-permute-start(f32[16,384]{1,0:T(8,128)S(1)} %get-tuple-element.61), channel_id=1, source_target_pairs={{0,1},{2,3},{4,5},{6,7},{8,9},{10,11},{12,13},{14,15},{1,0},{3,2},... | collective-permute-start | bytes 73736 | tf_op jit(solution)/shard_map/ppermute | solution.py:529
  19.9 4.5 %collective-permute-start.6 = (f32[16,384]{1,0:T(8,128)S(1)}, f32[16,384]{1,0:T(8,128)S(1)}, u32[]{:S(2)}, u32[]{:S(2)}) collective-permute-start(f32[16,384]{1,0:T(8,128)S(1)} %get-tuple-element.62), channel_id=1, source_target_pairs={{16,32},{48,64},{80,96},{112,0},{32,16},{64,48},{96,80},{0,112},{1... | collective-permute-start | bytes 73736 | tf_op jit(solution)/shard_map/ppermute | solution.py:529
  20.6 3.7 %collective-permute-start.7 = (f32[16,384]{1,0:T(8,128)S(1)}, f32[16,384]{1,0:T(8,128)S(1)}, u32[]{:S(2)}, u32[]{:S(2)}) collective-permute-start(f32[16,384]{1,0:T(8,128)S(1)} %get-tuple-element.63), channel_id=1, source_target_pairs={{0,16},{32,48},{64,80},{96,112},{16,0},{48,32},{80,64},{112,96},{1... | collective-permute-start | bytes 73736 | tf_op jit(solution)/shard_map/ppermute | solution.py:529
  25.5 7.2 %collective-permute-start.10 = (f32[16,384]{1,0:T(8,128)S(1)}, f32[16,384]{1,0:T(8,128)S(1)}, u32[]{:S(2)}, u32[]{:S(2)}) collective-permute-start(f32[16,384]{1,0:T(8,128)S(1)} %get-tuple-element.71), channel_id=1, source_target_pairs={{1,2},{3,4},{5,6},{7,8},{9,10},{11,12},{13,14},{15,0},{2,1},{4,3},... | collective-permute-start | bytes 73736 | tf_op jit(solution)/shard_map/ppermute | solution.py:529
  28.3 4.5 %collective-permute-start.11 = (f32[16,384]{1,0:T(8,128)S(1)}, f32[16,384]{1,0:T(8,128)S(1)}, u32[]{:S(2)}, u32[]{:S(2)}) collective-permute-start(f32[16,384]{1,0:T(8,128)S(1)} %get-tuple-element.72), channel_id=1, source_target_pairs={{0,1},{2,3},{4,5},{6,7},{8,9},{10,11},{12,13},{14,15},{1,0},{3,2},... | collective-permute-start | bytes 73736 | tf_op jit(solution)/shard_map/ppermute | solution.py:529
  28.3 4.5 %collective-permute-start.8 = (f32[16,384]{1,0:T(8,128)S(1)}, f32[16,384]{1,0:T(8,128)S(1)}, u32[]{:S(2)}, u32[]{:S(2)}) collective-permute-start(f32[16,384]{1,0:T(8,128)S(1)} %get-tuple-element.69), channel_id=1, source_target_pairs={{16,32},{48,64},{80,96},{112,0},{32,16},{64,48},{96,80},{0,112},{1... | collective-permute-start | bytes 73736 | tf_op jit(solution)/shard_map/ppermute | solution.py:529
  29.9 2.8 %collective-permute-start.9 = (f32[16,384]{1,0:T(8,128)S(1)}, f32[16,384]{1,0:T(8,128)S(1)}, u32[]{:S(2)}, u32[]{:S(2)}) collective-permute-start(f32[16,384]{1,0:T(8,128)S(1)} %get-tuple-element.70), channel_id=1, source_target_pairs={{0,16},{32,48},{64,80},{96,112},{16,0},{48,32},{80,64},{112,96},{1... | collective-permute-start | bytes 73736 | tf_op jit(solution)/shard_map/ppermute | solution.py:529
  34.0 7.2 %collective-permute-start.12 = (f32[16,384]{1,0:T(8,128)S(1)}, f32[16,384]{1,0:T(8,128)S(1)}, u32[]{:S(2)}, u32[]{:S(2)}) collective-permute-start(f32[16,384]{1,0:T(8,128)S(1)} %get-tuple-element.78), channel_id=1, source_target_pairs={{1,2},{3,4},{5,6},{7,8},{9,10},{11,12},{13,14},{15,0},{2,1},{4,3},... | collective-permute-start | bytes 73736 | tf_op jit(solution)/shard_map/ppermute | solution.py:529
  36.7 4.5 %collective-permute-start.13 = (f32[16,384]{1,0:T(8,128)S(1)}, f32[16,384]{1,0:T(8,128)S(1)}, u32[]{:S(2)}, u32[]{:S(2)}) collective-permute-start(f32[16,384]{1,0:T(8,128)S(1)} %get-tuple-element.79), channel_id=1, source_target_pairs={{0,1},{2,3},{4,5},{6,7},{8,9},{10,11},{12,13},{14,15},{1,0},{3,2},... | collective-permute-start | bytes 73736 | tf_op jit(solution)/shard_map/ppermute | solution.py:529
  36.7 4.5 %collective-permute-start.14 = (f32[16,384]{1,0:T(8,128)S(1)}, f32[16,384]{1,0:T(8,128)S(1)}, u32[]{:S(2)}, u32[]{:S(2)}) collective-permute-start(f32[16,384]{1,0:T(8,128)S(1)} %get-tuple-element.80), channel_id=1, source_target_pairs={{16,32},{48,64},{80,96},{112,0},{32,16},{64,48},{96,80},{0,112},{1... | collective-permute-start | bytes 73736 | tf_op jit(solution)/shard_map/ppermute | solution.py:529
  37.3 3.8 %collective-permute-start.15 = (f32[16,384]{1,0:T(8,128)S(1)}, f32[16,384]{1,0:T(8,128)S(1)}, u32[]{:S(2)}, u32[]{:S(2)}) collective-permute-start(f32[16,384]{1,0:T(8,128)S(1)} %get-tuple-element.81), channel_id=1, source_target_pairs={{0,16},{32,48},{64,80},{96,112},{16,0},{48,32},{80,64},{112,96},{1... | collective-permute-start | bytes 73736 | tf_op jit(solution)/shard_map/ppermute | solution.py:529
  38.4 2.8 %copy-start.1 = (f32[64,8,128]{2,1,0:T(8,128)S(1)}, f32[64,8,128]{2,1,0:T(8,128)}, u32[]{:S(2)}) copy-start(f32[64,8,128]{2,1,0:T(8,128)} %constant.23.clone.lines_ref) | copy-start | bytes 786436
  38.4 2.8 %copy-start.2 = (bf16[256,128]{1,0:T(8,128)(2,1)S(1)}, bf16[256,128]{1,0:T(8,128)(2,1)}, u32[]{:S(2)}) copy-start(bf16[256,128]{1,0:T(8,128)(2,1)} %constant.21.clone.wa_ref) | copy-start | bytes 196612
  38.4 2.8 %copy-start.3 = (bf16[256,128]{1,0:T(8,128)(2,1)S(1)}, bf16[256,128]{1,0:T(8,128)(2,1)}, u32[]{:S(2)}) copy-start(bf16[256,128]{1,0:T(8,128)(2,1)} %constant.22.clone.wb_ref) | copy-start | bytes 196612
  44.9 5.8 %copy-start.6 = (s32[2,8]{1,0:T(2,128)S(1)}, s32[2,8]{1,0:T(2,128)}, u32[]{:S(2)}) copy-start(s32[2,8]{1,0:T(2,128)} %param.14) | copy-start | bytes 196
  44.9 17.7 %all-to-all-start = ((f32[16,9,8,128]{3,2,1,0:T(8,128)}), f32[16,9,8,128]{3,2,1,0:T(8,128)S(1)}, u32[]{:S(2)}, u32[]{:S(2)}) async-start(f32[16,9,8,128]{3,2,1,0:T(8,128)} %get-tuple-element.85), calls=%async_computation | async-start | bytes 1179648 | tf_op jit(solution)/shard_map/all_to_all | solution.py:566

commit v4 on v3

--- a/solution.py
+++ b/solution.py
@@ -333,9 +333,11 @@
 
 
 def add_faces(part_ref, r_refs, remote_ref, factor, out_ref, face_ref):
-    arrived = jnp.concatenate([r[...] for r in r_refs], axis=0).T * factor
-    both = jnp.concatenate(split(arrived), axis=1)
-    face_ref[...] = part_ref[...] + jnp.dot(both, remote_ref[...], preferred_element_type=F32)
+    arrived = jnp.concatenate([r[...] for r in r_refs], axis=0) * factor
+    both = jnp.concatenate(split(arrived), axis=0)
+    face_ref[...] = part_ref[...] + lax.dot_general(
+        both, remote_ref[...], (((0,), (0,)), ((), ())), preferred_element_type=F32
+    )
     low = low_half()
     for direction in range(3):
         for value in range(6):
@@ -370,7 +372,7 @@
 
 def end_kernel(
     factor, order, keys_ref, vol_ref, part_ref, ra, rb, rc, rd, remote_ref, acc_ref, place_ref, wa_ref, wb_ref, lines_ref,
-    total_ref, home_ref, away_ref, face_ref, turn_ref, ranked_ref, rows_ref, plane_ref, parent_ref,
+    total_ref, parent_ref, away_ref, face_ref, turn_ref, ranked_ref, rows_ref, plane_ref,
 ):
     add_faces(part_ref, in_order(order, (ra, rb, rc, rd)), remote_ref, factor, total_ref, face_ref)
     place = jnp.where(
@@ -410,15 +412,8 @@
                 sums[i] = term if k == 0 else sums[i] + term
         for i in range(9):
             parent_ref[i, t] = sums[i]
-    home_ref[...] = jnp.zeros_like(home_ref)
     for g in range(P_DEV):
         key = keys_ref[g]
-
-        @pl.when(key < P_DEV)
-        def _():
-            for i in range(9):
-                for t in range(4):
-                    home_ref[i, t, pl.ds(key, 1), :] = parent_ref[i, t, pl.ds(g, 1), :]
 
         @pl.when(key >= P_DEV)
         def _():
@@ -441,13 +436,16 @@
     lax.fori_loop(0, 9, body, 0)
 
 
-def parent_kernel(table_ref, home_ref, arrived_ref, out_ref):
-    for i in range(9):
-        for t in range(4):
-            out_ref[i, :, pl.ds(128 * t, 128)] = home_ref[i, t]
+def parent_kernel(table_ref, groups_ref, arrived_ref, out_ref):
     for p in range(P_DEV):
         holder = table_ref[0, p]
         slot = table_ref[1, p]
+
+        @pl.when(slot < 0)
+        def _():
+            for i in range(9):
+                for t in range(4):
+                    out_ref[i, pl.ds(p, 1), pl.ds(128 * t, 128)] = groups_ref[i, t, pl.ds(holder, 1), :]
 
         @pl.when(slot >= 0)
         def _():
@@ -497,7 +495,9 @@
     keys = jnp.sum(
         jnp.where(first[:, None] & (rank[:, None] == jnp.arange(P_DEV)[None, :]), key[:, None], 0), axis=0
     )
-    source = jnp.stack([children[0], jnp.where(children[0] == own_seg, -1, children[1])])
+    stays = children[0] == own_seg
+    group = jnp.sum((keys[:, None] < jnp.arange(P_DEV)[None, :]).astype(jnp.int32), axis=0)
+    source = jnp.stack([jnp.where(stays, group, children[0]), jnp.where(stays, -1, children[1])])
 
     state = shape(9, 4, 64, 128)
     table = shape(LOCAL, 2 * LOCAL, dtype=BF)
@@ -506,13 +506,10 @@
     face_scratch = pltpu.VMEM((LOCAL, LOCAL), F32)
     turn = pltpu.VMEM((NODES, 128), F32)
 
-    pack = jnp.concatenate(
-        [
-            jnp.pad(material[None], ((0, 0), (0, 0), (0, 64))),
-            jnp.pad(send_faces, ((0, 0), (0, 1), (0, 128 - CAP))).astype(F32),
-        ],
-        axis=1,
-    )
+    zero = jnp.float32(0)
+    pack = lax.pad(material[None], zero, ((0, 0, 0), (0, 5, 0), (0, 64, 0))) + lax.pad(
+        send_faces, jnp.int32(0), ((0, 0, 0), (3, 1, 0), (0, 128 - CAP, 0))
+    ).astype(F32)
     faces = jnp.pad(face_partner.T.astype(F32), ((0, 2), (0, 64)))
     outs = call(
         begin_kernel,
@@ -548,7 +545,7 @@
             )(vol, part, *arrived, remote_hot, mat, send_hot)
             v, t, out_going = outs[0], outs[1], outs[2:]
     wa, wb, lines = (jnp.asarray(x) for x in refine_parts())
-    total, home, away = call(
+    total, groups, away = call(
         functools.partial(end_kernel, factor, order),
         [state, shape(9, 4, P_DEV, 128), shape(N_SEG, 9, 8, 128)],
         [
@@ -557,7 +554,6 @@
             pltpu.VMEM((9, 64, NODES), F32),
             pltpu.VMEM((9, 128, 256), F32),
             pltpu.VMEM((9, 128, 128), F32),
-            pltpu.VMEM((9, 4, 8, 128), F32),
         ],
         smem=(0,),
         aliases={1: 0},
@@ -565,7 +561,7 @@
     )(keys, vol, part, *arrived, remote_hot, acc, place, wa, wb, lines)
     fetched = lax.all_to_all(away, "seg", split_axis=0, concat_axis=0, tiled=True)
     updated = call(next_kernel, [shape(9, E_DEV, NODES)], [turn], count=1)(total)[0]
-    parents = call(parent_kernel, [shape(9, P_DEV, NODES)], smem=(0,), count=3)(source, home, fetched)[0]
+    parents = call(parent_kernel, [shape(9, P_DEV, NODES)], smem=(0,), count=3)(source, groups, fetched)[0]
     return (updated, parents)
 
 

time: 64.2 us -> 62.8 us (0.978)
  Pallas kernels: 22 us -> 21.3 us
    add x0 -> x1, other arithmetic: none -> 0.72 us  [shards(): lax.pad(material[None], zero, ((0, 0, 0), (0, 5, 0), (0, 64, 0)))]
    convert_element_type x1 -> x0, other arithmetic: 0.7 us -> none  [shards(): jnp.pad(send_faces, ((0, 0), (0, 1), (0, 128 - CAP))).astype(F32)]
    concatenate x1 -> x0, other arithmetic: 0.69 us -> none  [shards(): jnp.concatenate([jnp.pad(material[None], ((0, 0), (0, 0), (0, 64))), jnp....]
where the time goes in v4:
time: 62.8 us; the launch traced here: 62.5 us
  starting transfers between devices  27.5 us (44%)
  Pallas kernels  21.3 us (34%)
  waiting for transfers between devices  10.5 us (17%)
  local copies, waits for them, and re-layouts  1.3 us (2%)
  other arithmetic  1.14 us (2%)
  between operations  0.79 us (1%)
    ppermute x16, starting transfers between devices, shards(): arrived = [lax.ppermute(out_going[k], *pairs[k]) for k in order]  21.7 us
    all_to_all x1, waiting for transfers between devices, shards(): lax.all_to_all(away, 'seg', split_axis=0, concat_axis=0, tiled=True)  8.72 us
    pallas_call x3, Pallas kernels, shards(): call(functools.partial(volume_kernel, factor), [state, face_part, state],...  6.78 us
    all_to_all x1, starting transfers between devices, shards(): lax.all_to_all(away, 'seg', split_axis=0, concat_axis=0, tiled=True)  5.78 us
    pallas_call x1, Pallas kernels, shards(): call(functools.partial(end_kernel, factor, order), [state, shape(9, 4, P_...  3.44 us
    pallas_call x1, Pallas kernels, shards(): call(next_kernel, [shape(9, E_DEV, NODES)], [turn], count=1)(total)[0]  3.1 us
    pallas_call x3, Pallas kernels, shards(): call(functools.partial(finish_kernel, factor, order), [state, table] + pa...  2.98 us
    pallas_call x1, Pallas kernels, shards(): call(functools.partial(first_volume_kernel, factor), [state, face_part, s...  2.1 us
  transfers between devices with their start and end apart: 17, of which 5 were waited for; matrix products, arithmetic and copies ran while one was open for 1% of the time, Pallas kernels for 19%

profile of v4, /device:TPU:0, one launch (start us, length us, event | category | flops | bytes accessed | tf_op | source)
XLA Modules:
  0.0 62.5 jit_solution(10098832683315619909)
XLA Ops:
  0.7 0.7 %convert_add_fusion.pack_ref = f32[1,8,128]{2,1,0:T(8,128)S(1)} fusion(s32[1,4,16]{2,1,0:T(4,128)} %param.12, f32[1,3,64]{2,1,0:T(4,128)} %bitcast.19), kind=kLoop, calls=%fused_computation.3 | loop fusion | flops 2048 | bytes 5120 | tf_op jit(solution)/shard_map/add | solution.py:510
  1.4 1.3 %copy-done = f32[9,64,512]{2,1,0:T(8,128)S(1)} copy-done((f32[9,64,512]{2,1,0:T(8,128)S(1)}, f32[9,64,512]{2,1,0:T(8,128)}, u32[]{:S(2)}) %copy-start) | copy-done | bytes 1179672
  2.6 1.5 %shard_map.104 = (f32[9,4,64,128]{3,2,1,0:T(8,128)S(1)}, bf16[384,768]{1,0:T(8,128)(2,1)S(1)}, f32[3,8,128]{2,1,0:T(8,128)S(1)}, bf16[64,768]{1,0:T(8,128)(2,1)S...) custom-call(f32[1,8,128]{2,1,0:T(8,128)S(1)} %convert_add_fusion.pack_ref, ...), custom_call_target="tpu_custom_call" | custom-call | flops 100000000 | bytes 6000000 | tf_op jit(solution)/shard_map/pallas_call | solution.py:514
  4.1 6.6 %collective-permute-start = (f32[16,384]{1,0:T(8,128)S(1)}, f32[16,384]{1,0:T(8,128)S(1)}, u32[]{:S(2)}, u32[]{:S(2)}) collective-permute-start(f32[16,384]{1,0:T(8,128)S(1)} %get-tuple-element.49), channel_id=1, source_target_pairs={{1,2},{3,4},{5,6},{7,8},{9,10},{11,12},{13,14},{15,0},{2,1},{4,3},... | collective-permute-start | bytes 73736 | tf_op jit(solution)/shard_map/ppermute | solution.py:526
  10.8 0.0 collective-permute-start.1
  10.8 1.9 %collective-permute-start.2 = (f32[16,384]{1,0:T(8,128)S(1)}, f32[16,384]{1,0:T(8,128)S(1)}, u32[]{:S(2)}, u32[]{:S(2)}) collective-permute-start(f32[16,384]{1,0:T(8,128)S(1)} %get-tuple-element.51), channel_id=1, source_target_pairs={{16,32},{48,64},{80,96},{112,0},{32,16},{64,48},{96,80},{0,112},{1... | collective-permute-start | bytes 73736 | tf_op jit(solution)/shard_map/ppermute | solution.py:526
  12.7 0.0 collective-permute-start.3
  12.8 0.1 convert_reduce_fusion
  12.9 2.1 %shard_map.105 = (f32[9,4,64,128]{3,2,1,0:T(8,128)S(1)}, f32[384,384]{1,0:T(8,128)S(1)}, bf16[768,384]{1,0:T(8,128)(2,1)S(1)}, bf16[128,384]{1,0:T(8,128)(2,1)S(1)}) custom-call(f32[8,128]{1,0:T(8,128)S(1)} %pad.10.faces_ref, f32[9,4,64,128]{3,2,1,0:T(8,128)S(1)} %get-tuple-element.44.v_ref.acc_ref, bf16[384,768]{1,0:T(8,128)(2,1)S(1)} %get-tuple-element.45.t_ref, ...), custom_call_target="tpu_custom_call" | custom-call | flops 100000000 | bytes 6000000 | tf_op jit(solution)/shard_map/pallas_call | solution.py:528
  15.0 0.0 collective-permute-done.ra
  15.0 0.0 collective-permute-done.1.rb
  15.0 0.2 collective-permute-done.2.rc
  15.2 0.0 collective-permute-done.3.rd
  15.2 1.0 %shard_map.106 = (f32[9,4,64,128]{3,2,1,0:T(8,128)S(1)}, bf16[384,768]{1,0:T(8,128)(2,1)S(1)}, f32[16,384]{1,0:T(8,128)S(1)}, f32[16,384]{1,0:T(8,128)S(1)}, f32...) custom-call(f32[9,4,64,128]{3,2,1,0:T(8,128)S(1)} %get-tuple-element.47.vol_ref, ...), custom_call_target="tpu_custom_call", output_to_operand_aliasing={{0}: (0, {})} | custom-call | flops 100000000 | bytes 6000000 | tf_op jit(solution)/shard_map/pallas_call | solution.py:539
  16.2 2.8 %collective-permute-start.4 = (f32[16,384]{1,0:T(8,128)S(1)}, f32[16,384]{1,0:T(8,128)S(1)}, u32[]{:S(2)}, u32[]{:S(2)}) collective-permute-start(f32[16,384]{1,0:T(8,128)S(1)} %get-tuple-element.60), channel_id=1, source_target_pairs={{1,2},{3,4},{5,6},{7,8},{9,10},{11,12},{13,14},{15,0},{2,1},{4,3},... | collective-permute-start | bytes 73736 | tf_op jit(solution)/shard_map/ppermute | solution.py:526
  19.0 0.8 %collective-permute-start.6 = (f32[16,384]{1,0:T(8,128)S(1)}, f32[16,384]{1,0:T(8,128)S(1)}, u32[]{:S(2)}, u32[]{:S(2)}) collective-permute-start(f32[16,384]{1,0:T(8,128)S(1)} %get-tuple-element.62), channel_id=1, source_target_pairs={{16,32},{48,64},{80,96},{112,0},{32,16},{64,48},{96,80},{0,112},{1... | collective-permute-start | bytes 73736 | tf_op jit(solution)/shard_map/ppermute | solution.py:526
  19.8 0.8 %collective-permute-start.7 = (f32[16,384]{1,0:T(8,128)S(1)}, f32[16,384]{1,0:T(8,128)S(1)}, u32[]{:S(2)}, u32[]{:S(2)}) collective-permute-start(f32[16,384]{1,0:T(8,128)S(1)} %get-tuple-element.63), channel_id=1, source_target_pairs={{0,16},{32,48},{64,80},{96,112},{16,0},{48,32},{80,64},{112,96},{1... | collective-permute-start | bytes 73736 | tf_op jit(solution)/shard_map/ppermute | solution.py:526
  20.6 2.2 %shard_map.107 = (f32[9,4,64,128]{3,2,1,0:T(8,128)S(1)}, f32[384,384]{1,0:T(8,128)S(1)}, f32[9,4,64,128]{3,2,1,0:T(8,128)S(1)}) custom-call(f32[9,4,64,128]{3,2,1,0:T(8,128)S(1)} %get-tuple-element.55.v_ref, bf16[384,768]{1,0:T(8,128)(2,1)S(1)} %get-tuple-element.56.t_ref, bf16[768,384]{1,0:T(8,128)(2,1)S(1)} %get-tuple-element.57.local_ref, ...), custom_call_target="tpu_custom_call" | custom-call | flops 100000000 | bytes 6000000 | tf_op jit(solution)/shard_map/pallas_call | solution.py:535
  22.8 0.6 collective-permute-done.4.ra
  23.5 0.0 collective-permute-done.5.rb
  23.5 0.0 collective-permute-done.6.rc
  23.5 0.0 collective-permute-done.7.rd
  23.5 1.0 %shard_map.108 = (f32[9,4,64,128]{3,2,1,0:T(8,128)S(1)}, bf16[384,768]{1,0:T(8,128)(2,1)S(1)}, f32[16,384]{1,0:T(8,128)S(1)}, f32[16,384]{1,0:T(8,128)S(1)}, f32...) custom-call(f32[9,4,64,128]{3,2,1,0:T(8,128)S(1)} %get-tuple-element.58.vol_ref, ...), custom_call_target="tpu_custom_call", output_to_operand_aliasing={{0}: (0, {})} | custom-call | flops 100000000 | bytes 6000000 | tf_op jit(solution)/shard_map/pallas_call | solution.py:539
  24.5 2.8 %collective-permute-start.10 = (f32[16,384]{1,0:T(8,128)S(1)}, f32[16,384]{1,0:T(8,128)S(1)}, u32[]{:S(2)}, u32[]{:S(2)}) collective-permute-start(f32[16,384]{1,0:T(8,128)S(1)} %get-tuple-element.71), channel_id=1, source_target_pairs={{1,2},{3,4},{5,6},{7,8},{9,10},{11,12},{13,14},{15,0},{2,1},{4,3},... | collective-permute-start | bytes 73736 | tf_op jit(solution)/shard_map/ppermute | solution.py:526
  27.2 0.0 collective-permute-start.11
  27.2 1.6 %collective-permute-start.8 = (f32[16,384]{1,0:T(8,128)S(1)}, f32[16,384]{1,0:T(8,128)S(1)}, u32[]{:S(2)}, u32[]{:S(2)}) collective-permute-start(f32[16,384]{1,0:T(8,128)S(1)} %get-tuple-element.69), channel_id=1, source_target_pairs={{16,32},{48,64},{80,96},{112,0},{32,16},{64,48},{96,80},{0,112},{1... | collective-permute-start | bytes 73736 | tf_op jit(solution)/shard_map/ppermute | solution.py:526
  28.8 0.0 collective-permute-start.9
  28.8 0.1 select_reduce_fusion.keys_ref
  29.0 2.3 %shard_map.109 = (f32[9,4,64,128]{3,2,1,0:T(8,128)S(1)}, f32[384,384]{1,0:T(8,128)S(1)}, f32[9,4,64,128]{3,2,1,0:T(8,128)S(1)}) custom-call(f32[9,4,64,128]{3,2,1,0:T(8,128)S(1)} %get-tuple-element.64.v_ref, bf16[384,768]{1,0:T(8,128)(2,1)S(1)} %get-tuple-element.65.t_ref, bf16[768,384]{1,0:T(8,128)(2,1)S(1)} %get-tuple-element.57.local_ref, ...), custom_call_target="tpu_custom_call" | custom-call | flops 100000000 | bytes 6000000 | tf_op jit(solution)/shard_map/pallas_call | solution.py:535
  31.3 0.4 collective-permute-done.10.rc
  31.7 0.0 collective-permute-done.8.ra
  31.7 1.0 %shard_map.110 = (f32[9,4,64,128]{3,2,1,0:T(8,128)S(1)}, bf16[384,768]{1,0:T(8,128)(2,1)S(1)}, f32[16,384]{1,0:T(8,128)S(1)}, f32[16,384]{1,0:T(8,128)S(1)}, f32...) custom-call(f32[9,4,64,128]{3,2,1,0:T(8,128)S(1)} %get-tuple-element.67.vol_ref, ...), custom_call_target="tpu_custom_call", output_to_operand_aliasing={{0}: (0, {})} | custom-call | flops 100000000 | bytes 6000000 | tf_op jit(solution)/shard_map/pallas_call | solution.py:539
  32.7 2.8 %collective-permute-start.12 = (f32[16,384]{1,0:T(8,128)S(1)}, f32[16,384]{1,0:T(8,128)S(1)}, u32[]{:S(2)}, u32[]{:S(2)}) collective-permute-start(f32[16,384]{1,0:T(8,128)S(1)} %get-tuple-element.78), channel_id=1, source_target_pairs={{1,2},{3,4},{5,6},{7,8},{9,10},{11,12},{13,14},{15,0},{2,1},{4,3},... | collective-permute-start | bytes 73736 | tf_op jit(solution)/shard_map/ppermute | solution.py:526
  35.5 0.0 collective-permute-start.13
  35.5 0.6 %collective-permute-start.14 = (f32[16,384]{1,0:T(8,128)S(1)}, f32[16,384]{1,0:T(8,128)S(1)}, u32[]{:S(2)}, u32[]{:S(2)}) collective-permute-start(f32[16,384]{1,0:T(8,128)S(1)} %get-tuple-element.80), channel_id=1, source_target_pairs={{16,32},{48,64},{80,96},{112,0},{32,16},{64,48},{96,80},{0,112},{1... | collective-permute-start | bytes 73736 | tf_op jit(solution)/shard_map/ppermute | solution.py:526
  36.1 1.0 %collective-permute-start.15 = (f32[16,384]{1,0:T(8,128)S(1)}, f32[16,384]{1,0:T(8,128)S(1)}, u32[]{:S(2)}, u32[]{:S(2)}) collective-permute-start(f32[16,384]{1,0:T(8,128)S(1)} %get-tuple-element.81), channel_id=1, source_target_pairs={{0,16},{32,48},{64,80},{96,112},{16,0},{48,32},{80,64},{112,96},{1... | collective-permute-start | bytes 73736 | tf_op jit(solution)/shard_map/ppermute | solution.py:526
  37.1 0.1 add_bitcast_fusion.place_ref
  37.1 2.3 %shard_map.111 = (f32[9,4,64,128]{3,2,1,0:T(8,128)S(1)}, f32[384,384]{1,0:T(8,128)S(1)}, f32[9,4,64,128]{3,2,1,0:T(8,128)S(1)}) custom-call(f32[9,4,64,128]{3,2,1,0:T(8,128)S(1)} %get-tuple-element.73.v_ref, bf16[384,768]{1,0:T(8,128)(2,1)S(1)} %get-tuple-element.74.t_ref, bf16[768,384]{1,0:T(8,128)(2,1)S(1)} %get-tuple-element.57.local_ref, ...), custom_call_target="tpu_custom_call" | custom-call | flops 100000000 | bytes 6000000 | tf_op jit(solution)/shard_map/pallas_call | solution.py:535
  39.4 0.5 collective-permute-done.12.ra
  39.9 0.0 collective-permute-done.13.rb
  39.9 0.0 collective-permute-done.14.rc
  39.9 0.0 collective-permute-done.15.rd
  40.0 3.4 %shard_map.112 = (f32[9,4,64,128]{3,2,1,0:T(8,128)S(1)}, f32[9,4,8,128]{3,2,1,0:T(8,128)S(1)}, f32[16,9,8,128]{3,2,1,0:T(8,128)}) custom-call(s32[8]{0:T(128)S(1)} %select_reduce_fusion.keys_ref, f32[9,4,64,128]{3,2,1,0:T(8,128)S(1)} %get-tuple-element.76.vol_ref, f32[384,384]{1,0:T(8,128)S(1)} %get-tuple-element.77.part_ref, ...), custom_call_target="tpu_custom_call", output_to_operand_aliasing={{0}: (1, {})} | custom-call | flops 100000000 | bytes 6000000 | tf_op jit(solution)/shard_map/pallas_call | solution.py:548
  43.4 5.8 %all-to-all-start = ((f32[16,9,8,128]{3,2,1,0:T(8,128)}), f32[16,9,8,128]{3,2,1,0:T(8,128)S(1)}, u32[]{:S(2)}, u32[]{:S(2)}) async-start(f32[16,9,8,128]{3,2,1,0:T(8,128)} %get-tuple-element.85), calls=%async_computation | async-start | bytes 1179648 | tf_op jit(solution)/shard_map/all_to_all | solution.py:562
  49.2 0.1 convert_reduce_fusion.1
  49.3 3.1 %shard_map.113 = f32[9,64,512]{2,1,0:T(8,128)} custom-call(f32[9,4,64,128]{3,2,1,0:T(8,128)S(1)} %get-tuple-element.83.total_ref), custom_call_target="tpu_custom_call" | custom-call | flops 100000000 | bytes 6000000 | tf_op jit(solution)/shard_map/pallas_call | solution.py:563
  52.4 8.7 %all-to-all-done.arrived_ref = f32[16,9,8,128]{3,2,1,0:T(8,128)S(1)} async-done(((f32[16,9,8,128]{3,2,1,0:T(8,128)}), f32[16,9,8,128]{3,2,1,0:T(8,128)S(1)}, u32[]{:S(2)}, u32[]{:S(2)}) %all-to-all-start) | async-done | bytes 589856 | tf_op jit(solution)/shard_map/all_to_all | solution.py:562
  61.1 1.4 %shard_map.114 = f32[9,8,512]{2,1,0:T(8,128)} custom-call(s32[2,8]{1,0:T(2,128)S(1)} %pad_add_fusion.table_ref, f32[9,4,8,128]{3,2,1,0:T(8,128)S(1)} %get-tuple-element.84.groups_ref, f32[16,9,8,128]{3,2,1,0:T(8,128)S(1)} %all-to-all-done.arrived_ref), custom_call_target="tpu_custom_call" | custom-call | flops 100000000 | bytes 6000000 | tf_op jit(solution)/shard_map/pallas_call | solution.py:564
  (24 shorter events, 0.1 us)
Async XLA Ops:
  0.6 12.1 %copy-start.5 = (s32[3,64]{1,0:T(4,128)S(1)}, s32[3,64]{1,0:T(4,128)}, u32[]{:S(2)}) copy-start(s32[3,64]{1,0:T(4,128)} %param.13) | copy-start | bytes 2308
  0.6 12.1 %copy-start.4 = (s32[64,6]{0,1:T(8,128)S(1)}, s32[64,6]{0,1:T(8,128)}, u32[]{:S(2)}) copy-start(s32[64,6]{0,1:T(8,128)} %param.11) | copy-start | bytes 4612
  1.4 1.3 %copy-start = (f32[9,64,512]{2,1,0:T(8,128)S(1)}, f32[9,64,512]{2,1,0:T(8,128)}, u32[]{:S(2)}) copy-start(f32[9,64,512]{2,1,0:T(8,128)} %adjoint_ref.1) | copy-start | bytes 3538948
  4.1 10.8 %collective-permute-start = (f32[16,384]{1,0:T(8,128)S(1)}, f32[16,384]{1,0:T(8,128)S(1)}, u32[]{:S(2)}, u32[]{:S(2)}) collective-permute-start(f32[16,384]{1,0:T(8,128)S(1)} %get-tuple-element.49), channel_id=1, source_target_pairs={{1,2},{3,4},{5,6},{7,8},{9,10},{11,12},{13,14},{15,0},{2,1},{4,3},... | collective-permute-start | bytes 73736 | tf_op jit(solution)/shard_map/ppermute | solution.py:526
  10.8 4.2 %collective-permute-start.1 = (f32[16,384]{1,0:T(8,128)S(1)}, f32[16,384]{1,0:T(8,128)S(1)}, u32[]{:S(2)}, u32[]{:S(2)}) collective-permute-start(f32[16,384]{1,0:T(8,128)S(1)} %get-tuple-element.50), channel_id=1, source_target_pairs={{0,1},{2,3},{4,5},{6,7},{8,9},{10,11},{12,13},{14,15},{1,0},{3,2},... | collective-permute-start | bytes 73736 | tf_op jit(solution)/shard_map/ppermute | solution.py:526
  10.8 4.5 %collective-permute-start.2 = (f32[16,384]{1,0:T(8,128)S(1)}, f32[16,384]{1,0:T(8,128)S(1)}, u32[]{:S(2)}, u32[]{:S(2)}) collective-permute-start(f32[16,384]{1,0:T(8,128)S(1)} %get-tuple-element.51), channel_id=1, source_target_pairs={{16,32},{48,64},{80,96},{112,0},{32,16},{64,48},{96,80},{0,112},{1... | collective-permute-start | bytes 73736 | tf_op jit(solution)/shard_map/ppermute | solution.py:526
  12.7 2.5 %collective-permute-start.3 = (f32[16,384]{1,0:T(8,128)S(1)}, f32[16,384]{1,0:T(8,128)S(1)}, u32[]{:S(2)}, u32[]{:S(2)}) collective-permute-start(f32[16,384]{1,0:T(8,128)S(1)} %get-tuple-element.52), channel_id=1, source_target_pairs={{0,16},{32,48},{64,80},{96,112},{16,0},{48,32},{80,64},{112,96},{1... | collective-permute-start | bytes 73736 | tf_op jit(solution)/shard_map/ppermute | solution.py:526
  16.2 7.2 %collective-permute-start.4 = (f32[16,384]{1,0:T(8,128)S(1)}, f32[16,384]{1,0:T(8,128)S(1)}, u32[]{:S(2)}, u32[]{:S(2)}) collective-permute-start(f32[16,384]{1,0:T(8,128)S(1)} %get-tuple-element.60), channel_id=1, source_target_pairs={{1,2},{3,4},{5,6},{7,8},{9,10},{11,12},{13,14},{15,0},{2,1},{4,3},... | collective-permute-start | bytes 73736 | tf_op jit(solution)/shard_map/ppermute | solution.py:526
  19.0 4.5 %collective-permute-start.5 = (f32[16,384]{1,0:T(8,128)S(1)}, f32[16,384]{1,0:T(8,128)S(1)}, u32[]{:S(2)}, u32[]{:S(2)}) collective-permute-start(f32[16,384]{1,0:T(8,128)S(1)} %get-tuple-element.61), channel_id=1, source_target_pairs={{0,1},{2,3},{4,5},{6,7},{8,9},{10,11},{12,13},{14,15},{1,0},{3,2},... | collective-permute-start | bytes 73736 | tf_op jit(solution)/shard_map/ppermute | solution.py:526
  19.0 4.5 %collective-permute-start.6 = (f32[16,384]{1,0:T(8,128)S(1)}, f32[16,384]{1,0:T(8,128)S(1)}, u32[]{:S(2)}, u32[]{:S(2)}) collective-permute-start(f32[16,384]{1,0:T(8,128)S(1)} %get-tuple-element.62), channel_id=1, source_target_pairs={{16,32},{48,64},{80,96},{112,0},{32,16},{64,48},{96,80},{0,112},{1... | collective-permute-start | bytes 73736 | tf_op jit(solution)/shard_map/ppermute | solution.py:526
  19.8 3.7 %collective-permute-start.7 = (f32[16,384]{1,0:T(8,128)S(1)}, f32[16,384]{1,0:T(8,128)S(1)}, u32[]{:S(2)}, u32[]{:S(2)}) collective-permute-start(f32[16,384]{1,0:T(8,128)S(1)} %get-tuple-element.63), channel_id=1, source_target_pairs={{0,16},{32,48},{64,80},{96,112},{16,0},{48,32},{80,64},{112,96},{1... | collective-permute-start | bytes 73736 | tf_op jit(solution)/shard_map/ppermute | solution.py:526
  24.5 7.2 %collective-permute-start.10 = (f32[16,384]{1,0:T(8,128)S(1)}, f32[16,384]{1,0:T(8,128)S(1)}, u32[]{:S(2)}, u32[]{:S(2)}) collective-permute-start(f32[16,384]{1,0:T(8,128)S(1)} %get-tuple-element.71), channel_id=1, source_target_pairs={{1,2},{3,4},{5,6},{7,8},{9,10},{11,12},{13,14},{15,0},{2,1},{4,3},... | collective-permute-start | bytes 73736 | tf_op jit(solution)/shard_map/ppermute | solution.py:526
  27.2 4.5 %collective-permute-start.11 = (f32[16,384]{1,0:T(8,128)S(1)}, f32[16,384]{1,0:T(8,128)S(1)}, u32[]{:S(2)}, u32[]{:S(2)}) collective-permute-start(f32[16,384]{1,0:T(8,128)S(1)} %get-tuple-element.72), channel_id=1, source_target_pairs={{0,1},{2,3},{4,5},{6,7},{8,9},{10,11},{12,13},{14,15},{1,0},{3,2},... | collective-permute-start | bytes 73736 | tf_op jit(solution)/shard_map/ppermute | solution.py:526
  27.2 4.5 %collective-permute-start.8 = (f32[16,384]{1,0:T(8,128)S(1)}, f32[16,384]{1,0:T(8,128)S(1)}, u32[]{:S(2)}, u32[]{:S(2)}) collective-permute-start(f32[16,384]{1,0:T(8,128)S(1)} %get-tuple-element.69), channel_id=1, source_target_pairs={{16,32},{48,64},{80,96},{112,0},{32,16},{64,48},{96,80},{0,112},{1... | collective-permute-start | bytes 73736 | tf_op jit(solution)/shard_map/ppermute | solution.py:526
  28.8 2.9 %collective-permute-start.9 = (f32[16,384]{1,0:T(8,128)S(1)}, f32[16,384]{1,0:T(8,128)S(1)}, u32[]{:S(2)}, u32[]{:S(2)}) collective-permute-start(f32[16,384]{1,0:T(8,128)S(1)} %get-tuple-element.70), channel_id=1, source_target_pairs={{0,16},{32,48},{64,80},{96,112},{16,0},{48,32},{80,64},{112,96},{1... | collective-permute-start | bytes 73736 | tf_op jit(solution)/shard_map/ppermute | solution.py:526
  32.7 7.2 %collective-permute-start.12 = (f32[16,384]{1,0:T(8,128)S(1)}, f32[16,384]{1,0:T(8,128)S(1)}, u32[]{:S(2)}, u32[]{:S(2)}) collective-permute-start(f32[16,384]{1,0:T(8,128)S(1)} %get-tuple-element.78), channel_id=1, source_target_pairs={{1,2},{3,4},{5,6},{7,8},{9,10},{11,12},{13,14},{15,0},{2,1},{4,3},... | collective-permute-start | bytes 73736 | tf_op jit(solution)/shard_map/ppermute | solution.py:526
  35.5 4.5 %collective-permute-start.13 = (f32[16,384]{1,0:T(8,128)S(1)}, f32[16,384]{1,0:T(8,128)S(1)}, u32[]{:S(2)}, u32[]{:S(2)}) collective-permute-start(f32[16,384]{1,0:T(8,128)S(1)} %get-tuple-element.79), channel_id=1, source_target_pairs={{0,1},{2,3},{4,5},{6,7},{8,9},{10,11},{12,13},{14,15},{1,0},{3,2},... | collective-permute-start | bytes 73736 | tf_op jit(solution)/shard_map/ppermute | solution.py:526
  35.5 4.5 %collective-permute-start.14 = (f32[16,384]{1,0:T(8,128)S(1)}, f32[16,384]{1,0:T(8,128)S(1)}, u32[]{:S(2)}, u32[]{:S(2)}) collective-permute-start(f32[16,384]{1,0:T(8,128)S(1)} %get-tuple-element.80), channel_id=1, source_target_pairs={{16,32},{48,64},{80,96},{112,0},{32,16},{64,48},{96,80},{0,112},{1... | collective-permute-start | bytes 73736 | tf_op jit(solution)/shard_map/ppermute | solution.py:526
  36.1 3.8 %collective-permute-start.15 = (f32[16,384]{1,0:T(8,128)S(1)}, f32[16,384]{1,0:T(8,128)S(1)}, u32[]{:S(2)}, u32[]{:S(2)}) collective-permute-start(f32[16,384]{1,0:T(8,128)S(1)} %get-tuple-element.81), channel_id=1, source_target_pairs={{0,16},{32,48},{64,80},{96,112},{16,0},{48,32},{80,64},{112,96},{1... | collective-permute-start | bytes 73736 | tf_op jit(solution)/shard_map/ppermute | solution.py:526
  37.1 2.8 %copy-start.1 = (f32[64,8,128]{2,1,0:T(8,128)S(1)}, f32[64,8,128]{2,1,0:T(8,128)}, u32[]{:S(2)}) copy-start(f32[64,8,128]{2,1,0:T(8,128)} %constant.24.clone.lines_ref) | copy-start | bytes 786436
  37.1 2.8 %copy-start.2 = (bf16[256,128]{1,0:T(8,128)(2,1)S(1)}, bf16[256,128]{1,0:T(8,128)(2,1)}, u32[]{:S(2)}) copy-start(bf16[256,128]{1,0:T(8,128)(2,1)} %constant.22.clone.wa_ref) | copy-start | bytes 196612
  37.1 2.8 %copy-start.3 = (bf16[256,128]{1,0:T(8,128)(2,1)S(1)}, bf16[256,128]{1,0:T(8,128)(2,1)}, u32[]{:S(2)}) copy-start(bf16[256,128]{1,0:T(8,128)(2,1)} %constant.23.clone.wb_ref) | copy-start | bytes 196612
  43.4 5.9 %copy-start.6 = (s32[2,8]{1,0:T(2,128)S(1)}, s32[2,8]{1,0:T(2,128)}, u32[]{:S(2)}) copy-start(s32[2,8]{1,0:T(2,128)} %param.14) | copy-start | bytes 196
  43.4 17.7 %all-to-all-start = ((f32[16,9,8,128]{3,2,1,0:T(8,128)}), f32[16,9,8,128]{3,2,1,0:T(8,128)S(1)}, u32[]{:S(2)}, u32[]{:S(2)}) async-start(f32[16,9,8,128]{3,2,1,0:T(8,128)} %get-tuple-element.85), calls=%async_computation | async-start | bytes 1179648 | tf_op jit(solution)/shard_map/all_to_all | solution.py:562

commit v5 on v4

--- a/solution.py
+++ b/solution.py
@@ -151,17 +151,20 @@
     return value if value < 3 else voigt_index[value - 3][direction]
 
 
-def build_table(v_ref, mat, t_ref):
+def build_table(v_ref, mat, t_ref, directions):
     low = low_half()
 
     def put(value, block, direction, x0, x1):
         pair = jnp.concatenate([x0, x1], axis=0)
         high, rest = split(pair)
         rows = pl.ds(value * 64 + block * 16, 16)
-        t_ref[rows, pl.ds(direction * 128, 128)] = high
-        t_ref[rows, pl.ds(LOCAL + direction * 128, 128)] = rest
-
-    for direction in range(2):
+        column = 256 * directions.index(direction)
+        t_ref[rows, pl.ds(column, 128)] = high
+        t_ref[rows, pl.ds(column + 128, 128)] = rest
+
+    for direction in directions:
+        if direction == 2:
+            continue
         for j in range(4):
             if direction == 0:
                 ends = [image_rows(lambda i, r=r: v_ref[i, j, pl.ds(r, 8), :], mat, 0) for r in (0, 56)]
@@ -176,7 +179,7 @@
                     jnp.where(low, a0, swap_halves(a1)),
                     jnp.where(low, swap_halves(a0), a1),
                 )
-    for pair in range(4):
+    for pair in range(4 if 2 in directions else 0):
         blocks = []
         for b in (2 * pair, 2 * pair + 1):
             blocks.append(
@@ -198,9 +201,9 @@
 
 def send_values(send_ref, t_ref, out_refs):
     rows = lax.dot_general(
-        send_ref[...], t_ref[...], (((1,), (1,)), ((), ())), preferred_element_type=F32
+        send_ref[...], t_ref[:, pl.ds(0, 256)], (((1,), (1,)), ((), ())), preferred_element_type=F32
     )
-    for k in range(4):
+    for k in range(2):
         out_refs[k][...] = rows[16 * k : 16 * k + 16]
 
 
@@ -213,7 +216,7 @@
     return (q - 6 * element) * E_DEV + element
 
 
-def partner_tables(faces_ref, local_ref, remote_ref):
+def partner_tables(faces_ref, local_y_ref, local_ref, remote_ref):
     even_x, even_y = parities()
     low_row = lax.broadcasted_iota(jnp.int32, (1, 128), 1) < 64
     weight = jnp.where(low_row, lift_half, -lift_half)
@@ -231,14 +234,14 @@
         for start in range(0, LOCAL + 64, 64):
             source = lax.broadcasted_iota(jnp.int32, (64, 128), 0) + start
             hot = jnp.where(source == partner, weight, 0.0).astype(BF)
+            target = (local_ref, local_y_ref, local_ref, remote_ref)[start // 128]
+            base = start % 128 + (256 if start // 128 == 2 else 0)
+            gap = 64 if start == LOCAL else 128
             for part in range(2):
-                if start < LOCAL:
-                    local_ref[pl.ds(part * LOCAL + start, 64), lanes] = hot
-                else:
-                    remote_ref[pl.ds(part * 64, 64), lanes] = hot
-
-
-def send_table(pack_ref, send_ref, small_ref):
+                target[pl.ds(base + part * gap, 64), lanes] = hot
+
+
+def send_table(pack_ref, send_x_ref, send_y_ref, small_ref):
     even_x, even_y = parities()
     small_ref[pl.ds(0, 8), :] = pack_ref[0]
     small_ref[pl.ds(8, 120), :] = jnp.zeros((120, 128), F32)
@@ -248,15 +251,15 @@
         first, second = columns[2 * axis], columns[2 * axis + 1]
         for k, column in enumerate((first + even * (second - first), second + even * (first - second))):
             hot = jnp.where(
-                lax.broadcasted_iota(jnp.int32, (CAP, LOCAL), 1) == column, 1.0, 0.0
+                lax.broadcasted_iota(jnp.int32, (CAP, 128), 1) + 128 * axis == column, 1.0, 0.0
             ).astype(BF)
-            rows = pl.ds((2 * axis + k) * CAP, CAP)
-            send_ref[rows, pl.ds(0, LOCAL)] = hot
-            send_ref[rows, pl.ds(LOCAL, LOCAL)] = hot
+            for part in range(2):
+                (send_x_ref, send_y_ref)[axis][pl.ds(k * CAP, CAP), pl.ds(128 * part, 128)] = hot
 
 
 def begin_kernel(
-    pack_ref, adjoint_ref, v_ref, t_ref, mat_ref, send_ref, p0, p1, p2, p3, turn_ref, small_ref
+    pack_ref, adjoint_ref,
+    v_ref, ty_ref, t_ref, mat_ref, send_x_ref, send_y_ref, p0, p1, p2, p3, turn_ref, small_ref,
 ):
     low_row = lax.broadcasted_iota(jnp.int32, (1, 128), 1) < 64
     for i in range(3):
@@ -265,7 +268,7 @@
         if i == 0:
             row = 1.0 / row
         mat_ref[i] = jnp.broadcast_to(row, (8, 128))
-    send_table(pack_ref, send_ref, small_ref)
+    send_table(pack_ref, send_x_ref, send_y_ref, small_ref)
     low = lax.broadcasted_iota(jnp.int32, (64, 128), 1) < 64
     for i in range(9):
         x = adjoint_ref[i]
@@ -275,16 +278,26 @@
             v_ref[i, j] = jnp.where(
                 low, turn[pl.ds(2 * j, 64, stride=8), :], turn[pl.ds(2 * j + 1, 64, stride=8), :]
             )
-    build_table(v_ref, materials(mat_ref), t_ref)
-    send_values(send_ref, t_ref, (p0, p1, p2, p3))
-
-
-def first_volume_kernel(factor, faces_ref, v_ref, t_ref, mat_ref, vol_ref, part_ref, local_ref, remote_ref):
-    partner_tables(faces_ref, local_ref, remote_ref)
-    volume_kernel(factor, v_ref, t_ref, local_ref, mat_ref, None, vol_ref, part_ref, None)
-
-
-def volume_kernel(factor, v_ref, t_ref, local_ref, mat_ref, acc_ref, vol_ref, part_ref, sum_ref):
+    build_table(v_ref, materials(mat_ref), ty_ref, (1,))
+    send_values(send_y_ref, ty_ref, (p2, p3))
+    build_table(v_ref, materials(mat_ref), t_ref, (0, 2))
+    send_values(send_x_ref, t_ref, (p0, p1))
+
+
+def first_volume_kernel(
+    factor, faces_ref, v_ref, ty_ref, t_ref, mat_ref, vol_ref, part_ref, local_y_ref, local_ref, remote_ref
+):
+    partner_tables(faces_ref, local_y_ref, local_ref, remote_ref)
+    volume_kernel(factor, v_ref, ty_ref, t_ref, local_y_ref, local_ref, mat_ref, None, vol_ref, part_ref, None)
+
+
+def last_volume_kernel(factor, v_ref, ty_ref, t_ref, local_y_ref, local_ref, mat_ref, acc_ref, vol_ref, part_ref):
+    volume_kernel(factor, v_ref, ty_ref, t_ref, local_y_ref, local_ref, mat_ref, acc_ref, vol_ref, part_ref, None)
+
+
+def volume_kernel(
+    factor, v_ref, ty_ref, t_ref, local_y_ref, local_ref, mat_ref, acc_ref, vol_ref, part_ref, sum_ref
+):
     inv_density, lame, shear = [m * factor for m in materials(mat_ref)]
 
     def scaled(get, direction):
@@ -305,7 +318,10 @@
             for b, y in enumerate(line_product(x)):
                 vol_ref[row, j, along(b), :] = y
         chunk = pl.ds(j * 96, 96)
-        part_ref[chunk, :] = jnp.dot(t_ref[chunk, :], local_ref[...], preferred_element_type=F32) * factor
+        part_ref[chunk, :] = factor * (
+            jnp.dot(ty_ref[chunk, :], local_y_ref[...], preferred_element_type=F32)
+            + jnp.dot(t_ref[chunk, :], local_ref[...], preferred_element_type=F32)
+        )
         for row, x in scaled(lambda i: [v_ref[i, j, pl.ds(8 * a, 8), :] for a in range(8)], 0):
             for a, y in enumerate(line_product(x)):
                 if row not in (3, 7):
@@ -323,10 +339,14 @@
                 if row != 5:
                     y = y + vol_ref[row, j, rows, :]
                 vol_ref[row, j, rows, :] = y
-        if sum_ref is not None:
+        if acc_ref is not None:
             for i in range(9):
                 for j in range(4):
-                    sum_ref[i, j, rows, :] = acc_ref[i, j, rows, :] + v_ref[i, j, rows, :]
+                    y = acc_ref[i, j, rows, :] + v_ref[i, j, rows, :]
+                    if sum_ref is not None:
+                        sum_ref[i, j, rows, :] = y
+                    else:
+                        vol_ref[i, j, rows, :] += y
         return carry
 
     lax.fori_loop(0, 8, groups, 0, unroll=4)
@@ -358,12 +378,14 @@
 
 
 def finish_kernel(
-    factor, order, vol_ref, part_ref, ra, rb, rc, rd, remote_ref, mat_ref, send_ref,
-    v_ref, t_ref, p0, p1, p2, p3, face_ref,
+    factor, order, vol_ref, part_ref, ra, rb, rc, rd, remote_ref, mat_ref, send_x_ref, send_y_ref,
+    v_ref, ty_ref, t_ref, p0, p1, p2, p3, face_ref,
 ):
     add_faces(part_ref, in_order(order, (ra, rb, rc, rd)), remote_ref, factor, v_ref, face_ref)
-    build_table(v_ref, materials(mat_ref), t_ref)
-    send_values(send_ref, t_ref, (p0, p1, p2, p3))
+    build_table(v_ref, materials(mat_ref), ty_ref, (1,))
+    send_values(send_y_ref, ty_ref, (p2, p3))
+    build_table(v_ref, materials(mat_ref), t_ref, (0, 2))
+    send_values(send_x_ref, t_ref, (p0, p1))
 
 
 def in_order(order, refs):
@@ -371,7 +393,7 @@
 
 
 def end_kernel(
-    factor, order, keys_ref, vol_ref, part_ref, ra, rb, rc, rd, remote_ref, acc_ref, place_ref, wa_ref, wb_ref, lines_ref,
+    factor, order, keys_ref, vol_ref, part_ref, ra, rb, rc, rd, remote_ref, place_ref, wa_ref, wb_ref, lines_ref,
     total_ref, parent_ref, away_ref, face_ref, turn_ref, ranked_ref, rows_ref, plane_ref,
 ):
     add_faces(part_ref, in_order(order, (ra, rb, rc, rd)), remote_ref, factor, total_ref, face_ref)
@@ -382,8 +404,7 @@
     low = low_half()
     for i in range(9):
         for j in range(4):
-            tile = acc_ref[i, j] + total_ref[i, j]
-            total_ref[i, j] = tile
+            tile = total_ref[i, j]
             high = tile.astype(BF).astype(F32)
             rest = tile - high
             turn_ref[i, pl.ds(2 * j, 64, stride=8), :] = jnp.where(wide, high, pltpu.roll(rest, 64, 1))
@@ -500,7 +521,9 @@
     source = jnp.stack([jnp.where(stays, group, children[0]), jnp.where(stays, -1, children[1])])
 
     state = shape(9, 4, 64, 128)
-    table = shape(LOCAL, 2 * LOCAL, dtype=BF)
+    table_y = shape(LOCAL, 256, dtype=BF)
+    table = shape(LOCAL, 512, dtype=BF)
+    sent = shape(32, 256, dtype=BF)
     face_part = shape(LOCAL, LOCAL)
     payload = [shape(CAP, LOCAL)] * 4
     face_scratch = pltpu.VMEM((LOCAL, LOCAL), F32)
@@ -513,37 +536,47 @@
     faces = jnp.pad(face_partner.T.astype(F32), ((0, 2), (0, 64)))
     outs = call(
         begin_kernel,
-        [state, table, shape(3, 8, 128), shape(64, 2 * LOCAL, dtype=BF)] + payload,
+        [state, table_y, table, shape(3, 8, 128), sent, sent] + payload,
         [pltpu.VMEM((3, NODES, 128), F32), pltpu.VMEM((128, 128), F32)],
         count=2,
     )(pack, adjoint)
-    v, t, mat, send_hot = outs[:4]
-    out_going = outs[4:]
+    v, ty, t, mat, send_x, send_y = outs[:6]
+    out_going = outs[6:]
     pairs = exchange_pairs()
     for step in range(1, 5):
         factor = time_step / step
         order = (1, 0, 3, 2) if step == 3 else (3, 2, 1, 0)
         arrived = [lax.ppermute(out_going[k], *pairs[k]) for k in order]
         if step == 1:
-            vol, part, local_hot, remote_hot = call(
+            vol, part, local_y, local, remote_hot = call(
                 functools.partial(first_volume_kernel, factor),
-                [state, face_part, shape(2 * LOCAL, LOCAL, dtype=BF), shape(128, LOCAL, dtype=BF)],
-                count=4,
-            )(faces, v, t, mat)
+                [
+                    state,
+                    face_part,
+                    shape(256, LOCAL, dtype=BF),
+                    shape(512, LOCAL, dtype=BF),
+                    shape(128, LOCAL, dtype=BF),
+                ],
+                count=5,
+            )(faces, v, ty, t, mat)
             acc = v
+        elif step < 4:
+            vol, part, acc = call(
+                functools.partial(volume_kernel, factor), [state, face_part, state], count=7
+            )(v, ty, t, local_y, local, mat, acc)
         else:
-            vol, part, acc = call(
-                functools.partial(volume_kernel, factor), [state, face_part, state], count=5
-            )(v, t, local_hot, mat, acc)
+            vol, part = call(functools.partial(last_volume_kernel, factor), [state, face_part], count=7)(
+                v, ty, t, local_y, local, mat, acc
+            )
         if step < 4:
             outs = call(
                 functools.partial(finish_kernel, factor, order),
-                [state, table] + payload,
+                [state, table_y, table] + payload,
                 [face_scratch],
                 aliases={0: 0},
-                count=9,
-            )(vol, part, *arrived, remote_hot, mat, send_hot)
-            v, t, out_going = outs[0], outs[1], outs[2:]
+                count=10,
+            )(vol, part, *arrived, remote_hot, mat, send_x, send_y)
+            v, ty, t, out_going = outs[0], outs[1], outs[2], outs[3:]
     wa, wb, lines = (jnp.asarray(x) for x in refine_parts())
     total, groups, away = call(
         functools.partial(end_kernel, factor, order),
@@ -557,8 +590,8 @@
         ],
         smem=(0,),
         aliases={1: 0},
-        count=13,
-    )(keys, vol, part, *arrived, remote_hot, acc, place, wa, wb, lines)
+        count=12,
+    )(keys, vol, part, *arrived, remote_hot, place, wa, wb, lines)
     fetched = lax.all_to_all(away, "seg", split_axis=0, concat_axis=0, tiled=True)
     updated = call(next_kernel, [shape(9, E_DEV, NODES)], [turn], count=1)(total)[0]
     parents = call(parent_kernel, [shape(9, P_DEV, NODES)], smem=(0,), count=3)(source, groups, fetched)[0]

time: 62.8 us -> 62 us (0.987)
  Pallas kernels: 21.3 us -> 20.5 us
    pallas_call x3 -> x2, Pallas kernels: 6.78 us -> 4.5 us  [shards(): call(functools.partial(volume_kernel, factor), [state, face_part, state],...]
    pallas_call x4 -> x5, Pallas kernels: 4.48 us -> 6.15 us  [the longest x3 2.61 us: shards(): call(functools.partial(finish_kernel, factor, order), [state, table_y, ta...]
where the time goes in v5:
time: 62 us; the launch traced here: 61.8 us
  starting transfers between devices  27.5 us (44%)
  Pallas kernels  20.5 us (33%)
  waiting for transfers between devices  10.6 us (17%)
  local copies, waits for them, and re-layouts  1.3 us (2%)
  other arithmetic  1.14 us (2%)
  between operations  0.8 us (1%)
    ppermute x16, starting transfers between devices, shards(): arrived = [lax.ppermute(out_going[k], *pairs[k]) for k in order]  21.7 us
    all_to_all x1, waiting for transfers between devices, shards(): lax.all_to_all(away, 'seg', split_axis=0, concat_axis=0, tiled=True)  8.44 us
    all_to_all x1, starting transfers between devices, shards(): lax.all_to_all(away, 'seg', split_axis=0, concat_axis=0, tiled=True)  5.78 us
    pallas_call x2, Pallas kernels, shards(): call(functools.partial(volume_kernel, factor), [state, face_part, state],...  4.5 us
    pallas_call x1, Pallas kernels, shards(): call(functools.partial(end_kernel, factor, order), [state, shape(9, 4, P_...  3.27 us
    pallas_call x1, Pallas kernels, shards(): call(next_kernel, [shape(9, E_DEV, NODES)], [turn], count=1)(total)[0]  3.1 us
    pallas_call x3, Pallas kernels, shards(): call(functools.partial(finish_kernel, factor, order), [state, table_y, ta...  2.61 us
    ppermute x16, waiting for transfers between devices, shards(): arrived = [lax.ppermute(out_going[k], *pairs[k]) for k in order]  2.11 us
  transfers between devices with their start and end apart: 17, of which 5 were waited for; matrix products, arithmetic and copies ran while one was open for 1% of the time, Pallas kernels for 19%

profile of v5, /device:TPU:0, one launch (start us, length us, event | category | flops | bytes accessed | tf_op | source)
XLA Modules:
  0.0 61.8 jit_solution(16855468258359890928)
XLA Ops:
  0.7 0.7 %convert_add_fusion.pack_ref = f32[1,8,128]{2,1,0:T(8,128)S(1)} fusion(s32[1,4,16]{2,1,0:T(4,128)} %param.12, f32[1,3,64]{2,1,0:T(4,128)} %bitcast.19), kind=kLoop, calls=%fused_computation.3 | loop fusion | flops 2048 | bytes 5120 | tf_op jit(solution)/shard_map/add | solution.py:533
  1.4 1.3 %copy-done = f32[9,64,512]{2,1,0:T(8,128)S(1)} copy-done((f32[9,64,512]{2,1,0:T(8,128)S(1)}, f32[9,64,512]{2,1,0:T(8,128)}, u32[]{:S(2)}) %copy-start) | copy-done | bytes 1179672
  2.6 1.5 %shard_map.104 = (f32[9,4,64,128]{3,2,1,0:T(8,128)S(1)}, bf16[384,256]{1,0:T(8,128)(2,1)S(1)}, bf16[384,512]{1,0:T(8,128)(2,1)S(1)}, f32[3,8,128]{2,1,0:T(8,128)...) custom-call(f32[1,8,128]{2,1,0:T(8,128)S(1)} %convert_add_fusion.pac, ...), custom_call_target="tpu_custom_call" | custom-call | flops 100000000 | bytes 6000000 | tf_op jit(solution)/shard_map/pallas_call | solution.py:537
  4.2 6.6 %collective-permute-start = (f32[16,384]{1,0:T(8,128)S(1)}, f32[16,384]{1,0:T(8,128)S(1)}, u32[]{:S(2)}, u32[]{:S(2)}) collective-permute-start(f32[16,384]{1,0:T(8,128)S(1)} %get-tuple-element.55), channel_id=1, source_target_pairs={{1,2},{3,4},{5,6},{7,8},{9,10},{11,12},{13,14},{15,0},{2,1},{4,3},... | collective-permute-start | bytes 73736 | tf_op jit(solution)/shard_map/ppermute | solution.py:549
  10.8 0.0 collective-permute-start.1
  10.8 1.9 %collective-permute-start.2 = (f32[16,384]{1,0:T(8,128)S(1)}, f32[16,384]{1,0:T(8,128)S(1)}, u32[]{:S(2)}, u32[]{:S(2)}) collective-permute-start(f32[16,384]{1,0:T(8,128)S(1)} %get-tuple-element.57), channel_id=1, source_target_pairs={{16,32},{48,64},{80,96},{112,0},{32,16},{64,48},{96,80},{0,112},{1... | collective-permute-start | bytes 73736 | tf_op jit(solution)/shard_map/ppermute | solution.py:549
  12.7 0.0 collective-permute-start.3
  12.8 0.1 convert_reduce_fusion
  12.9 2.1 %shard_map.105 = (f32[9,4,64,128]{3,2,1,0:T(8,128)S(1)}, f32[384,384]{1,0:T(8,128)S(1)}, bf16[256,384]{1,0:T(8,128)(2,1)S(1)}, bf16[512,384]{1,0:T(8,128)(2,1)S(1)}, bf16[128,384]{1,0:T(8,128)(2,1)S(1)}) custom-call(f32[8,128]{1,0:T(8,128)S(1)} %pad.10.faces_ref, f32[9,4,64,128]{3,2,1,0:T(8,128)S(1)} %get-tuple-element.49.v_ref.acc_ref, ...), custom_call_target="tpu_custom_call" | custom-call | flops 100000000 | bytes 6000000 | tf_op jit(solution)/shard_map/pallas_call | solution.py:551
  15.0 0.0 collective-permute-done.ra
  15.0 0.0 collective-permute-done.1.rb
  15.0 0.3 collective-permute-done.2.rc
  15.3 0.0 collective-permute-done.3.rd
  15.3 0.9 %shard_map.106 = (f32[9,4,64,128]{3,2,1,0:T(8,128)S(1)}, bf16[384,256]{1,0:T(8,128)(2,1)S(1)}, bf16[384,512]{1,0:T(8,128)(2,1)S(1)}, f32[16,384]{1,0:T(8,128)S(1...) custom-call(f32[9,4,64,128]{3,2,1,0:T(8,128)S(1)} %get-tuple-element, ...), custom_call_target="tpu_custom_call", output_to_operand_aliasing={{0}: (0, {})} | custom-call | flops 100000000 | bytes 6000000 | tf_op jit(solution)/shard_map/pallas_call | solution.py:572
  16.2 2.8 %collective-permute-start.4 = (f32[16,384]{1,0:T(8,128)S(1)}, f32[16,384]{1,0:T(8,128)S(1)}, u32[]{:S(2)}, u32[]{:S(2)}) collective-permute-start(f32[16,384]{1,0:T(8,128)S(1)} %get-tuple-element.69), channel_id=1, source_target_pairs={{1,2},{3,4},{5,6},{7,8},{9,10},{11,12},{13,14},{15,0},{2,1},{4,3},... | collective-permute-start | bytes 73736 | tf_op jit(solution)/shard_map/ppermute | solution.py:549
  18.9 0.0 collective-permute-start.5
  18.9 0.8 %collective-permute-start.6 = (f32[16,384]{1,0:T(8,128)S(1)}, f32[16,384]{1,0:T(8,128)S(1)}, u32[]{:S(2)}, u32[]{:S(2)}) collective-permute-start(f32[16,384]{1,0:T(8,128)S(1)} %get-tuple-element.71), channel_id=1, source_target_pairs={{16,32},{48,64},{80,96},{112,0},{32,16},{64,48},{96,80},{0,112},{1... | collective-permute-start | bytes 73736 | tf_op jit(solution)/shard_map/ppermute | solution.py:549
  19.7 0.8 %collective-permute-start.7 = (f32[16,384]{1,0:T(8,128)S(1)}, f32[16,384]{1,0:T(8,128)S(1)}, u32[]{:S(2)}, u32[]{:S(2)}) collective-permute-start(f32[16,384]{1,0:T(8,128)S(1)} %get-tuple-element.72), channel_id=1, source_target_pairs={{0,16},{32,48},{64,80},{96,112},{16,0},{48,32},{80,64},{112,96},{1... | collective-permute-start | bytes 73736 | tf_op jit(solution)/shard_map/ppermute | solution.py:549
  20.5 2.2 %shard_map.107 = (f32[9,4,64,128]{3,2,1,0:T(8,128)S(1)}, f32[384,384]{1,0:T(8,128)S(1)}, f32[9,4,64,128]{3,2,1,0:T(8,128)S(1)}) custom-call(f32[9,4,64,128]{3,2,1,0:T(8,128)S(1)} %get-tuple-element.62.v_ref, bf16[384,256]{1,0:T(8,128)(2,1)S(1)} %get-tuple-element.63.ty_ref, bf16[384,512]{1,0:T(8,128)(2,1)S(1)} %get-tuple-element.64.t_ref, ...), custom_call_target="tpu_custom_call" | custom-call | flops 100000000 | bytes 6000000 | tf_op jit(solution)/shard_map/pallas_call | solution.py:564
  22.8 0.6 %collective-permute-done.4.ra = f32[16,384]{1,0:T(8,128)S(1)} collective-permute-done((f32[16,384]{1,0:T(8,128)S(1)}, f32[16,384]{1,0:T(8,128)S(1)}, u32[]{:S(2)}, u32[]{:S(2)}) %collective-permute-start.4) | collective-permute-done | bytes 24608 | tf_op jit(solution)/shard_map/ppermute | solution.py:549
  23.4 0.0 collective-permute-done.5.rb
  23.4 0.0 collective-permute-done.6.rc
  23.4 0.9 %shard_map.108 = (f32[9,4,64,128]{3,2,1,0:T(8,128)S(1)}, bf16[384,256]{1,0:T(8,128)(2,1)S(1)}, bf16[384,512]{1,0:T(8,128)(2,1)S(1)}, f32[16,384]{1,0:T(8,128)S(1...) custom-call(f32[9,4,64,128]{3,2,1,0:T(8,128)S(1)} %get-tuple-element, ...), custom_call_target="tpu_custom_call", output_to_operand_aliasing={{0}: (0, {})} | custom-call | flops 100000000 | bytes 6000000 | tf_op jit(solution)/shard_map/pallas_call | solution.py:572
  24.3 2.8 %collective-permute-start.10 = (f32[16,384]{1,0:T(8,128)S(1)}, f32[16,384]{1,0:T(8,128)S(1)}, u32[]{:S(2)}, u32[]{:S(2)}) collective-permute-start(f32[16,384]{1,0:T(8,128)S(1)} %get-tuple-element.81), channel_id=1, source_target_pairs={{1,2},{3,4},{5,6},{7,8},{9,10},{11,12},{13,14},{15,0},{2,1},{4,3},... | collective-permute-start | bytes 73736 | tf_op jit(solution)/shard_map/ppermute | solution.py:549
  27.0 0.0 collective-permute-start.11
  27.0 1.6 %collective-permute-start.8 = (f32[16,384]{1,0:T(8,128)S(1)}, f32[16,384]{1,0:T(8,128)S(1)}, u32[]{:S(2)}, u32[]{:S(2)}) collective-permute-start(f32[16,384]{1,0:T(8,128)S(1)} %get-tuple-element.79), channel_id=1, source_target_pairs={{16,32},{48,64},{80,96},{112,0},{32,16},{64,48},{96,80},{0,112},{1... | collective-permute-start | bytes 73736 | tf_op jit(solution)/shard_map/ppermute | solution.py:549
  28.6 0.0 collective-permute-start.9
  28.6 0.1 select_reduce_fusion.keys_ref
  28.8 2.3 %shard_map.109 = (f32[9,4,64,128]{3,2,1,0:T(8,128)S(1)}, f32[384,384]{1,0:T(8,128)S(1)}, f32[9,4,64,128]{3,2,1,0:T(8,128)S(1)}) custom-call(f32[9,4,64,128]{3,2,1,0:T(8,128)S(1)} %get-tuple-element.73.v_ref, bf16[384,256]{1,0:T(8,128)(2,1)S(1)} %get-tuple-element.74.ty_ref, bf16[384,512]{1,0:T(8,128)(2,1)S(1)} %get-tuple-element.75.t_ref, ...), custom_call_target="tpu_custom_call" | custom-call | flops 100000000 | bytes 6000000 | tf_op jit(solution)/shard_map/pallas_call | solution.py:564
  31.1 0.4 collective-permute-done.10.rc
  31.5 0.0 collective-permute-done.8.ra
  31.5 0.0 collective-permute-done.9.rb
  31.5 0.9 %shard_map.110 = (f32[9,4,64,128]{3,2,1,0:T(8,128)S(1)}, bf16[384,256]{1,0:T(8,128)(2,1)S(1)}, bf16[384,512]{1,0:T(8,128)(2,1)S(1)}, f32[16,384]{1,0:T(8,128)S(1...) custom-call(f32[9,4,64,128]{3,2,1,0:T(8,128)S(1)} %get-tuple-element, ...), custom_call_target="tpu_custom_call", output_to_operand_aliasing={{0}: (0, {})} | custom-call | flops 100000000 | bytes 6000000 | tf_op jit(solution)/shard_map/pallas_call | solution.py:572
  32.4 2.8 %collective-permute-start.12 = (f32[16,384]{1,0:T(8,128)S(1)}, f32[16,384]{1,0:T(8,128)S(1)}, u32[]{:S(2)}, u32[]{:S(2)}) collective-permute-start(f32[16,384]{1,0:T(8,128)S(1)} %get-tuple-element.89), channel_id=1, source_target_pairs={{1,2},{3,4},{5,6},{7,8},{9,10},{11,12},{13,14},{15,0},{2,1},{4,3},... | collective-permute-start | bytes 73736 | tf_op jit(solution)/shard_map/ppermute | solution.py:549
  35.1 0.0 collective-permute-start.13
  35.1 0.6 %collective-permute-start.14 = (f32[16,384]{1,0:T(8,128)S(1)}, f32[16,384]{1,0:T(8,128)S(1)}, u32[]{:S(2)}, u32[]{:S(2)}) collective-permute-start(f32[16,384]{1,0:T(8,128)S(1)} %get-tuple-element.91), channel_id=1, source_target_pairs={{16,32},{48,64},{80,96},{112,0},{32,16},{64,48},{96,80},{0,112},{1... | collective-permute-start | bytes 73736 | tf_op jit(solution)/shard_map/ppermute | solution.py:549
  35.8 1.0 %collective-permute-start.15 = (f32[16,384]{1,0:T(8,128)S(1)}, f32[16,384]{1,0:T(8,128)S(1)}, u32[]{:S(2)}, u32[]{:S(2)}) collective-permute-start(f32[16,384]{1,0:T(8,128)S(1)} %get-tuple-element.92), channel_id=1, source_target_pairs={{0,16},{32,48},{64,80},{96,112},{16,0},{48,32},{80,64},{112,96},{1... | collective-permute-start | bytes 73736 | tf_op jit(solution)/shard_map/ppermute | solution.py:549
  36.7 0.1 add_bitcast_fusion.place_ref
  36.8 2.0 %shard_map.111 = (f32[9,4,64,128]{3,2,1,0:T(8,128)S(1)}, f32[384,384]{1,0:T(8,128)S(1)}) custom-call(f32[9,4,64,128]{3,2,1,0:T(8,128)S(1)} %get-tuple-element.83.v_ref, bf16[384,256]{1,0:T(8,128)(2,1)S(1)} %get-tuple-element.84.ty_ref, bf16[384,512]{1,0:T(8,128)(2,1)S(1)} %get-tuple-element.85.t_ref, bf16[256,384]{1,0:T(8,128)(2,1)S(1)} %get-tuple-element.65.local_y_ref, ...), custom_call_target="tpu_custom_call" | custom-call | flops 100000000 | bytes 6000000 | tf_op jit(solution)/shard_map/pallas_call | solution.py:568
  38.8 0.8 %collective-permute-done.12.ra = f32[16,384]{1,0:T(8,128)S(1)} collective-permute-done((f32[16,384]{1,0:T(8,128)S(1)}, f32[16,384]{1,0:T(8,128)S(1)}, u32[]{:S(2)}, u32[]{:S(2)}) %collective-permute-start.12) | collective-permute-done | bytes 24608 | tf_op jit(solution)/shard_map/ppermute | solution.py:549
  39.6 0.0 collective-permute-done.13.rb
  39.6 0.0 collective-permute-done.14.rc
  39.6 3.3 %shard_map.112 = (f32[9,4,64,128]{3,2,1,0:T(8,128)S(1)}, f32[9,4,8,128]{3,2,1,0:T(8,128)S(1)}, f32[16,9,8,128]{3,2,1,0:T(8,128)}) custom-call(s32[8]{0:T(128)S(1)} %select_reduce_fusion.keys_ref, f32[9,4,64,128]{3,2,1,0:T(8,128)S(1)} %get-tuple-element.87.vol_ref, f32[384,384]{1,0:T(8,128)S(1)} %get-tuple-element.88.part_ref, ...), custom_call_target="tpu_custom_call", output_to_operand_aliasing={{0}: (1, {})} | custom-call | flops 100000000 | bytes 6000000 | tf_op jit(solution)/shard_map/pallas_call | solution.py:581
  42.9 5.8 %all-to-all-start = ((f32[16,9,8,128]{3,2,1,0:T(8,128)}), f32[16,9,8,128]{3,2,1,0:T(8,128)S(1)}, u32[]{:S(2)}, u32[]{:S(2)}) async-start(f32[16,9,8,128]{3,2,1,0:T(8,128)} %get-tuple-element.95), calls=%async_computation | async-start | bytes 1179648 | tf_op jit(solution)/shard_map/all_to_all | solution.py:595
  48.7 0.1 convert_reduce_fusion.1
  48.8 3.1 %shard_map.113 = f32[9,64,512]{2,1,0:T(8,128)} custom-call(f32[9,4,64,128]{3,2,1,0:T(8,128)S(1)} %get-tuple-element.93.total_ref), custom_call_target="tpu_custom_call" | custom-call | flops 100000000 | bytes 6000000 | tf_op jit(solution)/shard_map/pallas_call | solution.py:596
  51.9 8.4 %all-to-all-done.arrived_ref = f32[16,9,8,128]{3,2,1,0:T(8,128)S(1)} async-done(((f32[16,9,8,128]{3,2,1,0:T(8,128)}), f32[16,9,8,128]{3,2,1,0:T(8,128)S(1)}, u32[]{:S(2)}, u32[]{:S(2)}) %all-to-all-start) | async-done | bytes 589856 | tf_op jit(solution)/shard_map/all_to_all | solution.py:595
  60.3 1.4 %shard_map.114 = f32[9,8,512]{2,1,0:T(8,128)} custom-call(s32[2,8]{1,0:T(2,128)S(1)} %pad_add_fusion.table_ref, f32[9,4,8,128]{3,2,1,0:T(8,128)S(1)} %get-tuple-element.94.groups_ref, f32[16,9,8,128]{3,2,1,0:T(8,128)S(1)} %all-to-all-done.arrived_ref), custom_call_target="tpu_custom_call" | custom-call | flops 100000000 | bytes 6000000 | tf_op jit(solution)/shard_map/pallas_call | solution.py:597
  (24 shorter events, 0.1 us)
Async XLA Ops:
  0.6 12.1 %copy-start.5 = (s32[3,64]{1,0:T(4,128)S(1)}, s32[3,64]{1,0:T(4,128)}, u32[]{:S(2)}) copy-start(s32[3,64]{1,0:T(4,128)} %param.13) | copy-start | bytes 2308
  0.6 12.1 %copy-start.4 = (s32[64,6]{0,1:T(8,128)S(1)}, s32[64,6]{0,1:T(8,128)}, u32[]{:S(2)}) copy-start(s32[64,6]{0,1:T(8,128)} %param.11) | copy-start | bytes 4612
  1.4 1.3 %copy-start = (f32[9,64,512]{2,1,0:T(8,128)S(1)}, f32[9,64,512]{2,1,0:T(8,128)}, u32[]{:S(2)}) copy-start(f32[9,64,512]{2,1,0:T(8,128)} %adjoint_ref.1) | copy-start | bytes 3538948
  4.2 10.8 %collective-permute-start = (f32[16,384]{1,0:T(8,128)S(1)}, f32[16,384]{1,0:T(8,128)S(1)}, u32[]{:S(2)}, u32[]{:S(2)}) collective-permute-start(f32[16,384]{1,0:T(8,128)S(1)} %get-tuple-element.55), channel_id=1, source_target_pairs={{1,2},{3,4},{5,6},{7,8},{9,10},{11,12},{13,14},{15,0},{2,1},{4,3},... | collective-permute-start | bytes 73736 | tf_op jit(solution)/shard_map/ppermute | solution.py:549
  10.8 4.2 %collective-permute-start.1 = (f32[16,384]{1,0:T(8,128)S(1)}, f32[16,384]{1,0:T(8,128)S(1)}, u32[]{:S(2)}, u32[]{:S(2)}) collective-permute-start(f32[16,384]{1,0:T(8,128)S(1)} %get-tuple-element.56), channel_id=1, source_target_pairs={{0,1},{2,3},{4,5},{6,7},{8,9},{10,11},{12,13},{14,15},{1,0},{3,2},... | collective-permute-start | bytes 73736 | tf_op jit(solution)/shard_map/ppermute | solution.py:549
  10.8 4.5 %collective-permute-start.2 = (f32[16,384]{1,0:T(8,128)S(1)}, f32[16,384]{1,0:T(8,128)S(1)}, u32[]{:S(2)}, u32[]{:S(2)}) collective-permute-start(f32[16,384]{1,0:T(8,128)S(1)} %get-tuple-element.57), channel_id=1, source_target_pairs={{16,32},{48,64},{80,96},{112,0},{32,16},{64,48},{96,80},{0,112},{1... | collective-permute-start | bytes 73736 | tf_op jit(solution)/shard_map/ppermute | solution.py:549
  12.7 2.5 %collective-permute-start.3 = (f32[16,384]{1,0:T(8,128)S(1)}, f32[16,384]{1,0:T(8,128)S(1)}, u32[]{:S(2)}, u32[]{:S(2)}) collective-permute-start(f32[16,384]{1,0:T(8,128)S(1)} %get-tuple-element.58), channel_id=1, source_target_pairs={{0,16},{32,48},{64,80},{96,112},{16,0},{48,32},{80,64},{112,96},{1... | collective-permute-start | bytes 73736 | tf_op jit(solution)/shard_map/ppermute | solution.py:549
  16.2 7.2 %collective-permute-start.4 = (f32[16,384]{1,0:T(8,128)S(1)}, f32[16,384]{1,0:T(8,128)S(1)}, u32[]{:S(2)}, u32[]{:S(2)}) collective-permute-start(f32[16,384]{1,0:T(8,128)S(1)} %get-tuple-element.69), channel_id=1, source_target_pairs={{1,2},{3,4},{5,6},{7,8},{9,10},{11,12},{13,14},{15,0},{2,1},{4,3},... | collective-permute-start | bytes 73736 | tf_op jit(solution)/shard_map/ppermute | solution.py:549
  18.9 4.5 %collective-permute-start.5 = (f32[16,384]{1,0:T(8,128)S(1)}, f32[16,384]{1,0:T(8,128)S(1)}, u32[]{:S(2)}, u32[]{:S(2)}) collective-permute-start(f32[16,384]{1,0:T(8,128)S(1)} %get-tuple-element.70), channel_id=1, source_target_pairs={{0,1},{2,3},{4,5},{6,7},{8,9},{10,11},{12,13},{14,15},{1,0},{3,2},... | collective-permute-start | bytes 73736 | tf_op jit(solution)/shard_map/ppermute | solution.py:549
  18.9 4.5 %collective-permute-start.6 = (f32[16,384]{1,0:T(8,128)S(1)}, f32[16,384]{1,0:T(8,128)S(1)}, u32[]{:S(2)}, u32[]{:S(2)}) collective-permute-start(f32[16,384]{1,0:T(8,128)S(1)} %get-tuple-element.71), channel_id=1, source_target_pairs={{16,32},{48,64},{80,96},{112,0},{32,16},{64,48},{96,80},{0,112},{1... | collective-permute-start | bytes 73736 | tf_op jit(solution)/shard_map/ppermute | solution.py:549
  19.7 3.7 %collective-permute-start.7 = (f32[16,384]{1,0:T(8,128)S(1)}, f32[16,384]{1,0:T(8,128)S(1)}, u32[]{:S(2)}, u32[]{:S(2)}) collective-permute-start(f32[16,384]{1,0:T(8,128)S(1)} %get-tuple-element.72), channel_id=1, source_target_pairs={{0,16},{32,48},{64,80},{96,112},{16,0},{48,32},{80,64},{112,96},{1... | collective-permute-start | bytes 73736 | tf_op jit(solution)/shard_map/ppermute | solution.py:549
  24.3 7.2 %collective-permute-start.10 = (f32[16,384]{1,0:T(8,128)S(1)}, f32[16,384]{1,0:T(8,128)S(1)}, u32[]{:S(2)}, u32[]{:S(2)}) collective-permute-start(f32[16,384]{1,0:T(8,128)S(1)} %get-tuple-element.81), channel_id=1, source_target_pairs={{1,2},{3,4},{5,6},{7,8},{9,10},{11,12},{13,14},{15,0},{2,1},{4,3},... | collective-permute-start | bytes 73736 | tf_op jit(solution)/shard_map/ppermute | solution.py:549
  27.0 4.5 %collective-permute-start.11 = (f32[16,384]{1,0:T(8,128)S(1)}, f32[16,384]{1,0:T(8,128)S(1)}, u32[]{:S(2)}, u32[]{:S(2)}) collective-permute-start(f32[16,384]{1,0:T(8,128)S(1)} %get-tuple-element.82), channel_id=1, source_target_pairs={{0,1},{2,3},{4,5},{6,7},{8,9},{10,11},{12,13},{14,15},{1,0},{3,2},... | collective-permute-start | bytes 73736 | tf_op jit(solution)/shard_map/ppermute | solution.py:549
  27.0 4.5 %collective-permute-start.8 = (f32[16,384]{1,0:T(8,128)S(1)}, f32[16,384]{1,0:T(8,128)S(1)}, u32[]{:S(2)}, u32[]{:S(2)}) collective-permute-start(f32[16,384]{1,0:T(8,128)S(1)} %get-tuple-element.79), channel_id=1, source_target_pairs={{16,32},{48,64},{80,96},{112,0},{32,16},{64,48},{96,80},{0,112},{1... | collective-permute-start | bytes 73736 | tf_op jit(solution)/shard_map/ppermute | solution.py:549
  28.6 2.9 %collective-permute-start.9 = (f32[16,384]{1,0:T(8,128)S(1)}, f32[16,384]{1,0:T(8,128)S(1)}, u32[]{:S(2)}, u32[]{:S(2)}) collective-permute-start(f32[16,384]{1,0:T(8,128)S(1)} %get-tuple-element.80), channel_id=1, source_target_pairs={{0,16},{32,48},{64,80},{96,112},{16,0},{48,32},{80,64},{112,96},{1... | collective-permute-start | bytes 73736 | tf_op jit(solution)/shard_map/ppermute | solution.py:549
  32.4 7.2 %collective-permute-start.12 = (f32[16,384]{1,0:T(8,128)S(1)}, f32[16,384]{1,0:T(8,128)S(1)}, u32[]{:S(2)}, u32[]{:S(2)}) collective-permute-start(f32[16,384]{1,0:T(8,128)S(1)} %get-tuple-element.89), channel_id=1, source_target_pairs={{1,2},{3,4},{5,6},{7,8},{9,10},{11,12},{13,14},{15,0},{2,1},{4,3},... | collective-permute-start | bytes 73736 | tf_op jit(solution)/shard_map/ppermute | solution.py:549
  35.1 4.5 %collective-permute-start.13 = (f32[16,384]{1,0:T(8,128)S(1)}, f32[16,384]{1,0:T(8,128)S(1)}, u32[]{:S(2)}, u32[]{:S(2)}) collective-permute-start(f32[16,384]{1,0:T(8,128)S(1)} %get-tuple-element.90), channel_id=1, source_target_pairs={{0,1},{2,3},{4,5},{6,7},{8,9},{10,11},{12,13},{14,15},{1,0},{3,2},... | collective-permute-start | bytes 73736 | tf_op jit(solution)/shard_map/ppermute | solution.py:549
  35.1 4.5 %collective-permute-start.14 = (f32[16,384]{1,0:T(8,128)S(1)}, f32[16,384]{1,0:T(8,128)S(1)}, u32[]{:S(2)}, u32[]{:S(2)}) collective-permute-start(f32[16,384]{1,0:T(8,128)S(1)} %get-tuple-element.91), channel_id=1, source_target_pairs={{16,32},{48,64},{80,96},{112,0},{32,16},{64,48},{96,80},{0,112},{1... | collective-permute-start | bytes 73736 | tf_op jit(solution)/shard_map/ppermute | solution.py:549
  35.8 3.8 %collective-permute-start.15 = (f32[16,384]{1,0:T(8,128)S(1)}, f32[16,384]{1,0:T(8,128)S(1)}, u32[]{:S(2)}, u32[]{:S(2)}) collective-permute-start(f32[16,384]{1,0:T(8,128)S(1)} %get-tuple-element.92), channel_id=1, source_target_pairs={{0,16},{32,48},{64,80},{96,112},{16,0},{48,32},{80,64},{112,96},{1... | collective-permute-start | bytes 73736 | tf_op jit(solution)/shard_map/ppermute | solution.py:549
  36.8 2.8 %copy-start.1 = (f32[64,8,128]{2,1,0:T(8,128)S(1)}, f32[64,8,128]{2,1,0:T(8,128)}, u32[]{:S(2)}) copy-start(f32[64,8,128]{2,1,0:T(8,128)} %constant.24.clone.lines_ref) | copy-start | bytes 786436
  36.8 2.8 %copy-start.2 = (bf16[256,128]{1,0:T(8,128)(2,1)S(1)}, bf16[256,128]{1,0:T(8,128)(2,1)}, u32[]{:S(2)}) copy-start(bf16[256,128]{1,0:T(8,128)(2,1)} %constant.22.clone.wa_ref) | copy-start | bytes 196612
  36.8 2.8 %copy-start.3 = (bf16[256,128]{1,0:T(8,128)(2,1)S(1)}, bf16[256,128]{1,0:T(8,128)(2,1)}, u32[]{:S(2)}) copy-start(bf16[256,128]{1,0:T(8,128)(2,1)} %constant.23.clone.wb_ref) | copy-start | bytes 196612
  42.9 5.9 %copy-start.6 = (s32[2,8]{1,0:T(2,128)S(1)}, s32[2,8]{1,0:T(2,128)}, u32[]{:S(2)}) copy-start(s32[2,8]{1,0:T(2,128)} %param.14) | copy-start | bytes 196
  42.9 17.4 %all-to-all-start = ((f32[16,9,8,128]{3,2,1,0:T(8,128)}), f32[16,9,8,128]{3,2,1,0:T(8,128)S(1)}, u32[]{:S(2)}, u32[]{:S(2)}) async-start(f32[16,9,8,128]{3,2,1,0:T(8,128)} %get-tuple-element.95), calls=%async_computation | async-start | bytes 1179648 | tf_op jit(solution)/shard_map/all_to_all | solution.py:595

commit v6 on v5

--- a/solution.py
+++ b/solution.py
@@ -394,7 +394,7 @@
 
 def end_kernel(
     factor, order, keys_ref, vol_ref, part_ref, ra, rb, rc, rd, remote_ref, place_ref, wa_ref, wb_ref, lines_ref,
-    total_ref, parent_ref, away_ref, face_ref, turn_ref, ranked_ref, rows_ref, plane_ref,
+    total_ref, parent_ref, away_ref, face_ref, turn_ref, ranked_ref, rows_ref, plane_ref, block_ref, sem,
 ):
     add_faces(part_ref, in_order(order, (ra, rb, rc, rd)), remote_ref, factor, total_ref, face_ref)
     place = jnp.where(
@@ -433,16 +433,24 @@
                 sums[i] = term if k == 0 else sums[i] + term
         for i in range(9):
             parent_ref[i, t] = sums[i]
+    def send(g):
+        place = keys_ref[g] - P_DEV
+        return pltpu.make_async_copy(block_ref.at[g], away_ref.at[place // 2, place % 2], sem.at[g])
+
     for g in range(P_DEV):
-        key = keys_ref[g]
-
-        @pl.when(key >= P_DEV)
+
+        @pl.when(keys_ref[g] >= P_DEV)
         def _():
-            owner = (key - P_DEV) // 2
-            slot = (key - P_DEV) % 2
             for i in range(9):
                 for t in range(4):
-                    away_ref[owner, i, pl.ds(slot * 4 + t, 1), :] = parent_ref[i, t, pl.ds(g, 1), :]
+                    block_ref[g, i, pl.ds(t, 1), :] = parent_ref[i, t, pl.ds(g, 1), :]
+            send(g).start()
+
+    for g in range(P_DEV):
+
+        @pl.when(keys_ref[g] >= P_DEV)
+        def _():
+            send(g).wait()
 
 
 def next_kernel(total_ref, next_ref, turn_ref):
@@ -473,7 +481,7 @@
             for i in range(9):
                 for t in range(4):
                     out_ref[i, pl.ds(p, 1), pl.ds(128 * t, 128)] = arrived_ref[
-                        holder, i, pl.ds(slot * 4 + t, 1), :
+                        holder, slot, i, pl.ds(t, 1), :
                     ]
 
 
@@ -483,14 +491,15 @@
 
 VMEM = pl.BlockSpec(memory_space=pltpu.VMEM)
 SMEM = pl.BlockSpec(memory_space=pltpu.SMEM)
-
-
-def call(kernel, outs, scratch=(), smem=(), aliases={}, count=0, flops=10**8, traffic=6 * 10**6):
+ANYWHERE = pl.BlockSpec(memory_space=pl.ANY)
+
+
+def call(kernel, outs, scratch=(), smem=(), anywhere=(), aliases={}, count=0, flops=10**8, traffic=6 * 10**6):
     return pl.pallas_call(
         kernel,
         out_shape=outs,
         in_specs=[SMEM if k in smem else VMEM for k in range(count)],
-        out_specs=jax.tree.map(lambda _: VMEM, outs),
+        out_specs=[ANYWHERE if k in anywhere else VMEM for k in range(len(outs))],
         scratch_shapes=list(scratch),
         input_output_aliases=aliases,
         compiler_params=pltpu.CompilerParams(vmem_limit_bytes=32 * 2**20),
@@ -580,14 +589,17 @@
     wa, wb, lines = (jnp.asarray(x) for x in refine_parts())
     total, groups, away = call(
         functools.partial(end_kernel, factor, order),
-        [state, shape(9, 4, P_DEV, 128), shape(N_SEG, 9, 8, 128)],
+        [state, shape(9, 4, P_DEV, 128), shape(N_SEG, 2, 9, 4, 128)],
         [
             face_scratch,
             pltpu.VMEM((9, NODES, 128), F32),
             pltpu.VMEM((9, 64, NODES), F32),
             pltpu.VMEM((9, 128, 256), F32),
             pltpu.VMEM((9, 128, 128), F32),
+            pltpu.VMEM((P_DEV, 9, 4, 128), F32),
+            pltpu.SemaphoreType.DMA((P_DEV,)),
         ],
+        anywhere=(2,),
         smem=(0,),
         aliases={1: 0},
         count=12,

time: 62 us -> 61.8 us (level)
  no operation moved by 1% of the time
where the time goes in v6:
time: 61.8 us; the launch traced here: 61.5 us
  starting transfers between devices  27.3 us (44%)
  Pallas kernels  20.3 us (33%)
  waiting for transfers between devices  10.6 us (17%)
  local copies, waits for them, and re-layouts  1.3 us (2%)
  other arithmetic  1.14 us (2%)
  between operations  0.81 us (1%)
    ppermute x16, starting transfers between devices, shards(): arrived = [lax.ppermute(out_going[k], *pairs[k]) for k in order]  21.7 us
    all_to_all x1, waiting for transfers between devices, shards(): lax.all_to_all(away, 'seg', split_axis=0, concat_axis=0, tiled=True)  8.45 us
    all_to_all x1, starting transfers between devices, shards(): lax.all_to_all(away, 'seg', split_axis=0, concat_axis=0, tiled=True)  5.67 us
    pallas_call x2, Pallas kernels, shards(): call(functools.partial(volume_kernel, factor), [state, face_part, state],...  4.5 us
    pallas_call x1, Pallas kernels, shards(): call(next_kernel, [shape(9, E_DEV, NODES)], [turn], count=1)(total)[0]  3.1 us
    pallas_call x1, Pallas kernels, shards(): call(functools.partial(end_kernel, factor, order), [state, shape(9, 4, P_...  3.09 us
    pallas_call x3, Pallas kernels, shards(): call(functools.partial(finish_kernel, factor, order), [state, table_y, ta...  2.61 us
    ppermute x16, waiting for transfers between devices, shards(): arrived = [lax.ppermute(out_going[k], *pairs[k]) for k in order]  2.11 us
  transfers between devices with their start and end apart: 17, of which 5 were waited for; matrix products, arithmetic and copies ran while one was open for 1% of the time, Pallas kernels for 19%

profile of v6, /device:TPU:0, one launch (start us, length us, event | category | flops | bytes accessed | tf_op | source)
XLA Modules:
  0.0 61.5 jit_solution(11590270239950322599)
XLA Ops:
  0.7 0.7 %convert_add_fusion.pack_ref = f32[1,8,128]{2,1,0:T(8,128)S(1)} fusion(s32[1,4,16]{2,1,0:T(4,128)} %param.12, f32[1,3,64]{2,1,0:T(4,128)} %bitcast.19), kind=kLoop, calls=%fused_computation.3 | loop fusion | flops 2048 | bytes 5120 | tf_op jit(solution)/shard_map/add | solution.py:542
  1.4 1.3 %copy-done = f32[9,64,512]{2,1,0:T(8,128)S(1)} copy-done((f32[9,64,512]{2,1,0:T(8,128)S(1)}, f32[9,64,512]{2,1,0:T(8,128)}, u32[]{:S(2)}) %copy-start) | copy-done | bytes 1179672
  2.6 1.5 %shard_map.104 = (f32[9,4,64,128]{3,2,1,0:T(8,128)S(1)}, bf16[384,256]{1,0:T(8,128)(2,1)S(1)}, bf16[384,512]{1,0:T(8,128)(2,1)S(1)}, f32[3,8,128]{2,1,0:T(8,128)...) custom-call(f32[1,8,128]{2,1,0:T(8,128)S(1)} %convert_add_fusion.pac, ...), custom_call_target="tpu_custom_call" | custom-call | flops 100000000 | bytes 6000000 | tf_op jit(solution)/shard_map/pallas_call | solution.py:546
  4.2 6.6 %collective-permute-start = (f32[16,384]{1,0:T(8,128)S(1)}, f32[16,384]{1,0:T(8,128)S(1)}, u32[]{:S(2)}, u32[]{:S(2)}) collective-permute-start(f32[16,384]{1,0:T(8,128)S(1)} %get-tuple-element.55), channel_id=1, source_target_pairs={{1,2},{3,4},{5,6},{7,8},{9,10},{11,12},{13,14},{15,0},{2,1},{4,3},... | collective-permute-start | bytes 73736 | tf_op jit(solution)/shard_map/ppermute | solution.py:558
  10.8 0.0 collective-permute-start.1
  10.8 1.9 %collective-permute-start.2 = (f32[16,384]{1,0:T(8,128)S(1)}, f32[16,384]{1,0:T(8,128)S(1)}, u32[]{:S(2)}, u32[]{:S(2)}) collective-permute-start(f32[16,384]{1,0:T(8,128)S(1)} %get-tuple-element.57), channel_id=1, source_target_pairs={{16,32},{48,64},{80,96},{112,0},{32,16},{64,48},{96,80},{0,112},{1... | collective-permute-start | bytes 73736 | tf_op jit(solution)/shard_map/ppermute | solution.py:558
  12.7 0.0 collective-permute-start.3
  12.8 0.1 convert_reduce_fusion
  12.9 2.1 %shard_map.105 = (f32[9,4,64,128]{3,2,1,0:T(8,128)S(1)}, f32[384,384]{1,0:T(8,128)S(1)}, bf16[256,384]{1,0:T(8,128)(2,1)S(1)}, bf16[512,384]{1,0:T(8,128)(2,1)S(1)}, bf16[128,384]{1,0:T(8,128)(2,1)S(1)}) custom-call(f32[8,128]{1,0:T(8,128)S(1)} %pad.10.faces_ref, f32[9,4,64,128]{3,2,1,0:T(8,128)S(1)} %get-tuple-element.49.v_ref.acc_ref, ...), custom_call_target="tpu_custom_call" | custom-call | flops 100000000 | bytes 6000000 | tf_op jit(solution)/shard_map/pallas_call | solution.py:560
  15.0 0.0 collective-permute-done.ra
  15.0 0.0 collective-permute-done.1.rb
  15.0 0.3 collective-permute-done.2.rc
  15.3 0.0 collective-permute-done.3.rd
  15.3 0.9 %shard_map.106 = (f32[9,4,64,128]{3,2,1,0:T(8,128)S(1)}, bf16[384,256]{1,0:T(8,128)(2,1)S(1)}, bf16[384,512]{1,0:T(8,128)(2,1)S(1)}, f32[16,384]{1,0:T(8,128)S(1...) custom-call(f32[9,4,64,128]{3,2,1,0:T(8,128)S(1)} %get-tuple-element, ...), custom_call_target="tpu_custom_call", output_to_operand_aliasing={{0}: (0, {})} | custom-call | flops 100000000 | bytes 6000000 | tf_op jit(solution)/shard_map/pallas_call | solution.py:581
  16.2 2.8 %collective-permute-start.4 = (f32[16,384]{1,0:T(8,128)S(1)}, f32[16,384]{1,0:T(8,128)S(1)}, u32[]{:S(2)}, u32[]{:S(2)}) collective-permute-start(f32[16,384]{1,0:T(8,128)S(1)} %get-tuple-element.69), channel_id=1, source_target_pairs={{1,2},{3,4},{5,6},{7,8},{9,10},{11,12},{13,14},{15,0},{2,1},{4,3},... | collective-permute-start | bytes 73736 | tf_op jit(solution)/shard_map/ppermute | solution.py:558
  18.9 0.0 collective-permute-start.5
  18.9 0.8 %collective-permute-start.6 = (f32[16,384]{1,0:T(8,128)S(1)}, f32[16,384]{1,0:T(8,128)S(1)}, u32[]{:S(2)}, u32[]{:S(2)}) collective-permute-start(f32[16,384]{1,0:T(8,128)S(1)} %get-tuple-element.71), channel_id=1, source_target_pairs={{16,32},{48,64},{80,96},{112,0},{32,16},{64,48},{96,80},{0,112},{1... | collective-permute-start | bytes 73736 | tf_op jit(solution)/shard_map/ppermute | solution.py:558
  19.7 0.8 %collective-permute-start.7 = (f32[16,384]{1,0:T(8,128)S(1)}, f32[16,384]{1,0:T(8,128)S(1)}, u32[]{:S(2)}, u32[]{:S(2)}) collective-permute-start(f32[16,384]{1,0:T(8,128)S(1)} %get-tuple-element.72), channel_id=1, source_target_pairs={{0,16},{32,48},{64,80},{96,112},{16,0},{48,32},{80,64},{112,96},{1... | collective-permute-start | bytes 73736 | tf_op jit(solution)/shard_map/ppermute | solution.py:558
  20.5 2.2 %shard_map.107 = (f32[9,4,64,128]{3,2,1,0:T(8,128)S(1)}, f32[384,384]{1,0:T(8,128)S(1)}, f32[9,4,64,128]{3,2,1,0:T(8,128)S(1)}) custom-call(f32[9,4,64,128]{3,2,1,0:T(8,128)S(1)} %get-tuple-element.62.v_ref, bf16[384,256]{1,0:T(8,128)(2,1)S(1)} %get-tuple-element.63.ty_ref, bf16[384,512]{1,0:T(8,128)(2,1)S(1)} %get-tuple-element.64.t_ref, ...), custom_call_target="tpu_custom_call" | custom-call | flops 100000000 | bytes 6000000 | tf_op jit(solution)/shard_map/pallas_call | solution.py:573
  22.8 0.6 %collective-permute-done.4.ra = f32[16,384]{1,0:T(8,128)S(1)} collective-permute-done((f32[16,384]{1,0:T(8,128)S(1)}, f32[16,384]{1,0:T(8,128)S(1)}, u32[]{:S(2)}, u32[]{:S(2)}) %collective-permute-start.4) | collective-permute-done | bytes 24608 | tf_op jit(solution)/shard_map/ppermute | solution.py:558
  23.4 0.0 collective-permute-done.5.rb
  23.4 0.0 collective-permute-done.6.rc
  23.4 0.0 collective-permute-done.7.rd
  23.4 0.9 %shard_map.108 = (f32[9,4,64,128]{3,2,1,0:T(8,128)S(1)}, bf16[384,256]{1,0:T(8,128)(2,1)S(1)}, bf16[384,512]{1,0:T(8,128)(2,1)S(1)}, f32[16,384]{1,0:T(8,128)S(1...) custom-call(f32[9,4,64,128]{3,2,1,0:T(8,128)S(1)} %get-tuple-element, ...), custom_call_target="tpu_custom_call", output_to_operand_aliasing={{0}: (0, {})} | custom-call | flops 100000000 | bytes 6000000 | tf_op jit(solution)/shard_map/pallas_call | solution.py:581
  24.3 2.8 %collective-permute-start.10 = (f32[16,384]{1,0:T(8,128)S(1)}, f32[16,384]{1,0:T(8,128)S(1)}, u32[]{:S(2)}, u32[]{:S(2)}) collective-permute-start(f32[16,384]{1,0:T(8,128)S(1)} %get-tuple-element.81), channel_id=1, source_target_pairs={{1,2},{3,4},{5,6},{7,8},{9,10},{11,12},{13,14},{15,0},{2,1},{4,3},... | collective-permute-start | bytes 73736 | tf_op jit(solution)/shard_map/ppermute | solution.py:558
  27.0 0.0 collective-permute-start.11
  27.0 1.6 %collective-permute-start.8 = (f32[16,384]{1,0:T(8,128)S(1)}, f32[16,384]{1,0:T(8,128)S(1)}, u32[]{:S(2)}, u32[]{:S(2)}) collective-permute-start(f32[16,384]{1,0:T(8,128)S(1)} %get-tuple-element.79), channel_id=1, source_target_pairs={{16,32},{48,64},{80,96},{112,0},{32,16},{64,48},{96,80},{0,112},{1... | collective-permute-start | bytes 73736 | tf_op jit(solution)/shard_map/ppermute | solution.py:558
  28.6 0.0 collective-permute-start.9
  28.6 0.1 select_reduce_fusion.keys_ref
  28.8 2.3 %shard_map.109 = (f32[9,4,64,128]{3,2,1,0:T(8,128)S(1)}, f32[384,384]{1,0:T(8,128)S(1)}, f32[9,4,64,128]{3,2,1,0:T(8,128)S(1)}) custom-call(f32[9,4,64,128]{3,2,1,0:T(8,128)S(1)} %get-tuple-element.73.v_ref, bf16[384,256]{1,0:T(8,128)(2,1)S(1)} %get-tuple-element.74.ty_ref, bf16[384,512]{1,0:T(8,128)(2,1)S(1)} %get-tuple-element.75.t_ref, ...), custom_call_target="tpu_custom_call" | custom-call | flops 100000000 | bytes 6000000 | tf_op jit(solution)/shard_map/pallas_call | solution.py:573
  31.1 0.4 collective-permute-done.10.rc
  31.5 0.0 collective-permute-done.11.rd
  31.5 0.0 collective-permute-done.8.ra
  31.5 0.9 %shard_map.110 = (f32[9,4,64,128]{3,2,1,0:T(8,128)S(1)}, bf16[384,256]{1,0:T(8,128)(2,1)S(1)}, bf16[384,512]{1,0:T(8,128)(2,1)S(1)}, f32[16,384]{1,0:T(8,128)S(1...) custom-call(f32[9,4,64,128]{3,2,1,0:T(8,128)S(1)} %get-tuple-element, ...), custom_call_target="tpu_custom_call", output_to_operand_aliasing={{0}: (0, {})} | custom-call | flops 100000000 | bytes 6000000 | tf_op jit(solution)/shard_map/pallas_call | solution.py:581
  32.4 2.8 %collective-permute-start.12 = (f32[16,384]{1,0:T(8,128)S(1)}, f32[16,384]{1,0:T(8,128)S(1)}, u32[]{:S(2)}, u32[]{:S(2)}) collective-permute-start(f32[16,384]{1,0:T(8,128)S(1)} %get-tuple-element.89), channel_id=1, source_target_pairs={{1,2},{3,4},{5,6},{7,8},{9,10},{11,12},{13,14},{15,0},{2,1},{4,3},... | collective-permute-start | bytes 73736 | tf_op jit(solution)/shard_map/ppermute | solution.py:558
  35.1 0.6 %collective-permute-start.14 = (f32[16,384]{1,0:T(8,128)S(1)}, f32[16,384]{1,0:T(8,128)S(1)}, u32[]{:S(2)}, u32[]{:S(2)}) collective-permute-start(f32[16,384]{1,0:T(8,128)S(1)} %get-tuple-element.91), channel_id=1, source_target_pairs={{16,32},{48,64},{80,96},{112,0},{32,16},{64,48},{96,80},{0,112},{1... | collective-permute-start | bytes 73736 | tf_op jit(solution)/shard_map/ppermute | solution.py:558
  35.8 1.0 %collective-permute-start.15 = (f32[16,384]{1,0:T(8,128)S(1)}, f32[16,384]{1,0:T(8,128)S(1)}, u32[]{:S(2)}, u32[]{:S(2)}) collective-permute-start(f32[16,384]{1,0:T(8,128)S(1)} %get-tuple-element.92), channel_id=1, source_target_pairs={{0,16},{32,48},{64,80},{96,112},{16,0},{48,32},{80,64},{112,96},{1... | collective-permute-start | bytes 73736 | tf_op jit(solution)/shard_map/ppermute | solution.py:558
  36.7 0.1 add_bitcast_fusion.place_ref
  36.8 2.0 %shard_map.111 = (f32[9,4,64,128]{3,2,1,0:T(8,128)S(1)}, f32[384,384]{1,0:T(8,128)S(1)}) custom-call(f32[9,4,64,128]{3,2,1,0:T(8,128)S(1)} %get-tuple-element.83.v_ref, bf16[384,256]{1,0:T(8,128)(2,1)S(1)} %get-tuple-element.84.ty_ref, bf16[384,512]{1,0:T(8,128)(2,1)S(1)} %get-tuple-element.85.t_ref, bf16[256,384]{1,0:T(8,128)(2,1)S(1)} %get-tuple-element.65.local_y_ref, ...), custom_call_target="tpu_custom_call" | custom-call | flops 100000000 | bytes 6000000 | tf_op jit(solution)/shard_map/pallas_call | solution.py:577
  38.8 0.8 %collective-permute-done.12.ra = f32[16,384]{1,0:T(8,128)S(1)} collective-permute-done((f32[16,384]{1,0:T(8,128)S(1)}, f32[16,384]{1,0:T(8,128)S(1)}, u32[]{:S(2)}, u32[]{:S(2)}) %collective-permute-start.12) | collective-permute-done | bytes 24608 | tf_op jit(solution)/shard_map/ppermute | solution.py:558
  39.6 0.0 collective-permute-done.14.rc
  39.6 3.1 %shard_map.112 = (f32[9,4,64,128]{3,2,1,0:T(8,128)S(1)}, f32[9,4,8,128]{3,2,1,0:T(8,128)S(1)}, f32[16,2,9,4,128]{4,3,2,1,0:T(4,128)}) custom-call(s32[8]{0:T(128)S(1)} %select_reduce_fusion.keys_ref, f32[9,4,64,128]{3,2,1,0:T(8,128)S(1)} %get-tuple-element.87.vol_ref, f32[384,384]{1,0:T(8,128)S(1)} %get-tuple-element.88.part_ref, ...), custom_call_target="tpu_custom_call", output_to_operand_aliasing={{0}: (1, {})} | custom-call | flops 100000000 | bytes 6000000 | tf_op jit(solution)/shard_map/pallas_call | solution.py:590
  42.7 0.0 copy-start.6
  42.7 5.7 %all-to-all-start = ((f32[16,2,9,4,128]{4,3,2,1,0:T(4,128)}), f32[16,2,9,4,128]{4,3,2,1,0:T(4,128)S(1)}, u32[]{:S(2)}, u32[]{:S(2)}) async-start(f32[16,2,9,4,128]{4,3,2,1,0:T(4,128)} %get-tuple-element.95), calls=%async_computation | async-start | bytes 1179648 | tf_op jit(solution)/shard_map/all_to_all | solution.py:607
  48.4 0.1 convert_reduce_fusion.1
  48.5 3.1 %shard_map.113 = f32[9,64,512]{2,1,0:T(8,128)} custom-call(f32[9,4,64,128]{3,2,1,0:T(8,128)S(1)} %get-tuple-element.93.total_ref), custom_call_target="tpu_custom_call" | custom-call | flops 100000000 | bytes 6000000 | tf_op jit(solution)/shard_map/pallas_call | solution.py:608
  51.6 8.5 %all-to-all-done.arrived_ref = f32[16,2,9,4,128]{4,3,2,1,0:T(4,128)S(1)} async-done(((f32[16,2,9,4,128]{4,3,2,1,0:T(4,128)}), f32[16,2,9,4,128]{4,3,2,1,0:T(4,128)S(1)}, u32[]{:S(2)}, u32[]{:S(2)}) %all-to-all-start) | async-done | bytes 589856 | tf_op jit(solution)/shard_map/all_to_all | solution.py:607
  60.1 1.4 %shard_map.114 = f32[9,8,512]{2,1,0:T(8,128)} custom-call(s32[2,8]{1,0:T(2,128)S(1)} %pad_add_fusion.table_ref, f32[9,4,8,128]{3,2,1,0:T(8,128)S(1)} %get-tuple-element.94.groups_ref, f32[16,2,9,4,128]{4,3,2,1,0:T(4,128)S(1)} %all-to-all-done.arrived_ref), custom_call_target="tpu_custom_call" | custom-call | flops 100000000 | bytes 6000000 | tf_op jit(solution)/shard_map/pallas_call | solution.py:609
  (24 shorter events, 0.1 us)
Async XLA Ops:
  0.6 12.1 %copy-start.5 = (s32[3,64]{1,0:T(4,128)S(1)}, s32[3,64]{1,0:T(4,128)}, u32[]{:S(2)}) copy-start(s32[3,64]{1,0:T(4,128)} %param.13) | copy-start | bytes 2308
  0.6 12.1 %copy-start.4 = (s32[64,6]{0,1:T(8,128)S(1)}, s32[64,6]{0,1:T(8,128)}, u32[]{:S(2)}) copy-start(s32[64,6]{0,1:T(8,128)} %param.11) | copy-start | bytes 4612
  1.4 1.3 %copy-start = (f32[9,64,512]{2,1,0:T(8,128)S(1)}, f32[9,64,512]{2,1,0:T(8,128)}, u32[]{:S(2)}) copy-start(f32[9,64,512]{2,1,0:T(8,128)} %adjoint_ref.1) | copy-start | bytes 3538948
  4.2 10.8 %collective-permute-start = (f32[16,384]{1,0:T(8,128)S(1)}, f32[16,384]{1,0:T(8,128)S(1)}, u32[]{:S(2)}, u32[]{:S(2)}) collective-permute-start(f32[16,384]{1,0:T(8,128)S(1)} %get-tuple-element.55), channel_id=1, source_target_pairs={{1,2},{3,4},{5,6},{7,8},{9,10},{11,12},{13,14},{15,0},{2,1},{4,3},... | collective-permute-start | bytes 73736 | tf_op jit(solution)/shard_map/ppermute | solution.py:558
  10.8 4.2 %collective-permute-start.1 = (f32[16,384]{1,0:T(8,128)S(1)}, f32[16,384]{1,0:T(8,128)S(1)}, u32[]{:S(2)}, u32[]{:S(2)}) collective-permute-start(f32[16,384]{1,0:T(8,128)S(1)} %get-tuple-element.56), channel_id=1, source_target_pairs={{0,1},{2,3},{4,5},{6,7},{8,9},{10,11},{12,13},{14,15},{1,0},{3,2},... | collective-permute-start | bytes 73736 | tf_op jit(solution)/shard_map/ppermute | solution.py:558
  10.8 4.5 %collective-permute-start.2 = (f32[16,384]{1,0:T(8,128)S(1)}, f32[16,384]{1,0:T(8,128)S(1)}, u32[]{:S(2)}, u32[]{:S(2)}) collective-permute-start(f32[16,384]{1,0:T(8,128)S(1)} %get-tuple-element.57), channel_id=1, source_target_pairs={{16,32},{48,64},{80,96},{112,0},{32,16},{64,48},{96,80},{0,112},{1... | collective-permute-start | bytes 73736 | tf_op jit(solution)/shard_map/ppermute | solution.py:558
  12.7 2.5 %collective-permute-start.3 = (f32[16,384]{1,0:T(8,128)S(1)}, f32[16,384]{1,0:T(8,128)S(1)}, u32[]{:S(2)}, u32[]{:S(2)}) collective-permute-start(f32[16,384]{1,0:T(8,128)S(1)} %get-tuple-element.58), channel_id=1, source_target_pairs={{0,16},{32,48},{64,80},{96,112},{16,0},{48,32},{80,64},{112,96},{1... | collective-permute-start | bytes 73736 | tf_op jit(solution)/shard_map/ppermute | solution.py:558
  16.2 7.2 %collective-permute-start.4 = (f32[16,384]{1,0:T(8,128)S(1)}, f32[16,384]{1,0:T(8,128)S(1)}, u32[]{:S(2)}, u32[]{:S(2)}) collective-permute-start(f32[16,384]{1,0:T(8,128)S(1)} %get-tuple-element.69), channel_id=1, source_target_pairs={{1,2},{3,4},{5,6},{7,8},{9,10},{11,12},{13,14},{15,0},{2,1},{4,3},... | collective-permute-start | bytes 73736 | tf_op jit(solution)/shard_map/ppermute | solution.py:558
  18.9 4.5 %collective-permute-start.5 = (f32[16,384]{1,0:T(8,128)S(1)}, f32[16,384]{1,0:T(8,128)S(1)}, u32[]{:S(2)}, u32[]{:S(2)}) collective-permute-start(f32[16,384]{1,0:T(8,128)S(1)} %get-tuple-element.70), channel_id=1, source_target_pairs={{0,1},{2,3},{4,5},{6,7},{8,9},{10,11},{12,13},{14,15},{1,0},{3,2},... | collective-permute-start | bytes 73736 | tf_op jit(solution)/shard_map/ppermute | solution.py:558
  18.9 4.5 %collective-permute-start.6 = (f32[16,384]{1,0:T(8,128)S(1)}, f32[16,384]{1,0:T(8,128)S(1)}, u32[]{:S(2)}, u32[]{:S(2)}) collective-permute-start(f32[16,384]{1,0:T(8,128)S(1)} %get-tuple-element.71), channel_id=1, source_target_pairs={{16,32},{48,64},{80,96},{112,0},{32,16},{64,48},{96,80},{0,112},{1... | collective-permute-start | bytes 73736 | tf_op jit(solution)/shard_map/ppermute | solution.py:558
  19.7 3.7 %collective-permute-start.7 = (f32[16,384]{1,0:T(8,128)S(1)}, f32[16,384]{1,0:T(8,128)S(1)}, u32[]{:S(2)}, u32[]{:S(2)}) collective-permute-start(f32[16,384]{1,0:T(8,128)S(1)} %get-tuple-element.72), channel_id=1, source_target_pairs={{0,16},{32,48},{64,80},{96,112},{16,0},{48,32},{80,64},{112,96},{1... | collective-permute-start | bytes 73736 | tf_op jit(solution)/shard_map/ppermute | solution.py:558
  24.3 7.2 %collective-permute-start.10 = (f32[16,384]{1,0:T(8,128)S(1)}, f32[16,384]{1,0:T(8,128)S(1)}, u32[]{:S(2)}, u32[]{:S(2)}) collective-permute-start(f32[16,384]{1,0:T(8,128)S(1)} %get-tuple-element.81), channel_id=1, source_target_pairs={{1,2},{3,4},{5,6},{7,8},{9,10},{11,12},{13,14},{15,0},{2,1},{4,3},... | collective-permute-start | bytes 73736 | tf_op jit(solution)/shard_map/ppermute | solution.py:558
  27.0 4.5 %collective-permute-start.11 = (f32[16,384]{1,0:T(8,128)S(1)}, f32[16,384]{1,0:T(8,128)S(1)}, u32[]{:S(2)}, u32[]{:S(2)}) collective-permute-start(f32[16,384]{1,0:T(8,128)S(1)} %get-tuple-element.82), channel_id=1, source_target_pairs={{0,1},{2,3},{4,5},{6,7},{8,9},{10,11},{12,13},{14,15},{1,0},{3,2},... | collective-permute-start | bytes 73736 | tf_op jit(solution)/shard_map/ppermute | solution.py:558
  27.0 4.5 %collective-permute-start.8 = (f32[16,384]{1,0:T(8,128)S(1)}, f32[16,384]{1,0:T(8,128)S(1)}, u32[]{:S(2)}, u32[]{:S(2)}) collective-permute-start(f32[16,384]{1,0:T(8,128)S(1)} %get-tuple-element.79), channel_id=1, source_target_pairs={{16,32},{48,64},{80,96},{112,0},{32,16},{64,48},{96,80},{0,112},{1... | collective-permute-start | bytes 73736 | tf_op jit(solution)/shard_map/ppermute | solution.py:558
  28.6 2.9 %collective-permute-start.9 = (f32[16,384]{1,0:T(8,128)S(1)}, f32[16,384]{1,0:T(8,128)S(1)}, u32[]{:S(2)}, u32[]{:S(2)}) collective-permute-start(f32[16,384]{1,0:T(8,128)S(1)} %get-tuple-element.80), channel_id=1, source_target_pairs={{0,16},{32,48},{64,80},{96,112},{16,0},{48,32},{80,64},{112,96},{1... | collective-permute-start | bytes 73736 | tf_op jit(solution)/shard_map/ppermute | solution.py:558
  32.4 7.2 %collective-permute-start.12 = (f32[16,384]{1,0:T(8,128)S(1)}, f32[16,384]{1,0:T(8,128)S(1)}, u32[]{:S(2)}, u32[]{:S(2)}) collective-permute-start(f32[16,384]{1,0:T(8,128)S(1)} %get-tuple-element.89), channel_id=1, source_target_pairs={{1,2},{3,4},{5,6},{7,8},{9,10},{11,12},{13,14},{15,0},{2,1},{4,3},... | collective-permute-start | bytes 73736 | tf_op jit(solution)/shard_map/ppermute | solution.py:558
  35.1 4.5 %collective-permute-start.13 = (f32[16,384]{1,0:T(8,128)S(1)}, f32[16,384]{1,0:T(8,128)S(1)}, u32[]{:S(2)}, u32[]{:S(2)}) collective-permute-start(f32[16,384]{1,0:T(8,128)S(1)} %get-tuple-element.90), channel_id=1, source_target_pairs={{0,1},{2,3},{4,5},{6,7},{8,9},{10,11},{12,13},{14,15},{1,0},{3,2},... | collective-permute-start | bytes 73736 | tf_op jit(solution)/shard_map/ppermute | solution.py:558
  35.1 4.5 %collective-permute-start.14 = (f32[16,384]{1,0:T(8,128)S(1)}, f32[16,384]{1,0:T(8,128)S(1)}, u32[]{:S(2)}, u32[]{:S(2)}) collective-permute-start(f32[16,384]{1,0:T(8,128)S(1)} %get-tuple-element.91), channel_id=1, source_target_pairs={{16,32},{48,64},{80,96},{112,0},{32,16},{64,48},{96,80},{0,112},{1... | collective-permute-start | bytes 73736 | tf_op jit(solution)/shard_map/ppermute | solution.py:558
  35.8 3.8 %collective-permute-start.15 = (f32[16,384]{1,0:T(8,128)S(1)}, f32[16,384]{1,0:T(8,128)S(1)}, u32[]{:S(2)}, u32[]{:S(2)}) collective-permute-start(f32[16,384]{1,0:T(8,128)S(1)} %get-tuple-element.92), channel_id=1, source_target_pairs={{0,16},{32,48},{64,80},{96,112},{16,0},{48,32},{80,64},{112,96},{1... | collective-permute-start | bytes 73736 | tf_op jit(solution)/shard_map/ppermute | solution.py:558
  36.8 2.8 %copy-start.1 = (f32[64,8,128]{2,1,0:T(8,128)S(1)}, f32[64,8,128]{2,1,0:T(8,128)}, u32[]{:S(2)}) copy-start(f32[64,8,128]{2,1,0:T(8,128)} %constant.24.clone.lines_ref) | copy-start | bytes 786436
  36.8 2.8 %copy-start.2 = (bf16[256,128]{1,0:T(8,128)(2,1)S(1)}, bf16[256,128]{1,0:T(8,128)(2,1)}, u32[]{:S(2)}) copy-start(bf16[256,128]{1,0:T(8,128)(2,1)} %constant.22.clone.wa_ref) | copy-start | bytes 196612
  36.8 2.8 %copy-start.3 = (bf16[256,128]{1,0:T(8,128)(2,1)S(1)}, bf16[256,128]{1,0:T(8,128)(2,1)}, u32[]{:S(2)}) copy-start(bf16[256,128]{1,0:T(8,128)(2,1)} %constant.23.clone.wb_ref) | copy-start | bytes 196612
  42.7 5.8 %copy-start.6 = (s32[2,8]{1,0:T(2,128)S(1)}, s32[2,8]{1,0:T(2,128)}, u32[]{:S(2)}) copy-start(s32[2,8]{1,0:T(2,128)} %param.14) | copy-start | bytes 196
  42.7 17.3 %all-to-all-start = ((f32[16,2,9,4,128]{4,3,2,1,0:T(4,128)}), f32[16,2,9,4,128]{4,3,2,1,0:T(4,128)S(1)}, u32[]{:S(2)}, u32[]{:S(2)}) async-start(f32[16,2,9,4,128]{4,3,2,1,0:T(4,128)} %get-tuple-element.95), calls=%async_computation | async-start | bytes 1179648 | tf_op jit(solution)/shard_map/all_to_all | solution.py:607

commit v7 on v6

--- a/solution.py
+++ b/solution.py
@@ -258,7 +258,7 @@
 
 
 def begin_kernel(
-    pack_ref, adjoint_ref,
+    pack_ref, part0, part1, part2,
     v_ref, ty_ref, t_ref, mat_ref, send_x_ref, send_y_ref, p0, p1, p2, p3, turn_ref, small_ref,
 ):
     low_row = lax.broadcasted_iota(jnp.int32, (1, 128), 1) < 64
@@ -271,7 +271,7 @@
     send_table(pack_ref, send_x_ref, send_y_ref, small_ref)
     low = lax.broadcasted_iota(jnp.int32, (64, 128), 1) < 64
     for i in range(9):
-        x = adjoint_ref[i]
+        x = (part0, part1, part2)[i // 3][i % 3]
         turn = turn_ref.at[i % 3]
         turn[...] = jnp.concatenate([x, x], axis=0).T
         for j in range(4):
@@ -547,8 +547,8 @@
         begin_kernel,
         [state, table_y, table, shape(3, 8, 128), sent, sent] + payload,
         [pltpu.VMEM((3, NODES, 128), F32), pltpu.VMEM((128, 128), F32)],
-        count=2,
-    )(pack, adjoint)
+        count=4,
+    )(pack, adjoint[0:3], adjoint[3:6], adjoint[6:9])
     v, ty, t, mat, send_x, send_y = outs[:6]
     out_going = outs[6:]
     pairs = exchange_pairs()

time: 61.8 us -> 61.2 us (level)
  other arithmetic: 1.14 us -> 0.43 us
    slice x0 -> x1, local copies, waits for them, and re-layouts: none -> 1.36 us  [shards(): adjoint[6:9]]
    unnamed x14 -> x16, local copies, waits for them, and re-layouts: 1.3 us -> 0.04 us
    add x1, other arithmetic: 0.72 us -> 0.01 us  [shards(): lax.pad(material[None], zero, ((0, 0, 0), (0, 5, 0), (0, 64, 0)))]
where the time goes in v7:
time: 61.2 us; the launch traced here: 60.9 us
  starting transfers between devices  27.3 us (45%)
  Pallas kernels  20.3 us (33%)
  waiting for transfers between devices  10.6 us (17%)
  local copies, waits for them, and re-layouts  1.4 us (2%)
  between operations  0.85 us (1%)
    ppermute x16, starting transfers between devices, shards(): arrived = [lax.ppermute(out_going[k], *pairs[k]) for k in order]  21.7 us
    all_to_all x1, waiting for transfers between devices, shards(): lax.all_to_all(away, 'seg', split_axis=0, concat_axis=0, tiled=True)  8.46 us
    all_to_all x1, starting transfers between devices, shards(): lax.all_to_all(away, 'seg', split_axis=0, concat_axis=0, tiled=True)  5.66 us
    pallas_call x2, Pallas kernels, shards(): call(functools.partial(volume_kernel, factor), [state, face_part, state],...  4.5 us
    pallas_call x1, Pallas kernels, shards(): call(next_kernel, [shape(9, E_DEV, NODES)], [turn], count=1)(total)[0]  3.1 us
    pallas_call x1, Pallas kernels, shards(): call(functools.partial(end_kernel, factor, order), [state, shape(9, 4, P_...  3.09 us
    pallas_call x3, Pallas kernels, shards(): call(functools.partial(finish_kernel, factor, order), [state, table_y, ta...  2.6 us
    ppermute x16, waiting for transfers between devices, shards(): arrived = [lax.ppermute(out_going[k], *pairs[k]) for k in order]  2.11 us
  transfers between devices with their start and end apart: 17, of which 5 were waited for; matrix products, arithmetic and copies ran while one was open for 1% of the time, Pallas kernels for 19%

profile of v7, /device:TPU:0, one launch (start us, length us, event | category | flops | bytes accessed | tf_op | source)
XLA Modules:
  0.0 60.9 jit_solution(13053450740121798600)
XLA Ops:
  0.6 1.4 %fusion.2 = (f32[3,64,512]{2,1,0:T(8,128)S(1)}, f32[3,64,512]{2,1,0:T(8,128)S(1)}, f32[3,64,512]{2,1,0:T(8,128)S(1)}) fusion(f32[9,64,512]{2,1,0:T(8,128)} %param.9), kind=kLoop, calls=%fused_computation.18 | loop fusion | bytes 2359296 | tf_op jit(solution)/shard_map/slice | solution.py:551
  2.0 0.0 copy-start.4
  2.0 0.0 copy-start.3
  2.1 1.5 %shard_map.104 = (f32[9,4,64,128]{3,2,1,0:T(8,128)S(1)}, bf16[384,256]{1,0:T(8,128)(2,1)S(1)}, bf16[384,512]{1,0:T(8,128)(2,1)S(1)}, f32[3,8,128]{2,1,0:T(8,128)...) custom-call(f32[1,8,128]{2,1,0:T(8,128)S(1)} %convert_add_fusion.pac, ...), custom_call_target="tpu_custom_call" | custom-call | flops 100000000 | bytes 6000000 | tf_op jit(solution)/shard_map/pallas_call | solution.py:546
  3.6 6.6 %collective-permute-start = (f32[16,384]{1,0:T(8,128)S(1)}, f32[16,384]{1,0:T(8,128)S(1)}, u32[]{:S(2)}, u32[]{:S(2)}) collective-permute-start(f32[16,384]{1,0:T(8,128)S(1)} %get-tuple-element.55), channel_id=1, source_target_pairs={{1,2},{3,4},{5,6},{7,8},{9,10},{11,12},{13,14},{15,0},{2,1},{4,3},... | collective-permute-start | bytes 73736 | tf_op jit(solution)/shard_map/ppermute | solution.py:558
  10.3 0.0 collective-permute-start.1
  10.3 1.9 %collective-permute-start.2 = (f32[16,384]{1,0:T(8,128)S(1)}, f32[16,384]{1,0:T(8,128)S(1)}, u32[]{:S(2)}, u32[]{:S(2)}) collective-permute-start(f32[16,384]{1,0:T(8,128)S(1)} %get-tuple-element.57), channel_id=1, source_target_pairs={{16,32},{48,64},{80,96},{112,0},{32,16},{64,48},{96,80},{0,112},{1... | collective-permute-start | bytes 73736 | tf_op jit(solution)/shard_map/ppermute | solution.py:558
  12.2 0.0 collective-permute-start.3
  12.3 0.1 convert_reduce_fusion
  12.4 2.1 %shard_map.105 = (f32[9,4,64,128]{3,2,1,0:T(8,128)S(1)}, f32[384,384]{1,0:T(8,128)S(1)}, bf16[256,384]{1,0:T(8,128)(2,1)S(1)}, bf16[512,384]{1,0:T(8,128)(2,1)S(1)}, bf16[128,384]{1,0:T(8,128)(2,1)S(1)}) custom-call(f32[8,128]{1,0:T(8,128)S(1)} %pad.10.faces_ref, f32[9,4,64,128]{3,2,1,0:T(8,128)S(1)} %get-tuple-element.49.v_ref.acc_ref, ...), custom_call_target="tpu_custom_call" | custom-call | flops 100000000 | bytes 6000000 | tf_op jit(solution)/shard_map/pallas_call | solution.py:560
  14.4 0.0 collective-permute-done.ra
  14.5 0.0 collective-permute-done.1.rb
  14.5 0.3 collective-permute-done.2.rc
  14.7 0.0 collective-permute-done.3.rd
  14.7 0.9 %shard_map.106 = (f32[9,4,64,128]{3,2,1,0:T(8,128)S(1)}, bf16[384,256]{1,0:T(8,128)(2,1)S(1)}, bf16[384,512]{1,0:T(8,128)(2,1)S(1)}, f32[16,384]{1,0:T(8,128)S(1...) custom-call(f32[9,4,64,128]{3,2,1,0:T(8,128)S(1)} %get-tuple-element, ...), custom_call_target="tpu_custom_call", output_to_operand_aliasing={{0}: (0, {})} | custom-call | flops 100000000 | bytes 6000000 | tf_op jit(solution)/shard_map/pallas_call | solution.py:581
  15.6 2.8 %collective-permute-start.4 = (f32[16,384]{1,0:T(8,128)S(1)}, f32[16,384]{1,0:T(8,128)S(1)}, u32[]{:S(2)}, u32[]{:S(2)}) collective-permute-start(f32[16,384]{1,0:T(8,128)S(1)} %get-tuple-element.69), channel_id=1, source_target_pairs={{1,2},{3,4},{5,6},{7,8},{9,10},{11,12},{13,14},{15,0},{2,1},{4,3},... | collective-permute-start | bytes 73736 | tf_op jit(solution)/shard_map/ppermute | solution.py:558
  18.4 0.0 collective-permute-start.5
  18.4 0.8 %collective-permute-start.6 = (f32[16,384]{1,0:T(8,128)S(1)}, f32[16,384]{1,0:T(8,128)S(1)}, u32[]{:S(2)}, u32[]{:S(2)}) collective-permute-start(f32[16,384]{1,0:T(8,128)S(1)} %get-tuple-element.71), channel_id=1, source_target_pairs={{16,32},{48,64},{80,96},{112,0},{32,16},{64,48},{96,80},{0,112},{1... | collective-permute-start | bytes 73736 | tf_op jit(solution)/shard_map/ppermute | solution.py:558
  19.1 0.8 %collective-permute-start.7 = (f32[16,384]{1,0:T(8,128)S(1)}, f32[16,384]{1,0:T(8,128)S(1)}, u32[]{:S(2)}, u32[]{:S(2)}) collective-permute-start(f32[16,384]{1,0:T(8,128)S(1)} %get-tuple-element.72), channel_id=1, source_target_pairs={{0,16},{32,48},{64,80},{96,112},{16,0},{48,32},{80,64},{112,96},{1... | collective-permute-start | bytes 73736 | tf_op jit(solution)/shard_map/ppermute | solution.py:558
  20.0 2.2 %shard_map.107 = (f32[9,4,64,128]{3,2,1,0:T(8,128)S(1)}, f32[384,384]{1,0:T(8,128)S(1)}, f32[9,4,64,128]{3,2,1,0:T(8,128)S(1)}) custom-call(f32[9,4,64,128]{3,2,1,0:T(8,128)S(1)} %get-tuple-element.62.v_ref, bf16[384,256]{1,0:T(8,128)(2,1)S(1)} %get-tuple-element.63.ty_ref, bf16[384,512]{1,0:T(8,128)(2,1)S(1)} %get-tuple-element.64.t_ref, ...), custom_call_target="tpu_custom_call" | custom-call | flops 100000000 | bytes 6000000 | tf_op jit(solution)/shard_map/pallas_call | solution.py:573
  22.2 0.6 %collective-permute-done.4.ra = f32[16,384]{1,0:T(8,128)S(1)} collective-permute-done((f32[16,384]{1,0:T(8,128)S(1)}, f32[16,384]{1,0:T(8,128)S(1)}, u32[]{:S(2)}, u32[]{:S(2)}) %collective-permute-start.4) | collective-permute-done | bytes 24608 | tf_op jit(solution)/shard_map/ppermute | solution.py:558
  22.8 0.0 collective-permute-done.6.rc
  22.8 0.0 collective-permute-done.7.rd
  22.8 0.9 %shard_map.108 = (f32[9,4,64,128]{3,2,1,0:T(8,128)S(1)}, bf16[384,256]{1,0:T(8,128)(2,1)S(1)}, bf16[384,512]{1,0:T(8,128)(2,1)S(1)}, f32[16,384]{1,0:T(8,128)S(1...) custom-call(f32[9,4,64,128]{3,2,1,0:T(8,128)S(1)} %get-tuple-element, ...), custom_call_target="tpu_custom_call", output_to_operand_aliasing={{0}: (0, {})} | custom-call | flops 100000000 | bytes 6000000 | tf_op jit(solution)/shard_map/pallas_call | solution.py:581
  23.7 2.8 %collective-permute-start.10 = (f32[16,384]{1,0:T(8,128)S(1)}, f32[16,384]{1,0:T(8,128)S(1)}, u32[]{:S(2)}, u32[]{:S(2)}) collective-permute-start(f32[16,384]{1,0:T(8,128)S(1)} %get-tuple-element.81), channel_id=1, source_target_pairs={{1,2},{3,4},{5,6},{7,8},{9,10},{11,12},{13,14},{15,0},{2,1},{4,3},... | collective-permute-start | bytes 73736 | tf_op jit(solution)/shard_map/ppermute | solution.py:558
  26.5 1.6 %collective-permute-start.8 = (f32[16,384]{1,0:T(8,128)S(1)}, f32[16,384]{1,0:T(8,128)S(1)}, u32[]{:S(2)}, u32[]{:S(2)}) collective-permute-start(f32[16,384]{1,0:T(8,128)S(1)} %get-tuple-element.79), channel_id=1, source_target_pairs={{16,32},{48,64},{80,96},{112,0},{32,16},{64,48},{96,80},{0,112},{1... | collective-permute-start | bytes 73736 | tf_op jit(solution)/shard_map/ppermute | solution.py:558
  28.1 0.1 select_reduce_fusion.keys_ref
  28.2 2.3 %shard_map.109 = (f32[9,4,64,128]{3,2,1,0:T(8,128)S(1)}, f32[384,384]{1,0:T(8,128)S(1)}, f32[9,4,64,128]{3,2,1,0:T(8,128)S(1)}) custom-call(f32[9,4,64,128]{3,2,1,0:T(8,128)S(1)} %get-tuple-element.73.v_ref, bf16[384,256]{1,0:T(8,128)(2,1)S(1)} %get-tuple-element.74.ty_ref, bf16[384,512]{1,0:T(8,128)(2,1)S(1)} %get-tuple-element.75.t_ref, ...), custom_call_target="tpu_custom_call" | custom-call | flops 100000000 | bytes 6000000 | tf_op jit(solution)/shard_map/pallas_call | solution.py:573
  30.5 0.4 collective-permute-done.10.rc
  30.9 0.0 collective-permute-done.11.rd
  30.9 0.0 collective-permute-done.8.ra
  30.9 0.0 collective-permute-done.9.rb
  30.9 0.9 %shard_map.110 = (f32[9,4,64,128]{3,2,1,0:T(8,128)S(1)}, bf16[384,256]{1,0:T(8,128)(2,1)S(1)}, bf16[384,512]{1,0:T(8,128)(2,1)S(1)}, f32[16,384]{1,0:T(8,128)S(1...) custom-call(f32[9,4,64,128]{3,2,1,0:T(8,128)S(1)} %get-tuple-element, ...), custom_call_target="tpu_custom_call", output_to_operand_aliasing={{0}: (0, {})} | custom-call | flops 100000000 | bytes 6000000 | tf_op jit(solution)/shard_map/pallas_call | solution.py:581
  31.8 2.8 %collective-permute-start.12 = (f32[16,384]{1,0:T(8,128)S(1)}, f32[16,384]{1,0:T(8,128)S(1)}, u32[]{:S(2)}, u32[]{:S(2)}) collective-permute-start(f32[16,384]{1,0:T(8,128)S(1)} %get-tuple-element.89), channel_id=1, source_target_pairs={{1,2},{3,4},{5,6},{7,8},{9,10},{11,12},{13,14},{15,0},{2,1},{4,3},... | collective-permute-start | bytes 73736 | tf_op jit(solution)/shard_map/ppermute | solution.py:558
  34.6 0.6 %collective-permute-start.14 = (f32[16,384]{1,0:T(8,128)S(1)}, f32[16,384]{1,0:T(8,128)S(1)}, u32[]{:S(2)}, u32[]{:S(2)}) collective-permute-start(f32[16,384]{1,0:T(8,128)S(1)} %get-tuple-element.91), channel_id=1, source_target_pairs={{16,32},{48,64},{80,96},{112,0},{32,16},{64,48},{96,80},{0,112},{1... | collective-permute-start | bytes 73736 | tf_op jit(solution)/shard_map/ppermute | solution.py:558
  35.2 1.0 %collective-permute-start.15 = (f32[16,384]{1,0:T(8,128)S(1)}, f32[16,384]{1,0:T(8,128)S(1)}, u32[]{:S(2)}, u32[]{:S(2)}) collective-permute-start(f32[16,384]{1,0:T(8,128)S(1)} %get-tuple-element.92), channel_id=1, source_target_pairs={{0,16},{32,48},{64,80},{96,112},{16,0},{48,32},{80,64},{112,96},{1... | collective-permute-start | bytes 73736 | tf_op jit(solution)/shard_map/ppermute | solution.py:558
  36.2 0.1 add_bitcast_fusion.place_ref
  36.3 2.0 %shard_map.111 = (f32[9,4,64,128]{3,2,1,0:T(8,128)S(1)}, f32[384,384]{1,0:T(8,128)S(1)}) custom-call(f32[9,4,64,128]{3,2,1,0:T(8,128)S(1)} %get-tuple-element.83.v_ref, bf16[384,256]{1,0:T(8,128)(2,1)S(1)} %get-tuple-element.84.ty_ref, bf16[384,512]{1,0:T(8,128)(2,1)S(1)} %get-tuple-element.85.t_ref, bf16[256,384]{1,0:T(8,128)(2,1)S(1)} %get-tuple-element.65.local_y_ref, ...), custom_call_target="tpu_custom_call" | custom-call | flops 100000000 | bytes 6000000 | tf_op jit(solution)/shard_map/pallas_call | solution.py:577
  38.3 0.8 %collective-permute-done.12.ra = f32[16,384]{1,0:T(8,128)S(1)} collective-permute-done((f32[16,384]{1,0:T(8,128)S(1)}, f32[16,384]{1,0:T(8,128)S(1)}, u32[]{:S(2)}, u32[]{:S(2)}) %collective-permute-start.12) | collective-permute-done | bytes 24608 | tf_op jit(solution)/shard_map/ppermute | solution.py:558
  39.0 0.0 collective-permute-done.13.rb
  39.0 0.0 collective-permute-done.14.rc
  39.1 3.1 %shard_map.112 = (f32[9,4,64,128]{3,2,1,0:T(8,128)S(1)}, f32[9,4,8,128]{3,2,1,0:T(8,128)S(1)}, f32[16,2,9,4,128]{4,3,2,1,0:T(4,128)}) custom-call(s32[8]{0:T(128)S(1)} %select_reduce_fusion.keys_ref, f32[9,4,64,128]{3,2,1,0:T(8,128)S(1)} %get-tuple-element.87.vol_ref, f32[384,384]{1,0:T(8,128)S(1)} %get-tuple-element.88.part_ref, ...), custom_call_target="tpu_custom_call", output_to_operand_aliasing={{0}: (1, {})} | custom-call | flops 100000000 | bytes 6000000 | tf_op jit(solution)/shard_map/pallas_call | solution.py:590
  42.2 0.0 copy-start.7
  42.2 5.7 %all-to-all-start = ((f32[16,2,9,4,128]{4,3,2,1,0:T(4,128)}), f32[16,2,9,4,128]{4,3,2,1,0:T(4,128)S(1)}, u32[]{:S(2)}, u32[]{:S(2)}) async-start(f32[16,2,9,4,128]{4,3,2,1,0:T(4,128)} %get-tuple-element.95), calls=%async_computation | async-start | bytes 1179648 | tf_op jit(solution)/shard_map/all_to_all | solution.py:607
  47.8 0.1 convert_reduce_fusion.1
  48.0 3.1 %shard_map.113 = f32[9,64,512]{2,1,0:T(8,128)} custom-call(f32[9,4,64,128]{3,2,1,0:T(8,128)S(1)} %get-tuple-element.93.total_ref), custom_call_target="tpu_custom_call" | custom-call | flops 100000000 | bytes 6000000 | tf_op jit(solution)/shard_map/pallas_call | solution.py:608
  51.1 8.5 %all-to-all-done.arrived_ref = f32[16,2,9,4,128]{4,3,2,1,0:T(4,128)S(1)} async-done(((f32[16,2,9,4,128]{4,3,2,1,0:T(4,128)}), f32[16,2,9,4,128]{4,3,2,1,0:T(4,128)S(1)}, u32[]{:S(2)}, u32[]{:S(2)}) %all-to-all-start) | async-done | bytes 589856 | tf_op jit(solution)/shard_map/all_to_all | solution.py:607
  59.5 1.4 %shard_map.114 = f32[9,8,512]{2,1,0:T(8,128)} custom-call(s32[2,8]{1,0:T(2,128)S(1)} %pad_add_fusion.table_ref, f32[9,4,8,128]{3,2,1,0:T(8,128)S(1)} %get-tuple-element.94.groups_ref, f32[16,2,9,4,128]{4,3,2,1,0:T(4,128)S(1)} %all-to-all-done.arrived_ref), custom_call_target="tpu_custom_call" | custom-call | flops 100000000 | bytes 6000000 | tf_op jit(solution)/shard_map/pallas_call | solution.py:609
  (27 shorter events, 0.1 us)
Async XLA Ops:
  0.6 1.4 %copy-start.6 = (f32[3,64]{1,0:T(4,128)S(1)}, f32[3,64]{1,0:T(4,128)}, u32[]{:S(2)}) copy-start(f32[3,64]{1,0:T(4,128)} %param.10) | copy-start | bytes 2308
  0.6 1.4 %copy-start.5 = (s32[1,4,16]{2,1,0:T(4,128)S(1)}, s32[1,4,16]{2,1,0:T(4,128)}, u32[]{:S(2)}) copy-start(s32[1,4,16]{2,1,0:T(4,128)} %param.12) | copy-start | bytes 772
  2.0 10.2 %copy-start.4 = (s32[3,64]{1,0:T(4,128)S(1)}, s32[3,64]{1,0:T(4,128)}, u32[]{:S(2)}) copy-start(s32[3,64]{1,0:T(4,128)} %param.13) | copy-start | bytes 2308
  2.0 10.2 %copy-start.3 = (s32[64,6]{0,1:T(8,128)S(1)}, s32[64,6]{0,1:T(8,128)}, u32[]{:S(2)}) copy-start(s32[64,6]{0,1:T(8,128)} %param.11) | copy-start | bytes 4612
  3.6 10.8 %collective-permute-start = (f32[16,384]{1,0:T(8,128)S(1)}, f32[16,384]{1,0:T(8,128)S(1)}, u32[]{:S(2)}, u32[]{:S(2)}) collective-permute-start(f32[16,384]{1,0:T(8,128)S(1)} %get-tuple-element.55), channel_id=1, source_target_pairs={{1,2},{3,4},{5,6},{7,8},{9,10},{11,12},{13,14},{15,0},{2,1},{4,3},... | collective-permute-start | bytes 73736 | tf_op jit(solution)/shard_map/ppermute | solution.py:558
  10.3 4.2 %collective-permute-start.1 = (f32[16,384]{1,0:T(8,128)S(1)}, f32[16,384]{1,0:T(8,128)S(1)}, u32[]{:S(2)}, u32[]{:S(2)}) collective-permute-start(f32[16,384]{1,0:T(8,128)S(1)} %get-tuple-element.56), channel_id=1, source_target_pairs={{0,1},{2,3},{4,5},{6,7},{8,9},{10,11},{12,13},{14,15},{1,0},{3,2},... | collective-permute-start | bytes 73736 | tf_op jit(solution)/shard_map/ppermute | solution.py:558
  10.3 4.5 %collective-permute-start.2 = (f32[16,384]{1,0:T(8,128)S(1)}, f32[16,384]{1,0:T(8,128)S(1)}, u32[]{:S(2)}, u32[]{:S(2)}) collective-permute-start(f32[16,384]{1,0:T(8,128)S(1)} %get-tuple-element.57), channel_id=1, source_target_pairs={{16,32},{48,64},{80,96},{112,0},{32,16},{64,48},{96,80},{0,112},{1... | collective-permute-start | bytes 73736 | tf_op jit(solution)/shard_map/ppermute | solution.py:558
  12.2 2.5 %collective-permute-start.3 = (f32[16,384]{1,0:T(8,128)S(1)}, f32[16,384]{1,0:T(8,128)S(1)}, u32[]{:S(2)}, u32[]{:S(2)}) collective-permute-start(f32[16,384]{1,0:T(8,128)S(1)} %get-tuple-element.58), channel_id=1, source_target_pairs={{0,16},{32,48},{64,80},{96,112},{16,0},{48,32},{80,64},{112,96},{1... | collective-permute-start | bytes 73736 | tf_op jit(solution)/shard_map/ppermute | solution.py:558
  15.6 7.2 %collective-permute-start.4 = (f32[16,384]{1,0:T(8,128)S(1)}, f32[16,384]{1,0:T(8,128)S(1)}, u32[]{:S(2)}, u32[]{:S(2)}) collective-permute-start(f32[16,384]{1,0:T(8,128)S(1)} %get-tuple-element.69), channel_id=1, source_target_pairs={{1,2},{3,4},{5,6},{7,8},{9,10},{11,12},{13,14},{15,0},{2,1},{4,3},... | collective-permute-start | bytes 73736 | tf_op jit(solution)/shard_map/ppermute | solution.py:558
  18.4 4.5 %collective-permute-start.5 = (f32[16,384]{1,0:T(8,128)S(1)}, f32[16,384]{1,0:T(8,128)S(1)}, u32[]{:S(2)}, u32[]{:S(2)}) collective-permute-start(f32[16,384]{1,0:T(8,128)S(1)} %get-tuple-element.70), channel_id=1, source_target_pairs={{0,1},{2,3},{4,5},{6,7},{8,9},{10,11},{12,13},{14,15},{1,0},{3,2},... | collective-permute-start | bytes 73736 | tf_op jit(solution)/shard_map/ppermute | solution.py:558
  18.4 4.5 %collective-permute-start.6 = (f32[16,384]{1,0:T(8,128)S(1)}, f32[16,384]{1,0:T(8,128)S(1)}, u32[]{:S(2)}, u32[]{:S(2)}) collective-permute-start(f32[16,384]{1,0:T(8,128)S(1)} %get-tuple-element.71), channel_id=1, source_target_pairs={{16,32},{48,64},{80,96},{112,0},{32,16},{64,48},{96,80},{0,112},{1... | collective-permute-start | bytes 73736 | tf_op jit(solution)/shard_map/ppermute | solution.py:558
  19.1 3.7 %collective-permute-start.7 = (f32[16,384]{1,0:T(8,128)S(1)}, f32[16,384]{1,0:T(8,128)S(1)}, u32[]{:S(2)}, u32[]{:S(2)}) collective-permute-start(f32[16,384]{1,0:T(8,128)S(1)} %get-tuple-element.72), channel_id=1, source_target_pairs={{0,16},{32,48},{64,80},{96,112},{16,0},{48,32},{80,64},{112,96},{1... | collective-permute-start | bytes 73736 | tf_op jit(solution)/shard_map/ppermute | solution.py:558
  23.7 7.2 %collective-permute-start.10 = (f32[16,384]{1,0:T(8,128)S(1)}, f32[16,384]{1,0:T(8,128)S(1)}, u32[]{:S(2)}, u32[]{:S(2)}) collective-permute-start(f32[16,384]{1,0:T(8,128)S(1)} %get-tuple-element.81), channel_id=1, source_target_pairs={{1,2},{3,4},{5,6},{7,8},{9,10},{11,12},{13,14},{15,0},{2,1},{4,3},... | collective-permute-start | bytes 73736 | tf_op jit(solution)/shard_map/ppermute | solution.py:558
  26.5 4.5 %collective-permute-start.11 = (f32[16,384]{1,0:T(8,128)S(1)}, f32[16,384]{1,0:T(8,128)S(1)}, u32[]{:S(2)}, u32[]{:S(2)}) collective-permute-start(f32[16,384]{1,0:T(8,128)S(1)} %get-tuple-element.82), channel_id=1, source_target_pairs={{0,1},{2,3},{4,5},{6,7},{8,9},{10,11},{12,13},{14,15},{1,0},{3,2},... | collective-permute-start | bytes 73736 | tf_op jit(solution)/shard_map/ppermute | solution.py:558
  26.5 4.5 %collective-permute-start.8 = (f32[16,384]{1,0:T(8,128)S(1)}, f32[16,384]{1,0:T(8,128)S(1)}, u32[]{:S(2)}, u32[]{:S(2)}) collective-permute-start(f32[16,384]{1,0:T(8,128)S(1)} %get-tuple-element.79), channel_id=1, source_target_pairs={{16,32},{48,64},{80,96},{112,0},{32,16},{64,48},{96,80},{0,112},{1... | collective-permute-start | bytes 73736 | tf_op jit(solution)/shard_map/ppermute | solution.py:558
  28.1 2.9 %collective-permute-start.9 = (f32[16,384]{1,0:T(8,128)S(1)}, f32[16,384]{1,0:T(8,128)S(1)}, u32[]{:S(2)}, u32[]{:S(2)}) collective-permute-start(f32[16,384]{1,0:T(8,128)S(1)} %get-tuple-element.80), channel_id=1, source_target_pairs={{0,16},{32,48},{64,80},{96,112},{16,0},{48,32},{80,64},{112,96},{1... | collective-permute-start | bytes 73736 | tf_op jit(solution)/shard_map/ppermute | solution.py:558
  31.8 7.2 %collective-permute-start.12 = (f32[16,384]{1,0:T(8,128)S(1)}, f32[16,384]{1,0:T(8,128)S(1)}, u32[]{:S(2)}, u32[]{:S(2)}) collective-permute-start(f32[16,384]{1,0:T(8,128)S(1)} %get-tuple-element.89), channel_id=1, source_target_pairs={{1,2},{3,4},{5,6},{7,8},{9,10},{11,12},{13,14},{15,0},{2,1},{4,3},... | collective-permute-start | bytes 73736 | tf_op jit(solution)/shard_map/ppermute | solution.py:558
  34.6 4.5 %collective-permute-start.13 = (f32[16,384]{1,0:T(8,128)S(1)}, f32[16,384]{1,0:T(8,128)S(1)}, u32[]{:S(2)}, u32[]{:S(2)}) collective-permute-start(f32[16,384]{1,0:T(8,128)S(1)} %get-tuple-element.90), channel_id=1, source_target_pairs={{0,1},{2,3},{4,5},{6,7},{8,9},{10,11},{12,13},{14,15},{1,0},{3,2},... | collective-permute-start | bytes 73736 | tf_op jit(solution)/shard_map/ppermute | solution.py:558
  34.6 4.5 %collective-permute-start.14 = (f32[16,384]{1,0:T(8,128)S(1)}, f32[16,384]{1,0:T(8,128)S(1)}, u32[]{:S(2)}, u32[]{:S(2)}) collective-permute-start(f32[16,384]{1,0:T(8,128)S(1)} %get-tuple-element.91), channel_id=1, source_target_pairs={{16,32},{48,64},{80,96},{112,0},{32,16},{64,48},{96,80},{0,112},{1... | collective-permute-start | bytes 73736 | tf_op jit(solution)/shard_map/ppermute | solution.py:558
  35.2 3.8 %collective-permute-start.15 = (f32[16,384]{1,0:T(8,128)S(1)}, f32[16,384]{1,0:T(8,128)S(1)}, u32[]{:S(2)}, u32[]{:S(2)}) collective-permute-start(f32[16,384]{1,0:T(8,128)S(1)} %get-tuple-element.92), channel_id=1, source_target_pairs={{0,16},{32,48},{64,80},{96,112},{16,0},{48,32},{80,64},{112,96},{1... | collective-permute-start | bytes 73736 | tf_op jit(solution)/shard_map/ppermute | solution.py:558
  36.3 2.8 %copy-start = (f32[64,8,128]{2,1,0:T(8,128)S(1)}, f32[64,8,128]{2,1,0:T(8,128)}, u32[]{:S(2)}) copy-start(f32[64,8,128]{2,1,0:T(8,128)} %constant.24.clone.lines_ref) | copy-start | bytes 786436
  36.3 2.8 %copy-start.1 = (bf16[256,128]{1,0:T(8,128)(2,1)S(1)}, bf16[256,128]{1,0:T(8,128)(2,1)}, u32[]{:S(2)}) copy-start(bf16[256,128]{1,0:T(8,128)(2,1)} %constant.22.clone.wa_ref) | copy-start | bytes 196612
  36.3 2.8 %copy-start.2 = (bf16[256,128]{1,0:T(8,128)(2,1)S(1)}, bf16[256,128]{1,0:T(8,128)(2,1)}, u32[]{:S(2)}) copy-start(bf16[256,128]{1,0:T(8,128)(2,1)} %constant.23.clone.wb_ref) | copy-start | bytes 196612
  42.2 5.8 %copy-start.7 = (s32[2,8]{1,0:T(2,128)S(1)}, s32[2,8]{1,0:T(2,128)}, u32[]{:S(2)}) copy-start(s32[2,8]{1,0:T(2,128)} %param.14) | copy-start | bytes 196
  42.2 17.3 %all-to-all-start = ((f32[16,2,9,4,128]{4,3,2,1,0:T(4,128)}), f32[16,2,9,4,128]{4,3,2,1,0:T(4,128)S(1)}, u32[]{:S(2)}, u32[]{:S(2)}) async-start(f32[16,2,9,4,128]{4,3,2,1,0:T(4,128)} %get-tuple-element.95), calls=%async_computation | async-start | bytes 1179648 | tf_op jit(solution)/shard_map/all_to_all | solution.py:607

commit v8 on v7

--- a/solution.py
+++ b/solution.py
@@ -453,7 +453,16 @@
             send(g).wait()
 
 
-def next_kernel(total_ref, next_ref, turn_ref):
+def next_kernel(table_ref, total_ref, groups_ref, next_ref, home_ref, turn_ref):
+    home_ref[...] = jnp.zeros_like(home_ref)
+    for p in range(P_DEV):
+
+        @pl.when(table_ref[1, p] < 0)
+        def _():
+            for i in range(9):
+                for t in range(4):
+                    home_ref[i, pl.ds(p, 1), pl.ds(128 * t, 128)] = groups_ref[i, t, pl.ds(table_ref[0, p], 1), :]
+
     def body(i, carry):
         for j in range(4):
             tile = total_ref[i, j]
@@ -465,16 +474,11 @@
     lax.fori_loop(0, 9, body, 0)
 
 
-def parent_kernel(table_ref, groups_ref, arrived_ref, out_ref):
+def parent_kernel(table_ref, home_ref, arrived_ref, out_ref):
+    out_ref[...] = home_ref[...]
     for p in range(P_DEV):
         holder = table_ref[0, p]
         slot = table_ref[1, p]
-
-        @pl.when(slot < 0)
-        def _():
-            for i in range(9):
-                for t in range(4):
-                    out_ref[i, pl.ds(p, 1), pl.ds(128 * t, 128)] = groups_ref[i, t, pl.ds(holder, 1), :]
 
         @pl.when(slot >= 0)
         def _():
@@ -605,8 +609,10 @@
         count=12,
     )(keys, vol, part, *arrived, remote_hot, place, wa, wb, lines)
     fetched = lax.all_to_all(away, "seg", split_axis=0, concat_axis=0, tiled=True)
-    updated = call(next_kernel, [shape(9, E_DEV, NODES)], [turn], count=1)(total)[0]
-    parents = call(parent_kernel, [shape(9, P_DEV, NODES)], smem=(0,), count=3)(source, groups, fetched)[0]
+    updated, home = call(
+        next_kernel, [shape(9, E_DEV, NODES), shape(9, P_DEV, NODES)], [turn], smem=(0,), count=3
+    )(source, total, groups)
+    parents = call(parent_kernel, [shape(9, P_DEV, NODES)], smem=(0,), count=3)(source, home, fetched)[0]
     return (updated, parents)
 
 

time: 61.2 us -> 61.1 us (level)
  waiting for transfers between devices: 10.6 us -> 9.88 us
    all_to_all x1, waiting for transfers between devices: 8.46 us -> 7.77 us  [shards(): lax.all_to_all(away, 'seg', split_axis=0, concat_axis=0, tiled=True)]
    pallas_call x1, Pallas kernels: 3.1 us -> 3.77 us  [shards(): call(next_kernel, [shape(9, E_DEV, NODES), shape(9, P_DEV, NODES)], [turn...]
  transfers between devices with their start and end apart: 17 -> 17, of which waited for: 5 -> 5; matrix products, arithmetic and copies ran while one was open for 1% -> 1% of each run, Pallas kernels for 19% -> 20%
where the time goes in v8:
time: 61.1 us; the launch traced here: 60.8 us
  starting transfers between devices  27.3 us (45%)
  Pallas kernels  20.9 us (34%)
  waiting for transfers between devices  9.88 us (16%)
  local copies, waits for them, and re-layouts  1.4 us (2%)
  between operations  0.85 us (1%)
    ppermute x16, starting transfers between devices, shards(): arrived = [lax.ppermute(out_going[k], *pairs[k]) for k in order]  21.7 us
    all_to_all x1, waiting for transfers between devices, shards(): lax.all_to_all(away, 'seg', split_axis=0, concat_axis=0, tiled=True)  7.77 us
    all_to_all x1, starting transfers between devices, shards(): lax.all_to_all(away, 'seg', split_axis=0, concat_axis=0, tiled=True)  5.65 us
    pallas_call x2, Pallas kernels, shards(): call(functools.partial(volume_kernel, factor), [state, face_part, state],...  4.5 us
    pallas_call x1, Pallas kernels, shards(): call(next_kernel, [shape(9, E_DEV, NODES), shape(9, P_DEV, NODES)], [turn...  3.77 us
    pallas_call x1, Pallas kernels, shards(): call(functools.partial(end_kernel, factor, order), [state, shape(9, 4, P_...  3.1 us
    pallas_call x3, Pallas kernels, shards(): call(functools.partial(finish_kernel, factor, order), [state, table_y, ta...  2.6 us
    ppermute x16, waiting for transfers between devices, shards(): arrived = [lax.ppermute(out_going[k], *pairs[k]) for k in order]  2.11 us
  transfers between devices with their start and end apart: 17, of which 5 were waited for; matrix products, arithmetic and copies ran while one was open for 1% of the time, Pallas kernels for 20%

profile of v8, /device:TPU:0, one launch (start us, length us, event | category | flops | bytes accessed | tf_op | source)
XLA Modules:
  0.0 60.8 jit_solution(5241309324853502605)
XLA Ops:
  0.6 1.4 %fusion.2 = (f32[3,64,512]{2,1,0:T(8,128)S(1)}, f32[3,64,512]{2,1,0:T(8,128)S(1)}, f32[3,64,512]{2,1,0:T(8,128)S(1)}) fusion(f32[9,64,512]{2,1,0:T(8,128)} %param.9), kind=kLoop, calls=%fused_computation.18 | loop fusion | bytes 2359296 | tf_op jit(solution)/shard_map/slice | solution.py:555
  2.0 0.0 copy-start.4
  2.0 0.0 copy-start.3
  2.1 1.5 %shard_map.104 = (f32[9,4,64,128]{3,2,1,0:T(8,128)S(1)}, bf16[384,256]{1,0:T(8,128)(2,1)S(1)}, bf16[384,512]{1,0:T(8,128)(2,1)S(1)}, f32[3,8,128]{2,1,0:T(8,128)...) custom-call(f32[1,8,128]{2,1,0:T(8,128)S(1)} %convert_add_fusion.pac, ...), custom_call_target="tpu_custom_call" | custom-call | flops 100000000 | bytes 6000000 | tf_op jit(solution)/shard_map/pallas_call | solution.py:550
  3.6 6.6 %collective-permute-start = (f32[16,384]{1,0:T(8,128)S(1)}, f32[16,384]{1,0:T(8,128)S(1)}, u32[]{:S(2)}, u32[]{:S(2)}) collective-permute-start(f32[16,384]{1,0:T(8,128)S(1)} %get-tuple-element.57), channel_id=1, source_target_pairs={{1,2},{3,4},{5,6},{7,8},{9,10},{11,12},{13,14},{15,0},{2,1},{4,3},... | collective-permute-start | bytes 73736 | tf_op jit(solution)/shard_map/ppermute | solution.py:562
  10.3 0.0 collective-permute-start.1
  10.3 1.9 %collective-permute-start.2 = (f32[16,384]{1,0:T(8,128)S(1)}, f32[16,384]{1,0:T(8,128)S(1)}, u32[]{:S(2)}, u32[]{:S(2)}) collective-permute-start(f32[16,384]{1,0:T(8,128)S(1)} %get-tuple-element.59), channel_id=1, source_target_pairs={{16,32},{48,64},{80,96},{112,0},{32,16},{64,48},{96,80},{0,112},{1... | collective-permute-start | bytes 73736 | tf_op jit(solution)/shard_map/ppermute | solution.py:562
  12.2 0.0 collective-permute-start.3
  12.3 0.1 convert_reduce_fusion
  12.4 2.1 %shard_map.105 = (f32[9,4,64,128]{3,2,1,0:T(8,128)S(1)}, f32[384,384]{1,0:T(8,128)S(1)}, bf16[256,384]{1,0:T(8,128)(2,1)S(1)}, bf16[512,384]{1,0:T(8,128)(2,1)S(1)}, bf16[128,384]{1,0:T(8,128)(2,1)S(1)}) custom-call(f32[8,128]{1,0:T(8,128)S(1)} %pad.10.faces_ref, f32[9,4,64,128]{3,2,1,0:T(8,128)S(1)} %get-tuple-element.51.v_ref.acc_ref, ...), custom_call_target="tpu_custom_call" | custom-call | flops 100000000 | bytes 6000000 | tf_op jit(solution)/shard_map/pallas_call | solution.py:564
  14.4 0.0 collective-permute-done.ra
  14.5 0.0 collective-permute-done.1.rb
  14.5 0.3 collective-permute-done.2.rc
  14.7 0.0 collective-permute-done.3.rd
  14.7 0.9 %shard_map.106 = (f32[9,4,64,128]{3,2,1,0:T(8,128)S(1)}, bf16[384,256]{1,0:T(8,128)(2,1)S(1)}, bf16[384,512]{1,0:T(8,128)(2,1)S(1)}, f32[16,384]{1,0:T(8,128)S(1...) custom-call(f32[9,4,64,128]{3,2,1,0:T(8,128)S(1)} %get-tuple-element, ...), custom_call_target="tpu_custom_call", output_to_operand_aliasing={{0}: (0, {})} | custom-call | flops 100000000 | bytes 6000000 | tf_op jit(solution)/shard_map/pallas_call | solution.py:585
  15.6 2.8 %collective-permute-start.4 = (f32[16,384]{1,0:T(8,128)S(1)}, f32[16,384]{1,0:T(8,128)S(1)}, u32[]{:S(2)}, u32[]{:S(2)}) collective-permute-start(f32[16,384]{1,0:T(8,128)S(1)} %get-tuple-element.71), channel_id=1, source_target_pairs={{1,2},{3,4},{5,6},{7,8},{9,10},{11,12},{13,14},{15,0},{2,1},{4,3},... | collective-permute-start | bytes 73736 | tf_op jit(solution)/shard_map/ppermute | solution.py:562
  18.4 0.8 %collective-permute-start.6 = (f32[16,384]{1,0:T(8,128)S(1)}, f32[16,384]{1,0:T(8,128)S(1)}, u32[]{:S(2)}, u32[]{:S(2)}) collective-permute-start(f32[16,384]{1,0:T(8,128)S(1)} %get-tuple-element.73), channel_id=1, source_target_pairs={{16,32},{48,64},{80,96},{112,0},{32,16},{64,48},{96,80},{0,112},{1... | collective-permute-start | bytes 73736 | tf_op jit(solution)/shard_map/ppermute | solution.py:562
  19.1 0.8 %collective-permute-start.7 = (f32[16,384]{1,0:T(8,128)S(1)}, f32[16,384]{1,0:T(8,128)S(1)}, u32[]{:S(2)}, u32[]{:S(2)}) collective-permute-start(f32[16,384]{1,0:T(8,128)S(1)} %get-tuple-element.74), channel_id=1, source_target_pairs={{0,16},{32,48},{64,80},{96,112},{16,0},{48,32},{80,64},{112,96},{1... | collective-permute-start | bytes 73736 | tf_op jit(solution)/shard_map/ppermute | solution.py:562
  20.0 2.2 %shard_map.107 = (f32[9,4,64,128]{3,2,1,0:T(8,128)S(1)}, f32[384,384]{1,0:T(8,128)S(1)}, f32[9,4,64,128]{3,2,1,0:T(8,128)S(1)}) custom-call(f32[9,4,64,128]{3,2,1,0:T(8,128)S(1)} %get-tuple-element.64.v_ref, bf16[384,256]{1,0:T(8,128)(2,1)S(1)} %get-tuple-element.65.ty_ref, bf16[384,512]{1,0:T(8,128)(2,1)S(1)} %get-tuple-element.66.t_ref, ...), custom_call_target="tpu_custom_call" | custom-call | flops 100000000 | bytes 6000000 | tf_op jit(solution)/shard_map/pallas_call | solution.py:577
  22.2 0.6 %collective-permute-done.4.ra = f32[16,384]{1,0:T(8,128)S(1)} collective-permute-done((f32[16,384]{1,0:T(8,128)S(1)}, f32[16,384]{1,0:T(8,128)S(1)}, u32[]{:S(2)}, u32[]{:S(2)}) %collective-permute-start.4) | collective-permute-done | bytes 24608 | tf_op jit(solution)/shard_map/ppermute | solution.py:562
  22.8 0.0 collective-permute-done.6.rc
  22.8 0.0 collective-permute-done.7.rd
  22.8 0.9 %shard_map.108 = (f32[9,4,64,128]{3,2,1,0:T(8,128)S(1)}, bf16[384,256]{1,0:T(8,128)(2,1)S(1)}, bf16[384,512]{1,0:T(8,128)(2,1)S(1)}, f32[16,384]{1,0:T(8,128)S(1...) custom-call(f32[9,4,64,128]{3,2,1,0:T(8,128)S(1)} %get-tuple-element, ...), custom_call_target="tpu_custom_call", output_to_operand_aliasing={{0}: (0, {})} | custom-call | flops 100000000 | bytes 6000000 | tf_op jit(solution)/shard_map/pallas_call | solution.py:585
  23.7 2.8 %collective-permute-start.10 = (f32[16,384]{1,0:T(8,128)S(1)}, f32[16,384]{1,0:T(8,128)S(1)}, u32[]{:S(2)}, u32[]{:S(2)}) collective-permute-start(f32[16,384]{1,0:T(8,128)S(1)} %get-tuple-element.83), channel_id=1, source_target_pairs={{1,2},{3,4},{5,6},{7,8},{9,10},{11,12},{13,14},{15,0},{2,1},{4,3},... | collective-permute-start | bytes 73736 | tf_op jit(solution)/shard_map/ppermute | solution.py:562
  26.5 1.6 %collective-permute-start.8 = (f32[16,384]{1,0:T(8,128)S(1)}, f32[16,384]{1,0:T(8,128)S(1)}, u32[]{:S(2)}, u32[]{:S(2)}) collective-permute-start(f32[16,384]{1,0:T(8,128)S(1)} %get-tuple-element.81), channel_id=1, source_target_pairs={{16,32},{48,64},{80,96},{112,0},{32,16},{64,48},{96,80},{0,112},{1... | collective-permute-start | bytes 73736 | tf_op jit(solution)/shard_map/ppermute | solution.py:562
  28.1 0.1 select_reduce_fusion.keys_ref
  28.2 2.3 %shard_map.109 = (f32[9,4,64,128]{3,2,1,0:T(8,128)S(1)}, f32[384,384]{1,0:T(8,128)S(1)}, f32[9,4,64,128]{3,2,1,0:T(8,128)S(1)}) custom-call(f32[9,4,64,128]{3,2,1,0:T(8,128)S(1)} %get-tuple-element.75.v_ref, bf16[384,256]{1,0:T(8,128)(2,1)S(1)} %get-tuple-element.76.ty_ref, bf16[384,512]{1,0:T(8,128)(2,1)S(1)} %get-tuple-element.77.t_ref, ...), custom_call_target="tpu_custom_call" | custom-call | flops 100000000 | bytes 6000000 | tf_op jit(solution)/shard_map/pallas_call | solution.py:577
  30.5 0.4 collective-permute-done.10.rc
  30.9 0.0 collective-permute-done.11.rd
  30.9 0.0 collective-permute-done.8.ra
  30.9 0.0 collective-permute-done.9.rb
  30.9 0.9 %shard_map.110 = (f32[9,4,64,128]{3,2,1,0:T(8,128)S(1)}, bf16[384,256]{1,0:T(8,128)(2,1)S(1)}, bf16[384,512]{1,0:T(8,128)(2,1)S(1)}, f32[16,384]{1,0:T(8,128)S(1...) custom-call(f32[9,4,64,128]{3,2,1,0:T(8,128)S(1)} %get-tuple-element, ...), custom_call_target="tpu_custom_call", output_to_operand_aliasing={{0}: (0, {})} | custom-call | flops 100000000 | bytes 6000000 | tf_op jit(solution)/shard_map/pallas_call | solution.py:585
  31.8 2.8 %collective-permute-start.12 = (f32[16,384]{1,0:T(8,128)S(1)}, f32[16,384]{1,0:T(8,128)S(1)}, u32[]{:S(2)}, u32[]{:S(2)}) collective-permute-start(f32[16,384]{1,0:T(8,128)S(1)} %get-tuple-element.91), channel_id=1, source_target_pairs={{1,2},{3,4},{5,6},{7,8},{9,10},{11,12},{13,14},{15,0},{2,1},{4,3},... | collective-permute-start | bytes 73736 | tf_op jit(solution)/shard_map/ppermute | solution.py:562
  34.6 0.0 collective-permute-start.13
  34.6 0.6 %collective-permute-start.14 = (f32[16,384]{1,0:T(8,128)S(1)}, f32[16,384]{1,0:T(8,128)S(1)}, u32[]{:S(2)}, u32[]{:S(2)}) collective-permute-start(f32[16,384]{1,0:T(8,128)S(1)} %get-tuple-element.93), channel_id=1, source_target_pairs={{16,32},{48,64},{80,96},{112,0},{32,16},{64,48},{96,80},{0,112},{1... | collective-permute-start | bytes 73736 | tf_op jit(solution)/shard_map/ppermute | solution.py:562
  35.2 1.0 %collective-permute-start.15 = (f32[16,384]{1,0:T(8,128)S(1)}, f32[16,384]{1,0:T(8,128)S(1)}, u32[]{:S(2)}, u32[]{:S(2)}) collective-permute-start(f32[16,384]{1,0:T(8,128)S(1)} %get-tuple-element.94), channel_id=1, source_target_pairs={{0,16},{32,48},{64,80},{96,112},{16,0},{48,32},{80,64},{112,96},{1... | collective-permute-start | bytes 73736 | tf_op jit(solution)/shard_map/ppermute | solution.py:562
  36.2 0.1 add_bitcast_fusion.place_ref
  36.3 2.0 %shard_map.111 = (f32[9,4,64,128]{3,2,1,0:T(8,128)S(1)}, f32[384,384]{1,0:T(8,128)S(1)}) custom-call(f32[9,4,64,128]{3,2,1,0:T(8,128)S(1)} %get-tuple-element.85.v_ref, bf16[384,256]{1,0:T(8,128)(2,1)S(1)} %get-tuple-element.86.ty_ref, bf16[384,512]{1,0:T(8,128)(2,1)S(1)} %get-tuple-element.87.t_ref, bf16[256,384]{1,0:T(8,128)(2,1)S(1)} %get-tuple-element.67.local_y_ref, ...), custom_call_target="tpu_custom_call" | custom-call | flops 100000000 | bytes 6000000 | tf_op jit(solution)/shard_map/pallas_call | solution.py:581
  38.3 0.8 %collective-permute-done.12.ra = f32[16,384]{1,0:T(8,128)S(1)} collective-permute-done((f32[16,384]{1,0:T(8,128)S(1)}, f32[16,384]{1,0:T(8,128)S(1)}, u32[]{:S(2)}, u32[]{:S(2)}) %collective-permute-start.12) | collective-permute-done | bytes 24608 | tf_op jit(solution)/shard_map/ppermute | solution.py:562
  39.0 0.0 collective-permute-done.13.rb
  39.0 0.0 collective-permute-done.14.rc
  39.1 3.1 %shard_map.112 = (f32[9,4,64,128]{3,2,1,0:T(8,128)S(1)}, f32[9,4,8,128]{3,2,1,0:T(8,128)S(1)}, f32[16,2,9,4,128]{4,3,2,1,0:T(4,128)}) custom-call(s32[8]{0:T(128)S(1)} %select_reduce_fusion.keys_ref, f32[9,4,64,128]{3,2,1,0:T(8,128)S(1)} %get-tuple-element.89.vol_ref, f32[384,384]{1,0:T(8,128)S(1)} %get-tuple-element.90.part_ref, ...), custom_call_target="tpu_custom_call", output_to_operand_aliasing={{0}: (1, {})} | custom-call | flops 100000000 | bytes 6000000 | tf_op jit(solution)/shard_map/pallas_call | solution.py:594
  42.2 0.0 copy-start.7
  42.2 5.7 %all-to-all-start = ((f32[16,2,9,4,128]{4,3,2,1,0:T(4,128)}), f32[16,2,9,4,128]{4,3,2,1,0:T(4,128)S(1)}, u32[]{:S(2)}, u32[]{:S(2)}) async-start(f32[16,2,9,4,128]{4,3,2,1,0:T(4,128)} %get-tuple-element.99), calls=%async_computation | async-start | bytes 1179648 | tf_op jit(solution)/shard_map/all_to_all | solution.py:611
  47.9 0.1 convert_reduce_fusion.1
  48.0 3.8 %shard_map.113 = (f32[9,64,512]{2,1,0:T(8,128)}, f32[9,8,512]{2,1,0:T(8,128)S(1)}) custom-call(s32[2,8]{1,0:T(2,128)S(1)} %pad_add_fusion.table_ref, f32[9,4,64,128]{3,2,1,0:T(8,128)S(1)} %get-tuple-element.95.total_ref, f32[9,4,8,128]{3,2,1,0:T(8,128)S(1)} %get-tuple-element.96.groups_ref), custom_call_target="tpu_custom_call" | custom-call | flops 100000000 | bytes 6000000 | tf_op jit(solution)/shard_map/pallas_call | solution.py:612
  51.7 7.8 %all-to-all-done.arrived_ref = f32[16,2,9,4,128]{4,3,2,1,0:T(4,128)S(1)} async-done(((f32[16,2,9,4,128]{4,3,2,1,0:T(4,128)}), f32[16,2,9,4,128]{4,3,2,1,0:T(4,128)S(1)}, u32[]{:S(2)}, u32[]{:S(2)}) %all-to-all-start) | async-done | bytes 589856 | tf_op jit(solution)/shard_map/all_to_all | solution.py:611
  59.5 1.3 %shard_map.114 = f32[9,8,512]{2,1,0:T(8,128)} custom-call(s32[2,8]{1,0:T(2,128)S(1)} %pad_add_fusion.table_ref, f32[9,8,512]{2,1,0:T(8,128)S(1)} %get-tuple-element.98.home_ref, f32[16,2,9,4,128]{4,3,2,1,0:T(4,128)S(1)} %all-to-all-done.arrived_ref), custom_call_target="tpu_custom_call" | custom-call | flops 100000000 | bytes 6000000 | tf_op jit(solution)/shard_map/pallas_call | solution.py:615
  (27 shorter events, 0.1 us)
Async XLA Ops:
  0.6 1.4 %copy-start.6 = (f32[3,64]{1,0:T(4,128)S(1)}, f32[3,64]{1,0:T(4,128)}, u32[]{:S(2)}) copy-start(f32[3,64]{1,0:T(4,128)} %param.10) | copy-start | bytes 2308
  0.6 1.4 %copy-start.5 = (s32[1,4,16]{2,1,0:T(4,128)S(1)}, s32[1,4,16]{2,1,0:T(4,128)}, u32[]{:S(2)}) copy-start(s32[1,4,16]{2,1,0:T(4,128)} %param.12) | copy-start | bytes 772
  2.0 10.2 %copy-start.4 = (s32[3,64]{1,0:T(4,128)S(1)}, s32[3,64]{1,0:T(4,128)}, u32[]{:S(2)}) copy-start(s32[3,64]{1,0:T(4,128)} %param.13) | copy-start | bytes 2308
  2.0 10.2 %copy-start.3 = (s32[64,6]{0,1:T(8,128)S(1)}, s32[64,6]{0,1:T(8,128)}, u32[]{:S(2)}) copy-start(s32[64,6]{0,1:T(8,128)} %param.11) | copy-start | bytes 4612
  3.6 10.8 %collective-permute-start = (f32[16,384]{1,0:T(8,128)S(1)}, f32[16,384]{1,0:T(8,128)S(1)}, u32[]{:S(2)}, u32[]{:S(2)}) collective-permute-start(f32[16,384]{1,0:T(8,128)S(1)} %get-tuple-element.57), channel_id=1, source_target_pairs={{1,2},{3,4},{5,6},{7,8},{9,10},{11,12},{13,14},{15,0},{2,1},{4,3},... | collective-permute-start | bytes 73736 | tf_op jit(solution)/shard_map/ppermute | solution.py:562
  10.3 4.2 %collective-permute-start.1 = (f32[16,384]{1,0:T(8,128)S(1)}, f32[16,384]{1,0:T(8,128)S(1)}, u32[]{:S(2)}, u32[]{:S(2)}) collective-permute-start(f32[16,384]{1,0:T(8,128)S(1)} %get-tuple-element.58), channel_id=1, source_target_pairs={{0,1},{2,3},{4,5},{6,7},{8,9},{10,11},{12,13},{14,15},{1,0},{3,2},... | collective-permute-start | bytes 73736 | tf_op jit(solution)/shard_map/ppermute | solution.py:562
  10.3 4.5 %collective-permute-start.2 = (f32[16,384]{1,0:T(8,128)S(1)}, f32[16,384]{1,0:T(8,128)S(1)}, u32[]{:S(2)}, u32[]{:S(2)}) collective-permute-start(f32[16,384]{1,0:T(8,128)S(1)} %get-tuple-element.59), channel_id=1, source_target_pairs={{16,32},{48,64},{80,96},{112,0},{32,16},{64,48},{96,80},{0,112},{1... | collective-permute-start | bytes 73736 | tf_op jit(solution)/shard_map/ppermute | solution.py:562
  12.2 2.5 %collective-permute-start.3 = (f32[16,384]{1,0:T(8,128)S(1)}, f32[16,384]{1,0:T(8,128)S(1)}, u32[]{:S(2)}, u32[]{:S(2)}) collective-permute-start(f32[16,384]{1,0:T(8,128)S(1)} %get-tuple-element.60), channel_id=1, source_target_pairs={{0,16},{32,48},{64,80},{96,112},{16,0},{48,32},{80,64},{112,96},{1... | collective-permute-start | bytes 73736 | tf_op jit(solution)/shard_map/ppermute | solution.py:562
  15.6 7.2 %collective-permute-start.4 = (f32[16,384]{1,0:T(8,128)S(1)}, f32[16,384]{1,0:T(8,128)S(1)}, u32[]{:S(2)}, u32[]{:S(2)}) collective-permute-start(f32[16,384]{1,0:T(8,128)S(1)} %get-tuple-element.71), channel_id=1, source_target_pairs={{1,2},{3,4},{5,6},{7,8},{9,10},{11,12},{13,14},{15,0},{2,1},{4,3},... | collective-permute-start | bytes 73736 | tf_op jit(solution)/shard_map/ppermute | solution.py:562
  18.4 4.5 %collective-permute-start.5 = (f32[16,384]{1,0:T(8,128)S(1)}, f32[16,384]{1,0:T(8,128)S(1)}, u32[]{:S(2)}, u32[]{:S(2)}) collective-permute-start(f32[16,384]{1,0:T(8,128)S(1)} %get-tuple-element.72), channel_id=1, source_target_pairs={{0,1},{2,3},{4,5},{6,7},{8,9},{10,11},{12,13},{14,15},{1,0},{3,2},... | collective-permute-start | bytes 73736 | tf_op jit(solution)/shard_map/ppermute | solution.py:562
  18.4 4.5 %collective-permute-start.6 = (f32[16,384]{1,0:T(8,128)S(1)}, f32[16,384]{1,0:T(8,128)S(1)}, u32[]{:S(2)}, u32[]{:S(2)}) collective-permute-start(f32[16,384]{1,0:T(8,128)S(1)} %get-tuple-element.73), channel_id=1, source_target_pairs={{16,32},{48,64},{80,96},{112,0},{32,16},{64,48},{96,80},{0,112},{1... | collective-permute-start | bytes 73736 | tf_op jit(solution)/shard_map/ppermute | solution.py:562
  19.1 3.7 %collective-permute-start.7 = (f32[16,384]{1,0:T(8,128)S(1)}, f32[16,384]{1,0:T(8,128)S(1)}, u32[]{:S(2)}, u32[]{:S(2)}) collective-permute-start(f32[16,384]{1,0:T(8,128)S(1)} %get-tuple-element.74), channel_id=1, source_target_pairs={{0,16},{32,48},{64,80},{96,112},{16,0},{48,32},{80,64},{112,96},{1... | collective-permute-start | bytes 73736 | tf_op jit(solution)/shard_map/ppermute | solution.py:562
  23.7 7.2 %collective-permute-start.10 = (f32[16,384]{1,0:T(8,128)S(1)}, f32[16,384]{1,0:T(8,128)S(1)}, u32[]{:S(2)}, u32[]{:S(2)}) collective-permute-start(f32[16,384]{1,0:T(8,128)S(1)} %get-tuple-element.83), channel_id=1, source_target_pairs={{1,2},{3,4},{5,6},{7,8},{9,10},{11,12},{13,14},{15,0},{2,1},{4,3},... | collective-permute-start | bytes 73736 | tf_op jit(solution)/shard_map/ppermute | solution.py:562
  26.5 4.5 %collective-permute-start.11 = (f32[16,384]{1,0:T(8,128)S(1)}, f32[16,384]{1,0:T(8,128)S(1)}, u32[]{:S(2)}, u32[]{:S(2)}) collective-permute-start(f32[16,384]{1,0:T(8,128)S(1)} %get-tuple-element.84), channel_id=1, source_target_pairs={{0,1},{2,3},{4,5},{6,7},{8,9},{10,11},{12,13},{14,15},{1,0},{3,2},... | collective-permute-start | bytes 73736 | tf_op jit(solution)/shard_map/ppermute | solution.py:562
  26.5 4.5 %collective-permute-start.8 = (f32[16,384]{1,0:T(8,128)S(1)}, f32[16,384]{1,0:T(8,128)S(1)}, u32[]{:S(2)}, u32[]{:S(2)}) collective-permute-start(f32[16,384]{1,0:T(8,128)S(1)} %get-tuple-element.81), channel_id=1, source_target_pairs={{16,32},{48,64},{80,96},{112,0},{32,16},{64,48},{96,80},{0,112},{1... | collective-permute-start | bytes 73736 | tf_op jit(solution)/shard_map/ppermute | solution.py:562
  28.1 2.9 %collective-permute-start.9 = (f32[16,384]{1,0:T(8,128)S(1)}, f32[16,384]{1,0:T(8,128)S(1)}, u32[]{:S(2)}, u32[]{:S(2)}) collective-permute-start(f32[16,384]{1,0:T(8,128)S(1)} %get-tuple-element.82), channel_id=1, source_target_pairs={{0,16},{32,48},{64,80},{96,112},{16,0},{48,32},{80,64},{112,96},{1... | collective-permute-start | bytes 73736 | tf_op jit(solution)/shard_map/ppermute | solution.py:562
  31.8 7.2 %collective-permute-start.12 = (f32[16,384]{1,0:T(8,128)S(1)}, f32[16,384]{1,0:T(8,128)S(1)}, u32[]{:S(2)}, u32[]{:S(2)}) collective-permute-start(f32[16,384]{1,0:T(8,128)S(1)} %get-tuple-element.91), channel_id=1, source_target_pairs={{1,2},{3,4},{5,6},{7,8},{9,10},{11,12},{13,14},{15,0},{2,1},{4,3},... | collective-permute-start | bytes 73736 | tf_op jit(solution)/shard_map/ppermute | solution.py:562
  34.6 4.5 %collective-permute-start.13 = (f32[16,384]{1,0:T(8,128)S(1)}, f32[16,384]{1,0:T(8,128)S(1)}, u32[]{:S(2)}, u32[]{:S(2)}) collective-permute-start(f32[16,384]{1,0:T(8,128)S(1)} %get-tuple-element.92), channel_id=1, source_target_pairs={{0,1},{2,3},{4,5},{6,7},{8,9},{10,11},{12,13},{14,15},{1,0},{3,2},... | collective-permute-start | bytes 73736 | tf_op jit(solution)/shard_map/ppermute | solution.py:562
  34.6 4.5 %collective-permute-start.14 = (f32[16,384]{1,0:T(8,128)S(1)}, f32[16,384]{1,0:T(8,128)S(1)}, u32[]{:S(2)}, u32[]{:S(2)}) collective-permute-start(f32[16,384]{1,0:T(8,128)S(1)} %get-tuple-element.93), channel_id=1, source_target_pairs={{16,32},{48,64},{80,96},{112,0},{32,16},{64,48},{96,80},{0,112},{1... | collective-permute-start | bytes 73736 | tf_op jit(solution)/shard_map/ppermute | solution.py:562
  35.2 3.8 %collective-permute-start.15 = (f32[16,384]{1,0:T(8,128)S(1)}, f32[16,384]{1,0:T(8,128)S(1)}, u32[]{:S(2)}, u32[]{:S(2)}) collective-permute-start(f32[16,384]{1,0:T(8,128)S(1)} %get-tuple-element.94), channel_id=1, source_target_pairs={{0,16},{32,48},{64,80},{96,112},{16,0},{48,32},{80,64},{112,96},{1... | collective-permute-start | bytes 73736 | tf_op jit(solution)/shard_map/ppermute | solution.py:562
  36.3 2.8 %copy-start = (f32[64,8,128]{2,1,0:T(8,128)S(1)}, f32[64,8,128]{2,1,0:T(8,128)}, u32[]{:S(2)}) copy-start(f32[64,8,128]{2,1,0:T(8,128)} %constant.24.clone.lines_ref) | copy-start | bytes 786436
  36.3 2.8 %copy-start.1 = (bf16[256,128]{1,0:T(8,128)(2,1)S(1)}, bf16[256,128]{1,0:T(8,128)(2,1)}, u32[]{:S(2)}) copy-start(bf16[256,128]{1,0:T(8,128)(2,1)} %constant.22.clone.wa_ref) | copy-start | bytes 196612
  36.3 2.8 %copy-start.2 = (bf16[256,128]{1,0:T(8,128)(2,1)S(1)}, bf16[256,128]{1,0:T(8,128)(2,1)}, u32[]{:S(2)}) copy-start(bf16[256,128]{1,0:T(8,128)(2,1)} %constant.23.clone.wb_ref) | copy-start | bytes 196612
  42.2 5.8 %copy-start.7 = (s32[2,8]{1,0:T(2,128)S(1)}, s32[2,8]{1,0:T(2,128)}, u32[]{:S(2)}) copy-start(s32[2,8]{1,0:T(2,128)} %param.14) | copy-start | bytes 196
  42.2 17.3 %all-to-all-start = ((f32[16,2,9,4,128]{4,3,2,1,0:T(4,128)}), f32[16,2,9,4,128]{4,3,2,1,0:T(4,128)S(1)}, u32[]{:S(2)}, u32[]{:S(2)}) async-start(f32[16,2,9,4,128]{4,3,2,1,0:T(4,128)} %get-tuple-element.99), calls=%async_computation | async-start | bytes 1179648 | tf_op jit(solution)/shard_map/all_to_all | solution.py:611

commit v9 on v7

--- a/solution.py
+++ b/solution.py
@@ -383,8 +383,8 @@
 ):
     add_faces(part_ref, in_order(order, (ra, rb, rc, rd)), remote_ref, factor, v_ref, face_ref)
     build_table(v_ref, materials(mat_ref), ty_ref, (1,))
+    build_table(v_ref, materials(mat_ref), t_ref, (0, 2))
     send_values(send_y_ref, ty_ref, (p2, p3))
-    build_table(v_ref, materials(mat_ref), t_ref, (0, 2))
     send_values(send_x_ref, t_ref, (p0, p1))
 
 

time: 61.2 us -> 61.2 us (level)
  no operation moved by 1% of the time
where the time goes in v9:
time: 61.2 us; the launch traced here: 60.9 us
  starting transfers between devices  27.4 us (45%)
  Pallas kernels  20.3 us (33%)
  waiting for transfers between devices  10.5 us (17%)
  local copies, waits for them, and re-layouts  1.4 us (2%)
  between operations  0.85 us (1%)
    ppermute x16, starting transfers between devices, shards(): arrived = [lax.ppermute(out_going[k], *pairs[k]) for k in order]  21.7 us
    all_to_all x1, waiting for transfers between devices, shards(): lax.all_to_all(away, 'seg', split_axis=0, concat_axis=0, tiled=True)  8.44 us
    all_to_all x1, starting transfers between devices, shards(): lax.all_to_all(away, 'seg', split_axis=0, concat_axis=0, tiled=True)  5.66 us
    pallas_call x2, Pallas kernels, shards(): call(functools.partial(volume_kernel, factor), [state, face_part, state],...  4.5 us
    pallas_call x1, Pallas kernels, shards(): call(next_kernel, [shape(9, E_DEV, NODES)], [turn], count=1)(total)[0]  3.1 us
    pallas_call x1, Pallas kernels, shards(): call(functools.partial(end_kernel, factor, order), [state, shape(9, 4, P_...  3.09 us
    pallas_call x3, Pallas kernels, shards(): call(functools.partial(finish_kernel, factor, order), [state, table_y, ta...  2.6 us
    ppermute x16, waiting for transfers between devices, shards(): arrived = [lax.ppermute(out_going[k], *pairs[k]) for k in order]  2.11 us
  transfers between devices with their start and end apart: 17, of which 5 were waited for; matrix products, arithmetic and copies ran while one was open for 1% of the time, Pallas kernels for 19%

profile of v9, /device:TPU:0, one launch (start us, length us, event | category | flops | bytes accessed | tf_op | source)
XLA Modules:
  0.0 60.9 jit_solution(13053450740121798600)
XLA Ops:
  0.6 1.4 %fusion.2 = (f32[3,64,512]{2,1,0:T(8,128)S(1)}, f32[3,64,512]{2,1,0:T(8,128)S(1)}, f32[3,64,512]{2,1,0:T(8,128)S(1)}) fusion(f32[9,64,512]{2,1,0:T(8,128)} %param.9), kind=kLoop, calls=%fused_computation.18 | loop fusion | bytes 2359296 | tf_op jit(solution)/shard_map/slice | solution.py:551
  2.0 0.0 copy-start.4
  2.0 0.0 copy-start.3
  2.1 1.5 %shard_map.104 = (f32[9,4,64,128]{3,2,1,0:T(8,128)S(1)}, bf16[384,256]{1,0:T(8,128)(2,1)S(1)}, bf16[384,512]{1,0:T(8,128)(2,1)S(1)}, f32[3,8,128]{2,1,0:T(8,128)...) custom-call(f32[1,8,128]{2,1,0:T(8,128)S(1)} %convert_add_fusion.pac, ...), custom_call_target="tpu_custom_call" | custom-call | flops 100000000 | bytes 6000000 | tf_op jit(solution)/shard_map/pallas_call | solution.py:546
  3.6 6.6 %collective-permute-start = (f32[16,384]{1,0:T(8,128)S(1)}, f32[16,384]{1,0:T(8,128)S(1)}, u32[]{:S(2)}, u32[]{:S(2)}) collective-permute-start(f32[16,384]{1,0:T(8,128)S(1)} %get-tuple-element.55), channel_id=1, source_target_pairs={{1,2},{3,4},{5,6},{7,8},{9,10},{11,12},{13,14},{15,0},{2,1},{4,3},... | collective-permute-start | bytes 73736 | tf_op jit(solution)/shard_map/ppermute | solution.py:558
  10.3 0.0 collective-permute-start.1
  10.3 1.9 %collective-permute-start.2 = (f32[16,384]{1,0:T(8,128)S(1)}, f32[16,384]{1,0:T(8,128)S(1)}, u32[]{:S(2)}, u32[]{:S(2)}) collective-permute-start(f32[16,384]{1,0:T(8,128)S(1)} %get-tuple-element.57), channel_id=1, source_target_pairs={{16,32},{48,64},{80,96},{112,0},{32,16},{64,48},{96,80},{0,112},{1... | collective-permute-start | bytes 73736 | tf_op jit(solution)/shard_map/ppermute | solution.py:558
  12.2 0.0 collective-permute-start.3
  12.3 0.1 convert_reduce_fusion
  12.4 2.1 %shard_map.105 = (f32[9,4,64,128]{3,2,1,0:T(8,128)S(1)}, f32[384,384]{1,0:T(8,128)S(1)}, bf16[256,384]{1,0:T(8,128)(2,1)S(1)}, bf16[512,384]{1,0:T(8,128)(2,1)S(1)}, bf16[128,384]{1,0:T(8,128)(2,1)S(1)}) custom-call(f32[8,128]{1,0:T(8,128)S(1)} %pad.10.faces_ref, f32[9,4,64,128]{3,2,1,0:T(8,128)S(1)} %get-tuple-element.49.v_ref.acc_ref, ...), custom_call_target="tpu_custom_call" | custom-call | flops 100000000 | bytes 6000000 | tf_op jit(solution)/shard_map/pallas_call | solution.py:560
  14.4 0.0 collective-permute-done.ra
  14.5 0.0 collective-permute-done.1.rb
  14.5 0.3 collective-permute-done.2.rc
  14.7 0.0 collective-permute-done.3.rd
  14.7 0.9 %shard_map.106 = (f32[9,4,64,128]{3,2,1,0:T(8,128)S(1)}, bf16[384,256]{1,0:T(8,128)(2,1)S(1)}, bf16[384,512]{1,0:T(8,128)(2,1)S(1)}, f32[16,384]{1,0:T(8,128)S(1...) custom-call(f32[9,4,64,128]{3,2,1,0:T(8,128)S(1)} %get-tuple-element, ...), custom_call_target="tpu_custom_call", output_to_operand_aliasing={{0}: (0, {})} | custom-call | flops 100000000 | bytes 6000000 | tf_op jit(solution)/shard_map/pallas_call | solution.py:581
  15.6 2.8 %collective-permute-start.4 = (f32[16,384]{1,0:T(8,128)S(1)}, f32[16,384]{1,0:T(8,128)S(1)}, u32[]{:S(2)}, u32[]{:S(2)}) collective-permute-start(f32[16,384]{1,0:T(8,128)S(1)} %get-tuple-element.69), channel_id=1, source_target_pairs={{1,2},{3,4},{5,6},{7,8},{9,10},{11,12},{13,14},{15,0},{2,1},{4,3},... | collective-permute-start | bytes 73736 | tf_op jit(solution)/shard_map/ppermute | solution.py:558
  18.4 0.8 %collective-permute-start.6 = (f32[16,384]{1,0:T(8,128)S(1)}, f32[16,384]{1,0:T(8,128)S(1)}, u32[]{:S(2)}, u32[]{:S(2)}) collective-permute-start(f32[16,384]{1,0:T(8,128)S(1)} %get-tuple-element.71), channel_id=1, source_target_pairs={{16,32},{48,64},{80,96},{112,0},{32,16},{64,48},{96,80},{0,112},{1... | collective-permute-start | bytes 73736 | tf_op jit(solution)/shard_map/ppermute | solution.py:558
  19.1 0.8 %collective-permute-start.7 = (f32[16,384]{1,0:T(8,128)S(1)}, f32[16,384]{1,0:T(8,128)S(1)}, u32[]{:S(2)}, u32[]{:S(2)}) collective-permute-start(f32[16,384]{1,0:T(8,128)S(1)} %get-tuple-element.72), channel_id=1, source_target_pairs={{0,16},{32,48},{64,80},{96,112},{16,0},{48,32},{80,64},{112,96},{1... | collective-permute-start | bytes 73736 | tf_op jit(solution)/shard_map/ppermute | solution.py:558
  20.0 2.2 %shard_map.107 = (f32[9,4,64,128]{3,2,1,0:T(8,128)S(1)}, f32[384,384]{1,0:T(8,128)S(1)}, f32[9,4,64,128]{3,2,1,0:T(8,128)S(1)}) custom-call(f32[9,4,64,128]{3,2,1,0:T(8,128)S(1)} %get-tuple-element.62.v_ref, bf16[384,256]{1,0:T(8,128)(2,1)S(1)} %get-tuple-element.63.ty_ref, bf16[384,512]{1,0:T(8,128)(2,1)S(1)} %get-tuple-element.64.t_ref, ...), custom_call_target="tpu_custom_call" | custom-call | flops 100000000 | bytes 6000000 | tf_op jit(solution)/shard_map/pallas_call | solution.py:573
  22.2 0.6 %collective-permute-done.4.ra = f32[16,384]{1,0:T(8,128)S(1)} collective-permute-done((f32[16,384]{1,0:T(8,128)S(1)}, f32[16,384]{1,0:T(8,128)S(1)}, u32[]{:S(2)}, u32[]{:S(2)}) %collective-permute-start.4) | collective-permute-done | bytes 24608 | tf_op jit(solution)/shard_map/ppermute | solution.py:558
  22.8 0.0 collective-permute-done.6.rc
  22.8 0.0 collective-permute-done.7.rd
  22.8 0.9 %shard_map.108 = (f32[9,4,64,128]{3,2,1,0:T(8,128)S(1)}, bf16[384,256]{1,0:T(8,128)(2,1)S(1)}, bf16[384,512]{1,0:T(8,128)(2,1)S(1)}, f32[16,384]{1,0:T(8,128)S(1...) custom-call(f32[9,4,64,128]{3,2,1,0:T(8,128)S(1)} %get-tuple-element, ...), custom_call_target="tpu_custom_call", output_to_operand_aliasing={{0}: (0, {})} | custom-call | flops 100000000 | bytes 6000000 | tf_op jit(solution)/shard_map/pallas_call | solution.py:581
  23.7 2.8 %collective-permute-start.10 = (f32[16,384]{1,0:T(8,128)S(1)}, f32[16,384]{1,0:T(8,128)S(1)}, u32[]{:S(2)}, u32[]{:S(2)}) collective-permute-start(f32[16,384]{1,0:T(8,128)S(1)} %get-tuple-element.81), channel_id=1, source_target_pairs={{1,2},{3,4},{5,6},{7,8},{9,10},{11,12},{13,14},{15,0},{2,1},{4,3},... | collective-permute-start | bytes 73736 | tf_op jit(solution)/shard_map/ppermute | solution.py:558
  26.5 1.6 %collective-permute-start.8 = (f32[16,384]{1,0:T(8,128)S(1)}, f32[16,384]{1,0:T(8,128)S(1)}, u32[]{:S(2)}, u32[]{:S(2)}) collective-permute-start(f32[16,384]{1,0:T(8,128)S(1)} %get-tuple-element.79), channel_id=1, source_target_pairs={{16,32},{48,64},{80,96},{112,0},{32,16},{64,48},{96,80},{0,112},{1... | collective-permute-start | bytes 73736 | tf_op jit(solution)/shard_map/ppermute | solution.py:558
  28.1 0.1 select_reduce_fusion.keys_ref
  28.2 2.3 %shard_map.109 = (f32[9,4,64,128]{3,2,1,0:T(8,128)S(1)}, f32[384,384]{1,0:T(8,128)S(1)}, f32[9,4,64,128]{3,2,1,0:T(8,128)S(1)}) custom-call(f32[9,4,64,128]{3,2,1,0:T(8,128)S(1)} %get-tuple-element.73.v_ref, bf16[384,256]{1,0:T(8,128)(2,1)S(1)} %get-tuple-element.74.ty_ref, bf16[384,512]{1,0:T(8,128)(2,1)S(1)} %get-tuple-element.75.t_ref, ...), custom_call_target="tpu_custom_call" | custom-call | flops 100000000 | bytes 6000000 | tf_op jit(solution)/shard_map/pallas_call | solution.py:573
  30.5 0.4 collective-permute-done.10.rc
  30.9 0.0 collective-permute-done.11.rd
  30.9 0.0 collective-permute-done.8.ra
  30.9 0.0 collective-permute-done.9.rb
  30.9 0.9 %shard_map.110 = (f32[9,4,64,128]{3,2,1,0:T(8,128)S(1)}, bf16[384,256]{1,0:T(8,128)(2,1)S(1)}, bf16[384,512]{1,0:T(8,128)(2,1)S(1)}, f32[16,384]{1,0:T(8,128)S(1...) custom-call(f32[9,4,64,128]{3,2,1,0:T(8,128)S(1)} %get-tuple-element, ...), custom_call_target="tpu_custom_call", output_to_operand_aliasing={{0}: (0, {})} | custom-call | flops 100000000 | bytes 6000000 | tf_op jit(solution)/shard_map/pallas_call | solution.py:581
  31.8 2.8 %collective-permute-start.12 = (f32[16,384]{1,0:T(8,128)S(1)}, f32[16,384]{1,0:T(8,128)S(1)}, u32[]{:S(2)}, u32[]{:S(2)}) collective-permute-start(f32[16,384]{1,0:T(8,128)S(1)} %get-tuple-element.89), channel_id=1, source_target_pairs={{1,2},{3,4},{5,6},{7,8},{9,10},{11,12},{13,14},{15,0},{2,1},{4,3},... | collective-permute-start | bytes 73736 | tf_op jit(solution)/shard_map/ppermute | solution.py:558
  34.6 0.0 collective-permute-start.13
  34.6 0.6 %collective-permute-start.14 = (f32[16,384]{1,0:T(8,128)S(1)}, f32[16,384]{1,0:T(8,128)S(1)}, u32[]{:S(2)}, u32[]{:S(2)}) collective-permute-start(f32[16,384]{1,0:T(8,128)S(1)} %get-tuple-element.91), channel_id=1, source_target_pairs={{16,32},{48,64},{80,96},{112,0},{32,16},{64,48},{96,80},{0,112},{1... | collective-permute-start | bytes 73736 | tf_op jit(solution)/shard_map/ppermute | solution.py:558
  35.2 1.0 %collective-permute-start.15 = (f32[16,384]{1,0:T(8,128)S(1)}, f32[16,384]{1,0:T(8,128)S(1)}, u32[]{:S(2)}, u32[]{:S(2)}) collective-permute-start(f32[16,384]{1,0:T(8,128)S(1)} %get-tuple-element.92), channel_id=1, source_target_pairs={{0,16},{32,48},{64,80},{96,112},{16,0},{48,32},{80,64},{112,96},{1... | collective-permute-start | bytes 73736 | tf_op jit(solution)/shard_map/ppermute | solution.py:558
  36.2 0.1 add_bitcast_fusion.place_ref
  36.3 2.0 %shard_map.111 = (f32[9,4,64,128]{3,2,1,0:T(8,128)S(1)}, f32[384,384]{1,0:T(8,128)S(1)}) custom-call(f32[9,4,64,128]{3,2,1,0:T(8,128)S(1)} %get-tuple-element.83.v_ref, bf16[384,256]{1,0:T(8,128)(2,1)S(1)} %get-tuple-element.84.ty_ref, bf16[384,512]{1,0:T(8,128)(2,1)S(1)} %get-tuple-element.85.t_ref, bf16[256,384]{1,0:T(8,128)(2,1)S(1)} %get-tuple-element.65.local_y_ref, ...), custom_call_target="tpu_custom_call" | custom-call | flops 100000000 | bytes 6000000 | tf_op jit(solution)/shard_map/pallas_call | solution.py:577
  38.3 0.8 %collective-permute-done.12.ra = f32[16,384]{1,0:T(8,128)S(1)} collective-permute-done((f32[16,384]{1,0:T(8,128)S(1)}, f32[16,384]{1,0:T(8,128)S(1)}, u32[]{:S(2)}, u32[]{:S(2)}) %collective-permute-start.12) | collective-permute-done | bytes 24608 | tf_op jit(solution)/shard_map/ppermute | solution.py:558
  39.0 0.0 collective-permute-done.13.rb
  39.0 0.0 collective-permute-done.14.rc
  39.1 3.1 %shard_map.112 = (f32[9,4,64,128]{3,2,1,0:T(8,128)S(1)}, f32[9,4,8,128]{3,2,1,0:T(8,128)S(1)}, f32[16,2,9,4,128]{4,3,2,1,0:T(4,128)}) custom-call(s32[8]{0:T(128)S(1)} %select_reduce_fusion.keys_ref, f32[9,4,64,128]{3,2,1,0:T(8,128)S(1)} %get-tuple-element.87.vol_ref, f32[384,384]{1,0:T(8,128)S(1)} %get-tuple-element.88.part_ref, ...), custom_call_target="tpu_custom_call", output_to_operand_aliasing={{0}: (1, {})} | custom-call | flops 100000000 | bytes 6000000 | tf_op jit(solution)/shard_map/pallas_call | solution.py:590
  42.2 0.0 copy-start.7
  42.2 5.7 %all-to-all-start = ((f32[16,2,9,4,128]{4,3,2,1,0:T(4,128)}), f32[16,2,9,4,128]{4,3,2,1,0:T(4,128)S(1)}, u32[]{:S(2)}, u32[]{:S(2)}) async-start(f32[16,2,9,4,128]{4,3,2,1,0:T(4,128)} %get-tuple-element.95), calls=%async_computation | async-start | bytes 1179648 | tf_op jit(solution)/shard_map/all_to_all | solution.py:607
  47.9 0.1 convert_reduce_fusion.1
  48.0 3.1 %shard_map.113 = f32[9,64,512]{2,1,0:T(8,128)} custom-call(f32[9,4,64,128]{3,2,1,0:T(8,128)S(1)} %get-tuple-element.93.total_ref), custom_call_target="tpu_custom_call" | custom-call | flops 100000000 | bytes 6000000 | tf_op jit(solution)/shard_map/pallas_call | solution.py:608
  51.1 8.4 %all-to-all-done.arrived_ref = f32[16,2,9,4,128]{4,3,2,1,0:T(4,128)S(1)} async-done(((f32[16,2,9,4,128]{4,3,2,1,0:T(4,128)}), f32[16,2,9,4,128]{4,3,2,1,0:T(4,128)S(1)}, u32[]{:S(2)}, u32[]{:S(2)}) %all-to-all-start) | async-done | bytes 589856 | tf_op jit(solution)/shard_map/all_to_all | solution.py:607
  59.5 1.4 %shard_map.114 = f32[9,8,512]{2,1,0:T(8,128)} custom-call(s32[2,8]{1,0:T(2,128)S(1)} %pad_add_fusion.table_ref, f32[9,4,8,128]{3,2,1,0:T(8,128)S(1)} %get-tuple-element.94.groups_ref, f32[16,2,9,4,128]{4,3,2,1,0:T(4,128)S(1)} %all-to-all-done.arrived_ref), custom_call_target="tpu_custom_call" | custom-call | flops 100000000 | bytes 6000000 | tf_op jit(solution)/shard_map/pallas_call | solution.py:609
  (27 shorter events, 0.1 us)
Async XLA Ops:
  0.6 1.4 %copy-start.6 = (f32[3,64]{1,0:T(4,128)S(1)}, f32[3,64]{1,0:T(4,128)}, u32[]{:S(2)}) copy-start(f32[3,64]{1,0:T(4,128)} %param.10) | copy-start | bytes 2308
  0.6 1.4 %copy-start.5 = (s32[1,4,16]{2,1,0:T(4,128)S(1)}, s32[1,4,16]{2,1,0:T(4,128)}, u32[]{:S(2)}) copy-start(s32[1,4,16]{2,1,0:T(4,128)} %param.12) | copy-start | bytes 772
  2.0 10.2 %copy-start.4 = (s32[3,64]{1,0:T(4,128)S(1)}, s32[3,64]{1,0:T(4,128)}, u32[]{:S(2)}) copy-start(s32[3,64]{1,0:T(4,128)} %param.13) | copy-start | bytes 2308
  2.0 10.2 %copy-start.3 = (s32[64,6]{0,1:T(8,128)S(1)}, s32[64,6]{0,1:T(8,128)}, u32[]{:S(2)}) copy-start(s32[64,6]{0,1:T(8,128)} %param.11) | copy-start | bytes 4612
  3.6 10.8 %collective-permute-start = (f32[16,384]{1,0:T(8,128)S(1)}, f32[16,384]{1,0:T(8,128)S(1)}, u32[]{:S(2)}, u32[]{:S(2)}) collective-permute-start(f32[16,384]{1,0:T(8,128)S(1)} %get-tuple-element.55), channel_id=1, source_target_pairs={{1,2},{3,4},{5,6},{7,8},{9,10},{11,12},{13,14},{15,0},{2,1},{4,3},... | collective-permute-start | bytes 73736 | tf_op jit(solution)/shard_map/ppermute | solution.py:558
  10.3 4.2 %collective-permute-start.1 = (f32[16,384]{1,0:T(8,128)S(1)}, f32[16,384]{1,0:T(8,128)S(1)}, u32[]{:S(2)}, u32[]{:S(2)}) collective-permute-start(f32[16,384]{1,0:T(8,128)S(1)} %get-tuple-element.56), channel_id=1, source_target_pairs={{0,1},{2,3},{4,5},{6,7},{8,9},{10,11},{12,13},{14,15},{1,0},{3,2},... | collective-permute-start | bytes 73736 | tf_op jit(solution)/shard_map/ppermute | solution.py:558
  10.3 4.5 %collective-permute-start.2 = (f32[16,384]{1,0:T(8,128)S(1)}, f32[16,384]{1,0:T(8,128)S(1)}, u32[]{:S(2)}, u32[]{:S(2)}) collective-permute-start(f32[16,384]{1,0:T(8,128)S(1)} %get-tuple-element.57), channel_id=1, source_target_pairs={{16,32},{48,64},{80,96},{112,0},{32,16},{64,48},{96,80},{0,112},{1... | collective-permute-start | bytes 73736 | tf_op jit(solution)/shard_map/ppermute | solution.py:558
  12.2 2.5 %collective-permute-start.3 = (f32[16,384]{1,0:T(8,128)S(1)}, f32[16,384]{1,0:T(8,128)S(1)}, u32[]{:S(2)}, u32[]{:S(2)}) collective-permute-start(f32[16,384]{1,0:T(8,128)S(1)} %get-tuple-element.58), channel_id=1, source_target_pairs={{0,16},{32,48},{64,80},{96,112},{16,0},{48,32},{80,64},{112,96},{1... | collective-permute-start | bytes 73736 | tf_op jit(solution)/shard_map/ppermute | solution.py:558
  15.6 7.2 %collective-permute-start.4 = (f32[16,384]{1,0:T(8,128)S(1)}, f32[16,384]{1,0:T(8,128)S(1)}, u32[]{:S(2)}, u32[]{:S(2)}) collective-permute-start(f32[16,384]{1,0:T(8,128)S(1)} %get-tuple-element.69), channel_id=1, source_target_pairs={{1,2},{3,4},{5,6},{7,8},{9,10},{11,12},{13,14},{15,0},{2,1},{4,3},... | collective-permute-start | bytes 73736 | tf_op jit(solution)/shard_map/ppermute | solution.py:558
  18.4 4.5 %collective-permute-start.5 = (f32[16,384]{1,0:T(8,128)S(1)}, f32[16,384]{1,0:T(8,128)S(1)}, u32[]{:S(2)}, u32[]{:S(2)}) collective-permute-start(f32[16,384]{1,0:T(8,128)S(1)} %get-tuple-element.70), channel_id=1, source_target_pairs={{0,1},{2,3},{4,5},{6,7},{8,9},{10,11},{12,13},{14,15},{1,0},{3,2},... | collective-permute-start | bytes 73736 | tf_op jit(solution)/shard_map/ppermute | solution.py:558
  18.4 4.5 %collective-permute-start.6 = (f32[16,384]{1,0:T(8,128)S(1)}, f32[16,384]{1,0:T(8,128)S(1)}, u32[]{:S(2)}, u32[]{:S(2)}) collective-permute-start(f32[16,384]{1,0:T(8,128)S(1)} %get-tuple-element.71), channel_id=1, source_target_pairs={{16,32},{48,64},{80,96},{112,0},{32,16},{64,48},{96,80},{0,112},{1... | collective-permute-start | bytes 73736 | tf_op jit(solution)/shard_map/ppermute | solution.py:558
  19.1 3.7 %collective-permute-start.7 = (f32[16,384]{1,0:T(8,128)S(1)}, f32[16,384]{1,0:T(8,128)S(1)}, u32[]{:S(2)}, u32[]{:S(2)}) collective-permute-start(f32[16,384]{1,0:T(8,128)S(1)} %get-tuple-element.72), channel_id=1, source_target_pairs={{0,16},{32,48},{64,80},{96,112},{16,0},{48,32},{80,64},{112,96},{1... | collective-permute-start | bytes 73736 | tf_op jit(solution)/shard_map/ppermute | solution.py:558
  23.7 7.2 %collective-permute-start.10 = (f32[16,384]{1,0:T(8,128)S(1)}, f32[16,384]{1,0:T(8,128)S(1)}, u32[]{:S(2)}, u32[]{:S(2)}) collective-permute-start(f32[16,384]{1,0:T(8,128)S(1)} %get-tuple-element.81), channel_id=1, source_target_pairs={{1,2},{3,4},{5,6},{7,8},{9,10},{11,12},{13,14},{15,0},{2,1},{4,3},... | collective-permute-start | bytes 73736 | tf_op jit(solution)/shard_map/ppermute | solution.py:558
  26.5 4.5 %collective-permute-start.11 = (f32[16,384]{1,0:T(8,128)S(1)}, f32[16,384]{1,0:T(8,128)S(1)}, u32[]{:S(2)}, u32[]{:S(2)}) collective-permute-start(f32[16,384]{1,0:T(8,128)S(1)} %get-tuple-element.82), channel_id=1, source_target_pairs={{0,1},{2,3},{4,5},{6,7},{8,9},{10,11},{12,13},{14,15},{1,0},{3,2},... | collective-permute-start | bytes 73736 | tf_op jit(solution)/shard_map/ppermute | solution.py:558
  26.5 4.5 %collective-permute-start.8 = (f32[16,384]{1,0:T(8,128)S(1)}, f32[16,384]{1,0:T(8,128)S(1)}, u32[]{:S(2)}, u32[]{:S(2)}) collective-permute-start(f32[16,384]{1,0:T(8,128)S(1)} %get-tuple-element.79), channel_id=1, source_target_pairs={{16,32},{48,64},{80,96},{112,0},{32,16},{64,48},{96,80},{0,112},{1... | collective-permute-start | bytes 73736 | tf_op jit(solution)/shard_map/ppermute | solution.py:558
  28.1 2.9 %collective-permute-start.9 = (f32[16,384]{1,0:T(8,128)S(1)}, f32[16,384]{1,0:T(8,128)S(1)}, u32[]{:S(2)}, u32[]{:S(2)}) collective-permute-start(f32[16,384]{1,0:T(8,128)S(1)} %get-tuple-element.80), channel_id=1, source_target_pairs={{0,16},{32,48},{64,80},{96,112},{16,0},{48,32},{80,64},{112,96},{1... | collective-permute-start | bytes 73736 | tf_op jit(solution)/shard_map/ppermute | solution.py:558
  31.8 7.2 %collective-permute-start.12 = (f32[16,384]{1,0:T(8,128)S(1)}, f32[16,384]{1,0:T(8,128)S(1)}, u32[]{:S(2)}, u32[]{:S(2)}) collective-permute-start(f32[16,384]{1,0:T(8,128)S(1)} %get-tuple-element.89), channel_id=1, source_target_pairs={{1,2},{3,4},{5,6},{7,8},{9,10},{11,12},{13,14},{15,0},{2,1},{4,3},... | collective-permute-start | bytes 73736 | tf_op jit(solution)/shard_map/ppermute | solution.py:558
  34.6 4.5 %collective-permute-start.13 = (f32[16,384]{1,0:T(8,128)S(1)}, f32[16,384]{1,0:T(8,128)S(1)}, u32[]{:S(2)}, u32[]{:S(2)}) collective-permute-start(f32[16,384]{1,0:T(8,128)S(1)} %get-tuple-element.90), channel_id=1, source_target_pairs={{0,1},{2,3},{4,5},{6,7},{8,9},{10,11},{12,13},{14,15},{1,0},{3,2},... | collective-permute-start | bytes 73736 | tf_op jit(solution)/shard_map/ppermute | solution.py:558
  34.6 4.5 %collective-permute-start.14 = (f32[16,384]{1,0:T(8,128)S(1)}, f32[16,384]{1,0:T(8,128)S(1)}, u32[]{:S(2)}, u32[]{:S(2)}) collective-permute-start(f32[16,384]{1,0:T(8,128)S(1)} %get-tuple-element.91), channel_id=1, source_target_pairs={{16,32},{48,64},{80,96},{112,0},{32,16},{64,48},{96,80},{0,112},{1... | collective-permute-start | bytes 73736 | tf_op jit(solution)/shard_map/ppermute | solution.py:558
  35.2 3.8 %collective-permute-start.15 = (f32[16,384]{1,0:T(8,128)S(1)}, f32[16,384]{1,0:T(8,128)S(1)}, u32[]{:S(2)}, u32[]{:S(2)}) collective-permute-start(f32[16,384]{1,0:T(8,128)S(1)} %get-tuple-element.92), channel_id=1, source_target_pairs={{0,16},{32,48},{64,80},{96,112},{16,0},{48,32},{80,64},{112,96},{1... | collective-permute-start | bytes 73736 | tf_op jit(solution)/shard_map/ppermute | solution.py:558
  36.3 2.8 %copy-start = (f32[64,8,128]{2,1,0:T(8,128)S(1)}, f32[64,8,128]{2,1,0:T(8,128)}, u32[]{:S(2)}) copy-start(f32[64,8,128]{2,1,0:T(8,128)} %constant.24.clone.lines_ref) | copy-start | bytes 786436
  36.3 2.8 %copy-start.1 = (bf16[256,128]{1,0:T(8,128)(2,1)S(1)}, bf16[256,128]{1,0:T(8,128)(2,1)}, u32[]{:S(2)}) copy-start(bf16[256,128]{1,0:T(8,128)(2,1)} %constant.22.clone.wa_ref) | copy-start | bytes 196612
  36.3 2.8 %copy-start.2 = (bf16[256,128]{1,0:T(8,128)(2,1)S(1)}, bf16[256,128]{1,0:T(8,128)(2,1)}, u32[]{:S(2)}) copy-start(bf16[256,128]{1,0:T(8,128)(2,1)} %constant.23.clone.wb_ref) | copy-start | bytes 196612
  42.2 5.8 %copy-start.7 = (s32[2,8]{1,0:T(2,128)S(1)}, s32[2,8]{1,0:T(2,128)}, u32[]{:S(2)}) copy-start(s32[2,8]{1,0:T(2,128)} %param.14) | copy-start | bytes 196
  42.2 17.3 %all-to-all-start = ((f32[16,2,9,4,128]{4,3,2,1,0:T(4,128)}), f32[16,2,9,4,128]{4,3,2,1,0:T(4,128)S(1)}, u32[]{:S(2)}, u32[]{:S(2)}) async-start(f32[16,2,9,4,128]{4,3,2,1,0:T(4,128)} %get-tuple-element.95), calls=%async_computation | async-start | bytes 1179648 | tf_op jit(solution)/shard_map/all_to_all | solution.py:607
